TPU v7x, 32 devices: a whole 2x2x4 slice. The times are simulated.
32 devices in a mesh: dp: 8 (over z, x), head: 4 (over y, core).
Axes of the slice: x: 2, y: 2, z: 4, core: 2. Of those that a mesh axis runs over, the one named last changes fastest.
Arguments:
- series: bfloat16 [16384, 96], P(('dp', 'head')), may hold values from -6 to 6
- cotangent: float32 [16384, 512], P(('dp', 'head')), may hold values from -6 to 6
- window_lengths: int32 [16, 16], P('dp'), may hold values from 0 to 862, as said below
- owner_list: int32 [4, 96], P('head'), may hold values from 0 to 95, as said below
- master: float32 [4, 96, 128, 128], P('head', 'dp'), may hold values from -0.70710678 to 0.70710678
- first_moment: float32 [4, 96, 128, 128], P('head', 'dp'), may hold values from -320 to 320
- second_moment: float32 [4, 96, 128, 128], P('head', 'dp'), may hold values from 2621.44 to 10485.76
- left_stats: float32 [4, 96, 128, 128], P('head', 'dp'), may hold values from -2097.152 to 1342177.3, as said below
- right_stats: float32 [4, 96, 128, 128], P('head', 'dp'), may hold values from -2097.152 to 1342177.3, as said below
- left_basis: float32 [4, 96, 128, 128], P('head', 'dp'), may hold values from -1 to 1, as said below
- right_basis: float32 [4, 96, 128, 128], P('head', 'dp'), may hold values from -1 to 1, as said below
- vec_values: float32 [121, 512], replicated, may hold values from -1.2 to 1.4
- vec_first: float32 [121, 512], replicated, may hold values from -448 to 448
- vec_second: float32 [121, 512], replicated, may hold values from 5898.24 to 23592.96
Outputs:
- activations: float32 [16384, 512], P(('dp', 'head'))
- input_grad: float32 [16384, 96], P(('dp', 'head'))
- new_master: float32 [4, 96, 128, 128], P('head', 'dp')
- new_copy: bfloat16 [4, 96, 128, 128], P('head', 'dp')
- new_first: float32 [4, 96, 128, 128], P('head', 'dp')
- new_second: float32 [4, 96, 128, 128], P('head', 'dp')
- new_left_stats: float32 [4, 96, 128, 128], P('head', 'dp')
- new_right_stats: float32 [4, 96, 128, 128], P('head', 'dp')
- new_left_basis: float32 [4, 96, 128, 128], P('head', 'dp')
- new_right_basis: float32 [4, 96, 128, 128], P('head', 'dp')
- vec_new_values: float32 [121, 512], replicated
- vec_new_first: float32 [121, 512], replicated
- vec_new_second: float32 [121, 512], replicated
- branch_bias_grads: float32 [4, 512], replicated
Inputs may be any that keep to these rules, and one draw needn't show every extreme that they name: `window_lengths`: each row lists the variate counts of the windows packed into one bucket of 1024 rows, in order: nonzero entries come first, each 8 or more, and they sum to at most 1024; zeros mark unused slots. Some entry equals 862. `owner_list`: the entries of a row are distinct; slot s belongs to the device of index s // 12 along dp, and in each row some device owns 12 blocks. `left_stats`: each block is symmetric and positive definite. `right_stats`: each block is symmetric and positive definite. `left_basis`: each block is orthogonal. `right_basis`: each block is orthogonal.
All inputs are finite; a program needn't handle non-finite values.
Results may differ from a plain program's by a relative error of at most 0.03.
Values may be sent and summed in bfloat16 or wider, within the bound.
No kernel may reach another device: no remote copies, remote signals or barrier semaphores. Data moves between devices by JAX's collectives and lax.ppermute only.
A program may use at most 192 MiB of HBM per device.

v0:
```python
import jax
import jax.numpy as jnp
from jax import lax
from jax.sharding import PartitionSpec as P

D = 512
HEADS = 8
HD = 64
FF = 2048
LOOK = 96
LAYERS = 2
BLK = 128
STEP = 10


top_precision = lax.Precision.HIGHEST
norm_eps = 1e-05
beta_first = 0.5
beta_second = 0.5
beta_stats = 0.5
adam_eps = 1e-08
rate_matrix = 0.02
rate_vector = 0.15
weight_decay = 0.01
mask_fill = -1e30


def assemble(pieces, row_count, col_count):
    return (
        pieces.reshape(row_count, col_count, BLK, BLK)
        .transpose(0, 2, 1, 3)
        .reshape(row_count * BLK, col_count * BLK)
    )


def split_blocks(matrix):
    row_count = matrix.shape[0] // BLK
    col_count = matrix.shape[1] // BLK
    return (
        matrix.reshape(row_count, BLK, col_count, BLK)
        .transpose(0, 2, 1, 3)
        .reshape(row_count * col_count, BLK, BLK)
    )


def window_ids(lengths, bucket_rows):
    bounds = jnp.cumsum(lengths, axis=1, dtype=jnp.int32)
    places = jnp.arange(bucket_rows, dtype=jnp.int32)
    return jnp.sum(
        (places[None, :, None] >= bounds[:, None, :]).astype(jnp.int32), axis=2, dtype=jnp.int32
    )


def normalize_forward(resid, gain_vec, shift_vec):
    center = resid - jnp.mean(resid, axis=-1, keepdims=True)
    scale_inv = lax.rsqrt(jnp.mean(center * center, axis=-1, keepdims=True) + norm_eps)
    unit_rows = center * scale_inv
    return (unit_rows * gain_vec + shift_vec, unit_rows, scale_inv)


def normalize_backward(grad_in, unit_rows, scale_inv, gain_vec):
    grad_unit = grad_in * gain_vec
    grad_resid = scale_inv * (
        grad_unit
        - jnp.mean(grad_unit, axis=-1, keepdims=True)
        - unit_rows * jnp.mean(grad_unit * unit_rows, axis=-1, keepdims=True)
    )
    return (grad_resid, jnp.sum(grad_in * unit_rows, axis=0), jnp.sum(grad_in, axis=0))


def gelu_exact(values):
    return jax.nn.gelu(values, approximate=False)


def gelu_slope(values):
    result, pullback = jax.vjp(gelu_exact, values)
    return pullback(jnp.ones_like(values))[0]


def own_matrices(blocks_all, layer_at, width_head, ff_head):
    per_layer = blocks_all.shape[0] // LAYERS
    count_qkv = D // BLK * (3 * width_head // BLK)
    count_out = width_head // BLK * (D // BLK)
    count_up = D // BLK * (ff_head // BLK)
    pieces = blocks_all[layer_at * per_layer : (layer_at + 1) * per_layer]
    return (
        assemble(pieces[:count_qkv], D // BLK, 3 * width_head // BLK),
        assemble(pieces[count_qkv : count_qkv + count_out], width_head // BLK, D // BLK),
        assemble(
            pieces[count_qkv + count_out : count_qkv + count_out + count_up],
            D // BLK,
            ff_head // BLK,
        ),
        assemble(pieces[count_qkv + count_out + count_up :], ff_head // BLK, D // BLK),
    )


def depth_vectors(vec_table, layer_at):
    ff_ratio = FF // D
    base_row = LOOK + 1 + layer_at * (8 + ff_ratio)
    return (
        vec_table[base_row],
        vec_table[base_row + 1],
        vec_table[base_row + 2],
        vec_table[base_row + 3],
        vec_table[base_row + 4],
        vec_table[base_row + 5 : base_row + 5 + ff_ratio].reshape(FF),
        vec_table[base_row + 5 + ff_ratio],
        vec_table[base_row + 6 + ff_ratio],
        vec_table[base_row + 7 + ff_ratio],
    )


def attend_forward(operands):
    query_rows, key_rows, value_rows, window_row = operands
    scores = jnp.einsum(
        "qhd,khd->hqk", query_rows, key_rows, preferred_element_type=jnp.float32
    ) * HD ** (-0.5)
    joined = window_row[:, None] == window_row[None, :]
    scores = jnp.where(joined[None], scores, mask_fill)
    highest = jnp.max(scores, axis=-1, keepdims=True)
    exp_scores = jnp.exp(scores - highest)
    row_totals = jnp.sum(exp_scores, axis=-1, keepdims=True)
    weights = exp_scores / row_totals
    mixed = jnp.einsum(
        "hqk,khd->qhd", weights.astype(jnp.bfloat16), value_rows, preferred_element_type=jnp.float32
    )
    return (mixed.astype(jnp.bfloat16), (highest + jnp.log(row_totals))[..., 0])


def attend_backward(operands):
    query_rows, key_rows, value_rows, window_row, log_total, grad_mixed = operands
    scores = jnp.einsum(
        "qhd,khd->hqk", query_rows, key_rows, preferred_element_type=jnp.float32
    ) * HD ** (-0.5)
    joined = window_row[:, None] == window_row[None, :]
    weights = jnp.where(joined[None], jnp.exp(scores - log_total[..., None]), 0.0)
    grad_weights = jnp.einsum(
        "qhd,khd->hqk", grad_mixed, value_rows, preferred_element_type=jnp.float32
    )
    inner_sum = jnp.sum(weights * grad_weights, axis=-1, keepdims=True)
    grad_scores = (weights * (grad_weights - inner_sum)).astype(jnp.bfloat16)
    grad_query = jnp.einsum(
        "hqk,khd->qhd", grad_scores, key_rows, preferred_element_type=jnp.float32
    ) * HD ** (-0.5)
    grad_key = jnp.einsum(
        "hqk,qhd->khd", grad_scores, query_rows, preferred_element_type=jnp.float32
    ) * HD ** (-0.5)
    grad_value = jnp.einsum(
        "hqk,qhd->khd", weights.astype(jnp.bfloat16), grad_mixed, preferred_element_type=jnp.float32
    )
    return (
        grad_query.astype(jnp.bfloat16),
        grad_key.astype(jnp.bfloat16),
        grad_value.astype(jnp.bfloat16),
    )


def layer_forward(residual, matrices, vectors, windows, head_place, width_head, ff_head):
    joint_w, out_w, up_w, down_w = matrices
    query_b, value_b, out_b, gain_one, shift_one, up_b, down_b, gain_two, shift_two = vectors
    inputs = residual.astype(jnp.bfloat16)
    gathered = lax.all_gather(inputs, "head", axis=0, tiled=True)
    joint = jnp.dot(gathered, joint_w, preferred_element_type=jnp.float32)
    query_rows = (
        joint[:, :width_head]
        + lax.dynamic_slice_in_dim(query_b, head_place * width_head, width_head)
    ).astype(jnp.bfloat16)
    key_rows = joint[:, width_head : 2 * width_head].astype(jnp.bfloat16)
    value_rows = (
        joint[:, 2 * width_head :]
        + lax.dynamic_slice_in_dim(value_b, head_place * width_head, width_head)
    ).astype(jnp.bfloat16)
    shape_four = (windows.shape[0], windows.shape[1], width_head // HD, HD)
    mixed, log_total = lax.map(
        attend_forward,
        (
            query_rows.reshape(shape_four),
            key_rows.reshape(shape_four),
            value_rows.reshape(shape_four),
            windows,
        ),
    )
    mixed = mixed.reshape(-1, width_head)
    attended = lax.psum_scatter(
        jnp.dot(mixed, out_w, preferred_element_type=jnp.float32).astype(jnp.bfloat16),
        "head",
        scatter_dimension=0,
        tiled=True,
    ).astype(jnp.float32)
    normed, unit_one, inv_one = normalize_forward(residual + attended + out_b, gain_one, shift_one)
    normed_low = normed.astype(jnp.bfloat16)
    normed_rows = lax.all_gather(normed_low, "head", axis=0, tiled=True)
    hidden_pre = jnp.dot(
        normed_rows, up_w, preferred_element_type=jnp.float32
    ) + lax.dynamic_slice_in_dim(up_b, head_place * ff_head, ff_head)
    hidden = gelu_exact(hidden_pre).astype(jnp.bfloat16)
    fed_out = lax.psum_scatter(
        jnp.dot(hidden, down_w, preferred_element_type=jnp.float32).astype(jnp.bfloat16),
        "head",
        scatter_dimension=0,
        tiled=True,
    ).astype(jnp.float32)
    ffn_kept = (normed_rows, up_w, down_w)
    result, unit_two, inv_two = normalize_forward(normed + fed_out + down_b, gain_two, shift_two)
    return (
        result,
        (
            inputs,
            query_rows,
            key_rows,
            value_rows,
            mixed,
            log_total,
            unit_one,
            inv_one,
            ffn_kept,
            hidden_pre,
            hidden,
            unit_two,
            inv_two,
        ),
    )


def layer_backward(grad_out, matrices, vectors, kept, windows, head_place, width_head, ff_head):
    joint_w, out_w, up_w, down_w = matrices
    query_b, value_b, out_b, gain_one, shift_one, up_b, down_b, gain_two, shift_two = vectors
    (
        rows_kept,
        query_rows,
        key_rows,
        value_rows,
        mixed,
        log_total,
        unit_one,
        inv_one,
        ffn_kept,
        hidden_pre,
        hidden,
        unit_two,
        inv_two,
    ) = kept
    grad_two, grad_gain_two, grad_shift_two = normalize_backward(
        grad_out, unit_two, inv_two, gain_two
    )
    grad_down_b = jnp.sum(grad_two, axis=0)
    grad_fed = grad_two.astype(jnp.bfloat16)
    normed_rows, up_kept, down_kept = ffn_kept
    grad_rows = lax.all_gather(grad_fed, "head", axis=0, tiled=True)
    grad_down = jnp.einsum("rf,rd->fd", hidden, grad_rows, preferred_element_type=jnp.float32)
    grad_hidden = jnp.einsum("rd,fd->rf", grad_rows, down_kept, preferred_element_type=jnp.float32)
    grad_pre = (grad_hidden * gelu_slope(hidden_pre)).astype(jnp.bfloat16)
    grad_up_b = lax.dynamic_update_slice_in_dim(
        jnp.zeros((FF,), jnp.float32),
        jnp.sum(grad_pre.astype(jnp.float32), axis=0),
        head_place * ff_head,
        0,
    )
    grad_up = jnp.einsum("rd,rf->df", normed_rows, grad_pre, preferred_element_type=jnp.float32)
    grad_normed = grad_two + lax.psum_scatter(
        jnp.einsum("rf,df->rd", grad_pre, up_kept, preferred_element_type=jnp.float32).astype(
            jnp.bfloat16
        ),
        "head",
        scatter_dimension=0,
        tiled=True,
    ).astype(jnp.float32)
    grad_one, grad_gain_one, grad_shift_one = normalize_backward(
        grad_normed, unit_one, inv_one, gain_one
    )
    grad_out_b = jnp.sum(grad_one, axis=0)
    grad_attended = lax.all_gather(grad_one.astype(jnp.bfloat16), "head", axis=0, tiled=True)
    grad_out_w = jnp.einsum("rh,rd->hd", mixed, grad_attended, preferred_element_type=jnp.float32)
    grad_mixed = jnp.einsum(
        "rd,hd->rh", grad_attended, out_w, preferred_element_type=jnp.float32
    ).astype(jnp.bfloat16)
    shape_four = (windows.shape[0], windows.shape[1], width_head // HD, HD)
    grad_query, grad_key, grad_value = lax.map(
        attend_backward,
        (
            query_rows.reshape(shape_four),
            key_rows.reshape(shape_four),
            value_rows.reshape(shape_four),
            windows,
            log_total,
            grad_mixed.reshape(shape_four),
        ),
    )
    grad_query = grad_query.reshape(-1, width_head)
    grad_key = grad_key.reshape(-1, width_head)
    grad_value = grad_value.reshape(-1, width_head)
    grad_joint = jnp.concatenate([grad_query, grad_key, grad_value], axis=1)
    gathered = lax.all_gather(rows_kept, "head", axis=0, tiled=True)
    grad_joint_w = jnp.einsum("rd,rc->dc", gathered, grad_joint, preferred_element_type=jnp.float32)
    grad_residual = grad_one + lax.psum_scatter(
        jnp.einsum("rc,dc->rd", grad_joint, joint_w, preferred_element_type=jnp.float32).astype(
            jnp.bfloat16
        ),
        "head",
        scatter_dimension=0,
        tiled=True,
    ).astype(jnp.float32)
    query_grad_b = lax.dynamic_update_slice_in_dim(
        jnp.zeros((D,), jnp.float32),
        jnp.sum(grad_query.astype(jnp.float32), axis=0),
        head_place * width_head,
        0,
    )
    value_grad_b = lax.dynamic_update_slice_in_dim(
        jnp.zeros((D,), jnp.float32),
        jnp.sum(grad_value.astype(jnp.float32), axis=0),
        head_place * width_head,
        0,
    )
    table_rows = jnp.concatenate(
        [
            query_grad_b[None],
            value_grad_b[None],
            grad_out_b[None],
            grad_gain_one[None],
            grad_shift_one[None],
            grad_up_b.reshape(FF // D, D),
            grad_down_b[None],
            grad_gain_two[None],
            grad_shift_two[None],
        ],
        axis=0,
    )
    return (grad_residual, (grad_joint_w, grad_out_w, grad_up, grad_down), table_rows)


def rotate(left_mat, mid_mat, right_mat):
    inner_prod = jnp.einsum("...ji,...jk->...ik", left_mat, mid_mat, precision=top_precision)
    return jnp.einsum("...ik,...kl->...il", inner_prod, right_mat, precision=top_precision)


def rotate_back(left_mat, mid_mat, right_mat):
    inner_prod = jnp.einsum("...ij,...jk->...ik", left_mat, mid_mat, precision=top_precision)
    return jnp.einsum("...ik,...lk->...il", inner_prod, right_mat, precision=top_precision)


def orthonormal(matrix):
    gram_mat = jnp.einsum("...ji,...jk->...ik", matrix, matrix, precision=top_precision)
    factor = jnp.linalg.cholesky(gram_mat)
    solved = jax.vmap(
        lambda lower_part, full_part: jax.scipy.linalg.solve_triangular(
            lower_part, full_part.T, lower=True
        )
    )(factor, matrix)
    return jnp.swapaxes(solved, 1, 2)


def soap_update(
    gradient, master, moment_one, moment_two, left_stats, right_stats, left_basis, right_basis
):
    turned = rotate(left_basis, gradient, right_basis)
    new_first = beta_first * moment_one + (1.0 - beta_first) * turned
    new_second = beta_second * moment_two + (1.0 - beta_second) * turned * turned
    step_ratio = (
        new_first
        / (1.0 - beta_first**STEP)
        / (jnp.sqrt(new_second / (1.0 - beta_second**STEP)) + adam_eps)
    )
    update = rotate_back(left_basis, step_ratio, right_basis)
    new_master = master - rate_matrix * (update + weight_decay * master)
    new_left = beta_stats * left_stats + (1.0 - beta_stats) * jnp.einsum(
        "...ik,...jk->...ij", gradient, gradient, precision=top_precision
    )
    new_right = beta_stats * right_stats + (1.0 - beta_stats) * jnp.einsum(
        "...ki,...kj->...ij", gradient, gradient, precision=top_precision
    )
    left_next = orthonormal(
        jnp.einsum("...ij,...jk->...ik", new_left, left_basis, precision=top_precision)
    )
    right_next = orthonormal(
        jnp.einsum("...ij,...jk->...ik", new_right, right_basis, precision=top_precision)
    )
    return (
        new_master,
        new_master.astype(jnp.bfloat16),
        new_first,
        new_second,
        new_left,
        new_right,
        left_next,
        right_next,
    )


def adamw_update(gradient, values, moment_one, moment_two):
    new_first = beta_first * moment_one + (1.0 - beta_first) * gradient
    new_second = beta_second * moment_two + (1.0 - beta_second) * gradient * gradient
    step_ratio = (
        new_first
        / (1.0 - beta_first**STEP)
        / (jnp.sqrt(new_second / (1.0 - beta_second**STEP)) + adam_eps)
    )
    new_values = values - rate_vector * (step_ratio + weight_decay * values)
    return (new_values, new_first, new_second)


def branch_biases(grad_table):
    ff_ratio = FF // D
    bias_rows = []
    for layer_at in range(LAYERS):
        base_row = LOOK + 1 + layer_at * (8 + ff_ratio)
        bias_rows.append(grad_table[base_row + 2])
        bias_rows.append(grad_table[base_row + 5 + ff_ratio])
    return jnp.stack(bias_rows, axis=0)


def on_device(
    series,
    cotangent,
    window_lengths,
    owner_list,
    master,
    first_moment,
    second_moment,
    left_stats,
    right_stats,
    left_basis,
    right_basis,
    vec_values,
    vec_first,
    vec_second,
):
    head_count = lax.axis_size("head")
    head_place = lax.axis_index("head")
    width_head = HD * HEADS // head_count
    ff_head = FF // head_count
    own_rows = series.shape[0]
    copies = master[0].astype(jnp.bfloat16)
    every_slot = lax.all_gather(copies, "dp", axis=0, tiled=True)
    owner_row = owner_list[0]
    blocks_all = jnp.take(every_slot, owner_row, axis=0)
    windows = window_ids(window_lengths, own_rows * head_count // window_lengths.shape[0])
    valid_all = (windows < window_lengths.shape[1]).reshape(-1)
    valid_rows = lax.dynamic_slice_in_dim(valid_all, head_place * own_rows, own_rows).astype(
        jnp.float32
    )[:, None]
    series_float = series.astype(jnp.float32)
    residual = jnp.dot(series_float, vec_values[:LOOK], precision=top_precision) + vec_values[LOOK]
    matrices = [
        own_matrices(blocks_all, layer_at, width_head, ff_head) for layer_at in range(LAYERS)
    ]
    saved = []
    for layer_at in range(LAYERS):
        residual, kept = layer_forward(
            residual,
            matrices[layer_at],
            depth_vectors(vec_values, layer_at),
            windows,
            head_place,
            width_head,
            ff_head,
        )
        saved.append(kept)
    activations = residual * valid_rows
    grad_residual = cotangent * valid_rows
    grad_mats = [None] * LAYERS
    grad_rows = [None] * LAYERS
    for layer_at in reversed(range(LAYERS)):
        grad_residual, grad_mats[layer_at], grad_rows[layer_at] = layer_backward(
            grad_residual,
            matrices[layer_at],
            depth_vectors(vec_values, layer_at),
            saved[layer_at],
            windows,
            head_place,
            width_head,
            ff_head,
        )
    grad_embed = jnp.dot(series_float.T, grad_residual, precision=top_precision)
    input_grad = jnp.dot(grad_residual, vec_values[:LOOK].T, precision=top_precision)
    local_table = jnp.concatenate(
        [grad_embed, jnp.sum(grad_residual, axis=0)[None]] + grad_rows, axis=0
    )
    grad_table = lax.psum(local_table, ("dp", "head"))
    pieces = jnp.concatenate(
        [split_blocks(matrix) for layer_at in range(LAYERS) for matrix in grad_mats[layer_at]],
        axis=0,
    )
    routed = jnp.zeros((every_slot.shape[0], BLK, BLK), jnp.float32).at[owner_row].set(pieces)
    owned = lax.psum_scatter(routed, "dp", scatter_dimension=0, tiled=True)
    new_master, new_copy, new_first, new_second, new_left, new_right, left_next, right_next = (
        soap_update(
            owned,
            master[0],
            first_moment[0],
            second_moment[0],
            left_stats[0],
            right_stats[0],
            left_basis[0],
            right_basis[0],
        )
    )
    vec_new_values, vec_new_first, vec_new_second = adamw_update(
        grad_table, vec_values, vec_first, vec_second
    )
    branch_bias_grads = branch_biases(grad_table)
    return (
        activations,
        input_grad,
        new_master[None],
        new_copy[None],
        new_first[None],
        new_second[None],
        new_left[None],
        new_right[None],
        left_next[None],
        right_next[None],
        vec_new_values,
        vec_new_first,
        vec_new_second,
        branch_bias_grads,
    )


def solution(mesh):
    placed = (
        P(("dp", "head"), None),
        P(("dp", "head"), None),
        P("dp", None),
        P("head", None),
        P("head", "dp", None, None),
        P("head", "dp", None, None),
        P("head", "dp", None, None),
        P("head", "dp", None, None),
        P("head", "dp", None, None),
        P("head", "dp", None, None),
        P("head", "dp", None, None),
        P(),
        P(),
        P(),
    )
    return jax.shard_map(
        on_device,
        mesh=mesh,
        in_specs=placed,
        out_specs=(
            P(("dp", "head"), None),
            P(("dp", "head"), None),
            P("head", "dp", None, None),
            P("head", "dp", None, None),
            P("head", "dp", None, None),
            P("head", "dp", None, None),
            P("head", "dp", None, None),
            P("head", "dp", None, None),
            P("head", "dp", None, None),
            P("head", "dp", None, None),
            P(),
            P(),
            P(),
            P(),
        ),
        check_vma=False,
    )
```

profile of v0, /device:TPU:0, one launch (start us, length us, event | category | flops | bytes accessed | tf_op | source)
XLA Modules:
  0.0 1621.4 jit_solution(3223368770535040304)
XLA Ops:
  16.3 57.7 %all-gather.12.cloned.1.call-done = bf16[96,128,128]{2,1,0:T(8,128)(2,1)} async-done(((bf16[12,128,128]{2,1,0:T(8,128)(2,1)}), bf16[96,128,128]{2,1,0:T(8,128)(2,1)}) %all-gather.12.cloned.1.call-update) | async-done | bytes 3145744 | tf_op jit(solution)/shard_map/all_gather | solution.py:435
  85.4 12.0 all-gather.10.cloned.1.call-done
  115.4 16.2 while.52
  139.5 31.5 %reduce-scatter.10.cloned.1.call-done = bf16[512,512]{0,1:T(8,128)(2,1)} async-done(((bf16[2048,512]{0,1:T(8,128)(2,1)}), bf16[512,512]{0,1:T(8,128)(2,1)}) %reduce-scatter.10.cloned.1.call-update) | async-done | bytes 524304 | tf_op jit(solution)/shard_map/reduce_scatter | solution.py:185
  179.2 17.7 %all-gather.14.cloned.1.call-done = bf16[2048,512]{0,1:T(8,128)(2,1)} async-done(((bf16[512,512]{0,1:T(8,128)(2,1)}), bf16[2048,512]{0,1:T(8,128)(2,1)}) %all-gather.14.cloned.1.call-update) | async-done | bytes 2097168 | tf_op jit(solution)/shard_map/all_gather | solution.py:193
  196.9 13.4 multiply_convert_fusion.5
  214.5 31.5 %reduce-scatter.12.cloned.1.call-done = bf16[512,512]{0,1:T(8,128)(2,1)} async-done(((bf16[2048,512]{0,1:T(8,128)(2,1)}), bf16[512,512]{0,1:T(8,128)(2,1)}) %reduce-scatter.12.cloned.1.call-update) | async-done | bytes 524304 | tf_op jit(solution)/shard_map/reduce_scatter | solution.py:198
  249.9 21.6 %all-gather.16.cloned.1.call-done = bf16[2048,512]{0,1:T(8,128)(2,1)} async-done(((bf16[512,512]{0,1:T(8,128)(2,1)}), bf16[2048,512]{0,1:T(8,128)(2,1)}) %all-gather.16.cloned.1.call-update) | async-done | bytes 2097168 | tf_op jit(solution)/shard_map/all_gather | solution.py:163
  290.4 17.3 %while.53 = (s32[]{:T(128)}, bf16[2,1024,2,64]{1,3,2,0:T(8,128)(2,1)}, f32[2,2,1024]{2,1,0:T(2,128)}, bf16[2,1024,2,64]{1,3,2,0:T(8,128)(2,1)S(1)}, s32[2,1024]{...) while((s32[]{:T(128)}, ...), condition=%wide.region_15.16_spmd, body=%wide.region_12.15_spmd.sunk | while | flops 563214336 | bytes 30489176 | solution.py:175
  312.7 31.5 %reduce-scatter.14.cloned.1.call-done = bf16[512,512]{0,1:T(8,128)(2,1)} async-done(((bf16[2048,512]{0,1:T(8,128)(2,1)}), bf16[512,512]{0,1:T(8,128)(2,1)}) %reduce-scatter.14.cloned.1.call-update) | async-done | bytes 524304 | tf_op jit(solution)/shard_map/reduce_scatter | solution.py:185
  351.1 19.2 %all-gather.18.cloned.1.call-done = bf16[2048,512]{0,1:T(8,128)(2,1)} async-done(((bf16[512,512]{0,1:T(8,128)(2,1)}), bf16[2048,512]{0,1:T(8,128)(2,1)}) %all-gather.18.cloned.1.call-update) | async-done | bytes 2097168 | tf_op jit(solution)/shard_map/all_gather | solution.py:193
  370.4 13.3 multiply_convert_fusion.4
  391.3 28.0 %reduce-scatter.16.cloned.1.call-done = bf16[512,512]{0,1:T(8,128)(2,1)} async-done(((bf16[2048,512]{0,1:T(8,128)(2,1)}), bf16[512,512]{0,1:T(8,128)(2,1)}) %reduce-scatter.16.cloned.1.call-update) | async-done | bytes 524304 | tf_op jit(solution)/shard_map/reduce_scatter | solution.py:198
  425.5 22.7 %all-gather.20.cloned.1.call-done = bf16[2048,512]{0,1:T(8,128)(2,1)} async-done(((bf16[512,512]{0,1:T(8,128)(2,1)}), bf16[2048,512]{0,1:T(8,128)(2,1)}) %all-gather.20.cloned.1.call-update) | async-done | bytes 2097168 | tf_op jit(solution)/shard_map/all_gather | solution.py:250
  448.1 7.5 convert_reduce_fusion
  459.9 31.3 %reduce-scatter.18.cloned.1.call-done = bf16[512,512]{0,1:T(8,128)(2,1)} async-done(((bf16[2048,512]{0,1:T(8,128)(2,1)}), bf16[512,512]{0,1:T(8,128)(2,1)}) %reduce-scatter.18.cloned.1.call-update) | async-done | bytes 524304 | tf_op jit(solution)/shard_map/reduce_scatter | solution.py:261
  496.1 22.7 %all-gather.22.cloned.1.call-done = bf16[2048,512]{0,1:T(8,128)(2,1)} async-done(((bf16[512,512]{0,1:T(8,128)(2,1)}), bf16[2048,512]{0,1:T(8,128)(2,1)}) %all-gather.22.cloned.1.call-update) | async-done | bytes 2097168 | tf_op jit(solution)/shard_map/all_gather | solution.py:273
  526.7 27.4 %while.54 = (s32[]{:T(128)}, bf16[2,1024,2,64]{1,3,2,0:T(8,128)(2,1)S(1)}, bf16[2,1024,2,64]{1,3,2,0:T(8,128)(2,1)}, bf16[2,1024,2,64]{1,3,2,0:T(8,128)(2,1)}, b...) while((s32[]{:T(128)}, ...), condition=%wide.region_29.30_spmd, body=%wide.region_27.29_spmd.sunk | while | flops 1375336448 | bytes 73999536 | solution.py:279
  562.3 31.5 %reduce-scatter.20.cloned.1.call-done = bf16[512,512]{0,1:T(8,128)(2,1)} async-done(((bf16[2048,512]{0,1:T(8,128)(2,1)}), bf16[512,512]{0,1:T(8,128)(2,1)}) %reduce-scatter.20.cloned.1.call-update) | async-done | bytes 524304 | tf_op jit(solution)/shard_map/reduce_scatter | solution.py:296
  598.7 22.7 %all-gather.24.cloned.1.call-done = bf16[2048,512]{0,1:T(8,128)(2,1)} async-done(((bf16[512,512]{0,1:T(8,128)(2,1)}), bf16[2048,512]{0,1:T(8,128)(2,1)}) %all-gather.24.cloned.1.call-update) | async-done | bytes 2097168 | tf_op jit(solution)/shard_map/all_gather | solution.py:250
  621.4 7.4 convert_reduce_fusion.1
  632.9 31.5 %reduce-scatter.22.cloned.1.call-done = bf16[512,512]{0,1:T(8,128)(2,1)} async-done(((bf16[2048,512]{0,1:T(8,128)(2,1)}), bf16[512,512]{0,1:T(8,128)(2,1)}) %reduce-scatter.22.cloned.1.call-update) | async-done | bytes 524304 | tf_op jit(solution)/shard_map/reduce_scatter | solution.py:261
  672.7 19.3 %all-gather.26.cloned.1.call-done = bf16[2048,512]{0,1:T(8,128)(2,1)} async-done(((bf16[512,512]{0,1:T(8,128)(2,1)}), bf16[2048,512]{0,1:T(8,128)(2,1)}) %all-gather.26.cloned.1.call-update) | async-done | bytes 2097168 | tf_op jit(solution)/shard_map/all_gather | solution.py:273
  700.1 25.6 %while.55 = (s32[]{:T(128)}, bf16[2,1024,2,64]{1,3,2,0:T(8,128)(2,1)S(1)}, bf16[2,1024,2,64]{1,3,2,0:T(8,128)(2,1)}, bf16[2,1024,2,64]{1,3,2,0:T(8,128)(2,1)}, b...) while((s32[]{:T(128)}, ...), condition=%wide.region_38.39_spmd, body=%wide.region_36.38_spmd.sunk | while | flops 1375336448 | bytes 74065096 | solution.py:279
  791.0 5.3 concatenate.15
  801.3 17.8 %scatter_fusion = f32[96,128,128]{2,1,0:T(8,128)} fusion(f32[96,128,128]{2,1,0:T(8,128)} %broadcast_in_dim.206, s32[96]{0:T(128)S(1)} %copy-done.100, f32[96,128,128]{2,1,0:T(8,128)} %constant_dynamic-update-slice_fusion.6), kind=kCustom, calls=%fused_computation.1 | custom fusion | bytes 18874752 | tf_op jit(solution)/shard_map/scatter | solution.py:485
  823.4 98.4 %all-reduce.2.cloned.1.call-done = f32[121,512]{1,0:T(8,128)} async-done(((f32[121,512]{1,0:T(8,128)}), f32[121,512]{1,0:T(8,128)}) %all-reduce.2.cloned.1.call-update) | async-done | bytes 247824 | tf_op jit(solution)/shard_map/psum | solution.py:480
  925.3 117.0 %reduce-scatter.26.cloned.1.call-done = f32[12,128,128]{2,1,0:T(8,128)} async-done(((f32[96,128,128]{2,1,0:T(8,128)}), f32[12,128,128]{2,1,0:T(8,128)}) %reduce-scatter.26.cloned.1.call-update) | async-done | bytes 786448 | tf_op jit(solution)/shard_map/reduce_scatter | solution.py:486
  1060.1 142.3 %custom-call.8 = f32[12,128,128]{2,1,0:T(8,128)} custom-call(f32[12,128,128]{2,1,0:T(8,128)} %fusion.149), custom_call_target="Cholesky" | custom-call | tf_op jit(solution)/shard_map/jit(cholesky)/cholesky | solution.py:345
  1213.7 142.3 %custom-call.10 = f32[12,128,128]{2,1,0:T(8,128)} custom-call(f32[12,128,128]{2,1,0:T(8,128)} %fusion.146), custom_call_target="Cholesky" | custom-call | tf_op jit(solution)/shard_map/jit(cholesky)/cholesky | solution.py:345
  1360.5 119.3 %custom-call.11 = f32[12,1,128,128]{2,3,1,0:T(8,128)} custom-call(f32[12,1,128,128]{3,2,1,0:T(8,128)} %get-tuple-element.658), custom_call_target="InvertDiagBlocksLowerTriangular" | custom-call | tf_op jit(solution)/shard_map/vmap(jit(_solve_triangular))/triangular_solve | solution.py:347
  1485.7 119.3 %custom-call.9 = f32[12,1,128,128]{2,3,1,0:T(8,128)} custom-call(f32[12,1,128,128]{3,2,1,0:T(8,128)} %get-tuple-element.659), custom_call_target="InvertDiagBlocksLowerTriangular" | custom-call | tf_op jit(solution)/shard_map/vmap(jit(_solve_triangular))/triangular_solve | solution.py:347
  (544 shorter events, 369.1 us)
Async XLA Ops:
  7.2 1035.2 %copy-start = (f32[1,12,128,128]{3,2,1,0:T(8,128)S(1)}, f32[1,12,128,128]{3,2,1,0:T(8,128)}, u32[]{:S(2)}) copy-start(f32[1,12,128,128]{3,2,1,0:T(8,128)} %param.34) | copy-start | bytes 2359300
  7.2 66.8 %all-gather.12.cloned.1.call-start = ((), (), s32[]{:S(2)}) async-start(), calls=%async_computation.10 | async-start | bytes 3538944 | tf_op jit(solution)/shard_map/all_gather | solution.py:435
  9.3 88.1 %all-gather.10.cloned.1.call-start = ((), (), s32[]{:S(2)}) async-start(), calls=%async_computation.9 | async-start | bytes 2621440 | tf_op jit(solution)/shard_map/all_gather | solution.py:163
  11.0 235.0 %copy-start.73 = (f32[1,512]{1,0:T(1,128)}, f32[1,512]{1,0:T(1,128)S(1)}, u32[]{:S(2)}) copy-start(f32[1,512]{1,0:T(1,128)S(1)} %get-tuple-element.650) | copy-start | bytes 6148
  13.4 157.6 %reduce-scatter.10.cloned.1.call-start = ((), (), s32[]{:S(2)}) async-start(), calls=%async_computation.11 | async-start | bytes 2621440 | tf_op jit(solution)/shard_map/reduce_scatter | solution.py:185
  131.6 39.5 %copy-start.6 = (bf16[2,1024,2,64]{1,3,2,0:T(8,128)(2,1)}, bf16[2,1024,2,64]{1,3,2,0:T(8,128)(2,1)S(1)}, u32[]{:S(2)}) copy-start(bf16[2,1024,2,64]{1,3,2,0:T(8,128)(2,1)S(1)} %get-tuple-element.1032) | copy-start | bytes 1572868
  131.6 39.5 %copy-start.8 = (bf16[2,1024,2,64]{1,3,2,0:T(8,128)(2,1)}, bf16[2,1024,2,64]{1,3,2,0:T(8,128)(2,1)S(1)}, u32[]{:S(2)}) copy-start(bf16[2,1024,2,64]{1,3,2,0:T(8,128)(2,1)S(1)} %get-tuple-element.1034) | copy-start | bytes 1572868
  131.6 40.7 %copy-start.20 = (bf16[2,1024,2,64]{1,3,2,0:T(8,128)(2,1)}, bf16[2,1024,2,64]{1,3,2,0:T(8,128)(2,1)S(1)}, u32[]{:S(2)}) copy-start(bf16[2,1024,2,64]{1,3,2,0:T(8,128)(2,1)S(1)} %get-tuple-element.1042) | copy-start | bytes 1572868
  139.5 57.5 %all-gather.14.cloned.1.call-start = ((), (), s32[]{:S(2)}) async-start(), calls=%async_computation.12 | async-start | bytes 2621440 | tf_op jit(solution)/shard_map/all_gather | solution.py:193
  172.3 73.7 %copy-start.1 = (f32[512,512]{0,1:T(8,128)}, f32[512,512]{0,1:T(8,128)S(1)}, u32[]{:S(2)}) copy-start(f32[512,512]{0,1:T(8,128)S(1)} %get-tuple-element.611) | copy-start | bytes 3145732
  172.3 73.7 %copy-start.69 = (f32[512]{0:T(512)}, f32[512]{0:T(512)S(1)}, u32[]{:S(2)}) copy-start(f32[512]{0:T(512)S(1)} %broadcast_multiply_fusion.11) | copy-start | bytes 6148
  174.2 71.8 %reduce-scatter.12.cloned.1.call-start = ((), (), s32[]{:S(2)}) async-start(), calls=%async_computation.13 | async-start | bytes 2621440 | tf_op jit(solution)/shard_map/reduce_scatter | solution.py:198
  214.5 57.0 %all-gather.16.cloned.1.call-start = ((), (), s32[]{:S(2)}) async-start(), calls=%async_computation.14 | async-start | bytes 2621440 | tf_op jit(solution)/shard_map/all_gather | solution.py:163
  247.5 96.8 %copy-start.3 = (f32[512,512]{0,1:T(8,128)}, f32[512,512]{0,1:T(8,128)S(1)}, u32[]{:S(2)}) copy-start(f32[512,512]{0,1:T(8,128)S(1)} %get-tuple-element.607) | copy-start | bytes 3145732
  247.5 96.8 %copy-start.71 = (f32[512]{0:T(512)}, f32[512]{0:T(512)S(1)}, u32[]{:S(2)}) copy-start(f32[512]{0:T(512)S(1)} %broadcast_multiply_fusion.10) | copy-start | bytes 6148
  248.7 95.5 %reduce-scatter.14.cloned.1.call-start = ((), (), s32[]{:S(2)}) async-start(), calls=%async_computation.15 | async-start | bytes 2621440 | tf_op jit(solution)/shard_map/reduce_scatter | solution.py:185
  307.7 36.6 %copy-start.76 = (f32[1,512]{1,0:T(1,128)S(1)}, f32[1,512]{1,0:T(1,128)}, u32[]{:S(2)}) copy-start(f32[1,512]{1,0:T(1,128)} %get-tuple-element.647) | copy-start | bytes 6148
  312.7 57.7 %all-gather.18.cloned.1.call-start = ((), (), s32[]{:S(2)}) async-start(), calls=%async_computation.16 | async-start | bytes 2621440 | tf_op jit(solution)/shard_map/all_gather | solution.py:193
  347.6 71.7 %reduce-scatter.16.cloned.1.call-start = ((), (), s32[]{:S(2)}) async-start(), calls=%async_computation.17 | async-start | bytes 2621440 | tf_op jit(solution)/shard_map/reduce_scatter | solution.py:198
  387.7 60.5 %all-gather.20.cloned.1.call-start = ((), (), s32[]{:S(2)}) async-start(), calls=%async_computation.18 | async-start | bytes 2621440 | tf_op jit(solution)/shard_map/all_gather | solution.py:250
  425.4 65.8 %reduce-scatter.18.cloned.1.call-start = ((), (), s32[]{:S(2)}) async-start(), calls=%async_computation.19 | async-start | bytes 2621440 | tf_op jit(solution)/shard_map/reduce_scatter | solution.py:261
  459.6 59.1 %all-gather.22.cloned.1.call-start = ((), (), s32[]{:S(2)}) async-start(), calls=%async_computation.20 | async-start | bytes 2621440 | tf_op jit(solution)/shard_map/all_gather | solution.py:273
  496.0 97.8 %reduce-scatter.20.cloned.1.call-start = ((), (), s32[]{:S(2)}) async-start(), calls=%async_computation.21 | async-start | bytes 2621440 | tf_op jit(solution)/shard_map/reduce_scatter | solution.py:296
  562.2 59.1 %copy-start.102 = (f32[512]{0:T(512)S(1)}, f32[512]{0:T(512)}, u32[]{:S(2)}) copy-start(f32[512]{0:T(512)} %copy-done.101) | copy-start | bytes 6148
  562.2 59.1 %all-gather.24.cloned.1.call-start = ((), (), s32[]{:S(2)}) async-start(), calls=%async_computation.22 | async-start | bytes 2621440 | tf_op jit(solution)/shard_map/all_gather | solution.py:250
  598.6 65.8 %reduce-scatter.22.cloned.1.call-start = ((), (), s32[]{:S(2)}) async-start(), calls=%async_computation.23 | async-start | bytes 2621440 | tf_op jit(solution)/shard_map/reduce_scatter | solution.py:261
  632.9 59.2 %all-gather.26.cloned.1.call-start = ((), (), s32[]{:S(2)}) async-start(), calls=%async_computation.24 | async-start | bytes 2621440 | tf_op jit(solution)/shard_map/all_gather | solution.py:273
  669.3 118.6 %reduce-scatter.24.cloned.1.call-start = ((), (), s32[]{:S(2)}) async-start(), calls=%async_computation.25 | async-start | bytes 2621440 | tf_op jit(solution)/shard_map/reduce_scatter | solution.py:296
  733.8 188.0 %all-reduce.2.cloned.1.call-start = ((), (), s32[]{:S(2)}) async-start(), calls=%async_computation.27 | async-start | bytes 524288 | tf_op jit(solution)/shard_map/psum | solution.py:480
  796.4 246.0 %reduce-scatter.26.cloned.1.call-start = ((), (), s32[]{:S(2)}) async-start(), calls=%async_computation.26 | async-start | bytes 7077888 | tf_op jit(solution)/shard_map/reduce_scatter | solution.py:486
  819.2 225.9 %copy-start.19 = (f32[1,12,128,128]{3,2,1,0:T(8,128)S(1)}, f32[1,12,128,128]{3,2,1,0:T(8,128)}, u32[]{:S(2)}) copy-start(f32[1,12,128,128]{3,2,1,0:T(8,128)} %param.35) | copy-start | bytes 2359300
  1483.3 127.4 %copy-start.35 = (f32[1,12,128,128]{3,2,1,0:T(8,128)S(1)}, f32[1,12,128,128]{3,2,1,0:T(8,128)}, u32[]{:S(2)}) copy-start(f32[1,12,128,128]{3,2,1,0:T(8,128)} %param.29) | copy-start | bytes 2359300
  (102 other events, 1418.0 us)
Sparse Core Ops, SparseCore 0:
  10.8 63.1 all-gather.11
  76.1 21.2 all-gather.9
  139.6 31.4 reduce-scatter.9
  174.3 22.5 all-gather.13
  214.6 31.3 reduce-scatter.11
  248.9 22.5 all-gather.15
  312.8 31.4 reduce-scatter.13
  347.7 22.5 all-gather.17
  387.8 31.4 reduce-scatter.15
  425.5 22.5 all-gather.19
  459.8 31.4 reduce-scatter.17
  496.1 22.5 all-gather.21
  562.4 31.4 reduce-scatter.19
  598.7 22.5 all-gather.23
  633.0 31.4 reduce-scatter.21
  669.4 22.5 all-gather.25
  733.9 31.4 reduce-scatter.23
  796.5 125.2 all-reduce.1
  925.4 116.9 reduce-scatter.25
where the time goes:
time: 1630 us; the launch traced here: 1620 us
  waiting for transfers between devices  648 us (40%)
  other arithmetic  607 us (37%)
  matrix products  190 us (12%)
  local copies, waits for them, and re-layouts  159 us (10%)
    another operation x6, other arithmetic, orthonormal(): factor = jnp.linalg.cholesky(gram_mat)  286 us
    another operation x4, other arithmetic, orthonormal(): jax.scipy.linalg.solve_triangular(lower_part, full_part.T, lower=True)  241 us
    reduce_scatter x1, waiting for transfers between devices, on_device(): owned = lax.psum_scatter(routed, 'dp', scatter_dimension=0, tiled=True)  117 us
    psum x1, waiting for transfers between devices, on_device(): grad_table = lax.psum(local_table, ('dp', 'head'))  98.4 us
    reduce_scatter x2, waiting for transfers between devices, layer_forward(): lax.psum_scatter(jnp.dot(mixed, out_w, preferred_element_type=jnp.float32...  63.1 us
    reduce_scatter x2, waiting for transfers between devices, layer_backward(): lax.psum_scatter(jnp.einsum('rf,df->rd', grad_pre, up_kept, preferred_ele...  62.8 us
    reduce_scatter x2, waiting for transfers between devices, layer_forward(): lax.psum_scatter(jnp.dot(hidden, down_w, preferred_element_type=jnp.float...  59.5 us
    all_gather x1, waiting for transfers between devices, on_device(): every_slot = lax.all_gather(copies, 'dp', axis=0, tiled=True)  57.7 us
  transfers between devices with their start and end apart: 19, of which 18 were waited for; matrix products, arithmetic and copies ran while one was open for 7% of the time, Pallas kernels for 0%

commit v1 on v0

v1 whole, which is shorter than its diff:
```python
import functools

import jax
import jax.numpy as jnp
from jax import lax
from jax.experimental import pallas as pl
from jax.experimental.pallas import tpu as pltpu
from jax.sharding import PartitionSpec as P

D = 512
HEADS = 8
HD = 64
FF = 2048
LOOK = 96
LAYERS = 2
BLK = 128
STEP = 10

f32 = jnp.float32
HI = lax.Precision.HIGHEST
norm_eps = 1e-05
beta_first = 0.5
beta_second = 0.5
beta_stats = 0.5
adam_eps = 1e-08
rate_matrix = 0.02
rate_vector = 0.15
weight_decay = 0.01


def window_ids(lengths, bucket_rows):
    bounds = jnp.cumsum(lengths, axis=1, dtype=jnp.int32)
    places = jnp.arange(bucket_rows, dtype=jnp.int32)
    return jnp.sum(
        (places[None, :, None] >= bounds[:, None, :]).astype(jnp.int32), axis=2, dtype=jnp.int32
    )


def depth_vectors(vec_table, layer_at):
    ff_ratio = FF // D
    base_row = LOOK + 1 + layer_at * (8 + ff_ratio)
    return (
        vec_table[base_row],
        vec_table[base_row + 1],
        vec_table[base_row + 2],
        vec_table[base_row + 3],
        vec_table[base_row + 4],
        vec_table[base_row + 5 : base_row + 5 + ff_ratio].reshape(FF),
        vec_table[base_row + 5 + ff_ratio],
        vec_table[base_row + 6 + ff_ratio],
        vec_table[base_row + 7 + ff_ratio],
    )


def adamw_update(gradient, values, moment_one, moment_two):
    new_first = beta_first * moment_one + (1.0 - beta_first) * gradient
    new_second = beta_second * moment_two + (1.0 - beta_second) * gradient * gradient
    step_ratio = (
        new_first
        / (1.0 - beta_first**STEP)
        / (jnp.sqrt(new_second / (1.0 - beta_second**STEP)) + adam_eps)
    )
    new_values = values - rate_vector * (step_ratio + weight_decay * values)
    return (new_values, new_first, new_second)


def branch_biases(grad_table):
    ff_ratio = FF // D
    bias_rows = []
    for layer_at in range(LAYERS):
        base_row = LOOK + 1 + layer_at * (8 + ff_ratio)
        bias_rows.append(grad_table[base_row + 2])
        bias_rows.append(grad_table[base_row + 5 + ff_ratio])
    return jnp.stack(bias_rows, axis=0)


def dot_hi(a,b,ca,cb):
    return lax.dot_general(a,b,(((ca,),(cb,)),((),())),precision=HI,preferred_element_type=f32)
PANEL=32
def qr_batch(a_ref, count):
    lane = lax.broadcasted_iota(jnp.int32,(1,1,BLK),2)
    sub8 = lax.broadcasted_iota(jnp.int32,(1,8,1),1)
    sub32 = lax.broadcasted_iota(jnp.int32,(1,PANEL,1),1)
    def panel(sp, carry):
        r0 = pl.multiple_of(sp*PANEL, PANEL)
        block = a_ref[:, pl.ds(r0,PANEL), :]
        block = pltpu.roll(block.reshape(count*PANEL,BLK), lax.rem(BLK - r0, BLK), 1).reshape(count,PANEL,BLK)
        tiles = [block[:, 8*t:8*t+8, :] for t in range(PANEL//8)]
        for k in range(PANEL):
            t0, s = divmod(k,8)
            row = tiles[t0][:, s:s+1, :]
            inv = 1.0/row[:, :, k:k+1]
            pn = (row + (lane==k).astype(f32))*inv
            for t in range(t0,PANEL//8):
                c = tiles[t][:, :, k:k+1]
                if t==t0:
                    if s==7: continue
                    c = jnp.where(sub8 > s, c, 0.0)
                tiles[t] = tiles[t] - c*pn
        done = jnp.concatenate(tiles, axis=1)
        diag = lane==sub32
        piv = jnp.sum(jnp.where(diag, done, 0.0), axis=2, keepdims=True)
        done = jnp.where(diag, 1.0, jnp.where((lane > sub32) & (lane < PANEL), 0.0, done))
        done = pltpu.roll(done.reshape(count*PANEL,BLK), r0, 1).reshape(count,PANEL,BLK)
        scale = lax.rsqrt(piv)
        done = done*scale
        a_ref[:, pl.ds(r0,PANEL), :] = done
        @pl.when(sp < BLK//PANEL-1)
        def _():
            lane2 = lax.broadcasted_iota(jnp.int32,(BLK,BLK),1)
            row2 = lax.broadcasted_iota(jnp.int32,(BLK,BLK),0)
            clear = (row2 >= r0+PANEL) & (lane2 >= r0) & (lane2 < r0+PANEL)
            lanep = lax.broadcasted_iota(jnp.int32,(PANEL,BLK),1)
            for b in range(count):
                z = a_ref[b, pl.ds(r0,PANEL), :]
                zm = jnp.where(lanep >= r0+PANEL, z, 0.0)
                upd = dot_hi(zm, z, 0, 0)
                a_ref[b] = jnp.where(clear, 0.0, a_ref[b]) - upd
        return carry
    lax.fori_loop(0, BLK//PANEL, panel, 0)

def soap_kernel(count, *refs):
    g = sum(ref[0].astype(f32) for ref in refs[:count])
    soap_body(g, *refs[count:])


def soap_body(g, mas_ref, m1_ref, m2_ref, ls_ref, rs_ref, lb_ref, rb_ref,
                nm_ref, nc_ref, n1_ref, n2_ref, nl_ref, nr_ref, ql_ref, qr_ref, mat_ref, a_ref):
    n = pl.num_programs(0); i = pl.program_id(0)
    lb = lb_ref[0]; rb = rb_ref[0]
    rot = dot_hi(dot_hi(lb,g,0,0), rb, 1, 0)
    n1 = 0.5*m1_ref[0]+0.5*rot
    n2 = 0.5*m2_ref[0]+0.5*rot*rot
    n1_ref[0]=n1; n2_ref[0]=n2
    corr = 1.0-0.5**STEP
    ratio = n1/corr/(jnp.sqrt(n2/corr)+1e-8)
    upd = dot_hi(dot_hi(lb,ratio,1,0), rb, 1, 1)
    mas = mas_ref[0]
    nm = mas - 0.02*(upd+0.01*mas)
    nm_ref[0]=nm; nc_ref[0]=nm.astype(jnp.bfloat16)
    nl = 0.5*ls_ref[0]+0.5*dot_hi(g,g,1,1)
    nr = 0.5*rs_ref[0]+0.5*dot_hi(g,g,0,0)
    nl_ref[0]=nl; nr_ref[0]=nr
    for side,(st,ba) in enumerate(((nl,lb),(nr,rb))):
        m = dot_hi(st,ba,1,0)
        m = m*lax.rsqrt(jnp.sum(m*m,axis=0,keepdims=True))
        mat_ref[2*i+side] = m
        a_ref[2*i+side] = dot_hi(m,m,0,0)
    @pl.when(i==n-1)
    def _():
        count = a_ref.shape[0]
        qr_batch(a_ref, count)
        keep = lax.broadcasted_iota(jnp.int32,(BLK,BLK),1) <= lax.broadcasted_iota(jnp.int32,(BLK,BLK),0)
        def fin(j, c):
            for side,ref in enumerate((ql_ref,qr_ref)):
                x = jnp.where(keep, a_ref[2*j+side], 0.0)
                ref[j] = dot_hi(mat_ref[2*j+side], x, 1, 1)
            return c
        lax.fori_loop(0, n, fin, 0)

def soap(gs, master, m1, m2, ls, rs, lb, rb):
    n = master.shape[0]
    one = pl.BlockSpec((1,BLK,BLK), lambda i:(i,0,0))
    whole = pl.BlockSpec((n,BLK,BLK), lambda i:(0,0,0))
    sh = jax.ShapeDtypeStruct((n,BLK,BLK), f32)
    shb = jax.ShapeDtypeStruct((n,BLK,BLK), jnp.bfloat16)
    return pl.pallas_call(functools.partial(soap_kernel, len(gs)), grid=(n,), in_specs=[one]*(len(gs)+7),
        out_specs=[one]*6+[whole]*2, out_shape=[sh,shb,sh,sh,sh,sh,sh,sh],
        scratch_shapes=[pltpu.VMEM((2*n,BLK,BLK),f32)]*2,
        compiler_params=pltpu.CompilerParams(vmem_limit_bytes=50*2**20), name="soap")(*gs,master,m1,m2,ls,rs,lb,rb)


bf16 = jnp.bfloat16
LANES = 128
ROW_TILE = 256
BIG = 1e30
CORR = 1.0 - 0.5**STEP


def params(mib=48):
    return pltpu.CompilerParams(vmem_limit_bytes=mib * 2**20)


def shape(dims, kind=f32):
    return jax.ShapeDtypeStruct(dims, kind)


def dot(a, b, ca=1, cb=0):
    return lax.dot_general(a, b, (((ca,), (cb,)), ((), ())), preferred_element_type=f32)


def place_blocks(dst, refs, first, rows, cols, row_step, col_step, col_base=0):
    for r, ref in enumerate(refs):
        for j in range(rows * cols):
            row, col = divmod(j, cols)
            r0 = r * row_step + row * BLK
            c0 = col_base + r * col_step + col * BLK
            dst[r0 : r0 + BLK, c0 : c0 + BLK] = ref[first + j]


def place_qkv(dst, refs):
    for r, ref in enumerate(refs):
        for j in range(12):
            row, col = divmod(j, 3)
            c0 = col * D + r * BLK
            dst[row * BLK : (row + 1) * BLK, c0 : c0 + BLK] = ref[j]


def layer_norm(resid):
    center = resid - jnp.mean(resid, axis=1, keepdims=True)
    inv = lax.rsqrt(jnp.mean(center * center, axis=1, keepdims=True) + norm_eps)
    return center * inv, inv


def layer_norm_grad(grad, unit, inv, gain):
    dn = grad * gain
    return inv * (
        dn
        - jnp.mean(dn, axis=1, keepdims=True)
        - unit * jnp.mean(dn * unit, axis=1, keepdims=True)
    )


def col_sum(values):
    return jnp.sum(values, axis=0, keepdims=True)


def embed_kernel(series_ref, we_ref, be_ref, x_ref):
    x_ref[...] = dot_hi(series_ref[...].astype(f32), we_ref[...], 1, 0) + be_ref[...]


def embed(series, table):
    rows = series.shape[0]
    return pl.pallas_call(
        embed_kernel, out_shape=shape((rows, D)), compiler_params=params(), name="embed"
    )(series, table[:LOOK], table[LOOK : LOOK + 1])


def proj_kernel(x_ref, bq_ref, bv_ref, w0, w1, w2, w3, xs_ref, q_ref, k_ref, v_ref, w_s):
    place_qkv(w_s, (w0, w1, w2, w3))

    def tile(t, c):
        at = pl.ds(t * ROW_TILE, ROW_TILE)
        xs = x_ref[at].astype(bf16)
        xs_ref[at] = xs
        q_ref[at] = (dot(xs, w_s[:, :D]) + bq_ref[...]).astype(bf16)
        k_ref[at] = dot(xs, w_s[:, D : 2 * D]).astype(bf16)
        v_ref[at] = (dot(xs, w_s[:, 2 * D :]) + bv_ref[...]).astype(bf16)
        return c

    lax.fori_loop(0, x_ref.shape[0] // ROW_TILE, tile, 0)


def project(x, bq, bv, wqkv):
    rows = x.shape[0]
    return pl.pallas_call(
        proj_kernel,
        out_shape=[shape((rows, D), bf16)] * 4,
        scratch_shapes=[pltpu.VMEM((D, 3 * D), bf16)],
        compiler_params=params(),
        name="project",
    )(x, bq, bv, *wqkv)


def half_mask(i, kind=bf16):
    lane = lax.broadcasted_iota(jnp.int32, (1, LANES), 1)
    return ((lane >= HD * i) & (lane < HD * (i + 1))).astype(f32).astype(kind)


def three_terms(col):
    first = col.astype(bf16).astype(f32)
    second = (col - first).astype(bf16).astype(f32)
    return first, second, col - first - second


def lanes_with(base, at, cols):
    lane = lax.broadcasted_iota(jnp.int32, base.shape, 1)
    for i, col in enumerate(cols):
        base = jnp.where(lane == at + i, col, base)
    return base.astype(bf16)


def attend_kernel(q_ref, k_ref, kp_ref, v_ref, vp_ref, ohq_ref, ohk_ref, o_ref, lse_ref, ka, va):
    rows = q_ref.shape[0]
    ka[:rows, :LANES] = k_ref[...]
    ka[rows:, :LANES] = kp_ref[...]
    ka[:, LANES:] = ohk_ref[...]
    lane = lax.broadcasted_iota(jnp.int32, (ROW_TILE, LANES), 1)
    for i in range(2):
        m = half_mask(i)
        va[i, :rows, :LANES] = v_ref[...] * m
        va[i, rows:, :LANES] = vp_ref[...] * m
        va[i, :, LANES:] = jnp.ones((2 * rows, LANES), bf16)

    def tile(t, c):
        at = pl.ds(t * ROW_TILE, ROW_TILE)
        total = jnp.zeros((ROW_TILE, LANES), f32)
        stat = jnp.zeros((ROW_TILE, LANES), f32)
        for i in range(2):
            qa = jnp.concatenate([q_ref[at] * (half_mask(i) * bf16(0.125)), ohq_ref[at]], axis=1)
            s = dot(qa, ka[...], 1, 1)
            high = jnp.max(s, axis=1, keepdims=True)
            e = jnp.exp(s - high).astype(bf16)
            out = dot(e, va[i])
            norm = out[:, LANES:]
            total = total + out[:, :LANES] / norm
            stat = jnp.where(lane == i, high + jnp.log(norm), stat)
        o_ref[at] = total.astype(bf16)
        lse_ref[at] = stat
        return c

    lax.fori_loop(0, rows // ROW_TILE, tile, 0)


def attend(q, k, kp, v, vp, ohq, ohk):
    rows = q.shape[0]
    pair = pl.BlockSpec((rows, LANES), lambda h: (0, h))
    other = pl.BlockSpec((rows, LANES), lambda h: (0, h + 1 - 2 * lax.rem(h, 2)))
    return pl.pallas_call(
        attend_kernel,
        grid=(D // LANES,),
        in_specs=[pair, pair, other, pair, other]
        + [
            pl.BlockSpec((rows, LANES), lambda h: (0, 0)),
            pl.BlockSpec((2 * rows, LANES), lambda h: (0, 0)),
        ],
        out_specs=[pair, pair],
        out_shape=[shape((rows, D), bf16), shape((rows, D))],
        scratch_shapes=[
            pltpu.VMEM((2 * rows, 2 * LANES), bf16),
            pltpu.VMEM((2, 2 * rows, 2 * LANES), bf16),
        ],
        compiler_params=params(),
        name="attend",
    )(q, k, kp, v, vp, ohq, ohk)


def post_kernel(
    o_ref, x_ref, vec_ref, b1_ref, a0, a1, a2, a3, f0, f1, f2, f3,
    n1_ref, i1_ref, y_ref, hid_ref, slope_ref, n2_ref, i2_ref, x2_ref,
    wo_s, w1_s, w2_s,
):
    place_blocks(wo_s, (a0, a1, a2, a3), 0, 1, 4, BLK, 0)
    place_blocks(w1_s, (f0, f1, f2, f3), 0, 4, 4, 0, D)
    place_blocks(w2_s, (f0, f1, f2, f3), 16, 4, 4, D, 0)

    def tile(t, c):
        at = pl.ds(t * ROW_TILE, ROW_TILE)
        vec = [vec_ref[i : i + 1, :] for i in range(6)]
        unit, inv = layer_norm(x_ref[at] + dot(o_ref[at], wo_s[...]) + vec[0])
        n1_ref[at] = unit
        i1_ref[at] = jnp.broadcast_to(inv, (ROW_TILE, LANES))
        y = unit * vec[1] + vec[2]
        yb = y.astype(bf16)
        y_ref[at] = yb
        fed = jnp.zeros((ROW_TILE, D), f32)
        for r in range(FF // D):
            cols = slice(r * D, (r + 1) * D)
            pre = dot(yb, w1_s[:, cols]) + b1_ref[:, cols]
            phi = 0.5 * (1.0 + lax.erf(pre * (0.5**0.5)))
            hid = (pre * phi).astype(bf16)
            hid_ref[at, cols] = hid
            slope_ref[at, cols] = (
                phi + pre * (jnp.exp(-0.5 * pre * pre) * 0.3989422804014327)
            ).astype(bf16)
            fed = fed + dot(hid, w2_s[cols, :])
        unit, inv = layer_norm(y + fed + vec[3])
        n2_ref[at] = unit
        i2_ref[at] = jnp.broadcast_to(inv, (ROW_TILE, LANES))
        x2_ref[at] = unit * vec[4] + vec[5]
        return c

    lax.fori_loop(0, x_ref.shape[0] // ROW_TILE, tile, 0)


def post(o, x, vec, b1, wout, wffn):
    rows = x.shape[0]
    return pl.pallas_call(
        post_kernel,
        out_shape=[
            shape((rows, D)),
            shape((rows, LANES)),
            shape((rows, D), bf16),
            shape((rows, FF), bf16),
            shape((rows, FF), bf16),
            shape((rows, D)),
            shape((rows, LANES)),
            shape((rows, D)),
        ],
        scratch_shapes=[
            pltpu.VMEM((D, D), bf16),
            pltpu.VMEM((D, FF), bf16),
            pltpu.VMEM((FF, D), bf16),
        ],
        compiler_params=params(),
        name="post",
    )(o, x, vec, b1, *wout, *wffn)


def store_blocks(refs, r, first, rows, cols, value):
    keep_ref, send_ref = refs
    ref = send_ref if r % 2 else keep_ref
    for j in range(rows * cols):
        row, col = divmod(j, cols)
        ref[r // 2, first + j] = value[row * BLK : (row + 1) * BLK, col * BLK : (col + 1) * BLK]


def ffn_grad_kernel(
    e_ref, n2_ref, i2_ref, n1_ref, i1_ref, y_ref, hid_ref, slope_ref, o_ref, vec_ref,
    a0, a1, a2, a3, f0, f1, f2, f3,
    gk_ref, gs_ref, ok_ref, os_ref, dr1_ref, do_ref, db1_ref, sums_ref,
    wo_s, w1_s, w2_s, dr2_s, dfr_s, dpre_s, dar_s,
):
    rows = e_ref.shape[0]
    place_blocks(wo_s, (a0, a1, a2, a3), 0, 1, 4, BLK, 0)
    place_blocks(w1_s, (f0, f1, f2, f3), 0, 4, 4, 0, D)
    place_blocks(w2_s, (f0, f1, f2, f3), 16, 4, 4, D, 0)
    tiles = rows // ROW_TILE
    gain_two = vec_ref[4:5, :]
    gain_one = vec_ref[1:2, :]
    zero = jnp.zeros((1, D), f32)

    def tile_two(t, c):
        at = pl.ds(t * ROW_TILE, ROW_TILE)
        grad = e_ref[at]
        unit = n2_ref[at]
        dr2 = layer_norm_grad(grad, unit, i2_ref[at, 0:1], gain_two)
        dr2_s[at] = dr2
        dfr_s[at] = dr2.astype(bf16)
        return (c[0] + col_sum(dr2), c[1] + col_sum(grad * unit), c[2] + col_sum(grad))

    db2, dg2, dc2 = lax.fori_loop(0, tiles, tile_two, (zero, zero, zero))

    for r in range(FF // D):
        cols = slice(r * D, (r + 1) * D)

        def tile_up(t, c):
            at = pl.ds(t * ROW_TILE, ROW_TILE)
            dh = dot(dfr_s[at], w2_s[cols, :], 1, 1)
            dpre = (dh * slope_ref[at, cols].astype(f32)).astype(bf16)
            dpre_s[at, cols] = dpre
            dr2_s[at] = dr2_s[at] + dot(dpre, w1_s[:, cols], 1, 1)
            return c + col_sum(dpre.astype(f32))

        db1_ref[r : r + 1, :] = lax.fori_loop(0, tiles, tile_up, zero)
        store_blocks((gk_ref, gs_ref), r, 16, 4, 4, dot(hid_ref[:, cols], dfr_s[...], 0, 0).astype(bf16))
        store_blocks((gk_ref, gs_ref), r, 0, 4, 4, dot(y_ref[...], dpre_s[:, cols], 0, 0).astype(bf16))

    def tile_one(t, c):
        at = pl.ds(t * ROW_TILE, ROW_TILE)
        grad = dr2_s[at]
        unit = n1_ref[at]
        dr1 = layer_norm_grad(grad, unit, i1_ref[at, 0:1], gain_one)
        dr1_ref[at] = dr1
        dar = dr1.astype(bf16)
        dar_s[at] = dar
        do_ref[at] = dot(dar, wo_s[...], 1, 1).astype(bf16)
        return (c[0] + col_sum(dr1), c[1] + col_sum(grad * unit), c[2] + col_sum(grad))

    dbo, dg1, dc1 = lax.fori_loop(0, tiles, tile_one, (zero, zero, zero))
    dwo = dot(o_ref[...], dar_s[...], 0, 0).astype(bf16)
    for r in range(4):
        store_blocks((ok_ref, os_ref), r, 0, 1, 4, dwo[r * BLK : (r + 1) * BLK])
    for i, value in enumerate((dbo, dg1, dc1, db2, dg2, dc2, zero, zero)):
        sums_ref[i : i + 1, :] = value


def ffn_grad(e, n2, i2, n1, i1, y, hid, slope, o, vec, wout, wffn):
    rows = e.shape[0]
    return pl.pallas_call(
        ffn_grad_kernel,
        out_shape=[
            shape((2, 32, BLK, BLK), bf16),
            shape((2, 32, BLK, BLK), bf16),
            shape((2, 4, BLK, BLK), bf16),
            shape((2, 4, BLK, BLK), bf16),
            shape((rows, D)),
            shape((rows, D), bf16),
            shape((FF // D, D)),
            shape((8, D)),
        ],
        scratch_shapes=[
            pltpu.VMEM((D, D), bf16),
            pltpu.VMEM((D, FF), bf16),
            pltpu.VMEM((FF, D), bf16),
            pltpu.VMEM((rows, D), f32),
            pltpu.VMEM((rows, D), bf16),
            pltpu.VMEM((rows, FF), bf16),
            pltpu.VMEM((rows, D), bf16),
        ],
        compiler_params=params(),
        name="ffn_grad",
    )(e, n2, i2, n1, i1, y, hid, slope, o, vec, *wout, *wffn)


def attend_grad_kernel(
    q_ref, k_ref, kp_ref, v_ref, vp_ref, do_ref, o_ref, lse_ref, ohq_ref, ohk_ref,
    dq_ref, dk_ref, dkp_ref, dv_ref, dvp_ref,
    ka, va, qa, da, kt,
):
    rows = q_ref.shape[0]
    ka[:rows, :LANES] = k_ref[...]
    ka[rows:, :LANES] = kp_ref[...]
    ka[:, LANES:] = ohk_ref[...]
    va[:rows, :LANES] = v_ref[...]
    va[rows:, :LANES] = vp_ref[...]
    va[:, LANES:] = jnp.ones((2 * rows, LANES), bf16)
    kt[...] = ka[:, :LANES].T
    product = do_ref[...].astype(f32) * o_ref[...].astype(f32)
    for i in range(2):
        m = half_mask(i)
        qa[i, :, :LANES] = q_ref[...] * (m * bf16(0.125))
        qa[i, :, LANES:] = lanes_with(
            ohq_ref[...].astype(f32), 120, three_terms(-lse_ref[:, i : i + 1])
        )
        da[i, :, :LANES] = do_ref[...] * m
        delta = jnp.sum(product * half_mask(i, f32), axis=1, keepdims=True)
        da[i, :, LANES:] = lanes_with(jnp.zeros((rows, LANES), f32), 0, three_terms(-delta))

    def tile(t, sums):
        at = pl.ds(pl.multiple_of(t * ROW_TILE, ROW_TILE), ROW_TILE)
        dk = jnp.zeros((ROW_TILE, LANES), f32)
        dv = jnp.zeros((ROW_TILE, LANES), f32)
        new = []
        for i in range(2):
            p = jnp.exp(dot(ka[at], qa[i], 1, 1))
            ds = (p * dot(va[at], da[i], 1, 1)).astype(bf16)
            dv = dv + dot(p.astype(bf16), da[i, :, :LANES])
            dk = dk + dot(ds, qa[i, :, :LANES])
            new.append(sums[i] + dot(kt[:, at], ds))
        return tuple(new), dk.astype(bf16), dv.astype(bf16)

    sums = (jnp.zeros((LANES, rows), f32),) * 2
    half = rows // ROW_TILE

    def own(t, sums):
        sums, dk, dv = tile(t, sums)
        at = pl.ds(t * ROW_TILE, ROW_TILE)
        dk_ref[at] = dk
        dv_ref[at] = dv
        return sums

    def other(t, sums):
        sums, dk, dv = tile(t + half, sums)
        at = pl.ds(t * ROW_TILE, ROW_TILE)
        dkp_ref[at] = dk
        dvp_ref[at] = dv
        return sums

    sums = lax.fori_loop(0, half, own, sums)
    sums = lax.fori_loop(0, half, other, sums)
    row = lax.broadcasted_iota(jnp.int32, (LANES, rows), 0)
    dq_ref[...] = (jnp.where(row < HD, sums[0], sums[1]) * 0.125).T.astype(bf16)


def attend_grad(q, k, kp, v, vp, do, o, lse, ohq, ohk):
    rows = q.shape[0]
    pair = pl.BlockSpec((rows, LANES), lambda h: (0, h))
    other = pl.BlockSpec((rows, LANES), lambda h: (0, h + 1 - 2 * lax.rem(h, 2)))
    return pl.pallas_call(
        attend_grad_kernel,
        grid=(D // LANES,),
        in_specs=[pair, pair, other, pair, other, pair, pair, pair]
        + [
            pl.BlockSpec((rows, LANES), lambda h: (0, 0)),
            pl.BlockSpec((2 * rows, LANES), lambda h: (0, 0)),
        ],
        out_specs=[pair, pair, other, pair, other],
        out_shape=[shape((rows, D), bf16)] * 5,
        scratch_shapes=[
            pltpu.VMEM((2 * rows, 2 * LANES), bf16),
            pltpu.VMEM((2 * rows, 2 * LANES), bf16),
            pltpu.VMEM((2, rows, 2 * LANES), bf16),
            pltpu.VMEM((2, rows, 2 * LANES), bf16),
            pltpu.VMEM((LANES, 2 * rows), bf16),
        ],
        compiler_params=params(),
        name="attend_grad",
    )(q, k, kp, v, vp, do, o, lse, ohq, ohk)


def proj_grad_kernel(
    dq_ref, dk_ref, dv_ref, dkr_ref, dvr_ref, xs_ref, dr1_ref, w0, w1, w2, w3,
    gk_ref, gs_ref, dx_ref, sums_ref, w_s, dk_s, dv_s,
):
    place_qkv(w_s, (w0, w1, w2, w3))
    zero = jnp.zeros((1, D), f32)

    def tile(t, c):
        at = pl.ds(t * ROW_TILE, ROW_TILE)
        dq = dq_ref[at]
        dk = (dk_ref[at].astype(f32) + dkr_ref[at].astype(f32)).astype(bf16)
        dv = (dv_ref[at].astype(f32) + dvr_ref[at].astype(f32)).astype(bf16)
        dk_s[at] = dk
        dv_s[at] = dv
        dx_ref[at] = (
            dr1_ref[at]
            + dot(dq, w_s[:, :D], 1, 1)
            + dot(dk, w_s[:, D : 2 * D], 1, 1)
            + dot(dv, w_s[:, 2 * D :], 1, 1)
        )
        return (c[0] + col_sum(dq.astype(f32)), c[1] + col_sum(dv.astype(f32)))

    dbq, dbv = lax.fori_loop(0, xs_ref.shape[0] // ROW_TILE, tile, (zero, zero))
    sums_ref[0:1, :] = dbq
    sums_ref[1:2, :] = dbv
    sums_ref[2:8, :] = jnp.zeros((6, D), f32)
    for part, ref in enumerate((dq_ref, dk_s, dv_s)):
        grad = dot(xs_ref[...], ref[...], 0, 0).astype(bf16)
        for r in range(4):
            out = gs_ref if r % 2 else gk_ref
            for row in range(4):
                out[r // 2, row * 3 + part] = grad[row * BLK : (row + 1) * BLK, r * BLK : (r + 1) * BLK]


def proj_grad(dq, dk, dv, dkr, dvr, xs, dr1, wqkv):
    rows = xs.shape[0]
    return pl.pallas_call(
        proj_grad_kernel,
        out_shape=[
            shape((2, 12, BLK, BLK), bf16),
            shape((2, 12, BLK, BLK), bf16),
            shape((rows, D)),
            shape((8, D)),
        ],
        scratch_shapes=[
            pltpu.VMEM((D, 3 * D), bf16),
            pltpu.VMEM((rows, D), bf16),
            pltpu.VMEM((rows, D), bf16),
        ],
        compiler_params=params(),
        name="proj_grad",
    )(dq, dk, dv, dkr, dvr, xs, dr1, *wqkv)


def embed_grad_kernel(series_ref, g_ref, we_ref, in_ref, dwe_ref, dbe_ref):
    g = g_ref[...]
    in_ref[...] = dot_hi(g, we_ref[...], 1, 1)
    dwe_ref[...] = dot_hi(series_ref[...].astype(f32), g, 0, 0)
    dbe_ref[...] = col_sum(g)


def embed_grad(series, g, table):
    rows = series.shape[0]
    return pl.pallas_call(
        embed_grad_kernel,
        out_shape=[shape((rows, LOOK)), shape((LOOK, D)), shape((1, D))],
        compiler_params=params(),
        name="embed_grad",
    )(series, g, table[:LOOK])


PARTS = ((0, 12), (12, 4), (16, 32))


def natural_kernel(at_ref, *refs):
    count = len(refs) - 7
    slots, outs, held = refs[:count], refs[count : count + 6], refs[-1]
    step = slots[0].shape[0]
    for i in range(count):
        held[i * step : (i + 1) * step] = slots[i][...]
    for i, out in enumerate(outs):
        layer, part = divmod(i, 3)
        first, n = PARTS[part]
        for j in range(n):
            out[j] = held[at_ref[layer * 48 + first + j]]


def natural_order(at, slots):
    total = sum(s.shape[0] for s in slots)
    spec = pl.BlockSpec(memory_space=pltpu.VMEM)
    return pl.pallas_call(
        natural_kernel,
        in_specs=[pl.BlockSpec(memory_space=pltpu.SMEM)] + [spec] * len(slots),
        out_shape=[shape((n, BLK, BLK), bf16) for _ in range(LAYERS) for _, n in PARTS],
        scratch_shapes=[pltpu.VMEM((total, BLK, BLK), bf16)],
        compiler_params=params(),
        name="natural",
    )(at, *slots)


def routed_kernel(at_ref, tab_ref, tabr_ref, *refs):
    own, got, out = refs[:6], refs[6:12], refs[12]
    count, span = out.shape[0], out.shape[1]
    share = BLK // count
    out[...] = jnp.zeros(out.shape, bf16)
    for i in range(6):
        layer, part = divmod(i, 3)
        first, n = PARTS[part]
        for j in range(n):
            place = at_ref[layer * 48 + first + j]
            who = at_ref[96 + layer * 48 + first + j]
            value = own[i][j].astype(f32) + got[i][j].astype(f32)
            out[who, pl.ds(pl.multiple_of(place * BLK, BLK), BLK), :] = value.astype(bf16)
    table = (tab_ref[...].astype(f32) + tabr_ref[...].astype(f32)).astype(bf16)
    for d in range(count):
        who = at_ref[192 + d]
        out[who, span - share : span, :] = table[d * share : (d + 1) * share]


def routed(at, table, table_got, own, got, count, slots_each):
    spec = pl.BlockSpec(memory_space=pltpu.VMEM)
    return pl.pallas_call(
        routed_kernel,
        in_specs=[pl.BlockSpec(memory_space=pltpu.SMEM)] + [spec] * 14,
        out_shape=shape((count, slots_each * BLK + BLK // count, BLK), bf16),
        compiler_params=params(),
        name="routed",
    )(at, table, table_got, *own, *got)


def routed_plain_kernel(at_ref, *refs):
    own, got, out = refs[:6], refs[6:12], refs[12]
    out[...] = jnp.zeros(out.shape, bf16)
    for i in range(6):
        layer, part = divmod(i, 3)
        first, n = PARTS[part]
        for j in range(n):
            place = at_ref[layer * 48 + first + j]
            who = at_ref[96 + layer * 48 + first + j]
            value = own[i][j].astype(f32) + got[i][j].astype(f32)
            out[who, pl.ds(pl.multiple_of(place * BLK, BLK), BLK), :] = value.astype(bf16)


def routed_plain(at, own, got, count, slots_each):
    spec = pl.BlockSpec(memory_space=pltpu.VMEM)
    return pl.pallas_call(
        routed_plain_kernel,
        in_specs=[pl.BlockSpec(memory_space=pltpu.SMEM)] + [spec] * 12,
        out_shape=shape((count, slots_each * BLK, BLK), bf16),
        compiler_params=params(),
        name="routed",
    )(at, *own, *got)


def ring_of(count):
    half = count // 2
    return [2 * i for i in range(half)] + [2 * (half - 1 - i) + 1 for i in range(half)]


def ring_shift(value, order, by):
    n = len(order)
    return lax.ppermute(value, "dp", [(order[i], order[(i + by) % n]) for i in range(n)])


def ring_gather(value, order):
    n = len(order)
    held = [value] + [None] * (n - 1)
    ahead = behind = value
    for step in range(1, n // 2 + 1):
        behind = ring_shift(behind, order, 1)
        held[n - step] = behind
        if step < n // 2:
            ahead = ring_shift(ahead, order, -1)
            held[step] = ahead
    return held


def ring_reduce(pieces, order):
    n = len(order)
    up = pieces[n // 2]
    down = pieces[n // 2 + 1]
    for step in range(1, n // 2 + 1):
        up = ring_shift(up, order, 1)
        if step < n // 2:
            up = add_low(up, pieces[n // 2 - step])
            down = ring_shift(down, order, -1)
            if step < n // 2 - 1:
                down = add_low(down, pieces[n // 2 + 1 + step])
    return pieces[0], up, down


def add_low(a, b):
    return (a.astype(f32) + b.astype(f32)).astype(bf16)


def core_swap(value):
    return lax.ppermute(value, "head", [(i, i ^ 1) for i in range(4)])


def far_swap(value):
    return lax.ppermute(value, "head", [(i, i ^ 2) for i in range(4)])


def one_hots(ids):
    lane = jnp.arange(LANES, dtype=jnp.int32)[None, :]
    same = ids[:, None] == lane
    return jnp.where(same, -BIG, 0.0).astype(bf16), jnp.where(same, 0.0, 1.0).astype(bf16)


def relative(row, place):
    pieces = row.reshape(4, -1)
    return jnp.take(pieces, jnp.arange(4) ^ place, axis=0).reshape(1, -1)


def on_device(
    series,
    cotangent,
    window_lengths,
    owner_list,
    master,
    first_moment,
    second_moment,
    left_stats,
    right_stats,
    left_basis,
    right_basis,
    vec_values,
    vec_first,
    vec_second,
):
    place = lax.axis_index("head")
    spot = lax.axis_index("dp")
    dp = lax.axis_size("dp")
    ringed = dp == 8
    rows = series.shape[0]
    own_slots = master.shape[1]
    buckets, win = window_lengths.shape
    bucket_rows = rows * 4 // buckets
    owner_row = owner_list[0]
    who = owner_row // own_slots
    if ringed:
        order = ring_of(dp)
        ring_at = jnp.asarray([order.index(d) for d in range(dp)], jnp.int32)
        who = (ring_at[who] - ring_at[spot]) % dp
    inner = owner_row % own_slots
    gather_at = who * own_slots + inner

    copies = master[0].astype(bf16)
    if ringed:
        slots = ring_gather(copies, order)
    else:
        slots = [lax.all_gather(copies, "dp", axis=0, tiled=True)]
    mine = natural_order(gather_at, slots)
    weights = []
    for own in mine:
        far = far_swap(own)
        weights.append([own, core_swap(own), far, core_swap(far)])

    windows = window_ids(window_lengths, bucket_rows)
    ids = windows.reshape(4, rows)
    own_ids = lax.dynamic_index_in_dim(ids, place, 0, False)
    pair_ids = lax.dynamic_index_in_dim(ids, place ^ 1, 0, False)
    ohq, ohk_own = one_hots(own_ids)
    ohk = jnp.concatenate([ohk_own, one_hots(pair_ids)[1]], axis=0)
    valid = (own_ids < win).astype(f32)[:, None]

    x = embed(series, vec_values)
    saved = []
    for layer in range(LAYERS):
        bq, bv, bo, g1, c1, b1, b2, g2, c2 = depth_vectors(vec_values, layer)
        wqkv, wout, wffn = weights[3 * layer : 3 * layer + 3]
        xs, q, k, v = project(x, relative(bq, place), relative(bv, place), wqkv)
        kp, vp = core_swap(k), core_swap(v)
        o, lse = attend(q, k, kp, v, vp, ohq, ohk)
        vec = jnp.stack([bo, g1, c1, b2, g2, c2, g2, c2])
        n1, i1, y, hid, slope, n2, i2, x = post(o, x, vec, relative(b1, place), wout, wffn)
        saved.append((xs, q, k, v, kp, vp, o, lse, vec, n1, i1, y, hid, slope, n2, i2))
    activations = x * valid
    grad = cotangent * valid

    own_sums = [None] * (3 * LAYERS)
    far_sums = [None] * (3 * LAYERS)
    table_rows = [None] * LAYERS

    def reduce_head(at, keep, send):
        got = core_swap(send)
        own_sums[at] = add_low(keep[0], got[0])
        far_sums[at] = far_swap(add_low(keep[1], got[1]))

    for layer in reversed(range(LAYERS)):
        xs, q, k, v, kp, vp, o, lse, vec, n1, i1, y, hid, slope, n2, i2 = saved[layer]
        wqkv, wout, wffn = weights[3 * layer : 3 * layer + 3]
        gk, gs, ok, os, dr1, do, db1, sums = ffn_grad(
            grad, n2, i2, n1, i1, y, hid, slope, o, vec, wout, wffn
        )
        reduce_head(3 * layer + 2, gk, gs)
        reduce_head(3 * layer + 1, ok, os)
        dq, dk, dkp, dv, dvp = attend_grad(q, k, kp, v, vp, do, o, lse, ohq, ohk)
        dkr, dvr = core_swap(dkp), core_swap(dvp)
        pk, ps, grad, qsums = proj_grad(dq, dk, dv, dkr, dvr, xs, dr1, wqkv)
        reduce_head(3 * layer, pk, ps)
        table_rows[layer] = jnp.concatenate(
            [
                relative(qsums[0], place),
                relative(qsums[1], place),
                sums[0:3],
                relative(db1, place).reshape(FF // D, D),
                sums[3:6],
            ],
            axis=0,
        )
    input_grad, dwe, dbe = embed_grad(series, grad, vec_values)
    local_table = jnp.concatenate([dwe, dbe] + table_rows, axis=0)
    vrows = local_table.shape[0]
    padded = jnp.pad(local_table, ((0, BLK - vrows), (0, 0)))
    parts = jnp.take(padded.reshape(4, BLK, BLK), jnp.arange(4) ^ place, axis=0).astype(bf16)
    got = core_swap(parts[1::2])
    tab_own = add_low(parts[0], got[0])
    tab_far = far_swap(add_low(parts[2], got[1]))
    share = BLK // dp
    if ringed:
        dist = (jnp.asarray(ring_at) - ring_at[spot]) % dp
        at = jnp.concatenate([inner, who, dist]).astype(jnp.int32)
        pieces = routed(at, tab_own, tab_far, own_sums, far_sums, dp, own_slots)
        terms = ring_reduce([pieces[i] for i in range(dp)], order)
        grads = [t[: own_slots * BLK].reshape(own_slots, BLK, BLK) for t in terms]
        part = sum(t[own_slots * BLK :].astype(f32) for t in terms)
    else:
        at = jnp.concatenate([inner, who, jnp.arange(dp)]).astype(jnp.int32)
        pieces = routed_plain(at, own_sums, far_sums, dp, own_slots)
        whole = lax.psum_scatter(pieces, "dp", scatter_dimension=0, tiled=True)
        grads = [whole.reshape(own_slots, BLK, BLK)]
        part = lax.psum_scatter(
            tab_own.astype(f32) + tab_far.astype(f32), "dp", scatter_dimension=0, tiled=True
        )
    shares = lax.all_gather(part, ("head", "dp"), axis=0, tiled=True)
    grad_table = shares.reshape(4, BLK, BLK).reshape(BLK, D)[:vrows]
    new_master, new_copy, new_first, new_second, new_left, new_right, left_next, right_next = soap(
        grads,
        master[0],
        first_moment[0],
        second_moment[0],
        left_stats[0],
        right_stats[0],
        left_basis[0],
        right_basis[0],
    )
    vec_new_values, vec_new_first, vec_new_second = adamw_update(
        grad_table, vec_values, vec_first, vec_second
    )
    branch_bias_grads = branch_biases(grad_table)
    return (
        activations,
        input_grad,
        new_master[None],
        new_copy[None],
        new_first[None],
        new_second[None],
        new_left[None],
        new_right[None],
        left_next[None],
        right_next[None],
        vec_new_values,
        vec_new_first,
        vec_new_second,
        branch_bias_grads,
    )


def solution(mesh):
    placed = (
        P(("dp", "head"), None),
        P(("dp", "head"), None),
        P("dp", None),
        P("head", None),
        P("head", "dp", None, None),
        P("head", "dp", None, None),
        P("head", "dp", None, None),
        P("head", "dp", None, None),
        P("head", "dp", None, None),
        P("head", "dp", None, None),
        P("head", "dp", None, None),
        P(),
        P(),
        P(),
    )
    return jax.shard_map(
        on_device,
        mesh=mesh,
        in_specs=placed,
        out_specs=(
            P(("dp", "head"), None),
            P(("dp", "head"), None),
            P("head", "dp", None, None),
            P("head", "dp", None, None),
            P("head", "dp", None, None),
            P("head", "dp", None, None),
            P("head", "dp", None, None),
            P("head", "dp", None, None),
            P("head", "dp", None, None),
            P("head", "dp", None, None),
            P(),
            P(),
            P(),
            P(),
        ),
        check_vma=False,
    )
```

time: 1630 us -> 568 us (0.35)
  other arithmetic: 607 us -> 25 us
  waiting for transfers between devices: 648 us -> 159 us
  Pallas kernels: 0 us -> 210 us
  matrix products: 190 us -> 0 us
  local copies, waits for them, and re-layouts: 159 us -> 65 us
  blocking collectives: 0 us -> 65.9 us
  starting transfers between devices: 1.41 us -> 36 us
    another operation x10 -> x2, other arithmetic: 528 us -> 0.02 us  [on_device(): vec = jnp.stack([bo, g1, c1, b2, g2, c2, g2, c2])]
    reduce_scatter x9 -> x0, waiting for transfers between devices: 334 us -> none  [the longest x1 117 us: on_device(): owned = lax.psum_scatter(routed, 'dp', scatter_dimension=0, tiled=True)]
    all_gather x9 -> x0, waiting for transfers between devices: 216 us -> none  [the longest x1 57.7 us: on_device(): every_slot = lax.all_gather(copies, 'dp', axis=0, tiled=True)]
    pallas_call x0 -> x17, Pallas kernels: none -> 210 us  [the longest x1 65.2 us: soap(): pl.pallas_call(functools.partial(soap_kernel, len(gs)), grid=(n,), in_spe...]
    dot_general x65 -> x0, matrix products: 183 us -> none  [the longest x2 26.7 us: layer_forward(): jnp.dot(normed_rows, up_w, preferred_element_type=jnp.float32)]
    ppermute x0 -> x54, waiting for transfers between devices: none -> 159 us  [the longest x13 105 us: far_swap(): return lax.ppermute(value, 'head', [(i, i ^ 2) for i in range(4)])]
    psum x1 -> x0, waiting for transfers between devices: 98.4 us -> none  [on_device(): grad_table = lax.psum(local_table, ('dp', 'head'))]
    all_gather x0 -> x1, blocking collectives: none -> 65.9 us  [on_device(): shares = lax.all_gather(part, ('head', 'dp'), axis=0, tiled=True)]
  transfers between devices with their start and end apart: 19 -> 54, of which waited for: 18 -> 16; matrix products, arithmetic and copies ran while one was open for 7% -> 6% of each run, Pallas kernels for 0% -> 16%
where the time goes in v1:
time: 568 us; the launch traced here: 562 us
  Pallas kernels  210 us (37%)
  waiting for transfers between devices  159 us (28%)
  blocking collectives  65.9 us (12%)
  local copies, waits for them, and re-layouts  65 us (11%)
  starting transfers between devices  36 us (6%)
  other arithmetic  25 us (4%)
    ppermute x13, waiting for transfers between devices, far_swap(): return lax.ppermute(value, 'head', [(i, i ^ 2) for i in range(4)])  105 us
    all_gather x1, blocking collectives, on_device(): shares = lax.all_gather(part, ('head', 'dp'), axis=0, tiled=True)  65.9 us
    pallas_call x1, Pallas kernels, soap(): pl.pallas_call(functools.partial(soap_kernel, len(gs)), grid=(n,), in_spe...  65.2 us
    ppermute x14, waiting for transfers between devices, ring_shift(): lax.ppermute(value, 'dp', [(order[i], order[(i + by) % n]) for i in range...  53.3 us
    unnamed x232, local copies, waits for them, and re-layouts  46.7 us
    pallas_call x2, Pallas kernels, attend_grad(): pl.pallas_call(attend_grad_kernel, grid=(D // LANES,), in_specs=[pair, pa...  45.4 us
    pallas_call x2, Pallas kernels, ffn_grad(): pl.pallas_call(ffn_grad_kernel, out_shape=[shape((2, 32, BLK, BLK), bf16)...  32.2 us
    pallas_call x2, Pallas kernels, attend(): pl.pallas_call(attend_kernel, grid=(D // LANES,), in_specs=[pair, pair, o...  22 us
  transfers between devices with their start and end apart: 54, of which 16 were waited for; matrix products, arithmetic and copies ran while one was open for 6% of the time, Pallas kernels for 16%

profile of v1, /device:TPU:0, one launch (start us, length us, event | category | flops | bytes accessed | tf_op | source)
XLA Modules:
  0.0 562.2 jit_solution(14824411139362927596)
XLA Ops:
  1.9 3.1 collective-permute-start.3
  5.0 9.0 %collective-permute-done.3.refs_7_ = bf16[12,128,128]{2,1,0:T(8,128)(2,1)S(1)} collective-permute-done((bf16[12,128,128]{2,1,0:T(8,128)(2,1)S(1)}, bf16[12,128,128]{2,1,0:T(8,128)(2,1)S(1)}, u32[]{:S(2)}, u32[]{:S(2)}) %collective-permute-start.3) | collective-permute-done | bytes 393248 | tf_op jit(solution)/shard_map/ppermute | solution.py:743
  16.0 8.3 %collective-permute-done.4.refs_6_ = bf16[12,128,128]{2,1,0:T(8,128)(2,1)S(1)} collective-permute-done((bf16[12,128,128]{2,1,0:T(8,128)(2,1)S(1)}, bf16[12,128,128]{2,1,0:T(8,128)(2,1)S(1)}, u32[]{:S(2)}, u32[]{:S(2)}) %collective-permute-start.4) | collective-permute-done | bytes 393248 | tf_op jit(solution)/shard_map/ppermute | solution.py:743
  27.1 6.6 %collective-permute-done.5.refs_5_ = bf16[12,128,128]{2,1,0:T(8,128)(2,1)S(1)} collective-permute-done((bf16[12,128,128]{2,1,0:T(8,128)(2,1)S(1)}, bf16[12,128,128]{2,1,0:T(8,128)(2,1)S(1)}, u32[]{:S(2)}, u32[]{:S(2)}) %collective-permute-start.5) | collective-permute-done | bytes 393248 | tf_op jit(solution)/shard_map/ppermute | solution.py:743
  39.7 2.5 collective-permute-done.6.refs_4_
  57.5 26.6 %collective-permute-done.13.a2 = bf16[4,128,128]{2,1,0:T(8,128)(2,1)} collective-permute-done((bf16[4,128,128]{2,1,0:T(8,128)(2,1)S(1)}, bf16[4,128,128]{2,1,0:T(8,128)(2,1)}, u32[]{:S(2)}, u32[]{:S(2)}) %collective-permute-start.13) | collective-permute-done | bytes 131104 | tf_op jit(solution)/shard_map/ppermute | solution.py:782
  99.1 14.3 %collective-permute-done.19.w2 = bf16[12,128,128]{2,1,0:T(8,128)(2,1)} collective-permute-done((bf16[12,128,128]{2,1,0:T(8,128)(2,1)}, bf16[12,128,128]{2,1,0:T(8,128)(2,1)}, u32[]{:S(2)}, u32[]{:S(2)}) %collective-permute-start.19) | collective-permute-done | bytes 393248 | tf_op jit(solution)/shard_map/ppermute | solution.py:782
  115.7 11.0 %attend.2 = (bf16[512,512]{1,0:T(8,128)(2,1)S(1)}, f32[512,512]{1,0:T(8,128)S(1)}) custom-call(bf16[512,512]{1,0:T(8,128)(2,1)S(1)} %get-tuple-element.96.q_ref, bf16[512,512]{1,0:T(8,128)(2,1)S(1)} %get-tuple-element.97.k_ref, bf16[512,512]{1,0:T(8,128)(2,1)S(1)} %collective-permute-done.10.kp_ref, bf16[512,512]{1,0:T(8,128)(2,1)S(1)} %get-tuple-element.98.v_ref, ...), custom_call_target="tpu_custom_call" | custom-call | tf_op jit(solution)/shard_map/attend/pallas_call | solution.py:319
  126.8 11.0 %post.2 = (f32[512,512]{1,0:T(8,128)S(1)}, f32[512,128]{1,0:T(8,128)S(1)}, bf16[512,512]{1,0:T(8,128)(2,1)S(1)}, bf16[512,2048]{1,0:T(8,128)(2,1)}, bf16[512,204...) custom-call(bf16[512,512]{1,0:T(8,128)(2,1)S(1)} %get-tuple-element.99.o_ref, ...), custom_call_target="tpu_custom_call" | custom-call | tf_op jit(solution)/shard_map/post/pallas_call | solution.py:378
  141.4 3.3 project.3
  146.8 5.0 collective-permute-done.24.a2
  152.4 11.0 %attend.3 = (bf16[512,512]{1,0:T(8,128)(2,1)S(1)}, f32[512,512]{1,0:T(8,128)S(1)}) custom-call(bf16[512,512]{1,0:T(8,128)(2,1)S(1)} %get-tuple-element.104.q_ref, bf16[512,512]{1,0:T(8,128)(2,1)S(1)} %get-tuple-element.105.k_ref, bf16[512,512]{1,0:T(8,128)(2,1)S(1)} %collective-permute-done.21.kp_ref, bf16[512,512]{1,0:T(8,128)(2,1)S(1)} %get-tuple-element.106.v_ref, ...), custom_call_target="tpu_custom_call" | custom-call | tf_op jit(solution)/shard_map/attend/pallas_call | solution.py:319
  164.8 10.6 %post.3 = (f32[512,512]{1,0:T(8,128)S(1)}, f32[512,128]{1,0:T(8,128)S(1)}, bf16[512,512]{1,0:T(8,128)(2,1)S(1)}, bf16[512,2048]{1,0:T(8,128)(2,1)}, bf16[512,204...) custom-call(bf16[512,512]{1,0:T(8,128)(2,1)S(1)} %get-tuple-element.107.o_ref, ...), custom_call_target="tpu_custom_call" | custom-call | tf_op jit(solution)/shard_map/post/pallas_call | solution.py:378
  178.6 16.2 %ffn_grad.2 = (bf16[2,32,128,128]{3,2,1,0:T(8,128)(2,1)}, bf16[2,32,128,128]{3,2,1,0:T(8,128)(2,1)}, bf16[2,4,128,128]{3,2,1,0:T(8,128)(2,1)S(1)}, bf16[2,4,128,...) custom-call(f32[512,512]{1,0:T(8,128)S(1)} %get-tuple-element.255.e_, ...), custom_call_target="tpu_custom_call" | custom-call | tf_op jit(solution)/shard_map/ffn_grad/pallas_call | solution.py:470
  197.0 22.7 %attend_grad.2 = (bf16[512,512]{1,0:T(8,128)(2,1)S(1)}, bf16[512,512]{1,0:T(8,128)(2,1)S(1)}, bf16[512,512]{1,0:T(8,128)(2,1)}, bf16[512,512]{1,0:T(8,128)(2,1)S(1)}, bf16[512,512]{1,0:T(8,128)(2,1)}) custom-call(bf16[512,512]{1,0:T(8,128)(2,1)S(1)} %get-tuple-element.104.q_ref, bf16[512,512]{1,0:T(8,128)(2,1)S(1)} %get-tuple-element.105.k_ref, ...), custom_call_target="tpu_custom_call" | custom-call | tf_op jit(solution)/shard_map/attend_grad/pallas_call | solution.py:560
  233.1 4.9 proj_grad.2
  240.1 16.0 %ffn_grad.3 = (bf16[2,32,128,128]{3,2,1,0:T(8,128)(2,1)}, bf16[2,32,128,128]{3,2,1,0:T(8,128)(2,1)}, bf16[2,4,128,128]{3,2,1,0:T(8,128)(2,1)S(1)}, bf16[2,4,128,...) custom-call(f32[512,512]{1,0:T(8,128)S(1)} %copy-done.36, ...), custom_call_target="tpu_custom_call" | custom-call | tf_op jit(solution)/shard_map/ffn_grad/pallas_call | solution.py:470
  259.9 22.7 %attend_grad.3 = (bf16[512,512]{1,0:T(8,128)(2,1)S(1)}, bf16[512,512]{1,0:T(8,128)(2,1)S(1)}, bf16[512,512]{1,0:T(8,128)(2,1)}, bf16[512,512]{1,0:T(8,128)(2,1)S(1)}, bf16[512,512]{1,0:T(8,128)(2,1)}) custom-call(bf16[512,512]{1,0:T(8,128)(2,1)S(1)} %get-tuple-element.96.q_ref, bf16[512,512]{1,0:T(8,128)(2,1)S(1)} %get-tuple-element.97.k_ref, ...), custom_call_target="tpu_custom_call" | custom-call | tf_op jit(solution)/shard_map/attend_grad/pallas_call | solution.py:560
  294.2 4.6 proj_grad.3
  304.7 3.4 fusion.3
  309.4 2.7 fusion.2
  319.3 56.2 %collective-permute-done.42.refs_7_ = bf16[4,128,128]{2,1,0:T(8,128)(2,1)S(1)} collective-permute-done((bf16[4,128,128]{2,1,0:T(8,128)(2,1)S(1)}, bf16[4,128,128]{2,1,0:T(8,128)(2,1)S(1)}, u32[]{:S(2)}, u32[]{:S(2)}) %collective-permute-start.42) | collective-permute-done | bytes 131104 | tf_op jit(solution)/shard_map/ppermute | solution.py:782
  376.8 2.6 collective-permute-done.34.tabr_ref
  380.5 4.1 routed.1
  387.8 7.2 %collective-permute-done.47 = bf16[1552,128]{1,0:T(8,128)(2,1)S(1)} collective-permute-done((bf16[1552,128]{1,0:T(8,128)(2,1)S(1)}, bf16[1552,128]{1,0:T(8,128)(2,1)S(1)}, u32[]{:S(2)}, u32[]{:S(2)}) %collective-permute-start.47) | collective-permute-done | bytes 397344 | tf_op jit(solution)/shard_map/ppermute | solution.py:743
  397.8 6.8 %collective-permute-done.48 = bf16[1552,128]{1,0:T(8,128)(2,1)S(1)} collective-permute-done((bf16[1552,128]{1,0:T(8,128)(2,1)S(1)}, bf16[1552,128]{1,0:T(8,128)(2,1)S(1)}, u32[]{:S(2)}, u32[]{:S(2)}) %collective-permute-start.48) | collective-permute-done | bytes 397344 | tf_op jit(solution)/shard_map/ppermute | solution.py:743
  408.0 5.8 %collective-permute-done.52 = bf16[1552,128]{1,0:T(8,128)(2,1)S(1)} collective-permute-done((bf16[1552,128]{1,0:T(8,128)(2,1)S(1)}, bf16[1552,128]{1,0:T(8,128)(2,1)S(1)}, u32[]{:S(2)}, u32[]{:S(2)}) %collective-permute-start.52) | collective-permute-done | bytes 397344 | tf_op jit(solution)/shard_map/ppermute | solution.py:743
  413.8 2.3 collective-permute-done.49
  421.3 4.1 collective-permute-done.50
  426.9 65.9 %all_gather.3 = f32[512,128]{1,0:T(8,128)S(1)} all-gather(f32[16,128]{1,0:T(8,128)S(1)} %fusion.20), channel_id=1, replica_groups=mesh['dp'=8,'head'=4] {'head','dp'}, dimensions={0}, use_global_device_ids=true | all-gather | bytes 270336 | tf_op jit(solution)/shard_map/all_gather | solution.py:917
  492.9 2.2 multiply_subtract_fusion
  496.8 65.2 %soap.1 = (f32[12,128,128]{2,1,0:T(8,128)}, bf16[12,128,128]{2,1,0:T(8,128)(2,1)}, f32[12,128,128]{2,1,0:T(8,128)}, f32[12,128,128]{2,1,0:T(8,128)}, f32[12,128,...) custom-call(bf16[12,128,128]{2,1,0:T(8,128)(2,1)S(1)} %bitcast.148, ...), custom_call_target="tpu_custom_call" | custom-call | tf_op jit(solution)/shard_map/soap/pallas_call | solution.py:167
  (397 shorter events, 122.4 us)
Async XLA Ops:
  1.9 12.1 %collective-permute-start.3 = (bf16[12,128,128]{2,1,0:T(8,128)(2,1)S(1)}, bf16[12,128,128]{2,1,0:T(8,128)(2,1)S(1)}, u32[]{:S(2)}, u32[]{:S(2)}) collective-permute-start(bf16[12,128,128]{2,1,0:T(8,128)(2,1)S(1)} %bitcast_convert_fusion.refs_0_), channel_id=1, source_target_pairs={{0,8},{8,16},{16,24},{24,28},{28,20},{20,12},{12,4},{4,0},{1,9},{9... | collective-permute-start | bytes 1179656 | tf_op jit(solution)/shard_map/ppermute | solution.py:743
  5.0 10.9 %collective-permute-start = (bf16[12,128,128]{2,1,0:T(8,128)(2,1)S(1)}, bf16[12,128,128]{2,1,0:T(8,128)(2,1)S(1)}, u32[]{:S(2)}, u32[]{:S(2)}) collective-permute-start(bf16[12,128,128]{2,1,0:T(8,128)(2,1)S(1)} %bitcast_convert_fusion.refs_0_), channel_id=1, source_target_pairs={{0,4},{8,0},{16,8},{24,16},{28,24},{20,28},{12,20},{4,12},{1,5},{9... | collective-permute-start | bytes 1179656 | tf_op jit(solution)/shard_map/ppermute | solution.py:743
  14.0 10.3 %collective-permute-start.4 = (bf16[12,128,128]{2,1,0:T(8,128)(2,1)S(1)}, bf16[12,128,128]{2,1,0:T(8,128)(2,1)S(1)}, u32[]{:S(2)}, u32[]{:S(2)}) collective-permute-start(bf16[12,128,128]{2,1,0:T(8,128)(2,1)S(1)} %collective-permute-done.3.refs_7_), channel_id=1, source_target_pairs={{0,8},{8,16},{16,24},{24,28},{28,20},{20,12},{12,4},{4,0},{1,9},{9... | collective-permute-start | bytes 1179656 | tf_op jit(solution)/shard_map/ppermute | solution.py:743
  25.8 13.1 %collective-permute-start.2 = (bf16[12,128,128]{2,1,0:T(8,128)(2,1)S(1)}, bf16[12,128,128]{2,1,0:T(8,128)(2,1)S(1)}, u32[]{:S(2)}, u32[]{:S(2)}) collective-permute-start(bf16[12,128,128]{2,1,0:T(8,128)(2,1)S(1)} %collective-permute-done.1.refs_2_), channel_id=1, source_target_pairs={{0,4},{8,0},{16,8},{24,16},{28,24},{20,28},{12,20},{4,12},{1,5},{9... | collective-permute-start | bytes 1179656 | tf_op jit(solution)/shard_map/ppermute | solution.py:743
  49.6 37.7 %collective-permute-start.16 = (bf16[32,128,128]{2,1,0:T(8,128)(2,1)S(1)}, bf16[32,128,128]{2,1,0:T(8,128)(2,1)}, u32[]{:S(2)}, u32[]{:S(2)}) collective-permute-start(bf16[32,128,128]{2,1,0:T(8,128)(2,1)S(1)} %get-tuple-element.101.f0), channel_id=1, source_target_pairs={{0,2},{1,3},{2,0},{3,1},{4,6},{5,7},{6,4},{7,5},{8,10},{9,11},{10,... | collective-permute-start | bytes 3145736 | tf_op jit(solution)/shard_map/ppermute | solution.py:782
  51.5 33.6 %collective-permute-start.8 = (bf16[12,128,128]{2,1,0:T(8,128)(2,1)S(1)}, bf16[12,128,128]{2,1,0:T(8,128)(2,1)S(1)}, u32[]{:S(2)}, u32[]{:S(2)}) collective-permute-start(bf16[12,128,128]{2,1,0:T(8,128)(2,1)S(1)} %get-tuple-element.95.w0), channel_id=1, source_target_pairs={{0,2},{1,3},{2,0},{3,1},{4,6},{5,7},{6,4},{7,5},{8,10},{9,11},{10,... | collective-permute-start | bytes 1179656 | tf_op jit(solution)/shard_map/ppermute | solution.py:782
  53.3 31.9 %collective-permute-start.7 = (bf16[12,128,128]{2,1,0:T(8,128)(2,1)S(1)}, bf16[12,128,128]{2,1,0:T(8,128)(2,1)S(1)}, u32[]{:S(2)}, u32[]{:S(2)}) collective-permute-start(bf16[12,128,128]{2,1,0:T(8,128)(2,1)S(1)} %get-tuple-element.95.w0), channel_id=1, source_target_pairs={{0,1},{1,0},{2,3},{3,2},{4,5},{5,4},{6,7},{7,6},{8,9},{9,8},{10,11... | collective-permute-start | bytes 1179656 | tf_op jit(solution)/shard_map/ppermute | solution.py:778
  53.9 30.1 %collective-permute-start.13 = (bf16[4,128,128]{2,1,0:T(8,128)(2,1)S(1)}, bf16[4,128,128]{2,1,0:T(8,128)(2,1)}, u32[]{:S(2)}, u32[]{:S(2)}) collective-permute-start(bf16[4,128,128]{2,1,0:T(8,128)(2,1)S(1)} %get-tuple-element.100.a0), channel_id=1, source_target_pairs={{0,2},{1,3},{2,0},{3,1},{4,6},{5,7},{6,4},{7,5},{8,10},{9,11},{10,... | collective-permute-start | bytes 393224 | tf_op jit(solution)/shard_map/ppermute | solution.py:782
  57.5 56.2 %collective-permute-start.15 = (bf16[32,128,128]{2,1,0:T(8,128)(2,1)S(1)}, bf16[32,128,128]{2,1,0:T(8,128)(2,1)}, u32[]{:S(2)}, u32[]{:S(2)}) collective-permute-start(bf16[32,128,128]{2,1,0:T(8,128)(2,1)S(1)} %get-tuple-element.101.f0), channel_id=1, source_target_pairs={{0,1},{1,0},{2,3},{3,2},{4,5},{5,4},{6,7},{7,6},{8,9},{9,8},{10,11... | collective-permute-start | bytes 3145736 | tf_op jit(solution)/shard_map/ppermute | solution.py:778
  84.0 30.2 %collective-permute-start.27 = (bf16[32,128,128]{2,1,0:T(8,128)(2,1)}, bf16[32,128,128]{2,1,0:T(8,128)(2,1)}, u32[]{:S(2)}, u32[]{:S(2)}) collective-permute-start(bf16[32,128,128]{2,1,0:T(8,128)(2,1)} %get-tuple-element.109.f0), channel_id=1, source_target_pairs={{0,2},{1,3},{2,0},{3,1},{4,6},{5,7},{6,4},{7,5},{8,10},{9,11},{10,... | collective-permute-start | bytes 3145736 | tf_op jit(solution)/shard_map/ppermute | solution.py:782
  85.2 28.2 %collective-permute-start.19 = (bf16[12,128,128]{2,1,0:T(8,128)(2,1)}, bf16[12,128,128]{2,1,0:T(8,128)(2,1)}, u32[]{:S(2)}, u32[]{:S(2)}) collective-permute-start(bf16[12,128,128]{2,1,0:T(8,128)(2,1)} %get-tuple-element.103.w0), channel_id=1, source_target_pairs={{0,2},{1,3},{2,0},{3,1},{4,6},{5,7},{6,4},{7,5},{8,10},{9,11},{10,... | collective-permute-start | bytes 1179656 | tf_op jit(solution)/shard_map/ppermute | solution.py:782
  87.3 39.5 %collective-permute-start.17 = (bf16[32,128,128]{2,1,0:T(8,128)(2,1)}, bf16[32,128,128]{2,1,0:T(8,128)(2,1)}, u32[]{:S(2)}, u32[]{:S(2)}) collective-permute-start(bf16[32,128,128]{2,1,0:T(8,128)(2,1)} %collective-permute-done.16.f2), channel_id=1, source_target_pairs={{0,1},{1,0},{2,3},{3,2},{4,5},{5,4},{6,7},{7,6},{8,9},{9,8},{10,11... | collective-permute-start | bytes 3145736 | tf_op jit(solution)/shard_map/ppermute | solution.py:778
  98.8 16.3 %collective-permute-start.10 = (bf16[512,512]{1,0:T(8,128)(2,1)S(1)}, bf16[512,512]{1,0:T(8,128)(2,1)S(1)}, u32[]{:S(2)}, u32[]{:S(2)}) collective-permute-start(bf16[512,512]{1,0:T(8,128)(2,1)S(1)} %get-tuple-element.97.k_ref), channel_id=1, source_target_pairs={{0,1},{1,0},{2,3},{3,2},{4,5},{5,4},{6,7},{7,6},{8,9},{9,8},{10,11... | collective-permute-start | bytes 1572872 | tf_op jit(solution)/shard_map/ppermute | solution.py:778
  113.6 27.7 %collective-permute-start.18 = (bf16[12,128,128]{2,1,0:T(8,128)(2,1)}, bf16[12,128,128]{2,1,0:T(8,128)(2,1)S(1)}, u32[]{:S(2)}, u32[]{:S(2)}) collective-permute-start(bf16[12,128,128]{2,1,0:T(8,128)(2,1)} %get-tuple-element.103.w0), channel_id=1, source_target_pairs={{0,1},{1,0},{2,3},{3,2},{4,5},{5,4},{6,7},{7,6},{8,9},{9,8},{10,11... | collective-permute-start | bytes 1179656 | tf_op jit(solution)/shard_map/ppermute | solution.py:778
  114.2 27.1 %collective-permute-start.20 = (bf16[12,128,128]{2,1,0:T(8,128)(2,1)}, bf16[12,128,128]{2,1,0:T(8,128)(2,1)S(1)}, u32[]{:S(2)}, u32[]{:S(2)}) collective-permute-start(bf16[12,128,128]{2,1,0:T(8,128)(2,1)} %collective-permute-done.19.w2), channel_id=1, source_target_pairs={{0,1},{1,0},{2,3},{3,2},{4,5},{5,4},{6,7},{7,6},{8,9},{9,8},{10,11... | collective-permute-start | bytes 1179656 | tf_op jit(solution)/shard_map/ppermute | solution.py:778
  115.1 48.3 %collective-permute-start.26 = (bf16[32,128,128]{2,1,0:T(8,128)(2,1)S(1)}, bf16[32,128,128]{2,1,0:T(8,128)(2,1)S(1)}, u32[]{:S(2)}, u32[]{:S(2)}) collective-permute-start(bf16[32,128,128]{2,1,0:T(8,128)(2,1)S(1)} %copy-done.92), channel_id=1, source_target_pairs={{0,1},{1,0},{2,3},{3,2},{4,5},{5,4},{6,7},{7,6},{8,9},{9,8},{10,11... | collective-permute-start | bytes 3145736 | tf_op jit(solution)/shard_map/ppermute | solution.py:778
  115.6 47.9 %collective-permute-start.28 = (bf16[32,128,128]{2,1,0:T(8,128)(2,1)}, bf16[32,128,128]{2,1,0:T(8,128)(2,1)S(1)}, u32[]{:S(2)}, u32[]{:S(2)}) collective-permute-start(bf16[32,128,128]{2,1,0:T(8,128)(2,1)} %collective-permute-done.27.f2), channel_id=1, source_target_pairs={{0,1},{1,0},{2,3},{3,2},{4,5},{5,4},{6,7},{7,6},{8,9},{9,8},{10,11... | collective-permute-start | bytes 3145736 | tf_op jit(solution)/shard_map/ppermute | solution.py:778
  151.8 11.6 %collective-permute-start.23 = (bf16[4,128,128]{2,1,0:T(8,128)(2,1)S(1)}, bf16[4,128,128]{2,1,0:T(8,128)(2,1)S(1)}, u32[]{:S(2)}, u32[]{:S(2)}) collective-permute-start(bf16[4,128,128]{2,1,0:T(8,128)(2,1)S(1)} %copy-done.69), channel_id=1, source_target_pairs={{0,1},{1,0},{2,3},{3,2},{4,5},{5,4},{6,7},{7,6},{8,9},{9,8},{10,11... | collective-permute-start | bytes 393224 | tf_op jit(solution)/shard_map/ppermute | solution.py:778
  151.8 11.6 %collective-permute-start.25 = (bf16[4,128,128]{2,1,0:T(8,128)(2,1)S(1)}, bf16[4,128,128]{2,1,0:T(8,128)(2,1)S(1)}, u32[]{:S(2)}, u32[]{:S(2)}) collective-permute-start(bf16[4,128,128]{2,1,0:T(8,128)(2,1)S(1)} %collective-permute-done.24.a2), channel_id=1, source_target_pairs={{0,1},{1,0},{2,3},{3,2},{4,5},{5,4},{6,7},{7,6},{8,9},{9,8},{10,11... | collective-permute-start | bytes 393224 | tf_op jit(solution)/shard_map/ppermute | solution.py:778
  222.6 81.6 %collective-permute-start.40 = (bf16[2,32,128,128]{3,2,1,0:T(8,128)(2,1)}, bf16[2,32,128,128]{3,2,1,0:T(8,128)(2,1)}, u32[]{:S(2)}, u32[]{:S(2)}) collective-permute-start(bf16[2,32,128,128]{3,2,1,0:T(8,128)(2,1)} %get-tuple-element.165), channel_id=1, source_target_pairs={{0,1},{1,0},{2,3},{3,2},{4,5},{5,4},{6,7},{7,6},{8,9},{9,8},{10,11... | collective-permute-start | bytes 6291464 | tf_op jit(solution)/shard_map/ppermute | solution.py:778
  223.8 33.3 %collective-permute-start.39 = (bf16[2,4,128,128]{3,2,1,0:T(8,128)(2,1)}, bf16[2,4,128,128]{3,2,1,0:T(8,128)(2,1)}, u32[]{:S(2)}, u32[]{:S(2)}) collective-permute-start(bf16[2,4,128,128]{3,2,1,0:T(8,128)(2,1)} %get-tuple-element.163), channel_id=1, source_target_pairs={{0,1},{1,0},{2,3},{3,2},{4,5},{5,4},{6,7},{7,6},{8,9},{9,8},{10,11... | collective-permute-start | bytes 786440 | tf_op jit(solution)/shard_map/ppermute | solution.py:778
  257.1 51.0 %collective-permute-start.37 = (bf16[2,32,128,128]{3,2,1,0:T(8,128)(2,1)}, bf16[2,32,128,128]{3,2,1,0:T(8,128)(2,1)}, u32[]{:S(2)}, u32[]{:S(2)}) collective-permute-start(bf16[2,32,128,128]{3,2,1,0:T(8,128)(2,1)} %get-tuple-element.159), channel_id=1, source_target_pairs={{0,1},{1,0},{2,3},{3,2},{4,5},{5,4},{6,7},{7,6},{8,9},{9,8},{10,11... | collective-permute-start | bytes 6291464 | tf_op jit(solution)/shard_map/ppermute | solution.py:778
  259.0 55.9 %collective-permute-start.45 = (bf16[4,128,128]{2,1,0:T(8,128)(2,1)S(1)}, bf16[4,128,128]{2,1,0:T(8,128)(2,1)}, u32[]{:S(2)}, u32[]{:S(2)}) collective-permute-start(bf16[4,128,128]{2,1,0:T(8,128)(2,1)S(1)} %get-tuple-element.222), channel_id=1, source_target_pairs={{0,2},{1,3},{2,0},{3,1},{4,6},{5,7},{6,4},{7,5},{8,10},{9,11},{10,... | collective-permute-start | bytes 393224 | tf_op jit(solution)/shard_map/ppermute | solution.py:782
  287.3 28.8 %collective-permute-start.36 = (bf16[2,4,128,128]{3,2,1,0:T(8,128)(2,1)}, bf16[2,4,128,128]{3,2,1,0:T(8,128)(2,1)}, u32[]{:S(2)}, u32[]{:S(2)}) collective-permute-start(bf16[2,4,128,128]{3,2,1,0:T(8,128)(2,1)} %copy-done.91), channel_id=1, source_target_pairs={{0,1},{1,0},{2,3},{3,2},{4,5},{5,4},{6,7},{7,6},{8,9},{9,8},{10,11... | collective-permute-start | bytes 786440 | tf_op jit(solution)/shard_map/ppermute | solution.py:778
  287.9 24.2 %collective-permute-start.38 = (bf16[2,12,128,128]{3,2,1,0:T(8,128)(2,1)}, bf16[2,12,128,128]{3,2,1,0:T(8,128)(2,1)}, u32[]{:S(2)}, u32[]{:S(2)}) collective-permute-start(bf16[2,12,128,128]{3,2,1,0:T(8,128)(2,1)} %get-tuple-element.161), channel_id=1, source_target_pairs={{0,1},{1,0},{2,3},{3,2},{4,5},{5,4},{6,7},{7,6},{8,9},{9,8},{10,11... | collective-permute-start | bytes 2359304 | tf_op jit(solution)/shard_map/ppermute | solution.py:778
  304.3 10.3 %collective-permute-start.35 = (bf16[2,12,128,128]{3,2,1,0:T(8,128)(2,1)S(1)}, bf16[2,12,128,128]{3,2,1,0:T(8,128)(2,1)S(1)}, u32[]{:S(2)}, u32[]{:S(2)}) collective-permute-start(bf16[2,12,128,128]{3,2,1,0:T(8,128)(2,1)S(1)} %copy-done.112), channel_id=1, source_target_pairs={{0,1},{1,0},{2,3},{3,2},{4,5},{5,4},{6,7},{7,6},{8,9},{9,8},{10,11... | collective-permute-start | bytes 2359304 | tf_op jit(solution)/shard_map/ppermute | solution.py:778
  308.1 71.3 %collective-permute-start.46 = (bf16[32,128,128]{2,1,0:T(8,128)(2,1)S(1)}, bf16[32,128,128]{2,1,0:T(8,128)(2,1)S(1)}, u32[]{:S(2)}, u32[]{:S(2)}) collective-permute-start(bf16[32,128,128]{2,1,0:T(8,128)(2,1)S(1)} %get-tuple-element.208), channel_id=1, source_target_pairs={{0,2},{1,3},{2,0},{3,1},{4,6},{5,7},{6,4},{7,5},{8,10},{9,11},{10,... | collective-permute-start | bytes 3145736 | tf_op jit(solution)/shard_map/ppermute | solution.py:782
  312.1 67.4 %collective-permute-start.43 = (bf16[32,128,128]{2,1,0:T(8,128)(2,1)S(1)}, bf16[32,128,128]{2,1,0:T(8,128)(2,1)S(1)}, u32[]{:S(2)}, u32[]{:S(2)}) collective-permute-start(bf16[32,128,128]{2,1,0:T(8,128)(2,1)S(1)} %get-tuple-element.210), channel_id=1, source_target_pairs={{0,2},{1,3},{2,0},{3,1},{4,6},{5,7},{6,4},{7,5},{8,10},{9,11},{10,... | collective-permute-start | bytes 3145736 | tf_op jit(solution)/shard_map/ppermute | solution.py:782
  314.9 64.6 %collective-permute-start.44 = (bf16[12,128,128]{2,1,0:T(8,128)(2,1)S(1)}, bf16[12,128,128]{2,1,0:T(8,128)(2,1)S(1)}, u32[]{:S(2)}, u32[]{:S(2)}) collective-permute-start(bf16[12,128,128]{2,1,0:T(8,128)(2,1)S(1)} %get-tuple-element.218), channel_id=1, source_target_pairs={{0,2},{1,3},{2,0},{3,1},{4,6},{5,7},{6,4},{7,5},{8,10},{9,11},{10,... | collective-permute-start | bytes 1179656 | tf_op jit(solution)/shard_map/ppermute | solution.py:782
  316.1 63.3 %collective-permute-start.41 = (bf16[12,128,128]{2,1,0:T(8,128)(2,1)S(1)}, bf16[12,128,128]{2,1,0:T(8,128)(2,1)S(1)}, u32[]{:S(2)}, u32[]{:S(2)}) collective-permute-start(bf16[12,128,128]{2,1,0:T(8,128)(2,1)S(1)} %get-tuple-element.220), channel_id=1, source_target_pairs={{0,2},{1,3},{2,0},{3,1},{4,6},{5,7},{6,4},{7,5},{8,10},{9,11},{10,... | collective-permute-start | bytes 1179656 | tf_op jit(solution)/shard_map/ppermute | solution.py:782
  318.0 57.5 %collective-permute-start.42 = (bf16[4,128,128]{2,1,0:T(8,128)(2,1)S(1)}, bf16[4,128,128]{2,1,0:T(8,128)(2,1)S(1)}, u32[]{:S(2)}, u32[]{:S(2)}) collective-permute-start(bf16[4,128,128]{2,1,0:T(8,128)(2,1)S(1)} %get-tuple-element.224), channel_id=1, source_target_pairs={{0,2},{1,3},{2,0},{3,1},{4,6},{5,7},{6,4},{7,5},{8,10},{9,11},{10,... | collective-permute-start | bytes 393224 | tf_op jit(solution)/shard_map/ppermute | solution.py:782
  387.4 10.4 %collective-permute-start.51 = (bf16[1552,128]{1,0:T(8,128)(2,1)S(1)}, bf16[1552,128]{1,0:T(8,128)(2,1)S(1)}, u32[]{:S(2)}, u32[]{:S(2)}) collective-permute-start(bf16[1552,128]{1,0:T(8,128)(2,1)S(1)} %get-tuple-element.216), channel_id=1, source_target_pairs={{0,4},{8,0},{16,8},{24,16},{28,24},{20,28},{12,20},{4,12},{1,5},{9... | collective-permute-start | bytes 1191944 | tf_op jit(solution)/shard_map/ppermute | solution.py:743
  (136 other events, 1852.8 us)

commit v2 on v1

--- a/solution.py
+++ b/solution.py
@@ -167,7 +167,7 @@
     return pl.pallas_call(functools.partial(soap_kernel, len(gs)), grid=(n,), in_specs=[one]*(len(gs)+7),
         out_specs=[one]*6+[whole]*2, out_shape=[sh,shb,sh,sh,sh,sh,sh,sh],
         scratch_shapes=[pltpu.VMEM((2*n,BLK,BLK),f32)]*2,
-        compiler_params=pltpu.CompilerParams(vmem_limit_bytes=50*2**20), name="soap")(*gs,master,m1,m2,ls,rs,lb,rb)
+        compiler_params=pltpu.CompilerParams(vmem_limit_bytes=50*2**20), name="soap", cost_estimate=pl.CostEstimate(flops=60*10**9, bytes_accessed=0, transcendentals=0))(*gs,master,m1,m2,ls,rs,lb,rb)
 
 
 bf16 = jnp.bfloat16
@@ -179,6 +179,10 @@
 
 def params(mib=48):
     return pltpu.CompilerParams(vmem_limit_bytes=mib * 2**20)
+
+
+def cost(micros):
+    return pl.CostEstimate(flops=int(micros * 1e9), bytes_accessed=0, transcendentals=0)
 
 
 def shape(dims, kind=f32):
@@ -259,6 +263,7 @@
         scratch_shapes=[pltpu.VMEM((D, 3 * D), bf16)],
         compiler_params=params(),
         name="project",
+        cost_estimate=cost(3),
     )(x, bq, bv, *wqkv)
 
 
@@ -332,6 +337,7 @@
         ],
         compiler_params=params(),
         name="attend",
+        cost_estimate=cost(11),
     )(q, k, kp, v, vp, ohq, ohk)
 
 
@@ -394,6 +400,7 @@
         ],
         compiler_params=params(),
         name="post",
+        cost_estimate=cost(11),
     )(o, x, vec, b1, *wout, *wffn)
 
 
@@ -490,6 +497,7 @@
         ],
         compiler_params=params(),
         name="ffn_grad",
+        cost_estimate=cost(16),
     )(e, n2, i2, n1, i1, y, hid, slope, o, vec, *wout, *wffn)
 
 
@@ -576,6 +584,7 @@
         ],
         compiler_params=params(),
         name="attend_grad",
+        cost_estimate=cost(23),
     )(q, k, kp, v, vp, do, o, lse, ohq, ohk)
 
 
@@ -630,24 +639,99 @@
         ],
         compiler_params=params(),
         name="proj_grad",
+        cost_estimate=cost(5),
     )(dq, dk, dv, dkr, dvr, xs, dr1, *wqkv)
 
 
-def embed_grad_kernel(series_ref, g_ref, we_ref, in_ref, dwe_ref, dbe_ref):
+def embed_grad_kernel(
+    place_ref, series_ref, g_ref, we_ref, s0, q0, b0, s1, q1, b1, in_ref, keep_ref, send_ref, tab
+):
+    place = place_ref[0]
     g = g_ref[...]
     in_ref[...] = dot_hi(g, we_ref[...], 1, 1)
-    dwe_ref[...] = dot_hi(series_ref[...].astype(f32), g, 0, 0)
-    dbe_ref[...] = col_sum(g)
-
-
-def embed_grad(series, g, table):
+    tab[:LOOK] = dot_hi(series_ref[...].astype(f32), g, 0, 0)
+    tab[LOOK : LOOK + 1] = col_sum(g)
+    per_layer = 8 + FF // D
+    for layer, (sums, qsums, db1) in enumerate(((s0, q0, b0), (s1, q1, b1))):
+        base = LOOK + 1 + layer * per_layer
+        for r in range(4):
+            h = place ^ r
+            lanes = pl.ds(pl.multiple_of(h * BLK, BLK), BLK)
+            tab[base : base + 2, lanes] = qsums[0:2, r * BLK : (r + 1) * BLK]
+            tab[pl.ds(base + 5 + h, 1), :] = db1[r : r + 1, :]
+        tab[base + 2 : base + 5] = sums[0:3]
+        tab[base + 5 + FF // D : base + per_layer] = sums[3:6]
+    used = LOOK + 1 + LAYERS * per_layer
+    tab[used:] = jnp.zeros((BLK - used, D), f32)
+    for r in range(4):
+        rows = tab[pl.ds(pl.multiple_of((place ^ r) * 32, 32), 32), :].astype(bf16)
+        out = send_ref if r % 2 else keep_ref
+        for c in range(4):
+            out[r // 2, c * 32 : (c + 1) * 32] = rows[:, c * BLK : (c + 1) * BLK]
+
+
+def embed_grad(place, series, g, table, sums):
     rows = series.shape[0]
+    spec = pl.BlockSpec(memory_space=pltpu.VMEM)
     return pl.pallas_call(
         embed_grad_kernel,
-        out_shape=[shape((rows, LOOK)), shape((LOOK, D)), shape((1, D))],
+        in_specs=[pl.BlockSpec(memory_space=pltpu.SMEM)] + [spec] * 9,
+        out_shape=[
+            shape((rows, LOOK)),
+            shape((2, BLK, BLK), bf16),
+            shape((2, BLK, BLK), bf16),
+        ],
+        scratch_shapes=[pltpu.VMEM((BLK, D), f32)],
         compiler_params=params(),
         name="embed_grad",
-    )(series, g, table[:LOOK])
+        cost_estimate=cost(2),
+    )(place, series, g, table[:LOOK], *sums)
+
+
+def vector_kernel(at_ref, val_ref, first_ref, second_ref, *refs):
+    count = len(refs) - 6
+    parts = refs[:count]
+    nv_ref, n1_ref, n2_ref, bias_ref, held, tab = refs[count:]
+    share = BLK // count
+    for k in range(count):
+        held[k] = parts[k][...]
+    for d in range(count):
+        for h in range(4):
+            c, i = divmod(d * share, 32)
+            tab[h * 32 + i : h * 32 + i + share, c * BLK : (c + 1) * BLK] = held[
+                at_ref[d], at_ref[count] ^ h
+            ]
+    used = val_ref.shape[0]
+    grad = tab[:used]
+    val = val_ref[...]
+    first = 0.5 * first_ref[...] + 0.5 * grad
+    second = 0.5 * second_ref[...] + 0.5 * grad * grad
+    n1_ref[...] = first
+    n2_ref[...] = second
+    nv_ref[...] = val - rate_vector * (
+        first / CORR / (jnp.sqrt(second / CORR) + adam_eps) + weight_decay * val
+    )
+    per_layer = 8 + FF // D
+    for layer in range(LAYERS):
+        base = LOOK + 1 + layer * per_layer
+        bias_ref[2 * layer : 2 * layer + 1] = tab[base + 2 : base + 3]
+        bias_ref[2 * layer + 1 : 2 * layer + 2] = tab[base + 5 + FF // D : base + 6 + FF // D]
+
+
+def vector_update(at, values, first, second, parts):
+    spec = pl.BlockSpec(memory_space=pltpu.VMEM)
+    return pl.pallas_call(
+        vector_kernel,
+        in_specs=[pl.BlockSpec(memory_space=pltpu.SMEM)] + [spec] * (3 + len(parts)),
+        out_shape=[shape(values.shape)] * 3 + [shape((2 * LAYERS, D))],
+        scratch_shapes=[
+            pltpu.VMEM((len(parts), 4, BLK // len(parts), BLK), f32),
+            pltpu.VMEM((BLK, D), f32),
+        ],
+        compiler_params=params(),
+        name="vector",
+        cost_estimate=cost(2),
+    )(at, values, first, second, *parts)
 
 
 PARTS = ((0, 12), (12, 4), (16, 32))
@@ -676,6 +760,7 @@
         scratch_shapes=[pltpu.VMEM((total, BLK, BLK), bf16)],
         compiler_params=params(),
         name="natural",
+        cost_estimate=cost(3),
     )(at, *slots)
 
 
@@ -706,6 +791,7 @@
         out_shape=shape((count, slots_each * BLK + BLK // count, BLK), bf16),
         compiler_params=params(),
         name="routed",
+        cost_estimate=cost(4),
     )(at, table, table_got, *own, *got)
 
 
@@ -730,6 +816,7 @@
         out_shape=shape((count, slots_each * BLK, BLK), bf16),
         compiler_params=params(),
         name="routed",
+        cost_estimate=cost(4),
     )(at, *own, *got)
 
 
@@ -780,6 +867,10 @@
 
 def far_swap(value):
     return lax.ppermute(value, "head", [(i, i ^ 2) for i in range(4)])
+
+
+def tied(values, after):
+    return lax.optimization_barrier((values, after))[0]
 
 
 def one_hots(ids):
@@ -833,9 +924,14 @@
         slots = [lax.all_gather(copies, "dp", axis=0, tiled=True)]
     mine = natural_order(gather_at, slots)
     weights = []
-    for own in mine:
-        far = far_swap(own)
-        weights.append([own, core_swap(own), far, core_swap(far)])
+    far = None
+    for at in range(LAYERS):
+        for group in ((0,), (1, 2)):
+            group_own = [mine[3 * at + i] for i in group]
+            ready = group_own if far is None else tied(group_own, far)
+            far = [far_swap(one) for one in ready]
+            for own, there in zip(group_own, far):
+                weights.append([own, core_swap(own), there, core_swap(there)])
 
     windows = window_ids(window_lengths, bucket_rows)
     ids = windows.reshape(4, rows)
@@ -863,59 +959,71 @@
     far_sums = [None] * (3 * LAYERS)
     table_rows = [None] * LAYERS
 
-    def reduce_head(at, keep, send):
-        got = core_swap(send)
+    def chip_sum(at, keep, got):
         own_sums[at] = add_low(keep[0], got[0])
-        far_sums[at] = far_swap(add_low(keep[1], got[1]))
-
+        return add_low(keep[1], got[1])
+
+    moving = []
     for layer in reversed(range(LAYERS)):
         xs, q, k, v, kp, vp, o, lse, vec, n1, i1, y, hid, slope, n2, i2 = saved[layer]
         wqkv, wout, wffn = weights[3 * layer : 3 * layer + 3]
         gk, gs, ok, os, dr1, do, db1, sums = ffn_grad(
             grad, n2, i2, n1, i1, y, hid, slope, o, vec, wout, wffn
         )
-        reduce_head(3 * layer + 2, gk, gs)
-        reduce_head(3 * layer + 1, ok, os)
+        got = [core_swap(gs), core_swap(os)]
+        do, far = tied(
+            (do, [chip_sum(3 * layer + 2, gk, got[0]), chip_sum(3 * layer + 1, ok, got[1])]), moving
+        )
+        far_sums[3 * layer + 2] = far_swap(far[0])
+        far_sums[3 * layer + 1] = far_swap(far[1])
+        do = tied(do, far)
         dq, dk, dkp, dv, dvp = attend_grad(q, k, kp, v, vp, do, o, lse, ohq, ohk)
         dkr, dvr = core_swap(dkp), core_swap(dvp)
+        dkr, dvr = tied((dkr, dvr), far_sums[3 * layer + 1 : 3 * layer + 3])
         pk, ps, grad, qsums = proj_grad(dq, dk, dv, dkr, dvr, xs, dr1, wqkv)
-        reduce_head(3 * layer, pk, ps)
-        table_rows[layer] = jnp.concatenate(
-            [
-                relative(qsums[0], place),
-                relative(qsums[1], place),
-                sums[0:3],
-                relative(db1, place).reshape(FF // D, D),
-                sums[3:6],
-            ],
-            axis=0,
-        )
-    input_grad, dwe, dbe = embed_grad(series, grad, vec_values)
-    local_table = jnp.concatenate([dwe, dbe] + table_rows, axis=0)
-    vrows = local_table.shape[0]
-    padded = jnp.pad(local_table, ((0, BLK - vrows), (0, 0)))
-    parts = jnp.take(padded.reshape(4, BLK, BLK), jnp.arange(4) ^ place, axis=0).astype(bf16)
-    got = core_swap(parts[1::2])
-    tab_own = add_low(parts[0], got[0])
-    tab_far = far_swap(add_low(parts[2], got[1]))
-    share = BLK // dp
+        table_rows[layer] = (sums, qsums, db1)
+        got = core_swap(ps)
+        if layer:
+            far = chip_sum(3 * layer, pk, got)
+            grad = tied(grad, far)
+            far_sums[3 * layer] = far_swap(far)
+            moving = [far_sums[3 * layer]]
+    input_grad, tab_keep, tab_send = embed_grad(
+        place.astype(jnp.int32)[None], series, grad, vec_values, table_rows[0] + table_rows[1]
+    )
+    tab_got = core_swap(tab_send)
+    far_sums[0] = far_swap(chip_sum(0, pk, got))
+    tab_own = add_low(tab_keep[0], tab_got[0])
+    tab_far = far_swap(add_low(tab_keep[1], tab_got[1]))
     if ringed:
-        dist = (jnp.asarray(ring_at) - ring_at[spot]) % dp
+        dist = (ring_at - ring_at[spot]) % dp
         at = jnp.concatenate([inner, who, dist]).astype(jnp.int32)
         pieces = routed(at, tab_own, tab_far, own_sums, far_sums, dp, own_slots)
         terms = ring_reduce([pieces[i] for i in range(dp)], order)
         grads = [t[: own_slots * BLK].reshape(own_slots, BLK, BLK) for t in terms]
         part = sum(t[own_slots * BLK :].astype(f32) for t in terms)
+        group = jnp.stack(
+            [part] + [lax.ppermute(part, "head", [(i, i ^ r) for i in range(4)]) for r in (1, 2, 3)]
+        )
+        grads = tied(grads, group)
+        parts = [group] + [ring_shift(group, order, -k) for k in range(1, dp)]
+        vec_at = jnp.concatenate([dist, place[None]]).astype(jnp.int32)
+        vec_new_values, vec_new_first, vec_new_second, branch_bias_grads = vector_update(
+            vec_at, vec_values, vec_first, vec_second, parts
+        )
     else:
-        at = jnp.concatenate([inner, who, jnp.arange(dp)]).astype(jnp.int32)
+        at = jnp.concatenate([inner, who]).astype(jnp.int32)
         pieces = routed_plain(at, own_sums, far_sums, dp, own_slots)
         whole = lax.psum_scatter(pieces, "dp", scatter_dimension=0, tiled=True)
         grads = [whole.reshape(own_slots, BLK, BLK)]
-        part = lax.psum_scatter(
-            tab_own.astype(f32) + tab_far.astype(f32), "dp", scatter_dimension=0, tiled=True
+        total = lax.psum(tab_own.astype(f32) + tab_far.astype(f32), "dp")
+        shares = lax.all_gather(total, "head", axis=0)
+        grad_table = shares.reshape(4, 4, 32, BLK).transpose(0, 2, 1, 3).reshape(BLK, D)
+        grad_table = grad_table[: vec_values.shape[0]]
+        vec_new_values, vec_new_first, vec_new_second = adamw_update(
+            grad_table, vec_values, vec_first, vec_second
         )
-    shares = lax.all_gather(part, ("head", "dp"), axis=0, tiled=True)
-    grad_table = shares.reshape(4, BLK, BLK).reshape(BLK, D)[:vrows]
+        branch_bias_grads = branch_biases(grad_table)
     new_master, new_copy, new_first, new_second, new_left, new_right, left_next, right_next = soap(
         grads,
         master[0],
@@ -926,10 +1034,6 @@
         left_basis[0],
         right_basis[0],
     )
-    vec_new_values, vec_new_first, vec_new_second = adamw_update(
-        grad_table, vec_values, vec_first, vec_second
-    )
-    branch_bias_grads = branch_biases(grad_table)
     return (
         activations,
         input_grad,

time: 568 us -> 427 us (0.75)
  blocking collectives: 65.9 us -> 0 us
  local copies, waits for them, and re-layouts: 65 us -> 23.6 us
  waiting for transfers between devices: 159 us -> 125 us
  starting transfers between devices: 36 us -> 48.2 us
  other arithmetic: 25 us -> 17 us
    all_gather x1 -> x0, blocking collectives: 65.9 us -> none  [on_device(): shares = lax.all_gather(part, ('head', 'dp'), axis=0, tiled=True)]
    ppermute x13, waiting for transfers between devices: 105 us -> 57 us  [far_swap(): return lax.ppermute(value, 'head', [(i, i ^ 2) for i in range(4)])]
    unnamed x232 -> x134, local copies, waits for them, and re-layouts: 46.7 us -> 13.7 us
    ppermute x14 -> x21, starting transfers between devices: 16.4 us -> 27.4 us  [ring_shift(): lax.ppermute(value, 'dp', [(order[i], order[(i + by) % n]) for i in range...]
    ppermute x27, waiting for transfers between devices: 0.5 us -> 9.75 us  [core_swap(): return lax.ppermute(value, 'head', [(i, i ^ 1) for i in range(4)])]
    ppermute x14 -> x21, waiting for transfers between devices: 53.3 us -> 56.6 us  [ring_shift(): lax.ppermute(value, 'dp', [(order[i], order[(i + by) % n]) for i in range...]
  transfers between devices with their start and end apart: 54 -> 64, of which waited for: 16 -> 26; matrix products, arithmetic and copies ran while one was open for 6% -> 4% of each run, Pallas kernels for 16% -> 35%
where the time goes in v2:
time: 427 us; the launch traced here: 423 us
  Pallas kernels  207 us (48%)
  waiting for transfers between devices  125 us (29%)
  starting transfers between devices  48.2 us (11%)
  local copies, waits for them, and re-layouts  23.6 us (6%)
  other arithmetic  17 us (4%)
    pallas_call x1, Pallas kernels, soap(): pl.pallas_call(functools.partial(soap_kernel, len(gs)), grid=(n,), in_spe...  64.9 us
    ppermute x13, waiting for transfers between devices, far_swap(): return lax.ppermute(value, 'head', [(i, i ^ 2) for i in range(4)])  57 us
    ppermute x21, waiting for transfers between devices, ring_shift(): lax.ppermute(value, 'dp', [(order[i], order[(i + by) % n]) for i in range...  56.6 us
    pallas_call x2, Pallas kernels, attend_grad(): pl.pallas_call(attend_grad_kernel, grid=(D // LANES,), in_specs=[pair, pa...  44.4 us
    pallas_call x2, Pallas kernels, ffn_grad(): pl.pallas_call(ffn_grad_kernel, out_shape=[shape((2, 32, BLK, BLK), bf16)...  31.7 us
    ppermute x21, starting transfers between devices, ring_shift(): lax.ppermute(value, 'dp', [(order[i], order[(i + by) % n]) for i in range...  27.4 us
    pallas_call x2, Pallas kernels, attend(): pl.pallas_call(attend_kernel, grid=(D // LANES,), in_specs=[pair, pair, o...  22 us
    pallas_call x2, Pallas kernels, post(): pl.pallas_call(post_kernel, out_shape=[shape((rows, D)), shape((rows, LAN...  20.9 us
  transfers between devices with their start and end apart: 64, of which 26 were waited for; matrix products, arithmetic and copies ran while one was open for 4% of the time, Pallas kernels for 35%

profile of v2, /device:TPU:0, one launch (start us, length us, event | category | flops | bytes accessed | tf_op | source)
XLA Modules:
  0.0 422.8 jit_solution(8710639854659084632)
XLA Ops:
  1.8 3.1 collective-permute-start.3
  4.9 9.0 %collective-permute-done.3.refs_7_ = bf16[12,128,128]{2,1,0:T(8,128)(2,1)S(1)} collective-permute-done((bf16[12,128,128]{2,1,0:T(8,128)(2,1)S(1)}, bf16[12,128,128]{2,1,0:T(8,128)(2,1)S(1)}, u32[]{:S(2)}, u32[]{:S(2)}) %collective-permute-start.3) | collective-permute-done | bytes 393248 | tf_op jit(solution)/shard_map/ppermute | solution.py:830
  17.3 6.9 %collective-permute-done.4.refs_6_ = bf16[12,128,128]{2,1,0:T(8,128)(2,1)S(1)} collective-permute-done((bf16[12,128,128]{2,1,0:T(8,128)(2,1)S(1)}, bf16[12,128,128]{2,1,0:T(8,128)(2,1)S(1)}, u32[]{:S(2)}, u32[]{:S(2)}) %collective-permute-start.4) | collective-permute-done | bytes 393248 | tf_op jit(solution)/shard_map/ppermute | solution.py:830
  28.5 5.1 %collective-permute-done.5.refs_5_ = bf16[12,128,128]{2,1,0:T(8,128)(2,1)S(1)} collective-permute-done((bf16[12,128,128]{2,1,0:T(8,128)(2,1)S(1)}, bf16[12,128,128]{2,1,0:T(8,128)(2,1)S(1)}, u32[]{:S(2)}, u32[]{:S(2)}) %collective-permute-start.5) | collective-permute-done | bytes 393248 | tf_op jit(solution)/shard_map/ppermute | solution.py:830
  37.7 4.4 %collective-permute-done.6.refs_4_ = bf16[12,128,128]{2,1,0:T(8,128)(2,1)S(1)} collective-permute-done((bf16[12,128,128]{2,1,0:T(8,128)(2,1)S(1)}, bf16[12,128,128]{2,1,0:T(8,128)(2,1)S(1)}, u32[]{:S(2)}, u32[]{:S(2)}) %collective-permute-start.6) | collective-permute-done | bytes 393248 | tf_op jit(solution)/shard_map/ppermute | solution.py:830
  50.6 2.6 collective-permute-done.8.w2
  61.2 19.0 %collective-permute-done.16.f2 = bf16[32,128,128]{2,1,0:T(8,128)(2,1)} collective-permute-done((bf16[32,128,128]{2,1,0:T(8,128)(2,1)S(1)}, bf16[32,128,128]{2,1,0:T(8,128)(2,1)}, u32[]{:S(2)}, u32[]{:S(2)}) %collective-permute-start.16) | collective-permute-done | bytes 1048608 | tf_op jit(solution)/shard_map/ppermute | solution.py:869
  84.2 11.0 %attend.2 = (bf16[512,512]{1,0:T(8,128)(2,1)S(1)}, f32[512,512]{1,0:T(8,128)S(1)}) custom-call(bf16[512,512]{1,0:T(8,128)(2,1)S(1)} %get-tuple-element.121.q_ref, bf16[512,512]{1,0:T(8,128)(2,1)S(1)} %get-tuple-element.122.k_ref, bf16[512,512]{1,0:T(8,128)(2,1)S(1)} %collective-permute-done.10.kp_ref, bf16[512,512]{1,0:T(8,128)(2,1)S(1)} %get-tuple-element.123.v_ref, ...), custom_call_target="tpu_custom_call" | custom-call | flops 11000000512 | tf_op jit(solution)/shard_map/attend/pallas_call | solution.py:324
  98.8 10.4 %post.2 = (f32[512,512]{1,0:T(8,128)S(1)}, f32[512,128]{1,0:T(8,128)S(1)}, bf16[512,512]{1,0:T(8,128)(2,1)S(1)}, bf16[512,2048]{1,0:T(8,128)(2,1)}, bf16[512,204...) custom-call(bf16[512,512]{1,0:T(8,128)(2,1)S(1)} %get-tuple-element.124.o_ref, ...), custom_call_target="tpu_custom_call" | custom-call | flops 11000000512 | tf_op jit(solution)/shard_map/post/pallas_call | solution.py:384
  113.8 8.5 %collective-permute-done.27.f2 = bf16[32,128,128]{2,1,0:T(8,128)(2,1)} collective-permute-done((bf16[32,128,128]{2,1,0:T(8,128)(2,1)S(1)}, bf16[32,128,128]{2,1,0:T(8,128)(2,1)}, u32[]{:S(2)}, u32[]{:S(2)}) %collective-permute-start.27) | collective-permute-done | bytes 1048608 | tf_op jit(solution)/shard_map/ppermute | solution.py:869
  125.2 11.0 %attend.3 = (bf16[512,512]{1,0:T(8,128)(2,1)S(1)}, f32[512,512]{1,0:T(8,128)S(1)}) custom-call(bf16[512,512]{1,0:T(8,128)(2,1)S(1)} %get-tuple-element.132.q_ref, bf16[512,512]{1,0:T(8,128)(2,1)S(1)} %get-tuple-element.133.k_ref, bf16[512,512]{1,0:T(8,128)(2,1)S(1)} %collective-permute-done.21.kp_ref, bf16[512,512]{1,0:T(8,128)(2,1)S(1)} %get-tuple-element.134.v_ref, ...), custom_call_target="tpu_custom_call" | custom-call | flops 11000000512 | tf_op jit(solution)/shard_map/attend/pallas_call | solution.py:324
  138.5 10.5 %post.3 = (f32[512,512]{1,0:T(8,128)S(1)}, f32[512,128]{1,0:T(8,128)S(1)}, bf16[512,512]{1,0:T(8,128)(2,1)S(1)}, bf16[512,2048]{1,0:T(8,128)(2,1)}, bf16[512,204...) custom-call(bf16[512,512]{1,0:T(8,128)(2,1)S(1)} %get-tuple-element.135.o_ref, ...), custom_call_target="tpu_custom_call" | custom-call | flops 11000000512 | tf_op jit(solution)/shard_map/post/pallas_call | solution.py:384
  151.3 15.8 %ffn_grad.2 = (bf16[2,32,128,128]{3,2,1,0:T(8,128)(2,1)}, bf16[2,32,128,128]{3,2,1,0:T(8,128)(2,1)}, bf16[2,4,128,128]{3,2,1,0:T(8,128)(2,1)S(1)}, bf16[2,4,128,...) custom-call(f32[512,512]{1,0:T(8,128)S(1)} %get-tuple-element.289.e_, ...), custom_call_target="tpu_custom_call" | custom-call | flops 16000000000 | tf_op jit(solution)/shard_map/ffn_grad/pallas_call | solution.py:477
  167.7 3.7 collective-permute-done.30
  176.4 22.3 %attend_grad.2 = (bf16[512,512]{1,0:T(8,128)(2,1)S(1)}, bf16[512,512]{1,0:T(8,128)(2,1)S(1)}, bf16[512,512]{1,0:T(8,128)(2,1)S(1)}, bf16[512,512]{1,0:T(8,128)(2,1)S(1)}, bf16[512,512]{1,0:T(8,128)(2,1)S(1)}) custom-call(bf16[512,512]{1,0:T(8,128)(2,1)S(1)} %get-tuple-element.132.q_ref, bf16[512,512]{1,0:T(8,128)(2,1)S(1)} %get-tuple-element.133.k_ref, ...), custom_call_target="tpu_custom_call" | custom-call | flops 23000000512 | tf_op jit(solution)/shard_map/attend_grad/pallas_call | solution.py:568
  200.3 4.4 %collective-permute-done.33.refs_10_ = bf16[4,128,128]{2,1,0:T(8,128)(2,1)S(1)} collective-permute-done((bf16[4,128,128]{2,1,0:T(8,128)(2,1)S(1)}, bf16[4,128,128]{2,1,0:T(8,128)(2,1)S(1)}, u32[]{:S(2)}, u32[]{:S(2)}) %collective-permute-start.33) | collective-permute-done | bytes 131104 | tf_op jit(solution)/shard_map/ppermute | solution.py:869
  204.8 4.9 %proj_grad.2 = (bf16[2,12,128,128]{3,2,1,0:T(8,128)(2,1)S(1)}, bf16[2,12,128,128]{3,2,1,0:T(8,128)(2,1)}, f32[512,512]{1,0:T(8,128)}, f32[8,512]{1,0:T(8,128)S(1)}) custom-call(bf16[512,512]{1,0:T(8,128)(2,1)S(1)} %get-tuple-element.155.dq_ref, bf16[512,512]{1,0:T(8,128)(2,1)S(1)} %get-tuple-element.156.dk_ref, ...), custom_call_target="tpu_custom_call" | custom-call | flops 5000000000 | tf_op jit(solution)/shard_map/proj_grad/pallas_call | solution.py:627
  212.5 15.8 %ffn_grad.3 = (bf16[2,32,128,128]{3,2,1,0:T(8,128)(2,1)}, bf16[2,32,128,128]{3,2,1,0:T(8,128)(2,1)}, bf16[2,4,128,128]{3,2,1,0:T(8,128)(2,1)S(1)}, bf16[2,4,128,...) custom-call(f32[512,512]{1,0:T(8,128)S(1)} %copy-done.33, ...), custom_call_target="tpu_custom_call" | custom-call | flops 16000000000 | tf_op jit(solution)/shard_map/ffn_grad/pallas_call | solution.py:477
  230.0 2.7 collective-permute-done.37
  235.6 4.5 %collective-permute-done.38.refs_9_ = bf16[12,128,128]{2,1,0:T(8,128)(2,1)S(1)} collective-permute-done((bf16[12,128,128]{2,1,0:T(8,128)(2,1)S(1)}, bf16[12,128,128]{2,1,0:T(8,128)(2,1)S(1)}, u32[]{:S(2)}, u32[]{:S(2)}) %collective-permute-start.38) | collective-permute-done | bytes 393248 | tf_op jit(solution)/shard_map/ppermute | solution.py:869
  242.2 22.2 %attend_grad.3 = (bf16[512,512]{1,0:T(8,128)(2,1)S(1)}, bf16[512,512]{1,0:T(8,128)(2,1)S(1)}, bf16[512,512]{1,0:T(8,128)(2,1)S(1)}, bf16[512,512]{1,0:T(8,128)(2,1)S(1)}, bf16[512,512]{1,0:T(8,128)(2,1)S(1)}) custom-call(bf16[512,512]{1,0:T(8,128)(2,1)S(1)} %copy-done.28, bf16[512,512]{1,0:T(8,128)(2,1)S(1)} %get-tuple-element.122.k_ref, ...), custom_call_target="tpu_custom_call" | custom-call | flops 23000000512 | tf_op jit(solution)/shard_map/attend_grad/pallas_call | solution.py:568
  265.9 4.6 %collective-permute-done.41.refs_7_ = bf16[4,128,128]{2,1,0:T(8,128)(2,1)S(1)} collective-permute-done((bf16[4,128,128]{2,1,0:T(8,128)(2,1)S(1)}, bf16[4,128,128]{2,1,0:T(8,128)(2,1)S(1)}, u32[]{:S(2)}, u32[]{:S(2)}) %collective-permute-start.41) | collective-permute-done | bytes 131104 | tf_op jit(solution)/shard_map/ppermute | solution.py:869
  270.4 5.0 %proj_grad.3 = (bf16[2,12,128,128]{3,2,1,0:T(8,128)(2,1)S(1)}, bf16[2,12,128,128]{3,2,1,0:T(8,128)(2,1)}, f32[512,512]{1,0:T(8,128)}, f32[8,512]{1,0:T(8,128)S(1)}) custom-call(bf16[512,512]{1,0:T(8,128)(2,1)S(1)} %get-tuple-element.187.dq_ref, bf16[512,512]{1,0:T(8,128)(2,1)S(1)} %get-tuple-element.188.dk_ref, ...), custom_call_target="tpu_custom_call" | custom-call | flops 5000000000 | tf_op jit(solution)/shard_map/proj_grad/pallas_call | solution.py:627
  281.9 8.9 %collective-permute-done.44.tabr_ref = bf16[128,128]{1,0:T(8,128)(2,1)S(1)} collective-permute-done((bf16[128,128]{1,0:T(8,128)(2,1)S(1)}, bf16[128,128]{1,0:T(8,128)(2,1)S(1)}, u32[]{:S(2)}, u32[]{:S(2)}) %collective-permute-start.44) | collective-permute-done | bytes 32800 | tf_op jit(solution)/shard_map/ppermute | solution.py:869
  290.8 4.1 routed.1
  298.1 8.3 %collective-permute-done.47 = bf16[1552,128]{1,0:T(8,128)(2,1)S(1)} collective-permute-done((bf16[1552,128]{1,0:T(8,128)(2,1)S(1)}, bf16[1552,128]{1,0:T(8,128)(2,1)S(1)}, u32[]{:S(2)}, u32[]{:S(2)}) %collective-permute-start.47) | collective-permute-done | bytes 397344 | tf_op jit(solution)/shard_map/ppermute | solution.py:830
  309.1 7.8 %collective-permute-done.48 = bf16[1552,128]{1,0:T(8,128)(2,1)S(1)} collective-permute-done((bf16[1552,128]{1,0:T(8,128)(2,1)S(1)}, bf16[1552,128]{1,0:T(8,128)(2,1)S(1)}, u32[]{:S(2)}, u32[]{:S(2)}) %collective-permute-start.48) | collective-permute-done | bytes 397344 | tf_op jit(solution)/shard_map/ppermute | solution.py:830
  320.3 6.4 %collective-permute-done.52 = bf16[1552,128]{1,0:T(8,128)(2,1)S(1)} collective-permute-done((bf16[1552,128]{1,0:T(8,128)(2,1)S(1)}, bf16[1552,128]{1,0:T(8,128)(2,1)S(1)}, u32[]{:S(2)}, u32[]{:S(2)}) %collective-permute-start.52) | collective-permute-done | bytes 397344 | tf_op jit(solution)/shard_map/ppermute | solution.py:830
  331.3 5.8 %collective-permute-done.53 = bf16[1552,128]{1,0:T(8,128)(2,1)S(1)} collective-permute-done((bf16[1552,128]{1,0:T(8,128)(2,1)S(1)}, bf16[1552,128]{1,0:T(8,128)(2,1)S(1)}, u32[]{:S(2)}, u32[]{:S(2)}) %collective-permute-start.53) | collective-permute-done | bytes 397344 | tf_op jit(solution)/shard_map/ppermute | solution.py:830
  347.0 3.6 collective-permute-start.61
  350.8 2.6 collective-permute-start.59
  356.0 64.9 %soap.1 = (f32[12,128,128]{2,1,0:T(8,128)}, bf16[12,128,128]{2,1,0:T(8,128)(2,1)}, f32[12,128,128]{2,1,0:T(8,128)}, f32[12,128,128]{2,1,0:T(8,128)}, f32[12,128,...) custom-call(bf16[12,128,128]{2,1,0:T(8,128)(2,1)S(1)} %bitcast.139, ...), custom_call_target="tpu_custom_call" | custom-call | flops 60000002048 | tf_op jit(solution)/shard_map/soap/pallas_call | solution.py:167
  (296 shorter events, 101.4 us)
Async XLA Ops:
  1.8 12.1 %collective-permute-start.3 = (bf16[12,128,128]{2,1,0:T(8,128)(2,1)S(1)}, bf16[12,128,128]{2,1,0:T(8,128)(2,1)S(1)}, u32[]{:S(2)}, u32[]{:S(2)}) collective-permute-start(bf16[12,128,128]{2,1,0:T(8,128)(2,1)S(1)} %bitcast_convert_fusion.refs_0_), channel_id=1, source_target_pairs={{0,8},{8,16},{16,24},{24,28},{28,20},{20,12},{12,4},{4,0},{1,9},{9... | collective-permute-start | bytes 1179656 | tf_op jit(solution)/shard_map/ppermute | solution.py:830
  4.9 12.1 %collective-permute-start = (bf16[12,128,128]{2,1,0:T(8,128)(2,1)S(1)}, bf16[12,128,128]{2,1,0:T(8,128)(2,1)S(1)}, u32[]{:S(2)}, u32[]{:S(2)}) collective-permute-start(bf16[12,128,128]{2,1,0:T(8,128)(2,1)S(1)} %bitcast_convert_fusion.refs_0_), channel_id=1, source_target_pairs={{0,4},{8,0},{16,8},{24,16},{28,24},{20,28},{12,20},{4,12},{1,5},{9... | collective-permute-start | bytes 1179656 | tf_op jit(solution)/shard_map/ppermute | solution.py:830
  54.2 26.1 %collective-permute-start.16 = (bf16[32,128,128]{2,1,0:T(8,128)(2,1)S(1)}, bf16[32,128,128]{2,1,0:T(8,128)(2,1)}, u32[]{:S(2)}, u32[]{:S(2)}) collective-permute-start(bf16[32,128,128]{2,1,0:T(8,128)(2,1)S(1)} %get-tuple-element.128.f0), channel_id=1, source_target_pairs={{0,2},{1,3},{2,0},{3,1},{4,6},{5,7},{6,4},{7,5},{8,10},{9,11},{10,... | collective-permute-start | bytes 3145736 | tf_op jit(solution)/shard_map/ppermute | solution.py:869
  59.4 23.2 %collective-permute-start.10 = (bf16[512,512]{1,0:T(8,128)(2,1)S(1)}, bf16[512,512]{1,0:T(8,128)(2,1)S(1)}, u32[]{:S(2)}, u32[]{:S(2)}) collective-permute-start(bf16[512,512]{1,0:T(8,128)(2,1)S(1)} %get-tuple-element.122.k_ref), channel_id=1, source_target_pairs={{0,1},{1,0},{2,3},{3,2},{4,5},{5,4},{6,7},{7,6},{8,9},{9,8},{10,11... | collective-permute-start | bytes 1572872 | tf_op jit(solution)/shard_map/ppermute | solution.py:865
  59.6 23.5 %collective-permute-start.11 = (bf16[512,512]{1,0:T(8,128)(2,1)S(1)}, bf16[512,512]{1,0:T(8,128)(2,1)S(1)}, u32[]{:S(2)}, u32[]{:S(2)}) collective-permute-start(bf16[512,512]{1,0:T(8,128)(2,1)S(1)} %get-tuple-element.123.v_ref), channel_id=1, source_target_pairs={{0,1},{1,0},{2,3},{3,2},{4,5},{5,4},{6,7},{7,6},{8,9},{9,8},{10,11... | collective-permute-start | bytes 1572872 | tf_op jit(solution)/shard_map/ppermute | solution.py:865
  60.1 22.5 %collective-permute-start.13 = (bf16[4,128,128]{2,1,0:T(8,128)(2,1)S(1)}, bf16[4,128,128]{2,1,0:T(8,128)(2,1)S(1)}, u32[]{:S(2)}, u32[]{:S(2)}) collective-permute-start(bf16[4,128,128]{2,1,0:T(8,128)(2,1)S(1)} %get-tuple-element.127.a0), channel_id=1, source_target_pairs={{0,2},{1,3},{2,0},{3,1},{4,6},{5,7},{6,4},{7,5},{8,10},{9,11},{10,... | collective-permute-start | bytes 393224 | tf_op jit(solution)/shard_map/ppermute | solution.py:869
  61.1 36.3 %collective-permute-start.15 = (bf16[32,128,128]{2,1,0:T(8,128)(2,1)S(1)}, bf16[32,128,128]{2,1,0:T(8,128)(2,1)S(1)}, u32[]{:S(2)}, u32[]{:S(2)}) collective-permute-start(bf16[32,128,128]{2,1,0:T(8,128)(2,1)S(1)} %get-tuple-element.128.f0), channel_id=1, source_target_pairs={{0,1},{1,0},{2,3},{3,2},{4,5},{5,4},{6,7},{7,6},{8,9},{9,8},{10,11... | collective-permute-start | bytes 3145736 | tf_op jit(solution)/shard_map/ppermute | solution.py:865
  80.2 17.2 %collective-permute-start.17 = (bf16[32,128,128]{2,1,0:T(8,128)(2,1)}, bf16[32,128,128]{2,1,0:T(8,128)(2,1)S(1)}, u32[]{:S(2)}, u32[]{:S(2)}) collective-permute-start(bf16[32,128,128]{2,1,0:T(8,128)(2,1)} %collective-permute-done.16.f2), channel_id=1, source_target_pairs={{0,1},{1,0},{2,3},{3,2},{4,5},{5,4},{6,7},{7,6},{8,9},{9,8},{10,11... | collective-permute-start | bytes 3145736 | tf_op jit(solution)/shard_map/ppermute | solution.py:865
  82.6 13.6 %collective-permute-start.12 = (bf16[4,128,128]{2,1,0:T(8,128)(2,1)S(1)}, bf16[4,128,128]{2,1,0:T(8,128)(2,1)S(1)}, u32[]{:S(2)}, u32[]{:S(2)}) collective-permute-start(bf16[4,128,128]{2,1,0:T(8,128)(2,1)S(1)} %get-tuple-element.127.a0), channel_id=1, source_target_pairs={{0,1},{1,0},{2,3},{3,2},{4,5},{5,4},{6,7},{7,6},{8,9},{9,8},{10,11... | collective-permute-start | bytes 393224 | tf_op jit(solution)/shard_map/ppermute | solution.py:865
  82.6 14.7 %collective-permute-start.14 = (bf16[4,128,128]{2,1,0:T(8,128)(2,1)S(1)}, bf16[4,128,128]{2,1,0:T(8,128)(2,1)S(1)}, u32[]{:S(2)}, u32[]{:S(2)}) collective-permute-start(bf16[4,128,128]{2,1,0:T(8,128)(2,1)S(1)} %collective-permute-done.13.a2), channel_id=1, source_target_pairs={{0,1},{1,0},{2,3},{3,2},{4,5},{5,4},{6,7},{7,6},{8,9},{9,8},{10,11... | collective-permute-start | bytes 393224 | tf_op jit(solution)/shard_map/ppermute | solution.py:865
  83.1 13.1 %collective-permute-start.19 = (bf16[12,128,128]{2,1,0:T(8,128)(2,1)S(1)}, bf16[12,128,128]{2,1,0:T(8,128)(2,1)S(1)}, u32[]{:S(2)}, u32[]{:S(2)}) collective-permute-start(bf16[12,128,128]{2,1,0:T(8,128)(2,1)S(1)} %copy-done.8), channel_id=1, source_target_pairs={{0,2},{1,3},{2,0},{3,1},{4,6},{5,7},{6,4},{7,5},{8,10},{9,11},{10,... | collective-permute-start | bytes 1179656 | tf_op jit(solution)/shard_map/ppermute | solution.py:869
  96.2 13.0 %collective-permute-start.18 = (bf16[12,128,128]{2,1,0:T(8,128)(2,1)S(1)}, bf16[12,128,128]{2,1,0:T(8,128)(2,1)S(1)}, u32[]{:S(2)}, u32[]{:S(2)}) collective-permute-start(bf16[12,128,128]{2,1,0:T(8,128)(2,1)S(1)} %copy-done.8), channel_id=1, source_target_pairs={{0,1},{1,0},{2,3},{3,2},{4,5},{5,4},{6,7},{7,6},{8,9},{9,8},{10,11... | collective-permute-start | bytes 1179656 | tf_op jit(solution)/shard_map/ppermute | solution.py:865
  96.2 26.1 %collective-permute-start.27 = (bf16[32,128,128]{2,1,0:T(8,128)(2,1)S(1)}, bf16[32,128,128]{2,1,0:T(8,128)(2,1)}, u32[]{:S(2)}, u32[]{:S(2)}) collective-permute-start(bf16[32,128,128]{2,1,0:T(8,128)(2,1)S(1)} %copy-done.59), channel_id=1, source_target_pairs={{0,2},{1,3},{2,0},{3,1},{4,6},{5,7},{6,4},{7,5},{8,10},{9,11},{10,... | collective-permute-start | bytes 3145736 | tf_op jit(solution)/shard_map/ppermute | solution.py:869
  97.2 12.0 %collective-permute-start.20 = (bf16[12,128,128]{2,1,0:T(8,128)(2,1)S(1)}, bf16[12,128,128]{2,1,0:T(8,128)(2,1)S(1)}, u32[]{:S(2)}, u32[]{:S(2)}) collective-permute-start(bf16[12,128,128]{2,1,0:T(8,128)(2,1)S(1)} %collective-permute-done.19.w2), channel_id=1, source_target_pairs={{0,1},{1,0},{2,3},{3,2},{4,5},{5,4},{6,7},{7,6},{8,9},{9,8},{10,11... | collective-permute-start | bytes 1179656 | tf_op jit(solution)/shard_map/ppermute | solution.py:865
  112.2 12.5 %collective-permute-start.21 = (bf16[512,512]{1,0:T(8,128)(2,1)S(1)}, bf16[512,512]{1,0:T(8,128)(2,1)S(1)}, u32[]{:S(2)}, u32[]{:S(2)}) collective-permute-start(bf16[512,512]{1,0:T(8,128)(2,1)S(1)} %get-tuple-element.133.k_ref), channel_id=1, source_target_pairs={{0,1},{1,0},{2,3},{3,2},{4,5},{5,4},{6,7},{7,6},{8,9},{9,8},{10,11... | collective-permute-start | bytes 1572872 | tf_op jit(solution)/shard_map/ppermute | solution.py:865
  112.5 12.7 %collective-permute-start.22 = (bf16[512,512]{1,0:T(8,128)(2,1)S(1)}, bf16[512,512]{1,0:T(8,128)(2,1)S(1)}, u32[]{:S(2)}, u32[]{:S(2)}) collective-permute-start(bf16[512,512]{1,0:T(8,128)(2,1)S(1)} %get-tuple-element.134.v_ref), channel_id=1, source_target_pairs={{0,1},{1,0},{2,3},{3,2},{4,5},{5,4},{6,7},{7,6},{8,9},{9,8},{10,11... | collective-permute-start | bytes 1572872 | tf_op jit(solution)/shard_map/ppermute | solution.py:865
  112.7 12.0 %collective-permute-start.24 = (bf16[4,128,128]{2,1,0:T(8,128)(2,1)S(1)}, bf16[4,128,128]{2,1,0:T(8,128)(2,1)S(1)}, u32[]{:S(2)}, u32[]{:S(2)}) collective-permute-start(bf16[4,128,128]{2,1,0:T(8,128)(2,1)S(1)} %copy-done.18), channel_id=1, source_target_pairs={{0,2},{1,3},{2,0},{3,1},{4,6},{5,7},{6,4},{7,5},{8,10},{9,11},{10,... | collective-permute-start | bytes 393224 | tf_op jit(solution)/shard_map/ppermute | solution.py:869
  113.8 23.3 %collective-permute-start.26 = (bf16[32,128,128]{2,1,0:T(8,128)(2,1)S(1)}, bf16[32,128,128]{2,1,0:T(8,128)(2,1)S(1)}, u32[]{:S(2)}, u32[]{:S(2)}) collective-permute-start(bf16[32,128,128]{2,1,0:T(8,128)(2,1)S(1)} %copy-done.59), channel_id=1, source_target_pairs={{0,1},{1,0},{2,3},{3,2},{4,5},{5,4},{6,7},{7,6},{8,9},{9,8},{10,11... | collective-permute-start | bytes 3145736 | tf_op jit(solution)/shard_map/ppermute | solution.py:865
  122.4 14.8 %collective-permute-start.28 = (bf16[32,128,128]{2,1,0:T(8,128)(2,1)}, bf16[32,128,128]{2,1,0:T(8,128)(2,1)S(1)}, u32[]{:S(2)}, u32[]{:S(2)}) collective-permute-start(bf16[32,128,128]{2,1,0:T(8,128)(2,1)} %collective-permute-done.27.f2), channel_id=1, source_target_pairs={{0,1},{1,0},{2,3},{3,2},{4,5},{5,4},{6,7},{7,6},{8,9},{9,8},{10,11... | collective-permute-start | bytes 3145736 | tf_op jit(solution)/shard_map/ppermute | solution.py:865
  124.6 12.5 %collective-permute-start.23 = (bf16[4,128,128]{2,1,0:T(8,128)(2,1)S(1)}, bf16[4,128,128]{2,1,0:T(8,128)(2,1)S(1)}, u32[]{:S(2)}, u32[]{:S(2)}) collective-permute-start(bf16[4,128,128]{2,1,0:T(8,128)(2,1)S(1)} %copy-done.18), channel_id=1, source_target_pairs={{0,1},{1,0},{2,3},{3,2},{4,5},{5,4},{6,7},{7,6},{8,9},{9,8},{10,11... | collective-permute-start | bytes 393224 | tf_op jit(solution)/shard_map/ppermute | solution.py:865
  124.7 12.5 %collective-permute-start.25 = (bf16[4,128,128]{2,1,0:T(8,128)(2,1)S(1)}, bf16[4,128,128]{2,1,0:T(8,128)(2,1)S(1)}, u32[]{:S(2)}, u32[]{:S(2)}) collective-permute-start(bf16[4,128,128]{2,1,0:T(8,128)(2,1)S(1)} %collective-permute-done.24.a2), channel_id=1, source_target_pairs={{0,1},{1,0},{2,3},{3,2},{4,5},{5,4},{6,7},{7,6},{8,9},{9,8},{10,11... | collective-permute-start | bytes 393224 | tf_op jit(solution)/shard_map/ppermute | solution.py:865
  174.3 30.4 %collective-permute-start.34 = (bf16[32,128,128]{2,1,0:T(8,128)(2,1)S(1)}, bf16[32,128,128]{2,1,0:T(8,128)(2,1)}, u32[]{:S(2)}, u32[]{:S(2)}) collective-permute-start(bf16[32,128,128]{2,1,0:T(8,128)(2,1)S(1)} %get-tuple-element.161), channel_id=1, source_target_pairs={{0,2},{1,3},{2,0},{3,1},{4,6},{5,7},{6,4},{7,5},{8,10},{9,11},{10,... | collective-permute-start | bytes 3145736 | tf_op jit(solution)/shard_map/ppermute | solution.py:869
  228.9 11.2 %collective-permute-start.38 = (bf16[12,128,128]{2,1,0:T(8,128)(2,1)S(1)}, bf16[12,128,128]{2,1,0:T(8,128)(2,1)S(1)}, u32[]{:S(2)}, u32[]{:S(2)}) collective-permute-start(bf16[12,128,128]{2,1,0:T(8,128)(2,1)S(1)} %get-tuple-element.267), channel_id=1, source_target_pairs={{0,2},{1,3},{2,0},{3,1},{4,6},{5,7},{6,4},{7,5},{8,10},{9,11},{10,... | collective-permute-start | bytes 1179656 | tf_op jit(solution)/shard_map/ppermute | solution.py:869
  240.0 30.4 %collective-permute-start.42 = (bf16[32,128,128]{2,1,0:T(8,128)(2,1)S(1)}, bf16[32,128,128]{2,1,0:T(8,128)(2,1)S(1)}, u32[]{:S(2)}, u32[]{:S(2)}) collective-permute-start(bf16[32,128,128]{2,1,0:T(8,128)(2,1)S(1)} %get-tuple-element.183), channel_id=1, source_target_pairs={{0,2},{1,3},{2,0},{3,1},{4,6},{5,7},{6,4},{7,5},{8,10},{9,11},{10,... | collective-permute-start | bytes 3145736 | tf_op jit(solution)/shard_map/ppermute | solution.py:869
  278.9 11.8 %collective-permute-start.46 = (bf16[12,128,128]{2,1,0:T(8,128)(2,1)S(1)}, bf16[12,128,128]{2,1,0:T(8,128)(2,1)S(1)}, u32[]{:S(2)}, u32[]{:S(2)}) collective-permute-start(bf16[12,128,128]{2,1,0:T(8,128)(2,1)S(1)} %get-tuple-element.264), channel_id=1, source_target_pairs={{0,2},{1,3},{2,0},{3,1},{4,6},{5,7},{6,4},{7,5},{8,10},{9,11},{10,... | collective-permute-start | bytes 1179656 | tf_op jit(solution)/shard_map/ppermute | solution.py:869
  297.6 11.4 %collective-permute-start.51 = (bf16[1552,128]{1,0:T(8,128)(2,1)S(1)}, bf16[1552,128]{1,0:T(8,128)(2,1)S(1)}, u32[]{:S(2)}, u32[]{:S(2)}) collective-permute-start(bf16[1552,128]{1,0:T(8,128)(2,1)S(1)} %get-tuple-element.262), channel_id=1, source_target_pairs={{0,4},{8,0},{16,8},{24,16},{28,24},{20,28},{12,20},{4,12},{1,5},{9... | collective-permute-start | bytes 1191944 | tf_op jit(solution)/shard_map/ppermute | solution.py:830
  343.5 12.4 %collective-permute-start.62 = (f32[4,16,128]{2,1,0:T(8,128)S(1)}, f32[4,16,128]{2,1,0:T(8,128)S(1)}, u32[]{:S(2)}, u32[]{:S(2)}) collective-permute-start(f32[4,16,128]{2,1,0:T(8,128)S(1)} %pad_maximum_fusion.1.refs_0_), channel_id=1, source_target_pairs={{0,16},{8,24},{16,28},{24,20},{28,12},{20,4},{12,0},{4,8},{1,17},{... | collective-permute-start | bytes 98312 | tf_op jit(solution)/shard_map/ppermute | solution.py:830
  347.0 73.9 %collective-permute-start.61 = (f32[4,16,128]{2,1,0:T(8,128)S(1)}, f32[4,16,128]{2,1,0:T(8,128)S(1)}, u32[]{:S(2)}, u32[]{:S(2)}) collective-permute-start(f32[4,16,128]{2,1,0:T(8,128)S(1)} %pad_maximum_fusion.1.refs_0_), channel_id=1, source_target_pairs={{0,24},{8,28},{16,20},{24,12},{28,4},{20,0},{12,8},{4,16},{1,25},{... | collective-permute-start | bytes 98312 | tf_op jit(solution)/shard_map/ppermute | solution.py:830
  350.6 70.4 %collective-permute-start.60 = (f32[4,16,128]{2,1,0:T(8,128)S(1)}, f32[4,16,128]{2,1,0:T(8,128)S(1)}, u32[]{:S(2)}, u32[]{:S(2)}) collective-permute-start(f32[4,16,128]{2,1,0:T(8,128)S(1)} %pad_maximum_fusion.1.refs_0_), channel_id=1, source_target_pairs={{0,28},{8,20},{16,12},{24,4},{28,0},{20,8},{12,16},{4,24},{1,29},{... | collective-permute-start | bytes 98312 | tf_op jit(solution)/shard_map/ppermute | solution.py:830
  350.8 70.1 %collective-permute-start.59 = (f32[4,16,128]{2,1,0:T(8,128)S(1)}, f32[4,16,128]{2,1,0:T(8,128)S(1)}, u32[]{:S(2)}, u32[]{:S(2)}) collective-permute-start(f32[4,16,128]{2,1,0:T(8,128)S(1)} %pad_maximum_fusion.1.refs_0_), channel_id=1, source_target_pairs={{0,20},{8,12},{16,4},{24,0},{28,8},{20,16},{12,24},{4,28},{1,21},{... | collective-permute-start | bytes 98312 | tf_op jit(solution)/shard_map/ppermute | solution.py:830
  353.4 67.6 %collective-permute-start.58 = (f32[4,16,128]{2,1,0:T(8,128)S(1)}, f32[4,16,128]{2,1,0:T(8,128)S(1)}, u32[]{:S(2)}, u32[]{:S(2)}) collective-permute-start(f32[4,16,128]{2,1,0:T(8,128)S(1)} %pad_maximum_fusion.1.refs_0_), channel_id=1, source_target_pairs={{0,12},{8,4},{16,0},{24,8},{28,16},{20,24},{12,28},{4,20},{1,13},{... | collective-permute-start | bytes 98312 | tf_op jit(solution)/shard_map/ppermute | solution.py:830
  355.9 65.1 %collective-permute-start.57 = (f32[4,16,128]{2,1,0:T(8,128)S(1)}, f32[4,16,128]{2,1,0:T(8,128)S(1)}, u32[]{:S(2)}, u32[]{:S(2)}) collective-permute-start(f32[4,16,128]{2,1,0:T(8,128)S(1)} %pad_maximum_fusion.1.refs_0_), channel_id=1, source_target_pairs={{0,4},{8,0},{16,8},{24,16},{28,24},{20,28},{12,20},{4,12},{1,5},{9... | collective-permute-start | bytes 98312 | tf_op jit(solution)/shard_map/ppermute | solution.py:830
  (97 other events, 1004.2 us)

commit v3 on v2

--- a/solution.py
+++ b/solution.py
@@ -74,105 +74,159 @@
     return jnp.stack(bias_rows, axis=0)
 
 
-def dot_hi(a,b,ca,cb):
-    return lax.dot_general(a,b,(((ca,),(cb,)),((),())),precision=HI,preferred_element_type=f32)
-PANEL=32
+def dot_hi(a, b, ca, cb):
+    return lax.dot_general(
+        a, b, (((ca,), (cb,)), ((), ())), precision=HI, preferred_element_type=f32
+    )
+
+
+def terms(x, count):
+    out = []
+    for i in range(count):
+        part = x.astype(jnp.bfloat16)
+        out.append(part)
+        if i < count - 1:
+            x = x - part.astype(f32)
+    return out
+
+
+def dot_terms(a, b, ca, cb, full=False):
+    a = terms(a, 3 if full else 2)
+    b = terms(b, 3 if full else 2)
+    dims = (((ca,), (cb,)), ((), ()))
+    left = jnp.concatenate(a[:2], axis=ca)
+    right = jnp.concatenate(
+        [jnp.concatenate([b[0], b[1]], axis=cb), jnp.concatenate([b[1], b[0]], axis=cb)], axis=1 - cb
+    )
+    out = lax.dot_general(left, right, dims, preferred_element_type=f32)
+    out = out[:, :BLK] + out[:, BLK:]
+    if full:
+        out = out + lax.dot_general(
+            jnp.concatenate([a[0], a[2]], axis=ca),
+            jnp.concatenate([b[2], b[0]], axis=cb),
+            dims,
+            preferred_element_type=f32,
+        )
+    return out
+
+
+PANEL = 32
+
+
 def qr_batch(a_ref, count):
-    lane = lax.broadcasted_iota(jnp.int32,(1,1,BLK),2)
-    sub8 = lax.broadcasted_iota(jnp.int32,(1,8,1),1)
-    sub32 = lax.broadcasted_iota(jnp.int32,(1,PANEL,1),1)
-    def panel(sp, carry):
-        r0 = pl.multiple_of(sp*PANEL, PANEL)
-        block = a_ref[:, pl.ds(r0,PANEL), :]
-        block = pltpu.roll(block.reshape(count*PANEL,BLK), lax.rem(BLK - r0, BLK), 1).reshape(count,PANEL,BLK)
-        tiles = [block[:, 8*t:8*t+8, :] for t in range(PANEL//8)]
+    lane = lax.broadcasted_iota(jnp.int32, (1, 1, BLK), 2)
+    sub8 = lax.broadcasted_iota(jnp.int32, (1, 8, 1), 1)
+    sub = lax.broadcasted_iota(jnp.int32, (1, PANEL, 1), 1)
+    for r0 in range(0, BLK, PANEL):
+        tiles = [a_ref[:, r0 + 8 * t : r0 + 8 * t + 8, :] for t in range(PANEL // 8)]
         for k in range(PANEL):
-            t0, s = divmod(k,8)
-            row = tiles[t0][:, s:s+1, :]
-            inv = 1.0/row[:, :, k:k+1]
-            pn = (row + (lane==k).astype(f32))*inv
-            for t in range(t0,PANEL//8):
-                c = tiles[t][:, :, k:k+1]
-                if t==t0:
-                    if s==7: continue
+            t0, s = divmod(k, 8)
+            row = tiles[t0][:, s : s + 1, :]
+            pn = (row + (lane == r0 + k).astype(f32)) * (1.0 / row[:, :, r0 + k : r0 + k + 1])
+            for t in range(t0, PANEL // 8):
+                c = tiles[t][:, :, r0 + k : r0 + k + 1]
+                if t == t0:
+                    if s == 7:
+                        continue
                     c = jnp.where(sub8 > s, c, 0.0)
-                tiles[t] = tiles[t] - c*pn
+                tiles[t] = tiles[t] - c * pn
         done = jnp.concatenate(tiles, axis=1)
-        diag = lane==sub32
-        piv = jnp.sum(jnp.where(diag, done, 0.0), axis=2, keepdims=True)
-        done = jnp.where(diag, 1.0, jnp.where((lane > sub32) & (lane < PANEL), 0.0, done))
-        done = pltpu.roll(done.reshape(count*PANEL,BLK), r0, 1).reshape(count,PANEL,BLK)
-        scale = lax.rsqrt(piv)
-        done = done*scale
-        a_ref[:, pl.ds(r0,PANEL), :] = done
-        @pl.when(sp < BLK//PANEL-1)
-        def _():
-            lane2 = lax.broadcasted_iota(jnp.int32,(BLK,BLK),1)
-            row2 = lax.broadcasted_iota(jnp.int32,(BLK,BLK),0)
-            clear = (row2 >= r0+PANEL) & (lane2 >= r0) & (lane2 < r0+PANEL)
-            lanep = lax.broadcasted_iota(jnp.int32,(PANEL,BLK),1)
+        diag = lane == sub + r0
+        pivot = jnp.sum(jnp.where(diag, done, 0.0), axis=2, keepdims=True)
+        done = jnp.where(diag, 1.0, jnp.where((lane > sub + r0) & (lane < r0 + PANEL), 0.0, done))
+        done = done * lax.rsqrt(pivot)
+        a_ref[:, r0 : r0 + PANEL, :] = done
+        r1 = r0 + PANEL
+        if r1 < BLK:
+            lane2 = lax.broadcasted_iota(jnp.int32, (BLK - r1, BLK), 1)
+            clear = (lane2 >= r0) & (lane2 < r1)
+            z0, z1, z2 = terms(done, 3)
+            left = jnp.concatenate([z0, z0, z0, z1, z1, z2], axis=1)
+            right = jnp.concatenate([z0, z1, z2, z0, z1, z0], axis=1)
             for b in range(count):
-                z = a_ref[b, pl.ds(r0,PANEL), :]
-                zm = jnp.where(lanep >= r0+PANEL, z, 0.0)
-                upd = dot_hi(zm, z, 0, 0)
-                a_ref[b] = jnp.where(clear, 0.0, a_ref[b]) - upd
-        return carry
-    lax.fori_loop(0, BLK//PANEL, panel, 0)
+                update = lax.dot_general(
+                    left[b], right[b], (((0,), (0,)), ((), ())), preferred_element_type=f32
+                )
+                a_ref[b, r1:, :] = jnp.where(clear, 0.0, a_ref[b, r1:, :]) - update[r1:]
+
 
 def soap_kernel(count, *refs):
-    g = sum(ref[0].astype(f32) for ref in refs[:count])
-    soap_body(g, *refs[count:])
-
-
-def soap_body(g, mas_ref, m1_ref, m2_ref, ls_ref, rs_ref, lb_ref, rb_ref,
-                nm_ref, nc_ref, n1_ref, n2_ref, nl_ref, nr_ref, ql_ref, qr_ref, mat_ref, a_ref):
-    n = pl.num_programs(0); i = pl.program_id(0)
-    lb = lb_ref[0]; rb = rb_ref[0]
-    rot = dot_hi(dot_hi(lb,g,0,0), rb, 1, 0)
-    n1 = 0.5*m1_ref[0]+0.5*rot
-    n2 = 0.5*m2_ref[0]+0.5*rot*rot
-    n1_ref[0]=n1; n2_ref[0]=n2
-    corr = 1.0-0.5**STEP
-    ratio = n1/corr/(jnp.sqrt(n2/corr)+1e-8)
-    upd = dot_hi(dot_hi(lb,ratio,1,0), rb, 1, 1)
-    mas = mas_ref[0]
-    nm = mas - 0.02*(upd+0.01*mas)
-    nm_ref[0]=nm; nc_ref[0]=nm.astype(jnp.bfloat16)
-    nl = 0.5*ls_ref[0]+0.5*dot_hi(g,g,1,1)
-    nr = 0.5*rs_ref[0]+0.5*dot_hi(g,g,0,0)
-    nl_ref[0]=nl; nr_ref[0]=nr
-    for side,(st,ba) in enumerate(((nl,lb),(nr,rb))):
-        m = dot_hi(st,ba,1,0)
-        m = m*lax.rsqrt(jnp.sum(m*m,axis=0,keepdims=True))
-        mat_ref[2*i+side] = m
-        a_ref[2*i+side] = dot_hi(m,m,0,0)
-    @pl.when(i==n-1)
+    for s in range(refs[0].shape[0]):
+        soap_slot(s, sum(ref[s].astype(f32) for ref in refs[:count]), *refs[count:])
+    soap_finish(*refs[-4:])
+
+
+def soap_slot(
+    s, g, mas_ref, m1_ref, m2_ref, ls_ref, rs_ref, lb_ref, rb_ref,
+    nm_ref, nc_ref, n1_ref, n2_ref, nl_ref, nr_ref, ql_ref, qr_ref, mat_ref, a_ref,
+):
+    group = mas_ref.shape[0]
+    lb = lb_ref[s]
+    rb = rb_ref[s]
+    rot = dot_terms(dot_terms(lb, g, 0, 0), rb, 1, 0)
+    n1 = 0.5 * m1_ref[s] + 0.5 * rot
+    n2 = 0.5 * m2_ref[s] + 0.5 * rot * rot
+    n1_ref[s] = n1
+    n2_ref[s] = n2
+    corr = 1.0 - 0.5**STEP
+    ratio = n1 / corr / (jnp.sqrt(n2 / corr) + adam_eps)
+    upd = dot_terms(dot_terms(lb, ratio, 1, 0), rb, 1, 1)
+    mas = mas_ref[s]
+    nm = mas - rate_matrix * (upd + weight_decay * mas)
+    nm_ref[s] = nm
+    nc_ref[s] = nm.astype(jnp.bfloat16)
+    nl = 0.5 * ls_ref[s] + 0.5 * dot_terms(g, g, 1, 1)
+    nr = 0.5 * rs_ref[s] + 0.5 * dot_terms(g, g, 0, 0)
+    nl_ref[s] = nl
+    nr_ref[s] = nr
+    for side, (st, ba) in enumerate(((nl, lb), (nr, rb))):
+        m = dot_terms(st, ba, 1, 0, True)
+        m = m * lax.rsqrt(jnp.sum(m * m, axis=0, keepdims=True))
+        at = 2 * (pl.program_id(0) * group + s) + side
+        mat_ref[at] = m
+        a_ref[at] = dot_terms(m, m, 0, 0, True)
+
+
+def soap_finish(ql_ref, qr_ref, mat_ref, a_ref):
+    @pl.when(pl.program_id(0) == pl.num_programs(0) - 1)
     def _():
         count = a_ref.shape[0]
         qr_batch(a_ref, count)
-        keep = lax.broadcasted_iota(jnp.int32,(BLK,BLK),1) <= lax.broadcasted_iota(jnp.int32,(BLK,BLK),0)
-        def fin(j, c):
-            for side,ref in enumerate((ql_ref,qr_ref)):
-                x = jnp.where(keep, a_ref[2*j+side], 0.0)
-                ref[j] = dot_hi(mat_ref[2*j+side], x, 1, 1)
-            return c
-        lax.fori_loop(0, n, fin, 0)
+        keep = lax.broadcasted_iota(jnp.int32, (BLK, BLK), 1) <= lax.broadcasted_iota(
+            jnp.int32, (BLK, BLK), 0
+        )
+        for j in range(count // 2):
+            for side, ref in enumerate((ql_ref, qr_ref)):
+                x = jnp.where(keep, a_ref[2 * j + side], 0.0)
+                ref[j] = dot_terms(mat_ref[2 * j + side], x, 1, 1, True)
+
 
 def soap(gs, master, m1, m2, ls, rs, lb, rb):
     n = master.shape[0]
-    one = pl.BlockSpec((1,BLK,BLK), lambda i:(i,0,0))
-    whole = pl.BlockSpec((n,BLK,BLK), lambda i:(0,0,0))
-    sh = jax.ShapeDtypeStruct((n,BLK,BLK), f32)
-    shb = jax.ShapeDtypeStruct((n,BLK,BLK), jnp.bfloat16)
-    return pl.pallas_call(functools.partial(soap_kernel, len(gs)), grid=(n,), in_specs=[one]*(len(gs)+7),
-        out_specs=[one]*6+[whole]*2, out_shape=[sh,shb,sh,sh,sh,sh,sh,sh],
-        scratch_shapes=[pltpu.VMEM((2*n,BLK,BLK),f32)]*2,
-        compiler_params=pltpu.CompilerParams(vmem_limit_bytes=50*2**20), name="soap", cost_estimate=pl.CostEstimate(flops=60*10**9, bytes_accessed=0, transcendentals=0))(*gs,master,m1,m2,ls,rs,lb,rb)
+    group = SOAP_GROUP if n % SOAP_GROUP == 0 else n
+    one = pl.BlockSpec((group, BLK, BLK), lambda i: (i, 0, 0))
+    whole = pl.BlockSpec((n, BLK, BLK), lambda i: (0, 0, 0))
+    sh = jax.ShapeDtypeStruct((n, BLK, BLK), f32)
+    shb = jax.ShapeDtypeStruct((n, BLK, BLK), jnp.bfloat16)
+    return pl.pallas_call(
+        functools.partial(soap_kernel, len(gs)),
+        grid=(n // group,),
+        in_specs=[one] * (len(gs) + 7),
+        out_specs=[one] * 6 + [whole] * 2,
+        out_shape=[sh, shb, sh, sh, sh, sh, sh, sh],
+        scratch_shapes=[pltpu.VMEM((2 * n, BLK, BLK), f32)] * 2,
+        compiler_params=pltpu.CompilerParams(vmem_limit_bytes=50 * 2**20),
+        cost_estimate=pl.CostEstimate(flops=40 * 10**9, bytes_accessed=0, transcendentals=0),
+        name="soap",
+    )(*gs, master, m1, m2, ls, rs, lb, rb)
+
+
+SOAP_GROUP = 2
 
 
 bf16 = jnp.bfloat16
 LANES = 128
-ROW_TILE = 256
+ROW_TILE = 512
 BIG = 1e30
 CORR = 1.0 - 0.5**STEP
 

time: 427 us -> 379 us (0.89)
  Pallas kernels: 207 us -> 149 us
  waiting for transfers between devices: 125 us -> 134 us
    pallas_call x1, Pallas kernels: 64.9 us -> 37.3 us  [soap(): pl.pallas_call(functools.partial(soap_kernel, len(gs)), grid=(n // group,...]
    pallas_call x2, Pallas kernels: 44.4 us -> 32.3 us  [attend_grad(): pl.pallas_call(attend_grad_kernel, grid=(D // LANES,), in_specs=[pair, pa...]
    ppermute x13, waiting for transfers between devices: 57 us -> 66.1 us  [far_swap(): return lax.ppermute(value, 'head', [(i, i ^ 2) for i in range(4)])]
    pallas_call x2, Pallas kernels: 31.7 us -> 23.3 us  [ffn_grad(): pl.pallas_call(ffn_grad_kernel, out_shape=[shape((2, 32, BLK, BLK), bf16)...]
  transfers between devices with their start and end apart: 64 -> 64, of which waited for: 26 -> 26; matrix products, arithmetic and copies ran while one was open for 4% -> 5% of each run, Pallas kernels for 35% -> 27%
where the time goes in v3:
time: 379 us; the launch traced here: 374 us
  Pallas kernels  149 us (39%)
  waiting for transfers between devices  134 us (35%)
  starting transfers between devices  48.1 us (13%)
  local copies, waits for them, and re-layouts  24 us (6%)
  other arithmetic  17 us (4%)
    ppermute x13, waiting for transfers between devices, far_swap(): return lax.ppermute(value, 'head', [(i, i ^ 2) for i in range(4)])  66.1 us
    ppermute x21, waiting for transfers between devices, ring_shift(): lax.ppermute(value, 'dp', [(order[i], order[(i + by) % n]) for i in range...  56.5 us
    pallas_call x1, Pallas kernels, soap(): pl.pallas_call(functools.partial(soap_kernel, len(gs)), grid=(n // group,...  37.3 us
    pallas_call x2, Pallas kernels, attend_grad(): pl.pallas_call(attend_grad_kernel, grid=(D // LANES,), in_specs=[pair, pa...  32.3 us
    ppermute x21, starting transfers between devices, ring_shift(): lax.ppermute(value, 'dp', [(order[i], order[(i + by) % n]) for i in range...  27.4 us
    pallas_call x2, Pallas kernels, ffn_grad(): pl.pallas_call(ffn_grad_kernel, out_shape=[shape((2, 32, BLK, BLK), bf16)...  23.3 us
    pallas_call x2, Pallas kernels, attend(): pl.pallas_call(attend_kernel, grid=(D // LANES,), in_specs=[pair, pair, o...  18.4 us
    pallas_call x2, Pallas kernels, post(): pl.pallas_call(post_kernel, out_shape=[shape((rows, D)), shape((rows, LAN...  17.5 us
  transfers between devices with their start and end apart: 64, of which 26 were waited for; matrix products, arithmetic and copies ran while one was open for 5% of the time, Pallas kernels for 27%

profile of v3, /device:TPU:0, one launch (start us, length us, event | category | flops | bytes accessed | tf_op | source)
XLA Modules:
  0.0 374.3 jit_solution(467691067759232134)
XLA Ops:
  1.8 3.1 collective-permute-start.3
  4.9 9.0 %collective-permute-done.3.refs_7_ = bf16[12,128,128]{2,1,0:T(8,128)(2,1)S(1)} collective-permute-done((bf16[12,128,128]{2,1,0:T(8,128)(2,1)S(1)}, bf16[12,128,128]{2,1,0:T(8,128)(2,1)S(1)}, u32[]{:S(2)}, u32[]{:S(2)}) %collective-permute-start.3) | collective-permute-done | bytes 393248 | tf_op jit(solution)/shard_map/ppermute | solution.py:884
  17.3 6.9 %collective-permute-done.4.refs_6_ = bf16[12,128,128]{2,1,0:T(8,128)(2,1)S(1)} collective-permute-done((bf16[12,128,128]{2,1,0:T(8,128)(2,1)S(1)}, bf16[12,128,128]{2,1,0:T(8,128)(2,1)S(1)}, u32[]{:S(2)}, u32[]{:S(2)}) %collective-permute-start.4) | collective-permute-done | bytes 393248 | tf_op jit(solution)/shard_map/ppermute | solution.py:884
  28.5 5.1 %collective-permute-done.5.refs_5_ = bf16[12,128,128]{2,1,0:T(8,128)(2,1)S(1)} collective-permute-done((bf16[12,128,128]{2,1,0:T(8,128)(2,1)S(1)}, bf16[12,128,128]{2,1,0:T(8,128)(2,1)S(1)}, u32[]{:S(2)}, u32[]{:S(2)}) %collective-permute-start.5) | collective-permute-done | bytes 393248 | tf_op jit(solution)/shard_map/ppermute | solution.py:884
  37.7 4.4 %collective-permute-done.6.refs_4_ = bf16[12,128,128]{2,1,0:T(8,128)(2,1)S(1)} collective-permute-done((bf16[12,128,128]{2,1,0:T(8,128)(2,1)S(1)}, bf16[12,128,128]{2,1,0:T(8,128)(2,1)S(1)}, u32[]{:S(2)}, u32[]{:S(2)}) %collective-permute-start.6) | collective-permute-done | bytes 393248 | tf_op jit(solution)/shard_map/ppermute | solution.py:884
  50.6 2.6 collective-permute-done.8.w2
  60.4 19.9 %collective-permute-done.16.f2 = bf16[32,128,128]{2,1,0:T(8,128)(2,1)} collective-permute-done((bf16[32,128,128]{2,1,0:T(8,128)(2,1)S(1)}, bf16[32,128,128]{2,1,0:T(8,128)(2,1)}, u32[]{:S(2)}, u32[]{:S(2)}) %collective-permute-start.16) | collective-permute-done | bytes 1048608 | tf_op jit(solution)/shard_map/ppermute | solution.py:923
  84.2 9.3 %attend.2 = (bf16[512,512]{1,0:T(8,128)(2,1)S(1)}, f32[512,512]{1,0:T(8,128)S(1)}) custom-call(bf16[512,512]{1,0:T(8,128)(2,1)S(1)} %get-tuple-element.121.q_ref, bf16[512,512]{1,0:T(8,128)(2,1)S(1)} %get-tuple-element.122.k_ref, bf16[512,512]{1,0:T(8,128)(2,1)S(1)} %collective-permute-done.10.kp_ref, bf16[512,512]{1,0:T(8,128)(2,1)S(1)} %get-tuple-element.123.v_ref, ...), custom_call_target="tpu_custom_call" | custom-call | flops 11000000512 | tf_op jit(solution)/shard_map/attend/pallas_call | solution.py:378
  97.1 8.7 %post.2 = (f32[512,512]{1,0:T(8,128)S(1)}, f32[512,128]{1,0:T(8,128)S(1)}, bf16[512,512]{1,0:T(8,128)(2,1)S(1)}, bf16[512,2048]{1,0:T(8,128)(2,1)}, bf16[512,204...) custom-call(bf16[512,512]{1,0:T(8,128)(2,1)S(1)} %get-tuple-element.124.o_ref, ...), custom_call_target="tpu_custom_call" | custom-call | flops 11000000512 | tf_op jit(solution)/shard_map/post/pallas_call | solution.py:438
  110.5 10.2 %collective-permute-done.27.f2 = bf16[32,128,128]{2,1,0:T(8,128)(2,1)} collective-permute-done((bf16[32,128,128]{2,1,0:T(8,128)(2,1)S(1)}, bf16[32,128,128]{2,1,0:T(8,128)(2,1)}, u32[]{:S(2)}, u32[]{:S(2)}) %collective-permute-start.27) | collective-permute-done | bytes 1048608 | tf_op jit(solution)/shard_map/ppermute | solution.py:923
  123.5 9.0 %attend.3 = (bf16[512,512]{1,0:T(8,128)(2,1)S(1)}, f32[512,512]{1,0:T(8,128)S(1)}) custom-call(bf16[512,512]{1,0:T(8,128)(2,1)S(1)} %get-tuple-element.132.q_ref, bf16[512,512]{1,0:T(8,128)(2,1)S(1)} %get-tuple-element.133.k_ref, bf16[512,512]{1,0:T(8,128)(2,1)S(1)} %collective-permute-done.21.kp_ref, bf16[512,512]{1,0:T(8,128)(2,1)S(1)} %get-tuple-element.134.v_ref, ...), custom_call_target="tpu_custom_call" | custom-call | flops 11000000512 | tf_op jit(solution)/shard_map/attend/pallas_call | solution.py:378
  135.0 8.8 %post.3 = (f32[512,512]{1,0:T(8,128)S(1)}, f32[512,128]{1,0:T(8,128)S(1)}, bf16[512,512]{1,0:T(8,128)(2,1)S(1)}, bf16[512,2048]{1,0:T(8,128)(2,1)}, bf16[512,204...) custom-call(bf16[512,512]{1,0:T(8,128)(2,1)S(1)} %get-tuple-element.135.o_ref, ...), custom_call_target="tpu_custom_call" | custom-call | flops 11000000512 | tf_op jit(solution)/shard_map/post/pallas_call | solution.py:438
  146.1 11.6 %ffn_grad.2 = (bf16[2,32,128,128]{3,2,1,0:T(8,128)(2,1)}, bf16[2,32,128,128]{3,2,1,0:T(8,128)(2,1)}, bf16[2,4,128,128]{3,2,1,0:T(8,128)(2,1)S(1)}, bf16[2,4,128,...) custom-call(f32[512,512]{1,0:T(8,128)S(1)} %get-tuple-element.289.e_, ...), custom_call_target="tpu_custom_call" | custom-call | flops 16000000000 | tf_op jit(solution)/shard_map/ffn_grad/pallas_call | solution.py:531
  158.3 3.7 collective-permute-done.30
  166.9 16.1 %attend_grad.2 = (bf16[512,512]{1,0:T(8,128)(2,1)S(1)}, bf16[512,512]{1,0:T(8,128)(2,1)S(1)}, bf16[512,512]{1,0:T(8,128)(2,1)S(1)}, bf16[512,512]{1,0:T(8,128)(2,1)S(1)}, bf16[512,512]{1,0:T(8,128)(2,1)S(1)}) custom-call(bf16[512,512]{1,0:T(8,128)(2,1)S(1)} %get-tuple-element.132.q_ref, bf16[512,512]{1,0:T(8,128)(2,1)S(1)} %get-tuple-element.133.k_ref, ...), custom_call_target="tpu_custom_call" | custom-call | flops 23000000512 | tf_op jit(solution)/shard_map/attend_grad/pallas_call | solution.py:622
  184.8 8.2 %collective-permute-done.33.refs_10_ = bf16[4,128,128]{2,1,0:T(8,128)(2,1)S(1)} collective-permute-done((bf16[4,128,128]{2,1,0:T(8,128)(2,1)S(1)}, bf16[4,128,128]{2,1,0:T(8,128)(2,1)S(1)}, u32[]{:S(2)}, u32[]{:S(2)}) %collective-permute-start.33) | collective-permute-done | bytes 131104 | tf_op jit(solution)/shard_map/ppermute | solution.py:923
  193.0 4.1 %proj_grad.2 = (bf16[2,12,128,128]{3,2,1,0:T(8,128)(2,1)S(1)}, bf16[2,12,128,128]{3,2,1,0:T(8,128)(2,1)}, f32[512,512]{1,0:T(8,128)}, f32[8,512]{1,0:T(8,128)S(1)}) custom-call(bf16[512,512]{1,0:T(8,128)(2,1)S(1)} %get-tuple-element.155.dq_ref, bf16[512,512]{1,0:T(8,128)(2,1)S(1)} %get-tuple-element.156.dk_ref, ...), custom_call_target="tpu_custom_call" | custom-call | flops 5000000000 | tf_op jit(solution)/shard_map/proj_grad/pallas_call | solution.py:681
  200.0 11.6 %ffn_grad.3 = (bf16[2,32,128,128]{3,2,1,0:T(8,128)(2,1)}, bf16[2,32,128,128]{3,2,1,0:T(8,128)(2,1)}, bf16[2,4,128,128]{3,2,1,0:T(8,128)(2,1)S(1)}, bf16[2,4,128,...) custom-call(f32[512,512]{1,0:T(8,128)S(1)} %copy-done.33, ...), custom_call_target="tpu_custom_call" | custom-call | flops 16000000000 | tf_op jit(solution)/shard_map/ffn_grad/pallas_call | solution.py:531
  213.1 2.9 collective-permute-done.37
  218.8 4.5 %collective-permute-done.38.refs_9_ = bf16[12,128,128]{2,1,0:T(8,128)(2,1)S(1)} collective-permute-done((bf16[12,128,128]{2,1,0:T(8,128)(2,1)S(1)}, bf16[12,128,128]{2,1,0:T(8,128)(2,1)S(1)}, u32[]{:S(2)}, u32[]{:S(2)}) %collective-permute-start.38) | collective-permute-done | bytes 393248 | tf_op jit(solution)/shard_map/ppermute | solution.py:923
  225.3 16.2 %attend_grad.3 = (bf16[512,512]{1,0:T(8,128)(2,1)S(1)}, bf16[512,512]{1,0:T(8,128)(2,1)S(1)}, bf16[512,512]{1,0:T(8,128)(2,1)S(1)}, bf16[512,512]{1,0:T(8,128)(2,1)S(1)}, bf16[512,512]{1,0:T(8,128)(2,1)S(1)}) custom-call(bf16[512,512]{1,0:T(8,128)(2,1)S(1)} %copy-done.28, bf16[512,512]{1,0:T(8,128)(2,1)S(1)} %get-tuple-element.122.k_ref, ...), custom_call_target="tpu_custom_call" | custom-call | flops 23000000512 | tf_op jit(solution)/shard_map/attend_grad/pallas_call | solution.py:622
  243.2 7.3 %collective-permute-done.41.refs_7_ = bf16[4,128,128]{2,1,0:T(8,128)(2,1)S(1)} collective-permute-done((bf16[4,128,128]{2,1,0:T(8,128)(2,1)S(1)}, bf16[4,128,128]{2,1,0:T(8,128)(2,1)S(1)}, u32[]{:S(2)}, u32[]{:S(2)}) %collective-permute-start.41) | collective-permute-done | bytes 131104 | tf_op jit(solution)/shard_map/ppermute | solution.py:923
  250.5 4.0 %proj_grad.3 = (bf16[2,12,128,128]{3,2,1,0:T(8,128)(2,1)S(1)}, bf16[2,12,128,128]{3,2,1,0:T(8,128)(2,1)}, f32[512,512]{1,0:T(8,128)}, f32[8,512]{1,0:T(8,128)S(1)}) custom-call(bf16[512,512]{1,0:T(8,128)(2,1)S(1)} %get-tuple-element.187.dq_ref, bf16[512,512]{1,0:T(8,128)(2,1)S(1)} %get-tuple-element.188.dk_ref, ...), custom_call_target="tpu_custom_call" | custom-call | flops 5000000000 | tf_op jit(solution)/shard_map/proj_grad/pallas_call | solution.py:681
  261.0 8.9 %collective-permute-done.44.tabr_ref = bf16[128,128]{1,0:T(8,128)(2,1)S(1)} collective-permute-done((bf16[128,128]{1,0:T(8,128)(2,1)S(1)}, bf16[128,128]{1,0:T(8,128)(2,1)S(1)}, u32[]{:S(2)}, u32[]{:S(2)}) %collective-permute-start.44) | collective-permute-done | bytes 32800 | tf_op jit(solution)/shard_map/ppermute | solution.py:923
  269.9 4.1 %routed.1 = bf16[8,1552,128]{2,1,0:T(8,128)(2,1)} custom-call(s32[200]{0:T(256)S(1)} %pad_add_fusion.at_ref, bf16[128,128]{1,0:T(8,128)(2,1)S(1)} %get-tuple-element.286.tab_ref, bf16[128,128]{1,0:T(8,128)(2,1)S(1)} %collective-permute-done.44.tabr_ref, bf16[12,128,128]{2,1,0:T(8,128)(2,1)S(1)} %get-tuple-element.265.refs_0_, ...), custom_call_target="tpu_custom_call" | custom-call | flops 4000000000 | tf_op jit(solution)/shard_map/routed/pallas_call | solution.py:842
  277.2 8.3 %collective-permute-done.47 = bf16[1552,128]{1,0:T(8,128)(2,1)S(1)} collective-permute-done((bf16[1552,128]{1,0:T(8,128)(2,1)S(1)}, bf16[1552,128]{1,0:T(8,128)(2,1)S(1)}, u32[]{:S(2)}, u32[]{:S(2)}) %collective-permute-start.47) | collective-permute-done | bytes 397344 | tf_op jit(solution)/shard_map/ppermute | solution.py:884
  288.2 7.8 %collective-permute-done.48 = bf16[1552,128]{1,0:T(8,128)(2,1)S(1)} collective-permute-done((bf16[1552,128]{1,0:T(8,128)(2,1)S(1)}, bf16[1552,128]{1,0:T(8,128)(2,1)S(1)}, u32[]{:S(2)}, u32[]{:S(2)}) %collective-permute-start.48) | collective-permute-done | bytes 397344 | tf_op jit(solution)/shard_map/ppermute | solution.py:884
  299.4 6.4 %collective-permute-done.52 = bf16[1552,128]{1,0:T(8,128)(2,1)S(1)} collective-permute-done((bf16[1552,128]{1,0:T(8,128)(2,1)S(1)}, bf16[1552,128]{1,0:T(8,128)(2,1)S(1)}, u32[]{:S(2)}, u32[]{:S(2)}) %collective-permute-start.52) | collective-permute-done | bytes 397344 | tf_op jit(solution)/shard_map/ppermute | solution.py:884
  310.4 5.8 %collective-permute-done.53 = bf16[1552,128]{1,0:T(8,128)(2,1)S(1)} collective-permute-done((bf16[1552,128]{1,0:T(8,128)(2,1)S(1)}, bf16[1552,128]{1,0:T(8,128)(2,1)S(1)}, u32[]{:S(2)}, u32[]{:S(2)}) %collective-permute-start.53) | collective-permute-done | bytes 397344 | tf_op jit(solution)/shard_map/ppermute | solution.py:884
  326.1 3.6 collective-permute-start.61
  329.9 2.6 collective-permute-start.59
  335.1 37.3 %soap.1 = (f32[12,128,128]{2,1,0:T(8,128)}, bf16[12,128,128]{2,1,0:T(8,128)(2,1)}, f32[12,128,128]{2,1,0:T(8,128)}, f32[12,128,128]{2,1,0:T(8,128)}, f32[12,128,...) custom-call(bf16[12,128,128]{2,1,0:T(8,128)(2,1)S(1)} %bitcast.139, ...), custom_call_target="tpu_custom_call" | custom-call | flops 40000000000 | tf_op jit(solution)/shard_map/soap/pallas_call | solution.py:211
  (296 shorter events, 100.5 us)
Async XLA Ops:
  1.8 12.1 %collective-permute-start.3 = (bf16[12,128,128]{2,1,0:T(8,128)(2,1)S(1)}, bf16[12,128,128]{2,1,0:T(8,128)(2,1)S(1)}, u32[]{:S(2)}, u32[]{:S(2)}) collective-permute-start(bf16[12,128,128]{2,1,0:T(8,128)(2,1)S(1)} %bitcast_convert_fusion.refs_0_), channel_id=1, source_target_pairs={{0,8},{8,16},{16,24},{24,28},{28,20},{20,12},{12,4},{4,0},{1,9},{9... | collective-permute-start | bytes 1179656 | tf_op jit(solution)/shard_map/ppermute | solution.py:884
  4.9 12.1 %collective-permute-start = (bf16[12,128,128]{2,1,0:T(8,128)(2,1)S(1)}, bf16[12,128,128]{2,1,0:T(8,128)(2,1)S(1)}, u32[]{:S(2)}, u32[]{:S(2)}) collective-permute-start(bf16[12,128,128]{2,1,0:T(8,128)(2,1)S(1)} %bitcast_convert_fusion.refs_0_), channel_id=1, source_target_pairs={{0,4},{8,0},{16,8},{24,16},{28,24},{20,28},{12,20},{4,12},{1,5},{9... | collective-permute-start | bytes 1179656 | tf_op jit(solution)/shard_map/ppermute | solution.py:884
  17.1 10.9 %collective-permute-start.1 = (bf16[12,128,128]{2,1,0:T(8,128)(2,1)S(1)}, bf16[12,128,128]{2,1,0:T(8,128)(2,1)S(1)}, u32[]{:S(2)}, u32[]{:S(2)}) collective-permute-start(bf16[12,128,128]{2,1,0:T(8,128)(2,1)S(1)} %collective-permute-done.refs_1_), channel_id=1, source_target_pairs={{0,4},{8,0},{16,8},{24,16},{28,24},{20,28},{12,20},{4,12},{1,5},{9... | collective-permute-start | bytes 1179656 | tf_op jit(solution)/shard_map/ppermute | solution.py:884
  54.2 26.1 %collective-permute-start.16 = (bf16[32,128,128]{2,1,0:T(8,128)(2,1)S(1)}, bf16[32,128,128]{2,1,0:T(8,128)(2,1)}, u32[]{:S(2)}, u32[]{:S(2)}) collective-permute-start(bf16[32,128,128]{2,1,0:T(8,128)(2,1)S(1)} %get-tuple-element.128.f0), channel_id=1, source_target_pairs={{0,2},{1,3},{2,0},{3,1},{4,6},{5,7},{6,4},{7,5},{8,10},{9,11},{10,... | collective-permute-start | bytes 3145736 | tf_op jit(solution)/shard_map/ppermute | solution.py:923
  58.5 24.0 %collective-permute-start.10 = (bf16[512,512]{1,0:T(8,128)(2,1)S(1)}, bf16[512,512]{1,0:T(8,128)(2,1)S(1)}, u32[]{:S(2)}, u32[]{:S(2)}) collective-permute-start(bf16[512,512]{1,0:T(8,128)(2,1)S(1)} %get-tuple-element.122.k_ref), channel_id=1, source_target_pairs={{0,1},{1,0},{2,3},{3,2},{4,5},{5,4},{6,7},{7,6},{8,9},{9,8},{10,11... | collective-permute-start | bytes 1572872 | tf_op jit(solution)/shard_map/ppermute | solution.py:919
  58.8 24.3 %collective-permute-start.11 = (bf16[512,512]{1,0:T(8,128)(2,1)S(1)}, bf16[512,512]{1,0:T(8,128)(2,1)S(1)}, u32[]{:S(2)}, u32[]{:S(2)}) collective-permute-start(bf16[512,512]{1,0:T(8,128)(2,1)S(1)} %get-tuple-element.123.v_ref), channel_id=1, source_target_pairs={{0,1},{1,0},{2,3},{3,2},{4,5},{5,4},{6,7},{7,6},{8,9},{9,8},{10,11... | collective-permute-start | bytes 1572872 | tf_op jit(solution)/shard_map/ppermute | solution.py:919
  59.3 23.3 %collective-permute-start.13 = (bf16[4,128,128]{2,1,0:T(8,128)(2,1)S(1)}, bf16[4,128,128]{2,1,0:T(8,128)(2,1)S(1)}, u32[]{:S(2)}, u32[]{:S(2)}) collective-permute-start(bf16[4,128,128]{2,1,0:T(8,128)(2,1)S(1)} %get-tuple-element.127.a0), channel_id=1, source_target_pairs={{0,2},{1,3},{2,0},{3,1},{4,6},{5,7},{6,4},{7,5},{8,10},{9,11},{10,... | collective-permute-start | bytes 393224 | tf_op jit(solution)/shard_map/ppermute | solution.py:923
  60.3 35.5 %collective-permute-start.15 = (bf16[32,128,128]{2,1,0:T(8,128)(2,1)S(1)}, bf16[32,128,128]{2,1,0:T(8,128)(2,1)S(1)}, u32[]{:S(2)}, u32[]{:S(2)}) collective-permute-start(bf16[32,128,128]{2,1,0:T(8,128)(2,1)S(1)} %get-tuple-element.128.f0), channel_id=1, source_target_pairs={{0,1},{1,0},{2,3},{3,2},{4,5},{5,4},{6,7},{7,6},{8,9},{9,8},{10,11... | collective-permute-start | bytes 3145736 | tf_op jit(solution)/shard_map/ppermute | solution.py:919
  80.2 15.6 %collective-permute-start.17 = (bf16[32,128,128]{2,1,0:T(8,128)(2,1)}, bf16[32,128,128]{2,1,0:T(8,128)(2,1)S(1)}, u32[]{:S(2)}, u32[]{:S(2)}) collective-permute-start(bf16[32,128,128]{2,1,0:T(8,128)(2,1)} %collective-permute-done.16.f2), channel_id=1, source_target_pairs={{0,1},{1,0},{2,3},{3,2},{4,5},{5,4},{6,7},{7,6},{8,9},{9,8},{10,11... | collective-permute-start | bytes 3145736 | tf_op jit(solution)/shard_map/ppermute | solution.py:919
  82.6 12.0 %collective-permute-start.12 = (bf16[4,128,128]{2,1,0:T(8,128)(2,1)S(1)}, bf16[4,128,128]{2,1,0:T(8,128)(2,1)S(1)}, u32[]{:S(2)}, u32[]{:S(2)}) collective-permute-start(bf16[4,128,128]{2,1,0:T(8,128)(2,1)S(1)} %get-tuple-element.127.a0), channel_id=1, source_target_pairs={{0,1},{1,0},{2,3},{3,2},{4,5},{5,4},{6,7},{7,6},{8,9},{9,8},{10,11... | collective-permute-start | bytes 393224 | tf_op jit(solution)/shard_map/ppermute | solution.py:919
  82.6 13.0 %collective-permute-start.14 = (bf16[4,128,128]{2,1,0:T(8,128)(2,1)S(1)}, bf16[4,128,128]{2,1,0:T(8,128)(2,1)S(1)}, u32[]{:S(2)}, u32[]{:S(2)}) collective-permute-start(bf16[4,128,128]{2,1,0:T(8,128)(2,1)S(1)} %collective-permute-done.13.a2), channel_id=1, source_target_pairs={{0,1},{1,0},{2,3},{3,2},{4,5},{5,4},{6,7},{7,6},{8,9},{9,8},{10,11... | collective-permute-start | bytes 393224 | tf_op jit(solution)/shard_map/ppermute | solution.py:919
  83.1 11.5 %collective-permute-start.19 = (bf16[12,128,128]{2,1,0:T(8,128)(2,1)S(1)}, bf16[12,128,128]{2,1,0:T(8,128)(2,1)S(1)}, u32[]{:S(2)}, u32[]{:S(2)}) collective-permute-start(bf16[12,128,128]{2,1,0:T(8,128)(2,1)S(1)} %copy-done.8), channel_id=1, source_target_pairs={{0,2},{1,3},{2,0},{3,1},{4,6},{5,7},{6,4},{7,5},{8,10},{9,11},{10,... | collective-permute-start | bytes 1179656 | tf_op jit(solution)/shard_map/ppermute | solution.py:923
  94.5 11.3 %collective-permute-start.18 = (bf16[12,128,128]{2,1,0:T(8,128)(2,1)S(1)}, bf16[12,128,128]{2,1,0:T(8,128)(2,1)S(1)}, u32[]{:S(2)}, u32[]{:S(2)}) collective-permute-start(bf16[12,128,128]{2,1,0:T(8,128)(2,1)S(1)} %copy-done.8), channel_id=1, source_target_pairs={{0,1},{1,0},{2,3},{3,2},{4,5},{5,4},{6,7},{7,6},{8,9},{9,8},{10,11... | collective-permute-start | bytes 1179656 | tf_op jit(solution)/shard_map/ppermute | solution.py:919
  94.6 26.1 %collective-permute-start.27 = (bf16[32,128,128]{2,1,0:T(8,128)(2,1)S(1)}, bf16[32,128,128]{2,1,0:T(8,128)(2,1)}, u32[]{:S(2)}, u32[]{:S(2)}) collective-permute-start(bf16[32,128,128]{2,1,0:T(8,128)(2,1)S(1)} %copy-done.59), channel_id=1, source_target_pairs={{0,2},{1,3},{2,0},{3,1},{4,6},{5,7},{6,4},{7,5},{8,10},{9,11},{10,... | collective-permute-start | bytes 3145736 | tf_op jit(solution)/shard_map/ppermute | solution.py:923
  108.9 14.2 %collective-permute-start.21 = (bf16[512,512]{1,0:T(8,128)(2,1)S(1)}, bf16[512,512]{1,0:T(8,128)(2,1)S(1)}, u32[]{:S(2)}, u32[]{:S(2)}) collective-permute-start(bf16[512,512]{1,0:T(8,128)(2,1)S(1)} %get-tuple-element.133.k_ref), channel_id=1, source_target_pairs={{0,1},{1,0},{2,3},{3,2},{4,5},{5,4},{6,7},{7,6},{8,9},{9,8},{10,11... | collective-permute-start | bytes 1572872 | tf_op jit(solution)/shard_map/ppermute | solution.py:919
  109.2 14.3 %collective-permute-start.22 = (bf16[512,512]{1,0:T(8,128)(2,1)S(1)}, bf16[512,512]{1,0:T(8,128)(2,1)S(1)}, u32[]{:S(2)}, u32[]{:S(2)}) collective-permute-start(bf16[512,512]{1,0:T(8,128)(2,1)S(1)} %get-tuple-element.134.v_ref), channel_id=1, source_target_pairs={{0,1},{1,0},{2,3},{3,2},{4,5},{5,4},{6,7},{7,6},{8,9},{9,8},{10,11... | collective-permute-start | bytes 1572872 | tf_op jit(solution)/shard_map/ppermute | solution.py:919
  109.4 13.6 %collective-permute-start.24 = (bf16[4,128,128]{2,1,0:T(8,128)(2,1)S(1)}, bf16[4,128,128]{2,1,0:T(8,128)(2,1)S(1)}, u32[]{:S(2)}, u32[]{:S(2)}) collective-permute-start(bf16[4,128,128]{2,1,0:T(8,128)(2,1)S(1)} %copy-done.18), channel_id=1, source_target_pairs={{0,2},{1,3},{2,0},{3,1},{4,6},{5,7},{6,4},{7,5},{8,10},{9,11},{10,... | collective-permute-start | bytes 393224 | tf_op jit(solution)/shard_map/ppermute | solution.py:923
  110.5 23.1 %collective-permute-start.26 = (bf16[32,128,128]{2,1,0:T(8,128)(2,1)S(1)}, bf16[32,128,128]{2,1,0:T(8,128)(2,1)S(1)}, u32[]{:S(2)}, u32[]{:S(2)}) collective-permute-start(bf16[32,128,128]{2,1,0:T(8,128)(2,1)S(1)} %copy-done.59), channel_id=1, source_target_pairs={{0,1},{1,0},{2,3},{3,2},{4,5},{5,4},{6,7},{7,6},{8,9},{9,8},{10,11... | collective-permute-start | bytes 3145736 | tf_op jit(solution)/shard_map/ppermute | solution.py:919
  120.7 12.9 %collective-permute-start.28 = (bf16[32,128,128]{2,1,0:T(8,128)(2,1)}, bf16[32,128,128]{2,1,0:T(8,128)(2,1)S(1)}, u32[]{:S(2)}, u32[]{:S(2)}) collective-permute-start(bf16[32,128,128]{2,1,0:T(8,128)(2,1)} %collective-permute-done.27.f2), channel_id=1, source_target_pairs={{0,1},{1,0},{2,3},{3,2},{4,5},{5,4},{6,7},{7,6},{8,9},{9,8},{10,11... | collective-permute-start | bytes 3145736 | tf_op jit(solution)/shard_map/ppermute | solution.py:919
  123.0 10.5 %collective-permute-start.23 = (bf16[4,128,128]{2,1,0:T(8,128)(2,1)S(1)}, bf16[4,128,128]{2,1,0:T(8,128)(2,1)S(1)}, u32[]{:S(2)}, u32[]{:S(2)}) collective-permute-start(bf16[4,128,128]{2,1,0:T(8,128)(2,1)S(1)} %copy-done.18), channel_id=1, source_target_pairs={{0,1},{1,0},{2,3},{3,2},{4,5},{5,4},{6,7},{7,6},{8,9},{9,8},{10,11... | collective-permute-start | bytes 393224 | tf_op jit(solution)/shard_map/ppermute | solution.py:919
  123.0 10.6 %collective-permute-start.25 = (bf16[4,128,128]{2,1,0:T(8,128)(2,1)S(1)}, bf16[4,128,128]{2,1,0:T(8,128)(2,1)S(1)}, u32[]{:S(2)}, u32[]{:S(2)}) collective-permute-start(bf16[4,128,128]{2,1,0:T(8,128)(2,1)S(1)} %collective-permute-done.24.a2), channel_id=1, source_target_pairs={{0,1},{1,0},{2,3},{3,2},{4,5},{5,4},{6,7},{7,6},{8,9},{9,8},{10,11... | collective-permute-start | bytes 393224 | tf_op jit(solution)/shard_map/ppermute | solution.py:919
  164.9 28.1 %collective-permute-start.34 = (bf16[32,128,128]{2,1,0:T(8,128)(2,1)S(1)}, bf16[32,128,128]{2,1,0:T(8,128)(2,1)}, u32[]{:S(2)}, u32[]{:S(2)}) collective-permute-start(bf16[32,128,128]{2,1,0:T(8,128)(2,1)S(1)} %get-tuple-element.161), channel_id=1, source_target_pairs={{0,2},{1,3},{2,0},{3,1},{4,6},{5,7},{6,4},{7,5},{8,10},{9,11},{10,... | collective-permute-start | bytes 3145736 | tf_op jit(solution)/shard_map/ppermute | solution.py:923
  212.1 11.2 %collective-permute-start.38 = (bf16[12,128,128]{2,1,0:T(8,128)(2,1)S(1)}, bf16[12,128,128]{2,1,0:T(8,128)(2,1)S(1)}, u32[]{:S(2)}, u32[]{:S(2)}) collective-permute-start(bf16[12,128,128]{2,1,0:T(8,128)(2,1)S(1)} %get-tuple-element.267), channel_id=1, source_target_pairs={{0,2},{1,3},{2,0},{3,1},{4,6},{5,7},{6,4},{7,5},{8,10},{9,11},{10,... | collective-permute-start | bytes 1179656 | tf_op jit(solution)/shard_map/ppermute | solution.py:923
  223.3 27.2 %collective-permute-start.42 = (bf16[32,128,128]{2,1,0:T(8,128)(2,1)S(1)}, bf16[32,128,128]{2,1,0:T(8,128)(2,1)S(1)}, u32[]{:S(2)}, u32[]{:S(2)}) collective-permute-start(bf16[32,128,128]{2,1,0:T(8,128)(2,1)S(1)} %get-tuple-element.183), channel_id=1, source_target_pairs={{0,2},{1,3},{2,0},{3,1},{4,6},{5,7},{6,4},{7,5},{8,10},{9,11},{10,... | collective-permute-start | bytes 3145736 | tf_op jit(solution)/shard_map/ppermute | solution.py:923
  258.1 11.8 %collective-permute-start.46 = (bf16[12,128,128]{2,1,0:T(8,128)(2,1)S(1)}, bf16[12,128,128]{2,1,0:T(8,128)(2,1)S(1)}, u32[]{:S(2)}, u32[]{:S(2)}) collective-permute-start(bf16[12,128,128]{2,1,0:T(8,128)(2,1)S(1)} %get-tuple-element.264), channel_id=1, source_target_pairs={{0,2},{1,3},{2,0},{3,1},{4,6},{5,7},{6,4},{7,5},{8,10},{9,11},{10,... | collective-permute-start | bytes 1179656 | tf_op jit(solution)/shard_map/ppermute | solution.py:923
  276.7 11.4 %collective-permute-start.51 = (bf16[1552,128]{1,0:T(8,128)(2,1)S(1)}, bf16[1552,128]{1,0:T(8,128)(2,1)S(1)}, u32[]{:S(2)}, u32[]{:S(2)}) collective-permute-start(bf16[1552,128]{1,0:T(8,128)(2,1)S(1)} %get-tuple-element.262), channel_id=1, source_target_pairs={{0,4},{8,0},{16,8},{24,16},{28,24},{20,28},{12,20},{4,12},{1,5},{9... | collective-permute-start | bytes 1191944 | tf_op jit(solution)/shard_map/ppermute | solution.py:884
  322.6 12.4 %collective-permute-start.62 = (f32[4,16,128]{2,1,0:T(8,128)S(1)}, f32[4,16,128]{2,1,0:T(8,128)S(1)}, u32[]{:S(2)}, u32[]{:S(2)}) collective-permute-start(f32[4,16,128]{2,1,0:T(8,128)S(1)} %pad_maximum_fusion.1.refs_0_), channel_id=1, source_target_pairs={{0,16},{8,24},{16,28},{24,20},{28,12},{20,4},{12,0},{4,8},{1,17},{... | collective-permute-start | bytes 98312 | tf_op jit(solution)/shard_map/ppermute | solution.py:884
  326.1 46.3 %collective-permute-start.61 = (f32[4,16,128]{2,1,0:T(8,128)S(1)}, f32[4,16,128]{2,1,0:T(8,128)S(1)}, u32[]{:S(2)}, u32[]{:S(2)}) collective-permute-start(f32[4,16,128]{2,1,0:T(8,128)S(1)} %pad_maximum_fusion.1.refs_0_), channel_id=1, source_target_pairs={{0,24},{8,28},{16,20},{24,12},{28,4},{20,0},{12,8},{4,16},{1,25},{... | collective-permute-start | bytes 98312 | tf_op jit(solution)/shard_map/ppermute | solution.py:884
  329.7 42.7 %collective-permute-start.60 = (f32[4,16,128]{2,1,0:T(8,128)S(1)}, f32[4,16,128]{2,1,0:T(8,128)S(1)}, u32[]{:S(2)}, u32[]{:S(2)}) collective-permute-start(f32[4,16,128]{2,1,0:T(8,128)S(1)} %pad_maximum_fusion.1.refs_0_), channel_id=1, source_target_pairs={{0,28},{8,20},{16,12},{24,4},{28,0},{20,8},{12,16},{4,24},{1,29},{... | collective-permute-start | bytes 98312 | tf_op jit(solution)/shard_map/ppermute | solution.py:884
  329.9 42.5 %collective-permute-start.59 = (f32[4,16,128]{2,1,0:T(8,128)S(1)}, f32[4,16,128]{2,1,0:T(8,128)S(1)}, u32[]{:S(2)}, u32[]{:S(2)}) collective-permute-start(f32[4,16,128]{2,1,0:T(8,128)S(1)} %pad_maximum_fusion.1.refs_0_), channel_id=1, source_target_pairs={{0,20},{8,12},{16,4},{24,0},{28,8},{20,16},{12,24},{4,28},{1,21},{... | collective-permute-start | bytes 98312 | tf_op jit(solution)/shard_map/ppermute | solution.py:884
  332.5 39.9 %collective-permute-start.58 = (f32[4,16,128]{2,1,0:T(8,128)S(1)}, f32[4,16,128]{2,1,0:T(8,128)S(1)}, u32[]{:S(2)}, u32[]{:S(2)}) collective-permute-start(f32[4,16,128]{2,1,0:T(8,128)S(1)} %pad_maximum_fusion.1.refs_0_), channel_id=1, source_target_pairs={{0,12},{8,4},{16,0},{24,8},{28,16},{20,24},{12,28},{4,20},{1,13},{... | collective-permute-start | bytes 98312 | tf_op jit(solution)/shard_map/ppermute | solution.py:884
  335.0 37.5 %collective-permute-start.57 = (f32[4,16,128]{2,1,0:T(8,128)S(1)}, f32[4,16,128]{2,1,0:T(8,128)S(1)}, u32[]{:S(2)}, u32[]{:S(2)}) collective-permute-start(f32[4,16,128]{2,1,0:T(8,128)S(1)} %pad_maximum_fusion.1.refs_0_), channel_id=1, source_target_pairs={{0,4},{8,0},{16,8},{24,16},{28,24},{20,28},{12,20},{4,12},{1,5},{9... | collective-permute-start | bytes 98312 | tf_op jit(solution)/shard_map/ppermute | solution.py:884
  (97 other events, 912.1 us)

commit v4 on v3

--- a/solution.py
+++ b/solution.py
@@ -50,28 +50,6 @@
         vec_table[base_row + 6 + ff_ratio],
         vec_table[base_row + 7 + ff_ratio],
     )
-
-
-def adamw_update(gradient, values, moment_one, moment_two):
-    new_first = beta_first * moment_one + (1.0 - beta_first) * gradient
-    new_second = beta_second * moment_two + (1.0 - beta_second) * gradient * gradient
-    step_ratio = (
-        new_first
-        / (1.0 - beta_first**STEP)
-        / (jnp.sqrt(new_second / (1.0 - beta_second**STEP)) + adam_eps)
-    )
-    new_values = values - rate_vector * (step_ratio + weight_decay * values)
-    return (new_values, new_first, new_second)
-
-
-def branch_biases(grad_table):
-    ff_ratio = FF // D
-    bias_rows = []
-    for layer_at in range(LAYERS):
-        base_row = LOOK + 1 + layer_at * (8 + ff_ratio)
-        bias_rows.append(grad_table[base_row + 2])
-        bias_rows.append(grad_table[base_row + 5 + ff_ratio])
-    return jnp.stack(bias_rows, axis=0)
 
 
 def dot_hi(a, b, ca, cb):
@@ -216,7 +194,7 @@
         out_shape=[sh, shb, sh, sh, sh, sh, sh, sh],
         scratch_shapes=[pltpu.VMEM((2 * n, BLK, BLK), f32)] * 2,
         compiler_params=pltpu.CompilerParams(vmem_limit_bytes=50 * 2**20),
-        cost_estimate=pl.CostEstimate(flops=40 * 10**9, bytes_accessed=0, transcendentals=0),
+        cost_estimate=pl.CostEstimate(flops=40 * 10**6, bytes_accessed=0, transcendentals=0),
         name="soap",
     )(*gs, master, m1, m2, ls, rs, lb, rb)
 
@@ -236,7 +214,7 @@
 
 
 def cost(micros):
-    return pl.CostEstimate(flops=int(micros * 1e9), bytes_accessed=0, transcendentals=0)
+    return pl.CostEstimate(flops=int(micros * 1e6), bytes_accessed=0, transcendentals=0)
 
 
 def shape(dims, kind=f32):
@@ -401,8 +379,8 @@
     wo_s, w1_s, w2_s,
 ):
     place_blocks(wo_s, (a0, a1, a2, a3), 0, 1, 4, BLK, 0)
-    place_blocks(w1_s, (f0, f1, f2, f3), 0, 4, 4, 0, D)
-    place_blocks(w2_s, (f0, f1, f2, f3), 16, 4, 4, D, 0)
+    place_blocks(w1_s, (a0, a1, a2, a3), 4, 4, 4, 0, D)
+    place_blocks(w2_s, (f0, f1, f2, f3), 0, 4, 4, D, 0)
 
     def tile(t, c):
         at = pl.ds(t * ROW_TILE, ROW_TILE)
@@ -433,7 +411,7 @@
     lax.fori_loop(0, x_ref.shape[0] // ROW_TILE, tile, 0)
 
 
-def post(o, x, vec, b1, wout, wffn):
+def post(o, x, vec, b1, wmid, wdown):
     rows = x.shape[0]
     return pl.pallas_call(
         post_kernel,
@@ -455,7 +433,7 @@
         compiler_params=params(),
         name="post",
         cost_estimate=cost(11),
-    )(o, x, vec, b1, *wout, *wffn)
+    )(o, x, vec, b1, *wmid, *wdown)
 
 
 def store_blocks(refs, r, first, rows, cols, value):
@@ -474,8 +452,8 @@
 ):
     rows = e_ref.shape[0]
     place_blocks(wo_s, (a0, a1, a2, a3), 0, 1, 4, BLK, 0)
-    place_blocks(w1_s, (f0, f1, f2, f3), 0, 4, 4, 0, D)
-    place_blocks(w2_s, (f0, f1, f2, f3), 16, 4, 4, D, 0)
+    place_blocks(w1_s, (a0, a1, a2, a3), 4, 4, 4, 0, D)
+    place_blocks(w2_s, (f0, f1, f2, f3), 0, 4, 4, D, 0)
     tiles = rows // ROW_TILE
     gain_two = vec_ref[4:5, :]
     gain_one = vec_ref[1:2, :]
@@ -504,8 +482,8 @@
             return c + col_sum(dpre.astype(f32))
 
         db1_ref[r : r + 1, :] = lax.fori_loop(0, tiles, tile_up, zero)
-        store_blocks((gk_ref, gs_ref), r, 16, 4, 4, dot(hid_ref[:, cols], dfr_s[...], 0, 0).astype(bf16))
-        store_blocks((gk_ref, gs_ref), r, 0, 4, 4, dot(y_ref[...], dpre_s[:, cols], 0, 0).astype(bf16))
+        store_blocks((gk_ref, gs_ref), r, 0, 4, 4, dot(hid_ref[:, cols], dfr_s[...], 0, 0).astype(bf16))
+        store_blocks((ok_ref, os_ref), r, 4, 4, 4, dot(y_ref[...], dpre_s[:, cols], 0, 0).astype(bf16))
 
     def tile_one(t, c):
         at = pl.ds(t * ROW_TILE, ROW_TILE)
@@ -526,15 +504,15 @@
         sums_ref[i : i + 1, :] = value
 
 
-def ffn_grad(e, n2, i2, n1, i1, y, hid, slope, o, vec, wout, wffn):
+def ffn_grad(e, n2, i2, n1, i1, y, hid, slope, o, vec, wmid, wdown):
     rows = e.shape[0]
     return pl.pallas_call(
         ffn_grad_kernel,
         out_shape=[
-            shape((2, 32, BLK, BLK), bf16),
-            shape((2, 32, BLK, BLK), bf16),
-            shape((2, 4, BLK, BLK), bf16),
-            shape((2, 4, BLK, BLK), bf16),
+            shape((2, 16, BLK, BLK), bf16),
+            shape((2, 16, BLK, BLK), bf16),
+            shape((2, 20, BLK, BLK), bf16),
+            shape((2, 20, BLK, BLK), bf16),
             shape((rows, D)),
             shape((rows, D), bf16),
             shape((FF // D, D)),
@@ -552,7 +530,7 @@
         compiler_params=params(),
         name="ffn_grad",
         cost_estimate=cost(16),
-    )(e, n2, i2, n1, i1, y, hid, slope, o, vec, *wout, *wffn)
+    )(e, n2, i2, n1, i1, y, hid, slope, o, vec, *wmid, *wdown)
 
 
 def attend_grad_kernel(
@@ -718,7 +696,7 @@
     used = LOOK + 1 + LAYERS * per_layer
     tab[used:] = jnp.zeros((BLK - used, D), f32)
     for r in range(4):
-        rows = tab[pl.ds(pl.multiple_of((place ^ r) * 32, 32), 32), :].astype(bf16)
+        rows = tab[pl.ds(pl.multiple_of((place ^ r) * 32, 32), 32), :]
         out = send_ref if r % 2 else keep_ref
         for c in range(4):
             out[r // 2, c * 32 : (c + 1) * 32] = rows[:, c * BLK : (c + 1) * BLK]
@@ -732,8 +710,8 @@
         in_specs=[pl.BlockSpec(memory_space=pltpu.SMEM)] + [spec] * 9,
         out_shape=[
             shape((rows, LOOK)),
-            shape((2, BLK, BLK), bf16),
-            shape((2, BLK, BLK), bf16),
+            shape((2, BLK, BLK)),
+            shape((2, BLK, BLK)),
         ],
         scratch_shapes=[pltpu.VMEM((BLK, D), f32)],
         compiler_params=params(),
@@ -742,21 +720,14 @@
     )(place, series, g, table[:LOOK], *sums)
 
 
-def vector_kernel(at_ref, val_ref, first_ref, second_ref, *refs):
-    count = len(refs) - 6
-    parts = refs[:count]
-    nv_ref, n1_ref, n2_ref, bias_ref, held, tab = refs[count:]
-    share = BLK // count
-    for k in range(count):
-        held[k] = parts[k][...]
-    for d in range(count):
-        for h in range(4):
-            c, i = divmod(d * share, 32)
-            tab[h * 32 + i : h * 32 + i + share, c * BLK : (c + 1) * BLK] = held[
-                at_ref[d], at_ref[count] ^ h
-            ]
-    used = val_ref.shape[0]
-    grad = tab[:used]
+def vector_kernel(
+    place_ref, val_ref, first_ref, second_ref, p0, p1, p2, p3, nv_ref, n1_ref, n2_ref, bias_ref, tab
+):
+    for r, part in enumerate((p0, p1, p2, p3)):
+        rows = pl.ds(pl.multiple_of((place_ref[0] ^ r) * 32, 32), 32)
+        for c in range(4):
+            tab[rows, c * BLK : (c + 1) * BLK] = part[c * 32 : (c + 1) * 32]
+    grad = tab[: val_ref.shape[0]]
     val = val_ref[...]
     first = 0.5 * first_ref[...] + 0.5 * grad
     second = 0.5 * second_ref[...] + 0.5 * grad * grad
@@ -772,84 +743,54 @@
         bias_ref[2 * layer + 1 : 2 * layer + 2] = tab[base + 5 + FF // D : base + 6 + FF // D]
 
 
-def vector_update(at, values, first, second, parts):
+def vector_update(place, values, first, second, parts):
     spec = pl.BlockSpec(memory_space=pltpu.VMEM)
     return pl.pallas_call(
         vector_kernel,
-        in_specs=[pl.BlockSpec(memory_space=pltpu.SMEM)] + [spec] * (3 + len(parts)),
+        in_specs=[pl.BlockSpec(memory_space=pltpu.SMEM)] + [spec] * 7,
         out_shape=[shape(values.shape)] * 3 + [shape((2 * LAYERS, D))],
-        scratch_shapes=[
-            pltpu.VMEM((len(parts), 4, BLK // len(parts), BLK), f32),
-            pltpu.VMEM((BLK, D), f32),
-        ],
+        scratch_shapes=[pltpu.VMEM((BLK, D), f32)],
         compiler_params=params(),
         name="vector",
         cost_estimate=cost(2),
-    )(at, values, first, second, *parts)
-
-
-PARTS = ((0, 12), (12, 4), (16, 32))
-
-
-def natural_kernel(at_ref, *refs):
-    count = len(refs) - 7
-    slots, outs, held = refs[:count], refs[count : count + 6], refs[-1]
-    step = slots[0].shape[0]
-    for i in range(count):
-        held[i * step : (i + 1) * step] = slots[i][...]
+    )(place, values, first, second, *parts)
+
+
+PARTS = ((0, 12), (12, 20), (32, 16))
+
+
+def natural_kernel(plan, at_ref, *refs):
+    count = len(plan)
+    slots, outs, held = refs[:count], refs[count:-1], refs[-1]
+    for ref, start in zip(slots, plan):
+        held[start : start + ref.shape[0]] = ref[...]
     for i, out in enumerate(outs):
-        layer, part = divmod(i, 3)
+        plane, rest = divmod(i, 3 * LAYERS)
+        layer, part = divmod(rest, 3)
         first, n = PARTS[part]
         for j in range(n):
-            out[j] = held[at_ref[layer * 48 + first + j]]
-
-
-def natural_order(at, slots):
+            out[j] = held[at_ref[plane * 96 + layer * 48 + first + j]]
+
+
+def natural_order(at, slots, plan):
     total = sum(s.shape[0] for s in slots)
     spec = pl.BlockSpec(memory_space=pltpu.VMEM)
     return pl.pallas_call(
-        natural_kernel,
+        functools.partial(natural_kernel, plan),
         in_specs=[pl.BlockSpec(memory_space=pltpu.SMEM)] + [spec] * len(slots),
-        out_shape=[shape((n, BLK, BLK), bf16) for _ in range(LAYERS) for _, n in PARTS],
+        out_shape=[
+            shape((n, BLK, BLK), bf16)
+            for _ in range(at.shape[0] // 96 * LAYERS)
+            for _, n in PARTS
+        ],
         scratch_shapes=[pltpu.VMEM((total, BLK, BLK), bf16)],
         compiler_params=params(),
         name="natural",
-        cost_estimate=cost(3),
+        cost_estimate=cost(4),
     )(at, *slots)
 
 
-def routed_kernel(at_ref, tab_ref, tabr_ref, *refs):
-    own, got, out = refs[:6], refs[6:12], refs[12]
-    count, span = out.shape[0], out.shape[1]
-    share = BLK // count
-    out[...] = jnp.zeros(out.shape, bf16)
-    for i in range(6):
-        layer, part = divmod(i, 3)
-        first, n = PARTS[part]
-        for j in range(n):
-            place = at_ref[layer * 48 + first + j]
-            who = at_ref[96 + layer * 48 + first + j]
-            value = own[i][j].astype(f32) + got[i][j].astype(f32)
-            out[who, pl.ds(pl.multiple_of(place * BLK, BLK), BLK), :] = value.astype(bf16)
-    table = (tab_ref[...].astype(f32) + tabr_ref[...].astype(f32)).astype(bf16)
-    for d in range(count):
-        who = at_ref[192 + d]
-        out[who, span - share : span, :] = table[d * share : (d + 1) * share]
-
-
-def routed(at, table, table_got, own, got, count, slots_each):
-    spec = pl.BlockSpec(memory_space=pltpu.VMEM)
-    return pl.pallas_call(
-        routed_kernel,
-        in_specs=[pl.BlockSpec(memory_space=pltpu.SMEM)] + [spec] * 14,
-        out_shape=shape((count, slots_each * BLK + BLK // count, BLK), bf16),
-        compiler_params=params(),
-        name="routed",
-        cost_estimate=cost(4),
-    )(at, table, table_got, *own, *got)
-
-
-def routed_plain_kernel(at_ref, *refs):
+def routed_kernel(at_ref, *refs):
     own, got, out = refs[:6], refs[6:12], refs[12]
     out[...] = jnp.zeros(out.shape, bf16)
     for i in range(6):
@@ -862,10 +803,10 @@
             out[who, pl.ds(pl.multiple_of(place * BLK, BLK), BLK), :] = value.astype(bf16)
 
 
-def routed_plain(at, own, got, count, slots_each):
+def routed(at, own, got, count, slots_each):
     spec = pl.BlockSpec(memory_space=pltpu.VMEM)
     return pl.pallas_call(
-        routed_plain_kernel,
+        routed_kernel,
         in_specs=[pl.BlockSpec(memory_space=pltpu.SMEM)] + [spec] * 12,
         out_shape=shape((count, slots_each * BLK, BLK), bf16),
         compiler_params=params(),
@@ -886,29 +827,40 @@
 
 def ring_gather(value, order):
     n = len(order)
-    held = [value] + [None] * (n - 1)
+    half = value.shape[0] // 2
+    held = [(value, 0, 0)]
     ahead = behind = value
-    for step in range(1, n // 2 + 1):
+    for step in range(1, n // 2):
         behind = ring_shift(behind, order, 1)
-        held[n - step] = behind
-        if step < n // 2:
-            ahead = ring_shift(ahead, order, -1)
-            held[step] = ahead
+        ahead = ring_shift(ahead, order, -1)
+        held += [(behind, n - step, 0), (ahead, step, 0)]
+    held.append((ring_shift(behind[:half], order, 1), n // 2, 0))
+    held.append((ring_shift(ahead[half:], order, -1), n // 2, half))
     return held
 
 
 def ring_reduce(pieces, order):
     n = len(order)
-    up = pieces[n // 2]
-    down = pieces[n // 2 + 1]
-    for step in range(1, n // 2 + 1):
-        up = ring_shift(up, order, 1)
-        if step < n // 2:
-            up = add_low(up, pieces[n // 2 - step])
-            down = ring_shift(down, order, -1)
-            if step < n // 2 - 1:
-                down = add_low(down, pieces[n // 2 + 1 + step])
+    half = pieces[0].shape[0] // 2
+    up = ring_shift(pieces[n // 2][:half], order, 1)
+    down = ring_shift(pieces[n // 2][half:], order, -1)
+    for step in range(1, n // 2):
+        near, far = pieces[n // 2 - step], pieces[n // 2 + step]
+        if step == 1:
+            up = jnp.concatenate([add_low(up, near[:half]), near[half:]], axis=0)
+            down = jnp.concatenate([far[:half], add_low(down, far[half:])], axis=0)
+        else:
+            up, down = add_low(up, near), add_low(down, far)
+        up, down = ring_shift(up, order, 1), ring_shift(down, order, -1)
     return pieces[0], up, down
+
+
+def dp_sum(value, count):
+    bit = 1
+    while bit < count:
+        value = value + lax.ppermute(value, "dp", [(i, i ^ bit) for i in range(count)])
+        bit *= 2
+    return value
 
 
 def add_low(a, b):
@@ -973,20 +925,10 @@
 
     copies = master[0].astype(bf16)
     if ringed:
-        slots = ring_gather(copies, order)
+        held = ring_gather(copies, order)
+        slots, plan = [x[0] for x in held], tuple(x[1] * own_slots + x[2] for x in held)
     else:
-        slots = [lax.all_gather(copies, "dp", axis=0, tiled=True)]
-    mine = natural_order(gather_at, slots)
-    weights = []
-    far = None
-    for at in range(LAYERS):
-        for group in ((0,), (1, 2)):
-            group_own = [mine[3 * at + i] for i in group]
-            ready = group_own if far is None else tied(group_own, far)
-            far = [far_swap(one) for one in ready]
-            for own, there in zip(group_own, far):
-                weights.append([own, core_swap(own), there, core_swap(there)])
-
+        slots, plan = [lax.all_gather(copies, "dp", axis=0, tiled=True)], (0,)
     windows = window_ids(window_lengths, bucket_rows)
     ids = windows.reshape(4, rows)
     own_ids = lax.dynamic_index_in_dim(ids, place, 0, False)
@@ -996,15 +938,47 @@
     valid = (own_ids < win).astype(f32)[:, None]
 
     x = embed(series, vec_values)
+    vectors = []
+    for layer in range(LAYERS):
+        bq, bv, bo, g1, c1, b1, b2, g2, c2 = depth_vectors(vec_values, layer)
+        vec = jnp.stack([bo, g1, c1, b2, g2, c2, g2, c2])
+        vectors.append([vec] + [relative(row, place) for row in (bq, bv, b1)])
+    slots, (x, vectors, ohq, ohk, valid, gather_at) = lax.optimization_barrier(
+        (slots, (x, vectors, ohq, ohk, valid, gather_at))
+    )
+    mine = natural_order(gather_at, slots, plan)
+    moved = []
+
+    def cross(i, after=None):
+        own = mine[i] if after is None else tied(mine[i], after)
+        moved.append(far_swap(own))
+        return moved[-1]
+
+    def four(i, after=None):
+        there = moved[i] if after is None else tied(moved[i], after)
+        return [mine[i], core_swap(mine[i]), there, core_swap(there)]
+
+    weights = []
     saved = []
     for layer in range(LAYERS):
-        bq, bv, bo, g1, c1, b1, b2, g2, c2 = depth_vectors(vec_values, layer)
-        wqkv, wout, wffn = weights[3 * layer : 3 * layer + 3]
-        xs, q, k, v = project(x, relative(bq, place), relative(bv, place), wqkv)
+        vec, bq, bv, b1 = vectors[layer]
+        if layer == 0:
+            cross(0)
+        wqkv = four(3 * layer, x if layer else None)
+        x = tied(x, wqkv)
+        if layer == 0:
+            cross(1, moved[0])
+            cross(2, moved[0])
+        xs, q, k, v = project(x, bq, bv, wqkv)
         kp, vp = core_swap(k), core_swap(v)
         o, lse = attend(q, k, kp, v, vp, ohq, ohk)
-        vec = jnp.stack([bo, g1, c1, b2, g2, c2, g2, c2])
-        n1, i1, y, hid, slope, n2, i2, x = post(o, x, vec, relative(b1, place), wout, wffn)
+        wmid, wdown = four(3 * layer + 1, o), four(3 * layer + 2, o)
+        weights += [wqkv, wmid, wdown]
+        if layer + 1 < LAYERS:
+            done = moved[-1]
+            for i in range(3):
+                cross(3 * layer + 3 + i, done if i == 0 else (done, moved[3 * layer + 3]))
+        n1, i1, y, hid, slope, n2, i2, x = post(o, x, vec, b1, wmid, wdown)
         saved.append((xs, q, k, v, kp, vp, o, lse, vec, n1, i1, y, hid, slope, n2, i2))
     activations = x * valid
     grad = cotangent * valid
@@ -1020,20 +994,20 @@
     moving = []
     for layer in reversed(range(LAYERS)):
         xs, q, k, v, kp, vp, o, lse, vec, n1, i1, y, hid, slope, n2, i2 = saved[layer]
-        wqkv, wout, wffn = weights[3 * layer : 3 * layer + 3]
+        wqkv, wmid, wdown = weights[3 * layer : 3 * layer + 3]
         gk, gs, ok, os, dr1, do, db1, sums = ffn_grad(
-            grad, n2, i2, n1, i1, y, hid, slope, o, vec, wout, wffn
+            grad, n2, i2, n1, i1, y, hid, slope, o, vec, wmid, wdown
         )
-        got = [core_swap(gs), core_swap(os)]
-        do, far = tied(
-            (do, [chip_sum(3 * layer + 2, gk, got[0]), chip_sum(3 * layer + 1, ok, got[1])]), moving
-        )
-        far_sums[3 * layer + 2] = far_swap(far[0])
-        far_sums[3 * layer + 1] = far_swap(far[1])
-        do = tied(do, far)
+        os, gs, ok, gk, do = tied((os, gs, ok, gk, do), moving)
+        got = [core_swap(os), core_swap(gs)]
+        mid = chip_sum(3 * layer + 1, ok, got[0])
+        down = chip_sum(3 * layer + 2, gk, got[1])
+        far_sums[3 * layer + 1] = far_swap(mid)
+        do = tied(do, (mid, down))
         dq, dk, dkp, dv, dvp = attend_grad(q, k, kp, v, vp, do, o, lse, ohq, ohk)
+        dkp, dvp = tied((dkp, dvp), far_sums[3 * layer + 1])
+        far_sums[3 * layer + 2] = far_swap(tied(down, far_sums[3 * layer + 1]))
         dkr, dvr = core_swap(dkp), core_swap(dvp)
-        dkr, dvr = tied((dkr, dvr), far_sums[3 * layer + 1 : 3 * layer + 3])
         pk, ps, grad, qsums = proj_grad(dq, dk, dv, dkr, dvr, xs, dr1, wqkv)
         table_rows[layer] = (sums, qsums, db1)
         got = core_swap(ps)
@@ -1041,43 +1015,27 @@
             far = chip_sum(3 * layer, pk, got)
             grad = tied(grad, far)
             far_sums[3 * layer] = far_swap(far)
-            moving = [far_sums[3 * layer]]
+            moving = far_sums[3 * layer : 3 * layer + 3]
     input_grad, tab_keep, tab_send = embed_grad(
         place.astype(jnp.int32)[None], series, grad, vec_values, table_rows[0] + table_rows[1]
     )
-    tab_got = core_swap(tab_send)
     far_sums[0] = far_swap(chip_sum(0, pk, got))
-    tab_own = add_low(tab_keep[0], tab_got[0])
-    tab_far = far_swap(add_low(tab_keep[1], tab_got[1]))
+    tab = dp_sum(tab_keep + core_swap(tab_send), dp)
+    own_sums[0] = tied(own_sums[0], tab)
+    tab_part = tab[0] + far_swap(tab[1])
+    tab_there = far_swap(tab_part)
+    parts = [tab_part, core_swap(tab_part), tab_there, core_swap(tab_there)]
+    at = jnp.concatenate([inner, who]).astype(jnp.int32)
+    pieces = routed(at, own_sums, far_sums, dp, own_slots)
     if ringed:
-        dist = (ring_at - ring_at[spot]) % dp
-        at = jnp.concatenate([inner, who, dist]).astype(jnp.int32)
-        pieces = routed(at, tab_own, tab_far, own_sums, far_sums, dp, own_slots)
         terms = ring_reduce([pieces[i] for i in range(dp)], order)
-        grads = [t[: own_slots * BLK].reshape(own_slots, BLK, BLK) for t in terms]
-        part = sum(t[own_slots * BLK :].astype(f32) for t in terms)
-        group = jnp.stack(
-            [part] + [lax.ppermute(part, "head", [(i, i ^ r) for i in range(4)]) for r in (1, 2, 3)]
-        )
-        grads = tied(grads, group)
-        parts = [group] + [ring_shift(group, order, -k) for k in range(1, dp)]
-        vec_at = jnp.concatenate([dist, place[None]]).astype(jnp.int32)
-        vec_new_values, vec_new_first, vec_new_second, branch_bias_grads = vector_update(
-            vec_at, vec_values, vec_first, vec_second, parts
-        )
+        grads = [t.reshape(own_slots, BLK, BLK) for t in terms]
     else:
-        at = jnp.concatenate([inner, who]).astype(jnp.int32)
-        pieces = routed_plain(at, own_sums, far_sums, dp, own_slots)
         whole = lax.psum_scatter(pieces, "dp", scatter_dimension=0, tiled=True)
         grads = [whole.reshape(own_slots, BLK, BLK)]
-        total = lax.psum(tab_own.astype(f32) + tab_far.astype(f32), "dp")
-        shares = lax.all_gather(total, "head", axis=0)
-        grad_table = shares.reshape(4, 4, 32, BLK).transpose(0, 2, 1, 3).reshape(BLK, D)
-        grad_table = grad_table[: vec_values.shape[0]]
-        vec_new_values, vec_new_first, vec_new_second = adamw_update(
-            grad_table, vec_values, vec_first, vec_second
-        )
-        branch_bias_grads = branch_biases(grad_table)
+    vec_new_values, vec_new_first, vec_new_second, branch_bias_grads = vector_update(
+        place.astype(jnp.int32)[None], vec_values, vec_first, vec_second, parts
+    )
     new_master, new_copy, new_first, new_second, new_left, new_right, left_next, right_next = soap(
         grads,
         master[0],

time: 379 us -> 345 us (0.910)
  waiting for transfers between devices: 134 us -> 104 us
    ppermute x13 -> x14, waiting for transfers between devices: 66.1 us -> 42.7 us  [far_swap(): return lax.ppermute(value, 'head', [(i, i ^ 2) for i in range(4)])]
    ppermute x21 -> x16, waiting for transfers between devices: 56.5 us -> 35.4 us  [ring_shift(): lax.ppermute(value, 'dp', [(order[i], order[(i + by) % n]) for i in range...]
    ppermute x21 -> x16, starting transfers between devices: 27.4 us -> 17.6 us  [ring_shift(): lax.ppermute(value, 'dp', [(order[i], order[(i + by) % n]) for i in range...]
    ppermute x3, waiting for transfers between devices: 1.82 us -> 10.8 us  [dp_sum(): lax.ppermute(value, 'dp', [(i, i ^ bit) for i in range(count)])]
    ppermute x27 -> x29, waiting for transfers between devices: 9.92 us -> 15.3 us  [core_swap(): return lax.ppermute(value, 'head', [(i, i ^ 1) for i in range(4)])]
    ppermute x13 -> x14, starting transfers between devices: 13.6 us -> 18.2 us  [far_swap(): return lax.ppermute(value, 'head', [(i, i ^ 2) for i in range(4)])]
    unnamed x134 -> x130, local copies, waits for them, and re-layouts: 14.1 us -> 12.9 us
    convert_element_type x10 -> x9, other arithmetic: 9.17 us -> 8.02 us  [add_low(): return (a.astype(f32) + b.astype(f32)).astype(bf16)]
  transfers between devices with their start and end apart: 64 -> 62, of which waited for: 26 -> 35; matrix products, arithmetic and copies ran while one was open for 5% -> 7% of each run, Pallas kernels for 27% -> 23%
where the time goes in v4:
time: 345 us; the launch traced here: 340 us
  Pallas kernels  148 us (43%)
  waiting for transfers between devices  104 us (30%)
  starting transfers between devices  46.6 us (14%)
  local copies, waits for them, and re-layouts  23.3 us (7%)
  other arithmetic  15.9 us (5%)
    ppermute x14, waiting for transfers between devices, far_swap(): return lax.ppermute(value, 'head', [(i, i ^ 2) for i in range(4)])  42.7 us
    pallas_call x1, Pallas kernels, soap(): pl.pallas_call(functools.partial(soap_kernel, len(gs)), grid=(n // group,...  37.3 us
    ppermute x16, waiting for transfers between devices, ring_shift(): lax.ppermute(value, 'dp', [(order[i], order[(i + by) % n]) for i in range...  35.4 us
    pallas_call x2, Pallas kernels, attend_grad(): pl.pallas_call(attend_grad_kernel, grid=(D // LANES,), in_specs=[pair, pa...  32.3 us
    pallas_call x2, Pallas kernels, ffn_grad(): pl.pallas_call(ffn_grad_kernel, out_shape=[shape((2, 16, BLK, BLK), bf16)...  23 us
    pallas_call x2, Pallas kernels, attend(): pl.pallas_call(attend_kernel, grid=(D // LANES,), in_specs=[pair, pair, o...  18.4 us
    ppermute x14, starting transfers between devices, far_swap(): return lax.ppermute(value, 'head', [(i, i ^ 2) for i in range(4)])  18.2 us
    ppermute x16, starting transfers between devices, ring_shift(): lax.ppermute(value, 'dp', [(order[i], order[(i + by) % n]) for i in range...  17.6 us
  transfers between devices with their start and end apart: 62, of which 35 were waited for; matrix products, arithmetic and copies ran while one was open for 7% of the time, Pallas kernels for 23%

profile of v4, /device:TPU:0, one launch (start us, length us, event | category | flops | bytes accessed | tf_op | source)
XLA Modules:
  0.0 340.0 jit_solution(3122967037418848767)
XLA Ops:
  1.9 3.0 collective-permute-start.1
  8.9 5.2 %collective-permute-done.1.refs_2_ = bf16[12,128,128]{2,1,0:T(8,128)(2,1)S(1)} collective-permute-done((bf16[12,128,128]{2,1,0:T(8,128)(2,1)S(1)}, bf16[12,128,128]{2,1,0:T(8,128)(2,1)S(1)}, u32[]{:S(2)}, u32[]{:S(2)}) %collective-permute-start.1) | collective-permute-done | bytes 393248 | tf_op jit(solution)/shard_map/ppermute | solution.py:825
  17.0 7.4 %collective-permute-done.3.refs_4_ = bf16[12,128,128]{2,1,0:T(8,128)(2,1)S(1)} collective-permute-done((bf16[12,128,128]{2,1,0:T(8,128)(2,1)S(1)}, bf16[12,128,128]{2,1,0:T(8,128)(2,1)S(1)}, u32[]{:S(2)}, u32[]{:S(2)}) %collective-permute-start.3) | collective-permute-done | bytes 393248 | tf_op jit(solution)/shard_map/ppermute | solution.py:825
  37.5 2.9 collective-permute-done.7.refs_8_
  45.3 6.3 %collective-permute-done.9.w2 = bf16[12,128,128]{2,1,0:T(8,128)(2,1)S(1)} collective-permute-done((bf16[12,128,128]{2,1,0:T(8,128)(2,1)S(1)}, bf16[12,128,128]{2,1,0:T(8,128)(2,1)S(1)}, u32[]{:S(2)}, u32[]{:S(2)}) %collective-permute-start.9) | collective-permute-done | bytes 393248 | tf_op jit(solution)/shard_map/ppermute | solution.py:875
  57.2 9.3 %attend.2 = (bf16[512,512]{1,0:T(8,128)(2,1)S(1)}, f32[512,512]{1,0:T(8,128)S(1)}) custom-call(bf16[512,512]{1,0:T(8,128)(2,1)S(1)} %get-tuple-element.168.q_ref, bf16[512,512]{1,0:T(8,128)(2,1)S(1)} %get-tuple-element.169.k_ref, bf16[512,512]{1,0:T(8,128)(2,1)S(1)} %collective-permute-done.11.kp_ref, bf16[512,512]{1,0:T(8,128)(2,1)S(1)} %get-tuple-element.170.v_ref, ...), custom_call_target="tpu_custom_call" | custom-call | flops 11000000 | tf_op jit(solution)/shard_map/attend/pallas_call | solution.py:356
  69.6 10.3 %collective-permute-done.17.f2 = bf16[16,128,128]{2,1,0:T(8,128)(2,1)S(1)} collective-permute-done((bf16[16,128,128]{2,1,0:T(8,128)(2,1)S(1)}, bf16[16,128,128]{2,1,0:T(8,128)(2,1)S(1)}, u32[]{:S(2)}, u32[]{:S(2)}) %collective-permute-start.17) | collective-permute-done | bytes 524320 | tf_op jit(solution)/shard_map/ppermute | solution.py:875
  82.7 8.3 %post.2 = (f32[512,512]{1,0:T(8,128)}, f32[512,128]{1,0:T(8,128)S(1)}, bf16[512,512]{1,0:T(8,128)(2,1)S(1)}, bf16[512,2048]{1,0:T(8,128)(2,1)}, bf16[512,2048]{1...) custom-call(bf16[512,512]{1,0:T(8,128)(2,1)S(1)} %get-tuple-element.173.o_ref, ...), custom_call_target="tpu_custom_call" | custom-call | flops 11000000 | tf_op jit(solution)/shard_map/post/pallas_call | solution.py:416
  99.0 9.0 %attend.3 = (bf16[512,512]{1,0:T(8,128)(2,1)S(1)}, f32[512,512]{1,0:T(8,128)S(1)}) custom-call(bf16[512,512]{1,0:T(8,128)(2,1)S(1)} %get-tuple-element.189.q_ref, bf16[512,512]{1,0:T(8,128)(2,1)S(1)} %get-tuple-element.190.k_ref, bf16[512,512]{1,0:T(8,128)(2,1)S(1)} %collective-permute-done.22.kp_ref, bf16[512,512]{1,0:T(8,128)(2,1)S(1)} %get-tuple-element.191.v_ref, ...), custom_call_target="tpu_custom_call" | custom-call | flops 11000000 | tf_op jit(solution)/shard_map/attend/pallas_call | solution.py:356
  109.6 10.3 %collective-permute-done.28.f2 = bf16[16,128,128]{2,1,0:T(8,128)(2,1)S(1)} collective-permute-done((bf16[16,128,128]{2,1,0:T(8,128)(2,1)}, bf16[16,128,128]{2,1,0:T(8,128)(2,1)S(1)}, u32[]{:S(2)}, u32[]{:S(2)}) %collective-permute-start.28) | collective-permute-done | bytes 524320 | tf_op jit(solution)/shard_map/ppermute | solution.py:875
  122.6 8.5 %post.3 = (f32[512,512]{1,0:T(8,128)}, f32[512,128]{1,0:T(8,128)S(1)}, bf16[512,512]{1,0:T(8,128)(2,1)S(1)}, bf16[512,2048]{1,0:T(8,128)(2,1)}, bf16[512,2048]{1...) custom-call(bf16[512,512]{1,0:T(8,128)(2,1)S(1)} %get-tuple-element.192.o_ref, ...), custom_call_target="tpu_custom_call" | custom-call | flops 11000000 | tf_op jit(solution)/shard_map/post/pallas_call | solution.py:416
  131.1 3.1 broadcast_multiply_fusion
  134.2 11.6 %ffn_grad.2 = (bf16[2,16,128,128]{3,2,1,0:T(8,128)(2,1)}, bf16[2,16,128,128]{3,2,1,0:T(8,128)(2,1)}, bf16[2,20,128,128]{3,2,1,0:T(8,128)(2,1)}, bf16[2,20,128,12...) custom-call(f32[512,512]{1,0:T(8,128)} %get-tuple-element.372.e_ref,, ...), custom_call_target="tpu_custom_call" | custom-call | flops 16000000 | tf_op jit(solution)/shard_map/ffn_grad/pallas_call | solution.py:509
  146.3 2.7 collective-permute-done.30
  153.6 16.1 %attend_grad.2 = (bf16[512,512]{1,0:T(8,128)(2,1)S(1)}, bf16[512,512]{1,0:T(8,128)(2,1)S(1)}, bf16[512,512]{1,0:T(8,128)(2,1)S(1)}, bf16[512,512]{1,0:T(8,128)(2,1)S(1)}, bf16[512,512]{1,0:T(8,128)(2,1)S(1)}) custom-call(bf16[512,512]{1,0:T(8,128)(2,1)S(1)} %get-tuple-element.189.q_ref, bf16[512,512]{1,0:T(8,128)(2,1)S(1)} %get-tuple-element.190.k_ref, ...), custom_call_target="tpu_custom_call" | custom-call | flops 23000000 | tf_op jit(solution)/shard_map/attend_grad/pallas_call | solution.py:600
  173.5 4.1 %proj_grad.2 = (bf16[2,12,128,128]{3,2,1,0:T(8,128)(2,1)S(1)}, bf16[2,12,128,128]{3,2,1,0:T(8,128)(2,1)}, f32[512,512]{1,0:T(8,128)}, f32[8,512]{1,0:T(8,128)S(1)}) custom-call(bf16[512,512]{1,0:T(8,128)(2,1)S(1)} %get-tuple-element.222.dq_ref, bf16[512,512]{1,0:T(8,128)(2,1)S(1)} %get-tuple-element.223.dk_ref, ...), custom_call_target="tpu_custom_call" | custom-call | flops 5000000 | tf_op jit(solution)/shard_map/proj_grad/pallas_call | solution.py:659
  181.0 11.4 %ffn_grad.3 = (bf16[2,16,128,128]{3,2,1,0:T(8,128)(2,1)}, bf16[2,16,128,128]{3,2,1,0:T(8,128)(2,1)}, bf16[2,20,128,128]{3,2,1,0:T(8,128)(2,1)}, bf16[2,20,128,12...) custom-call(f32[512,512]{1,0:T(8,128)} %get-tuple-element.234.e_ref,, ...), custom_call_target="tpu_custom_call" | custom-call | flops 16000000 | tf_op jit(solution)/shard_map/ffn_grad/pallas_call | solution.py:509
  192.5 7.9 %collective-permute-done.36.refs_9_ = bf16[12,128,128]{2,1,0:T(8,128)(2,1)S(1)} collective-permute-done((bf16[12,128,128]{2,1,0:T(8,128)(2,1)S(1)}, bf16[12,128,128]{2,1,0:T(8,128)(2,1)S(1)}, u32[]{:S(2)}, u32[]{:S(2)}) %collective-permute-start.36) | collective-permute-done | bytes 393248 | tf_op jit(solution)/shard_map/ppermute | solution.py:875
  200.9 2.7 collective-permute-done.38
  206.5 16.2 %attend_grad.3 = (bf16[512,512]{1,0:T(8,128)(2,1)S(1)}, bf16[512,512]{1,0:T(8,128)(2,1)S(1)}, bf16[512,512]{1,0:T(8,128)(2,1)S(1)}, bf16[512,512]{1,0:T(8,128)(2,1)S(1)}, bf16[512,512]{1,0:T(8,128)(2,1)S(1)}) custom-call(bf16[512,512]{1,0:T(8,128)(2,1)S(1)} %get-tuple-element.168.q_ref, bf16[512,512]{1,0:T(8,128)(2,1)S(1)} %get-tuple-element.169.k_ref, ...), custom_call_target="tpu_custom_call" | custom-call | flops 23000000 | tf_op jit(solution)/shard_map/attend_grad/pallas_call | solution.py:600
  225.5 4.0 %proj_grad.3 = (bf16[2,12,128,128]{3,2,1,0:T(8,128)(2,1)S(1)}, bf16[2,12,128,128]{3,2,1,0:T(8,128)(2,1)}, f32[512,512]{1,0:T(8,128)}, f32[8,512]{1,0:T(8,128)S(1)}) custom-call(bf16[512,512]{1,0:T(8,128)(2,1)S(1)} %get-tuple-element.255.dq_ref, bf16[512,512]{1,0:T(8,128)(2,1)S(1)} %get-tuple-element.256.dk_ref, ...), custom_call_target="tpu_custom_call" | custom-call | flops 5000000 | tf_op jit(solution)/shard_map/proj_grad/pallas_call | solution.py:659
  237.3 2.4 collective-permute-done.45
  241.2 3.6 %collective-permute-done.46 = f32[2,128,128]{2,1,0:T(8,128)S(1)} collective-permute-done((f32[2,128,128]{2,1,0:T(8,128)S(1)}, f32[2,128,128]{2,1,0:T(8,128)S(1)}, u32[]{:S(2)}, u32[]{:S(2)}) %collective-permute-start.46) | collective-permute-done | bytes 131104 | tf_op jit(solution)/shard_map/ppermute | solution.py:861
  244.8 2.5 collective-permute-start.47
  247.3 4.8 %collective-permute-done.47 = f32[2,128,128]{2,1,0:T(8,128)S(1)} collective-permute-done((f32[2,128,128]{2,1,0:T(8,128)S(1)}, f32[2,128,128]{2,1,0:T(8,128)S(1)}, u32[]{:S(2)}, u32[]{:S(2)}) %collective-permute-start.47) | collective-permute-done | bytes 131104 | tf_op jit(solution)/shard_map/ppermute | solution.py:861
  252.2 3.0 collective-permute-done.48.refs_6_
  255.2 3.9 %routed.1 = bf16[8,1536,128]{2,1,0:T(8,128)(2,1)} custom-call(s32[192]{0:T(256)S(1)} %pad_add_fusion.at_ref, bf16[12,128,128]{2,1,0:T(8,128)(2,1)S(1)} %get-tuple-element.276.refs_0_, bf16[20,128,128]{2,1,0:T(8,128)(2,1)S(1)} %get-tuple-element.349.refs_1_, bf16[16,128,128]{2,1,0:T(8,128)(2,1)S(1)} %get-tuple-element.353.refs_2_, ...), custom_call_target="tpu_custom_call" | custom-call | flops 4000000 | tf_op jit(solution)/shard_map/routed/pallas_call | solution.py:808
  262.6 4.1 %collective-permute-done.54 = bf16[768,128]{1,0:T(8,128)(2,1)S(1)} collective-permute-done((bf16[768,128]{1,0:T(8,128)(2,1)S(1)}, bf16[768,128]{1,0:T(8,128)(2,1)S(1)}, u32[]{:S(2)}, u32[]{:S(2)}) %collective-permute-start.54) | collective-permute-done | bytes 196640 | tf_op jit(solution)/shard_map/ppermute | solution.py:825
  271.3 7.0 %collective-permute-done.51 = bf16[1536,128]{1,0:T(8,128)(2,1)S(1)} collective-permute-done((bf16[1536,128]{1,0:T(8,128)(2,1)S(1)}, bf16[1536,128]{1,0:T(8,128)(2,1)S(1)}, u32[]{:S(2)}, u32[]{:S(2)}) %collective-permute-start.51) | collective-permute-done | bytes 393248 | tf_op jit(solution)/shard_map/ppermute | solution.py:825
  282.6 4.4 %collective-permute-done.56 = bf16[1536,128]{1,0:T(8,128)(2,1)S(1)} collective-permute-done((bf16[1536,128]{1,0:T(8,128)(2,1)S(1)}, bf16[1536,128]{1,0:T(8,128)(2,1)S(1)}, u32[]{:S(2)}, u32[]{:S(2)}) %collective-permute-start.56) | collective-permute-done | bytes 393248 | tf_op jit(solution)/shard_map/ppermute | solution.py:825
  293.1 2.7 collective-permute-done.60.p2
  302.5 37.3 %soap.1 = (f32[12,128,128]{2,1,0:T(8,128)}, bf16[12,128,128]{2,1,0:T(8,128)(2,1)}, f32[12,128,128]{2,1,0:T(8,128)}, f32[12,128,128]{2,1,0:T(8,128)}, f32[12,128,...) custom-call(bf16[12,128,128]{2,1,0:T(8,128)(2,1)S(1)} %bitcast.144, ...), custom_call_target="tpu_custom_call" | custom-call | flops 40000000 | tf_op jit(solution)/shard_map/soap/pallas_call | solution.py:189
  (290 shorter events, 102.4 us)
Async XLA Ops:
  1.9 12.2 %collective-permute-start.1 = (bf16[12,128,128]{2,1,0:T(8,128)(2,1)S(1)}, bf16[12,128,128]{2,1,0:T(8,128)(2,1)S(1)}, u32[]{:S(2)}, u32[]{:S(2)}) collective-permute-start(bf16[12,128,128]{2,1,0:T(8,128)(2,1)S(1)} %bitcast_convert_fusion.refs_0_), channel_id=1, source_target_pairs={{0,4},{8,0},{16,8},{24,16},{28,24},{20,28},{12,20},{4,12},{1,5},{9... | collective-permute-start | bytes 1179656 | tf_op jit(solution)/shard_map/ppermute | solution.py:825
  4.9 10.9 %collective-permute-start = (bf16[12,128,128]{2,1,0:T(8,128)(2,1)S(1)}, bf16[12,128,128]{2,1,0:T(8,128)(2,1)S(1)}, u32[]{:S(2)}, u32[]{:S(2)}) collective-permute-start(bf16[12,128,128]{2,1,0:T(8,128)(2,1)S(1)} %bitcast_convert_fusion.refs_0_), channel_id=1, source_target_pairs={{0,8},{8,16},{16,24},{24,28},{28,20},{20,12},{12,4},{4,0},{1,9},{9... | collective-permute-start | bytes 1179656 | tf_op jit(solution)/shard_map/ppermute | solution.py:825
  14.1 10.3 %collective-permute-start.3 = (bf16[12,128,128]{2,1,0:T(8,128)(2,1)S(1)}, bf16[12,128,128]{2,1,0:T(8,128)(2,1)S(1)}, u32[]{:S(2)}, u32[]{:S(2)}) collective-permute-start(bf16[12,128,128]{2,1,0:T(8,128)(2,1)S(1)} %collective-permute-done.1.refs_2_), channel_id=1, source_target_pairs={{0,4},{8,0},{16,8},{24,16},{28,24},{20,28},{12,20},{4,12},{1,5},{9... | collective-permute-start | bytes 1179656 | tf_op jit(solution)/shard_map/ppermute | solution.py:825
  15.8 10.0 %collective-permute-start.2 = (bf16[12,128,128]{2,1,0:T(8,128)(2,1)S(1)}, bf16[12,128,128]{2,1,0:T(8,128)(2,1)S(1)}, u32[]{:S(2)}, u32[]{:S(2)}) collective-permute-start(bf16[12,128,128]{2,1,0:T(8,128)(2,1)S(1)} %collective-permute-done.refs_1_), channel_id=1, source_target_pairs={{0,8},{8,16},{16,24},{24,28},{28,20},{20,12},{12,4},{4,0},{1,9},{9... | collective-permute-start | bytes 1179656 | tf_op jit(solution)/shard_map/ppermute | solution.py:825
  24.4 10.2 %collective-permute-start.5 = (bf16[12,128,128]{2,1,0:T(8,128)(2,1)S(1)}, bf16[12,128,128]{2,1,0:T(8,128)(2,1)S(1)}, u32[]{:S(2)}, u32[]{:S(2)}) collective-permute-start(bf16[12,128,128]{2,1,0:T(8,128)(2,1)S(1)} %collective-permute-done.3.refs_4_), channel_id=1, source_target_pairs={{0,4},{8,0},{16,8},{24,16},{28,24},{20,28},{12,20},{4,12},{1,5},{9... | collective-permute-start | bytes 1179656 | tf_op jit(solution)/shard_map/ppermute | solution.py:825
  25.7 10.3 %collective-permute-start.4 = (bf16[12,128,128]{2,1,0:T(8,128)(2,1)S(1)}, bf16[12,128,128]{2,1,0:T(8,128)(2,1)S(1)}, u32[]{:S(2)}, u32[]{:S(2)}) collective-permute-start(bf16[12,128,128]{2,1,0:T(8,128)(2,1)S(1)} %collective-permute-done.2.refs_3_), channel_id=1, source_target_pairs={{0,8},{8,16},{16,24},{24,28},{28,20},{20,12},{12,4},{4,0},{1,9},{9... | collective-permute-start | bytes 1179656 | tf_op jit(solution)/shard_map/ppermute | solution.py:825
  43.7 7.8 %collective-permute-start.9 = (bf16[12,128,128]{2,1,0:T(8,128)(2,1)S(1)}, bf16[12,128,128]{2,1,0:T(8,128)(2,1)S(1)}, u32[]{:S(2)}, u32[]{:S(2)}) collective-permute-start(bf16[12,128,128]{2,1,0:T(8,128)(2,1)S(1)} %get-tuple-element.164.w0), channel_id=1, source_target_pairs={{0,2},{1,3},{2,0},{3,1},{4,6},{5,7},{6,4},{7,5},{8,10},{9,11},{10,... | collective-permute-start | bytes 1179656 | tf_op jit(solution)/shard_map/ppermute | solution.py:875
  45.3 7.8 %collective-permute-start.8 = (bf16[12,128,128]{2,1,0:T(8,128)(2,1)S(1)}, bf16[12,128,128]{2,1,0:T(8,128)(2,1)S(1)}, u32[]{:S(2)}, u32[]{:S(2)}) collective-permute-start(bf16[12,128,128]{2,1,0:T(8,128)(2,1)S(1)} %get-tuple-element.164.w0), channel_id=1, source_target_pairs={{0,1},{1,0},{2,3},{3,2},{4,5},{5,4},{6,7},{7,6},{8,9},{9,8},{10,11... | collective-permute-start | bytes 1179656 | tf_op jit(solution)/shard_map/ppermute | solution.py:871
  51.5 17.5 %collective-permute-start.14 = (bf16[20,128,128]{2,1,0:T(8,128)(2,1)S(1)}, bf16[20,128,128]{2,1,0:T(8,128)(2,1)S(1)}, u32[]{:S(2)}, u32[]{:S(2)}) collective-permute-start(bf16[20,128,128]{2,1,0:T(8,128)(2,1)S(1)} %get-tuple-element.177.a0), channel_id=1, source_target_pairs={{0,2},{1,3},{2,0},{3,1},{4,6},{5,7},{6,4},{7,5},{8,10},{9,11},{10,... | collective-permute-start | bytes 1966088 | tf_op jit(solution)/shard_map/ppermute | solution.py:875
  55.0 24.9 %collective-permute-start.17 = (bf16[16,128,128]{2,1,0:T(8,128)(2,1)S(1)}, bf16[16,128,128]{2,1,0:T(8,128)(2,1)S(1)}, u32[]{:S(2)}, u32[]{:S(2)}) collective-permute-start(bf16[16,128,128]{2,1,0:T(8,128)(2,1)S(1)} %get-tuple-element.180.f0), channel_id=1, source_target_pairs={{0,2},{1,3},{2,0},{3,1},{4,6},{5,7},{6,4},{7,5},{8,10},{9,11},{10,... | collective-permute-start | bytes 1572872 | tf_op jit(solution)/shard_map/ppermute | solution.py:875
  56.5 25.1 %collective-permute-start.13 = (bf16[20,128,128]{2,1,0:T(8,128)(2,1)S(1)}, bf16[20,128,128]{2,1,0:T(8,128)(2,1)S(1)}, u32[]{:S(2)}, u32[]{:S(2)}) collective-permute-start(bf16[20,128,128]{2,1,0:T(8,128)(2,1)S(1)} %get-tuple-element.177.a0), channel_id=1, source_target_pairs={{0,1},{1,0},{2,3},{3,2},{4,5},{5,4},{6,7},{7,6},{8,9},{9,8},{10,11... | collective-permute-start | bytes 1966088 | tf_op jit(solution)/shard_map/ppermute | solution.py:871
  69.1 12.8 %collective-permute-start.15 = (bf16[20,128,128]{2,1,0:T(8,128)(2,1)S(1)}, bf16[20,128,128]{2,1,0:T(8,128)(2,1)S(1)}, u32[]{:S(2)}, u32[]{:S(2)}) collective-permute-start(bf16[20,128,128]{2,1,0:T(8,128)(2,1)S(1)} %collective-permute-done.14.a2), channel_id=1, source_target_pairs={{0,1},{1,0},{2,3},{3,2},{4,5},{5,4},{6,7},{7,6},{8,9},{9,8},{10,11... | collective-permute-start | bytes 1966088 | tf_op jit(solution)/shard_map/ppermute | solution.py:871
  69.1 12.4 %collective-permute-start.16 = (bf16[16,128,128]{2,1,0:T(8,128)(2,1)S(1)}, bf16[16,128,128]{2,1,0:T(8,128)(2,1)S(1)}, u32[]{:S(2)}, u32[]{:S(2)}) collective-permute-start(bf16[16,128,128]{2,1,0:T(8,128)(2,1)S(1)} %get-tuple-element.180.f0), channel_id=1, source_target_pairs={{0,1},{1,0},{2,3},{3,2},{4,5},{5,4},{6,7},{7,6},{8,9},{9,8},{10,11... | collective-permute-start | bytes 1572872 | tf_op jit(solution)/shard_map/ppermute | solution.py:871
  79.9 11.5 %collective-permute-start.20 = (bf16[12,128,128]{2,1,0:T(8,128)(2,1)S(1)}, bf16[12,128,128]{2,1,0:T(8,128)(2,1)S(1)}, u32[]{:S(2)}, u32[]{:S(2)}) collective-permute-start(bf16[12,128,128]{2,1,0:T(8,128)(2,1)S(1)} %get-tuple-element.184.w0), channel_id=1, source_target_pairs={{0,2},{1,3},{2,0},{3,1},{4,6},{5,7},{6,4},{7,5},{8,10},{9,11},{10,... | collective-permute-start | bytes 1179656 | tf_op jit(solution)/shard_map/ppermute | solution.py:875
  81.5 11.5 %collective-permute-start.19 = (bf16[12,128,128]{2,1,0:T(8,128)(2,1)S(1)}, bf16[12,128,128]{2,1,0:T(8,128)(2,1)S(1)}, u32[]{:S(2)}, u32[]{:S(2)}) collective-permute-start(bf16[12,128,128]{2,1,0:T(8,128)(2,1)S(1)} %get-tuple-element.184.w0), channel_id=1, source_target_pairs={{0,1},{1,0},{2,3},{3,2},{4,5},{5,4},{6,7},{7,6},{8,9},{9,8},{10,11... | collective-permute-start | bytes 1179656 | tf_op jit(solution)/shard_map/ppermute | solution.py:871
  91.5 17.6 %collective-permute-start.25 = (bf16[20,128,128]{2,1,0:T(8,128)(2,1)S(1)}, bf16[20,128,128]{2,1,0:T(8,128)(2,1)S(1)}, u32[]{:S(2)}, u32[]{:S(2)}) collective-permute-start(bf16[20,128,128]{2,1,0:T(8,128)(2,1)S(1)} %copy-done.5), channel_id=1, source_target_pairs={{0,2},{1,3},{2,0},{3,1},{4,6},{5,7},{6,4},{7,5},{8,10},{9,11},{10,... | collective-permute-start | bytes 1966088 | tf_op jit(solution)/shard_map/ppermute | solution.py:875
  96.9 23.0 %collective-permute-start.28 = (bf16[16,128,128]{2,1,0:T(8,128)(2,1)}, bf16[16,128,128]{2,1,0:T(8,128)(2,1)S(1)}, u32[]{:S(2)}, u32[]{:S(2)}) collective-permute-start(bf16[16,128,128]{2,1,0:T(8,128)(2,1)} %get-tuple-element.199.f0), channel_id=1, source_target_pairs={{0,2},{1,3},{2,0},{3,1},{4,6},{5,7},{6,4},{7,5},{8,10},{9,11},{10,... | collective-permute-start | bytes 1572872 | tf_op jit(solution)/shard_map/ppermute | solution.py:875
  98.4 21.5 %collective-permute-start.24 = (bf16[20,128,128]{2,1,0:T(8,128)(2,1)S(1)}, bf16[20,128,128]{2,1,0:T(8,128)(2,1)S(1)}, u32[]{:S(2)}, u32[]{:S(2)}) collective-permute-start(bf16[20,128,128]{2,1,0:T(8,128)(2,1)S(1)} %copy-done.5), channel_id=1, source_target_pairs={{0,1},{1,0},{2,3},{3,2},{4,5},{5,4},{6,7},{7,6},{8,9},{9,8},{10,11... | collective-permute-start | bytes 1966088 | tf_op jit(solution)/shard_map/ppermute | solution.py:871
  109.1 12.7 %collective-permute-start.26 = (bf16[20,128,128]{2,1,0:T(8,128)(2,1)S(1)}, bf16[20,128,128]{2,1,0:T(8,128)(2,1)S(1)}, u32[]{:S(2)}, u32[]{:S(2)}) collective-permute-start(bf16[20,128,128]{2,1,0:T(8,128)(2,1)S(1)} %collective-permute-done.25.a2), channel_id=1, source_target_pairs={{0,1},{1,0},{2,3},{3,2},{4,5},{5,4},{6,7},{7,6},{8,9},{9,8},{10,11... | collective-permute-start | bytes 1966088 | tf_op jit(solution)/shard_map/ppermute | solution.py:871
  109.2 10.6 %collective-permute-start.27 = (bf16[16,128,128]{2,1,0:T(8,128)(2,1)}, bf16[16,128,128]{2,1,0:T(8,128)(2,1)S(1)}, u32[]{:S(2)}, u32[]{:S(2)}) collective-permute-start(bf16[16,128,128]{2,1,0:T(8,128)(2,1)} %get-tuple-element.199.f0), channel_id=1, source_target_pairs={{0,1},{1,0},{2,3},{3,2},{4,5},{5,4},{6,7},{7,6},{8,9},{9,8},{10,11... | collective-permute-start | bytes 1572872 | tf_op jit(solution)/shard_map/ppermute | solution.py:871
  150.8 18.9 %collective-permute-start.32 = (bf16[20,128,128]{2,1,0:T(8,128)(2,1)S(1)}, bf16[20,128,128]{2,1,0:T(8,128)(2,1)S(1)}, u32[]{:S(2)}, u32[]{:S(2)}) collective-permute-start(bf16[20,128,128]{2,1,0:T(8,128)(2,1)S(1)} %get-tuple-element.348), channel_id=1, source_target_pairs={{0,2},{1,3},{2,0},{3,1},{4,6},{5,7},{6,4},{7,5},{8,10},{9,11},{10,... | collective-permute-start | bytes 1966088 | tf_op jit(solution)/shard_map/ppermute | solution.py:875
  177.8 14.8 %collective-permute-start.37 = (bf16[16,128,128]{2,1,0:T(8,128)(2,1)S(1)}, bf16[16,128,128]{2,1,0:T(8,128)(2,1)S(1)}, u32[]{:S(2)}, u32[]{:S(2)}) collective-permute-start(bf16[16,128,128]{2,1,0:T(8,128)(2,1)S(1)} %copy-done.57), channel_id=1, source_target_pairs={{0,2},{1,3},{2,0},{3,1},{4,6},{5,7},{6,4},{7,5},{8,10},{9,11},{10,... | collective-permute-start | bytes 1572872 | tf_op jit(solution)/shard_map/ppermute | solution.py:875
  180.4 20.0 %collective-permute-start.36 = (bf16[12,128,128]{2,1,0:T(8,128)(2,1)S(1)}, bf16[12,128,128]{2,1,0:T(8,128)(2,1)S(1)}, u32[]{:S(2)}, u32[]{:S(2)}) collective-permute-start(bf16[12,128,128]{2,1,0:T(8,128)(2,1)S(1)} %get-tuple-element.358), channel_id=1, source_target_pairs={{0,2},{1,3},{2,0},{3,1},{4,6},{5,7},{6,4},{7,5},{8,10},{9,11},{10,... | collective-permute-start | bytes 1179656 | tf_op jit(solution)/shard_map/ppermute | solution.py:875
  205.5 17.3 %collective-permute-start.40 = (bf16[20,128,128]{2,1,0:T(8,128)(2,1)S(1)}, bf16[20,128,128]{2,1,0:T(8,128)(2,1)S(1)}, u32[]{:S(2)}, u32[]{:S(2)}) collective-permute-start(bf16[20,128,128]{2,1,0:T(8,128)(2,1)S(1)} %get-tuple-element.350), channel_id=1, source_target_pairs={{0,2},{1,3},{2,0},{3,1},{4,6},{5,7},{6,4},{7,5},{8,10},{9,11},{10,... | collective-permute-start | bytes 1966088 | tf_op jit(solution)/shard_map/ppermute | solution.py:875
  232.8 19.3 %collective-permute-start.49 = (bf16[16,128,128]{2,1,0:T(8,128)(2,1)S(1)}, bf16[16,128,128]{2,1,0:T(8,128)(2,1)S(1)}, u32[]{:S(2)}, u32[]{:S(2)}) collective-permute-start(bf16[16,128,128]{2,1,0:T(8,128)(2,1)S(1)} %get-tuple-element.277), channel_id=1, source_target_pairs={{0,2},{1,3},{2,0},{3,1},{4,6},{5,7},{6,4},{7,5},{8,10},{9,11},{10,... | collective-permute-start | bytes 1572872 | tf_op jit(solution)/shard_map/ppermute | solution.py:875
  236.3 18.9 %collective-permute-start.48 = (bf16[12,128,128]{2,1,0:T(8,128)(2,1)S(1)}, bf16[12,128,128]{2,1,0:T(8,128)(2,1)S(1)}, u32[]{:S(2)}, u32[]{:S(2)}) collective-permute-start(bf16[12,128,128]{2,1,0:T(8,128)(2,1)S(1)} %get-tuple-element.355), channel_id=1, source_target_pairs={{0,2},{1,3},{2,0},{3,1},{4,6},{5,7},{6,4},{7,5},{8,10},{9,11},{10,... | collective-permute-start | bytes 1179656 | tf_op jit(solution)/shard_map/ppermute | solution.py:875
  269.2 9.2 %collective-permute-start.51 = (bf16[1536,128]{1,0:T(8,128)(2,1)S(1)}, bf16[1536,128]{1,0:T(8,128)(2,1)S(1)}, u32[]{:S(2)}, u32[]{:S(2)}) collective-permute-start(bf16[1536,128]{1,0:T(8,128)(2,1)S(1)} %pad_maximum_fusion), channel_id=1, source_target_pairs={{0,8},{8,16},{16,24},{24,28},{28,20},{20,12},{12,4},{4,0},{1,9},{9... | collective-permute-start | bytes 1179656 | tf_op jit(solution)/shard_map/ppermute | solution.py:825
  269.7 9.0 %collective-permute-start.55 = (bf16[1536,128]{1,0:T(8,128)(2,1)S(1)}, bf16[1536,128]{1,0:T(8,128)(2,1)S(1)}, u32[]{:S(2)}, u32[]{:S(2)}) collective-permute-start(bf16[1536,128]{1,0:T(8,128)(2,1)S(1)} %pad_maximum_fusion.1), channel_id=1, source_target_pairs={{0,4},{8,0},{16,8},{24,16},{28,24},{20,28},{12,20},{4,12},{1,5},{9... | collective-permute-start | bytes 1179656 | tf_op jit(solution)/shard_map/ppermute | solution.py:825
  279.0 8.1 %collective-permute-start.56 = (bf16[1536,128]{1,0:T(8,128)(2,1)S(1)}, bf16[1536,128]{1,0:T(8,128)(2,1)S(1)}, u32[]{:S(2)}, u32[]{:S(2)}) collective-permute-start(bf16[1536,128]{1,0:T(8,128)(2,1)S(1)} %get-tuple-element.339), channel_id=1, source_target_pairs={{0,4},{8,0},{16,8},{24,16},{28,24},{20,28},{12,20},{4,12},{1,5},{9... | collective-permute-start | bytes 1179656 | tf_op jit(solution)/shard_map/ppermute | solution.py:825
  281.0 10.4 %collective-permute-start.58 = (f32[128,128]{1,0:T(8,128)S(1)}, f32[128,128]{1,0:T(8,128)S(1)}, u32[]{:S(2)}, u32[]{:S(2)}) collective-permute-start(f32[128,128]{1,0:T(8,128)S(1)} %slice_bitcast_fusion.10), channel_id=1, source_target_pairs={{0,2},{1,3},{2,0},{3,1},{4,6},{5,7},{6,4},{7,5},{8,10},{9,11},{10,... | collective-permute-start | bytes 196616 | tf_op jit(solution)/shard_map/ppermute | solution.py:875
  289.4 13.0 %collective-permute-start.57 = (bf16[1536,128]{1,0:T(8,128)(2,1)}, bf16[1536,128]{1,0:T(8,128)(2,1)S(1)}, u32[]{:S(2)}, u32[]{:S(2)}) collective-permute-start(bf16[1536,128]{1,0:T(8,128)(2,1)} %get-tuple-element.337), channel_id=1, source_target_pairs={{0,4},{8,0},{16,8},{24,16},{28,24},{20,28},{12,20},{4,12},{1,5},{9... | collective-permute-start | bytes 1179656 | tf_op jit(solution)/shard_map/ppermute | solution.py:825
  291.0 11.5 %collective-permute-start.53 = (bf16[1536,128]{1,0:T(8,128)(2,1)}, bf16[1536,128]{1,0:T(8,128)(2,1)S(1)}, u32[]{:S(2)}, u32[]{:S(2)}) collective-permute-start(bf16[1536,128]{1,0:T(8,128)(2,1)} %get-tuple-element.338), channel_id=1, source_target_pairs={{0,8},{8,16},{16,24},{24,28},{28,20},{20,12},{12,4},{4,0},{1,9},{9... | collective-permute-start | bytes 1179656 | tf_op jit(solution)/shard_map/ppermute | solution.py:825
  (93 other events, 804.2 us)

commit v5 on v4

--- a/solution.py
+++ b/solution.py
@@ -89,6 +89,13 @@
 
 
 PANEL = 32
+AHEAD = 2
+
+
+def recip(x):
+    guess = pl.reciprocal(x, approx=True)
+    guess = guess * (2.0 - x * guess)
+    return guess * (2.0 - x * guess)
 
 
 def qr_batch(a_ref, count):
@@ -97,17 +104,29 @@
     sub = lax.broadcasted_iota(jnp.int32, (1, PANEL, 1), 1)
     for r0 in range(0, BLK, PANEL):
         tiles = [a_ref[:, r0 + 8 * t : r0 + 8 * t + 8, :] for t in range(PANEL // 8)]
-        for k in range(PANEL):
-            t0, s = divmod(k, 8)
-            row = tiles[t0][:, s : s + 1, :]
-            pn = (row + (lane == r0 + k).astype(f32)) * (1.0 / row[:, :, r0 + k : r0 + k + 1])
-            for t in range(t0, PANEL // 8):
-                c = tiles[t][:, :, r0 + k : r0 + k + 1]
-                if t == t0:
-                    if s == 7:
-                        continue
-                    c = jnp.where(sub8 > s, c, 0.0)
-                tiles[t] = tiles[t] - c * pn
+        for k0 in range(0, PANEL, AHEAD):
+            t0, s0 = divmod(k0, 8)
+            cols = [
+                [
+                    jnp.broadcast_to(tiles[t][:, :, r0 + k : r0 + k + 1], (count, 8, BLK))
+                    for k in range(k0, k0 + AHEAD)
+                ]
+                for t in range(PANEL // 8)
+            ]
+            for i in range(AHEAD):
+                s = s0 + i
+                inv = recip(cols[t0][i][:, s : s + 1, :])
+                pn = (tiles[t0][:, s : s + 1, :] + (lane == r0 + k0 + i).astype(f32)) * inv
+                rest = [cols[t0][j][:, s : s + 1, :] * inv for j in range(i + 1, AHEAD)]
+                for t in range(t0, PANEL // 8):
+                    c = cols[t][i]
+                    if t == t0:
+                        if s == 7:
+                            continue
+                        c = jnp.where(sub8 > s, c, 0.0)
+                    tiles[t] = tiles[t] - c * pn
+                    for j, m in enumerate(rest):
+                        cols[t][i + 1 + j] = cols[t][i + 1 + j] - c * m
         done = jnp.concatenate(tiles, axis=1)
         diag = lane == sub + r0
         pivot = jnp.sum(jnp.where(diag, done, 0.0), axis=2, keepdims=True)
@@ -391,17 +410,13 @@
         y = unit * vec[1] + vec[2]
         yb = y.astype(bf16)
         y_ref[at] = yb
-        fed = jnp.zeros((ROW_TILE, D), f32)
-        for r in range(FF // D):
-            cols = slice(r * D, (r + 1) * D)
-            pre = dot(yb, w1_s[:, cols]) + b1_ref[:, cols]
-            phi = 0.5 * (1.0 + lax.erf(pre * (0.5**0.5)))
-            hid = (pre * phi).astype(bf16)
-            hid_ref[at, cols] = hid
-            slope_ref[at, cols] = (
-                phi + pre * (jnp.exp(-0.5 * pre * pre) * 0.3989422804014327)
-            ).astype(bf16)
-            fed = fed + dot(hid, w2_s[cols, :])
+        pre = dot(yb, w1_s[...]) + b1_ref[...]
+        phi = 0.5 * (1.0 + lax.erf(pre * (0.5**0.5)))
+        hid = (pre * phi).astype(bf16)
+        hid_ref[at] = hid
+        slope = phi + pre * (jnp.exp(-0.5 * pre * pre) * 0.3989422804014327)
+        slope_ref[at] = slope.astype(bf16)
+        fed = dot(hid, w2_s[...])
         unit, inv = layer_norm(y + fed + vec[3])
         n2_ref[at] = unit
         i2_ref[at] = jnp.broadcast_to(inv, (ROW_TILE, LANES))
@@ -839,7 +854,7 @@
     return held
 
 
-def ring_reduce(pieces, order):
+def ring_reduce(pieces, order, meanwhile):
     n = len(order)
     half = pieces[0].shape[0] // 2
     up = ring_shift(pieces[n // 2][:half], order, 1)
@@ -851,14 +866,19 @@
             down = jnp.concatenate([far[:half], add_low(down, far[half:])], axis=0)
         else:
             up, down = add_low(up, near), add_low(down, far)
+        up, down = tied((up, down), meanwhile[step - 1])
         up, down = ring_shift(up, order, 1), ring_shift(down, order, -1)
     return pieces[0], up, down
 
 
-def dp_sum(value, count):
+def dp_sum(value, count, after):
     bit = 1
     while bit < count:
-        value = value + lax.ppermute(value, "dp", [(i, i ^ bit) for i in range(count)])
+        if 2 * bit >= count:
+            value = tied(value, after)
+        low = value.astype(bf16)
+        there = lax.ppermute(low, "dp", [(i, i ^ bit) for i in range(count)])
+        value = low.astype(f32) + there.astype(f32)
         bit *= 2
     return value
 
@@ -943,8 +963,9 @@
         bq, bv, bo, g1, c1, b1, b2, g2, c2 = depth_vectors(vec_values, layer)
         vec = jnp.stack([bo, g1, c1, b2, g2, c2, g2, c2])
         vectors.append([vec] + [relative(row, place) for row in (bq, bv, b1)])
-    slots, (x, vectors, ohq, ohk, valid, gather_at) = lax.optimization_barrier(
-        (slots, (x, vectors, ohq, ohk, valid, gather_at))
+    grad = cotangent * valid
+    slots, (x, vectors, ohq, ohk, valid, gather_at, grad) = lax.optimization_barrier(
+        (slots, (x, vectors, ohq, ohk, valid, gather_at, grad))
     )
     mine = natural_order(gather_at, slots, plan)
     moved = []
@@ -981,15 +1002,22 @@
         n1, i1, y, hid, slope, n2, i2, x = post(o, x, vec, b1, wmid, wdown)
         saved.append((xs, q, k, v, kp, vp, o, lse, vec, n1, i1, y, hid, slope, n2, i2))
     activations = x * valid
-    grad = cotangent * valid
 
     own_sums = [None] * (3 * LAYERS)
     far_sums = [None] * (3 * LAYERS)
     table_rows = [None] * LAYERS
 
+    waiting = []
+
     def chip_sum(at, keep, got):
-        own_sums[at] = add_low(keep[0], got[0])
+        waiting.append((at, keep, got))
         return add_low(keep[1], got[1])
+
+    def own_chip_sums(after):
+        while waiting:
+            at, keep, got = waiting.pop()
+            keep, got = tied((keep[0], got[0]), after)
+            own_sums[at] = add_low(keep, got)
 
     moving = []
     for layer in reversed(range(LAYERS)):
@@ -999,6 +1027,7 @@
             grad, n2, i2, n1, i1, y, hid, slope, o, vec, wmid, wdown
         )
         os, gs, ok, gk, do = tied((os, gs, ok, gk, do), moving)
+        own_chip_sums(sums)
         got = [core_swap(os), core_swap(gs)]
         mid = chip_sum(3 * layer + 1, ok, got[0])
         down = chip_sum(3 * layer + 2, gk, got[1])
@@ -1020,22 +1049,24 @@
         place.astype(jnp.int32)[None], series, grad, vec_values, table_rows[0] + table_rows[1]
     )
     far_sums[0] = far_swap(chip_sum(0, pk, got))
-    tab = dp_sum(tab_keep + core_swap(tab_send), dp)
-    own_sums[0] = tied(own_sums[0], tab)
+    own_chip_sums(tab_send)
+    tab = dp_sum(tab_keep + core_swap(tab_send), dp, far_sums[0])
     tab_part = tab[0] + far_swap(tab[1])
     tab_there = far_swap(tab_part)
     parts = [tab_part, core_swap(tab_part), tab_there, core_swap(tab_there)]
+    vec_new_values, vec_new_first, vec_new_second, branch_bias_grads = vector_update(
+        place.astype(jnp.int32)[None], vec_values, vec_first, vec_second, parts
+    )
     at = jnp.concatenate([inner, who]).astype(jnp.int32)
     pieces = routed(at, own_sums, far_sums, dp, own_slots)
     if ringed:
-        terms = ring_reduce([pieces[i] for i in range(dp)], order)
+        meanwhile = (tab, tab_part, parts)
+        terms = ring_reduce([pieces[i] for i in range(dp)], order, meanwhile)
+        terms = tied(terms, vec_new_values)
         grads = [t.reshape(own_slots, BLK, BLK) for t in terms]
     else:
         whole = lax.psum_scatter(pieces, "dp", scatter_dimension=0, tiled=True)
         grads = [whole.reshape(own_slots, BLK, BLK)]
-    vec_new_values, vec_new_first, vec_new_second, branch_bias_grads = vector_update(
-        place.astype(jnp.int32)[None], vec_values, vec_first, vec_second, parts
-    )
     new_master, new_copy, new_first, new_second, new_left, new_right, left_next, right_next = soap(
         grads,
         master[0],

time: 345 us -> 336 us (0.974)
  waiting for transfers between devices: 104 us -> 99.1 us
    ppermute x3, waiting for transfers between devices: 10.8 us -> 5.42 us  [dp_sum(): there = lax.ppermute(low, 'dp', [(i, i ^ bit) for i in range(count)])]
    ppermute x14, waiting for transfers between devices: 42.7 us -> 47.6 us  [far_swap(): return lax.ppermute(value, 'head', [(i, i ^ 2) for i in range(4)])]
    convert_element_type x9 -> x15, other arithmetic: 8.02 us -> 10.2 us  [add_low(): return (a.astype(f32) + b.astype(f32)).astype(bf16)]
    unnamed x130 -> x136, local copies, waits for them, and re-layouts: 12.9 us -> 12.3 us
  transfers between devices with their start and end apart: 62 -> 62, of which waited for: 35 -> 35; matrix products, arithmetic and copies ran while one was open for 7% -> 7% of each run, Pallas kernels for 23% -> 26%
where the time goes in v5:
time: 336 us; the launch traced here: 331 us
  Pallas kernels  145 us (43%)
  waiting for transfers between devices  99.1 us (29%)
  starting transfers between devices  45.1 us (13%)
  local copies, waits for them, and re-layouts  22.7 us (7%)
  other arithmetic  17.2 us (5%)
    ppermute x14, waiting for transfers between devices, far_swap(): return lax.ppermute(value, 'head', [(i, i ^ 2) for i in range(4)])  47.6 us
    pallas_call x1, Pallas kernels, soap(): pl.pallas_call(functools.partial(soap_kernel, len(gs)), grid=(n // group,...  34.4 us
    ppermute x16, waiting for transfers between devices, ring_shift(): lax.ppermute(value, 'dp', [(order[i], order[(i + by) % n]) for i in range...  33.5 us
    pallas_call x2, Pallas kernels, attend_grad(): pl.pallas_call(attend_grad_kernel, grid=(D // LANES,), in_specs=[pair, pa...  32.5 us
    pallas_call x2, Pallas kernels, ffn_grad(): pl.pallas_call(ffn_grad_kernel, out_shape=[shape((2, 16, BLK, BLK), bf16)...  23.1 us
    pallas_call x2, Pallas kernels, attend(): pl.pallas_call(attend_kernel, grid=(D // LANES,), in_specs=[pair, pair, o...  18.6 us
    ppermute x16, starting transfers between devices, ring_shift(): lax.ppermute(value, 'dp', [(order[i], order[(i + by) % n]) for i in range...  17.7 us
    ppermute x14, starting transfers between devices, far_swap(): return lax.ppermute(value, 'head', [(i, i ^ 2) for i in range(4)])  16.3 us
  transfers between devices with their start and end apart: 62, of which 35 were waited for; matrix products, arithmetic and copies ran while one was open for 7% of the time, Pallas kernels for 26%

profile of v5, /device:TPU:0, one launch (start us, length us, event | category | flops | bytes accessed | tf_op | source)
XLA Modules:
  0.0 330.6 jit_solution(5624563754673514795)
XLA Ops:
  1.9 3.0 collective-permute-start.1
  12.0 2.1 collective-permute-done.1.refs_2_
  18.2 6.3 %collective-permute-done.3.refs_4_ = bf16[12,128,128]{2,1,0:T(8,128)(2,1)S(1)} collective-permute-done((bf16[12,128,128]{2,1,0:T(8,128)(2,1)S(1)}, bf16[12,128,128]{2,1,0:T(8,128)(2,1)S(1)}, u32[]{:S(2)}, u32[]{:S(2)}) %collective-permute-start.3) | collective-permute-done | bytes 393248 | tf_op jit(solution)/shard_map/ppermute | solution.py:840
  26.5 2.4 broadcast_multiply_fusion.1.e_ref
  28.9 5.0 %collective-permute-done.5.refs_6_ = bf16[12,128,128]{2,1,0:T(8,128)(2,1)S(1)} collective-permute-done((bf16[12,128,128]{2,1,0:T(8,128)(2,1)S(1)}, bf16[12,128,128]{2,1,0:T(8,128)(2,1)S(1)}, u32[]{:S(2)}, u32[]{:S(2)}) %collective-permute-start.5) | collective-permute-done | bytes 393248 | tf_op jit(solution)/shard_map/ppermute | solution.py:840
  36.6 2.9 collective-permute-done.7.refs_8_
  44.3 6.3 %collective-permute-done.9.w2 = bf16[12,128,128]{2,1,0:T(8,128)(2,1)S(1)} collective-permute-done((bf16[12,128,128]{2,1,0:T(8,128)(2,1)S(1)}, bf16[12,128,128]{2,1,0:T(8,128)(2,1)S(1)}, u32[]{:S(2)}, u32[]{:S(2)}) %collective-permute-start.9) | collective-permute-done | bytes 393248 | tf_op jit(solution)/shard_map/ppermute | solution.py:895
  56.2 9.4 %attend.2 = (bf16[512,512]{1,0:T(8,128)(2,1)S(1)}, f32[512,512]{1,0:T(8,128)S(1)}) custom-call(bf16[512,512]{1,0:T(8,128)(2,1)S(1)} %get-tuple-element.190.q_ref, bf16[512,512]{1,0:T(8,128)(2,1)S(1)} %get-tuple-element.191.k_ref, bf16[512,512]{1,0:T(8,128)(2,1)S(1)} %collective-permute-done.11.kp_ref, bf16[512,512]{1,0:T(8,128)(2,1)S(1)} %get-tuple-element.192.v_ref, ...), custom_call_target="tpu_custom_call" | custom-call | flops 11000000 | tf_op jit(solution)/shard_map/attend/pallas_call | solution.py:375
  68.6 10.3 %collective-permute-done.17.f2 = bf16[16,128,128]{2,1,0:T(8,128)(2,1)S(1)} collective-permute-done((bf16[16,128,128]{2,1,0:T(8,128)(2,1)S(1)}, bf16[16,128,128]{2,1,0:T(8,128)(2,1)S(1)}, u32[]{:S(2)}, u32[]{:S(2)}) %collective-permute-start.17) | collective-permute-done | bytes 524320 | tf_op jit(solution)/shard_map/ppermute | solution.py:895
  81.7 8.1 %post.2 = (f32[512,512]{1,0:T(8,128)}, f32[512,128]{1,0:T(8,128)S(1)}, bf16[512,512]{1,0:T(8,128)(2,1)S(1)}, bf16[512,2048]{1,0:T(8,128)(2,1)}, bf16[512,2048]{1...) custom-call(bf16[512,512]{1,0:T(8,128)(2,1)S(1)} %get-tuple-element.195.o_ref, ...), custom_call_target="tpu_custom_call" | custom-call | flops 11000000 | tf_op jit(solution)/shard_map/post/pallas_call | solution.py:431
  98.3 9.2 %attend.3 = (bf16[512,512]{1,0:T(8,128)(2,1)S(1)}, f32[512,512]{1,0:T(8,128)S(1)}) custom-call(bf16[512,512]{1,0:T(8,128)(2,1)S(1)} %get-tuple-element.211.q_ref, bf16[512,512]{1,0:T(8,128)(2,1)S(1)} %get-tuple-element.212.k_ref, bf16[512,512]{1,0:T(8,128)(2,1)S(1)} %collective-permute-done.22.kp_ref, bf16[512,512]{1,0:T(8,128)(2,1)S(1)} %get-tuple-element.213.v_ref, ...), custom_call_target="tpu_custom_call" | custom-call | flops 11000000 | tf_op jit(solution)/shard_map/attend/pallas_call | solution.py:375
  108.9 10.0 %collective-permute-done.28.f2 = bf16[16,128,128]{2,1,0:T(8,128)(2,1)S(1)} collective-permute-done((bf16[16,128,128]{2,1,0:T(8,128)(2,1)}, bf16[16,128,128]{2,1,0:T(8,128)(2,1)S(1)}, u32[]{:S(2)}, u32[]{:S(2)}) %collective-permute-start.28) | collective-permute-done | bytes 524320 | tf_op jit(solution)/shard_map/ppermute | solution.py:895
  121.7 8.2 %post.3 = (f32[512,512]{1,0:T(8,128)}, f32[512,128]{1,0:T(8,128)S(1)}, bf16[512,512]{1,0:T(8,128)(2,1)S(1)}, bf16[512,2048]{1,0:T(8,128)(2,1)}, bf16[512,2048]{1...) custom-call(bf16[512,512]{1,0:T(8,128)(2,1)S(1)} %get-tuple-element.214.o_ref, ...), custom_call_target="tpu_custom_call" | custom-call | flops 11000000 | tf_op jit(solution)/shard_map/post/pallas_call | solution.py:431
  129.9 11.6 %ffn_grad.2 = (bf16[2,16,128,128]{3,2,1,0:T(8,128)(2,1)}, bf16[2,16,128,128]{3,2,1,0:T(8,128)(2,1)}, bf16[2,20,128,128]{3,2,1,0:T(8,128)(2,1)}, bf16[2,20,128,12...) custom-call(f32[512,512]{1,0:T(8,128)} %broadcast_multiply_fusion.1., ...), custom_call_target="tpu_custom_call" | custom-call | flops 16000000 | tf_op jit(solution)/shard_map/ffn_grad/pallas_call | solution.py:524
  142.0 2.7 collective-permute-done.30
  144.7 2.2 fusion.4
  150.7 16.2 %attend_grad.2 = (bf16[512,512]{1,0:T(8,128)(2,1)S(1)}, bf16[512,512]{1,0:T(8,128)(2,1)S(1)}, bf16[512,512]{1,0:T(8,128)(2,1)S(1)}, bf16[512,512]{1,0:T(8,128)(2,1)S(1)}, bf16[512,512]{1,0:T(8,128)(2,1)S(1)}) custom-call(bf16[512,512]{1,0:T(8,128)(2,1)S(1)} %get-tuple-element.211.q_ref, bf16[512,512]{1,0:T(8,128)(2,1)S(1)} %get-tuple-element.212.k_ref, ...), custom_call_target="tpu_custom_call" | custom-call | flops 23000000 | tf_op jit(solution)/shard_map/attend_grad/pallas_call | solution.py:615
  169.7 4.2 %proj_grad.2 = (bf16[2,12,128,128]{3,2,1,0:T(8,128)(2,1)S(1)}, bf16[2,12,128,128]{3,2,1,0:T(8,128)(2,1)}, f32[512,512]{1,0:T(8,128)}, f32[8,512]{1,0:T(8,128)S(1)}) custom-call(bf16[512,512]{1,0:T(8,128)(2,1)S(1)} %get-tuple-element.245.dq_ref, bf16[512,512]{1,0:T(8,128)(2,1)S(1)} %get-tuple-element.246.dk_ref, ...), custom_call_target="tpu_custom_call" | custom-call | flops 5000000 | tf_op jit(solution)/shard_map/proj_grad/pallas_call | solution.py:674
  178.5 11.6 %ffn_grad.3 = (bf16[2,16,128,128]{3,2,1,0:T(8,128)(2,1)}, bf16[2,16,128,128]{3,2,1,0:T(8,128)(2,1)}, bf16[2,20,128,128]{3,2,1,0:T(8,128)(2,1)}, bf16[2,20,128,12...) custom-call(f32[512,512]{1,0:T(8,128)} %get-tuple-element.257.e_ref,, ...), custom_call_target="tpu_custom_call" | custom-call | flops 16000000 | tf_op jit(solution)/shard_map/ffn_grad/pallas_call | solution.py:524
  190.1 6.8 %collective-permute-done.36.refs_9_ = bf16[12,128,128]{2,1,0:T(8,128)(2,1)S(1)} collective-permute-done((bf16[12,128,128]{2,1,0:T(8,128)(2,1)S(1)}, bf16[12,128,128]{2,1,0:T(8,128)(2,1)S(1)}, u32[]{:S(2)}, u32[]{:S(2)}) %collective-permute-start.36) | collective-permute-done | bytes 393248 | tf_op jit(solution)/shard_map/ppermute | solution.py:895
  203.3 16.2 %attend_grad.3 = (bf16[512,512]{1,0:T(8,128)(2,1)S(1)}, bf16[512,512]{1,0:T(8,128)(2,1)S(1)}, bf16[512,512]{1,0:T(8,128)(2,1)S(1)}, bf16[512,512]{1,0:T(8,128)(2,1)S(1)}, bf16[512,512]{1,0:T(8,128)(2,1)S(1)}) custom-call(bf16[512,512]{1,0:T(8,128)(2,1)S(1)} %get-tuple-element.190.q_ref, bf16[512,512]{1,0:T(8,128)(2,1)S(1)} %get-tuple-element.191.k_ref, ...), custom_call_target="tpu_custom_call" | custom-call | flops 23000000 | tf_op jit(solution)/shard_map/attend_grad/pallas_call | solution.py:615
  222.4 4.1 %proj_grad.3 = (bf16[2,12,128,128]{3,2,1,0:T(8,128)(2,1)S(1)}, bf16[2,12,128,128]{3,2,1,0:T(8,128)(2,1)}, f32[512,512]{1,0:T(8,128)}, f32[8,512]{1,0:T(8,128)S(1)}) custom-call(bf16[512,512]{1,0:T(8,128)(2,1)S(1)} %get-tuple-element.278.dq_ref, bf16[512,512]{1,0:T(8,128)(2,1)S(1)} %get-tuple-element.279.dk_ref, ...), custom_call_target="tpu_custom_call" | custom-call | flops 5000000 | tf_op jit(solution)/shard_map/proj_grad/pallas_call | solution.py:674
  232.4 2.5 collective-permute-done.49
  236.4 2.9 collective-permute-done.50
  240.6 8.1 %collective-permute-done.44.refs_6_ = bf16[12,128,128]{2,1,0:T(8,128)(2,1)S(1)} collective-permute-done((bf16[12,128,128]{2,1,0:T(8,128)(2,1)S(1)}, bf16[12,128,128]{2,1,0:T(8,128)(2,1)S(1)}, u32[]{:S(2)}, u32[]{:S(2)}) %collective-permute-start.44) | collective-permute-done | bytes 393248 | tf_op jit(solution)/shard_map/ppermute | solution.py:895
  248.7 2.7 collective-permute-start.51
  251.5 4.0 %routed.1 = bf16[8,1536,128]{2,1,0:T(8,128)(2,1)} custom-call(s32[192]{0:T(256)S(1)} %pad_add_fusion.at_ref, bf16[12,128,128]{2,1,0:T(8,128)(2,1)S(1)} %add_convert_fusion.10.refs_0_, bf16[20,128,128]{2,1,0:T(8,128)(2,1)S(1)} %add_convert_fusion.1.refs_1_, bf16[16,128,128]{2,1,0:T(8,128)(2,1)S(1)} %add_convert_fusion.5.refs_2_, ...), custom_call_target="tpu_custom_call" | custom-call | flops 4000000 | tf_op jit(solution)/shard_map/routed/pallas_call | solution.py:823
  258.8 3.6 %collective-permute-done.47 = bf16[768,128]{1,0:T(8,128)(2,1)S(1)} collective-permute-done((bf16[768,128]{1,0:T(8,128)(2,1)S(1)}, bf16[768,128]{1,0:T(8,128)(2,1)S(1)}, u32[]{:S(2)}, u32[]{:S(2)}) %collective-permute-start.47) | collective-permute-done | bytes 196640 | tf_op jit(solution)/shard_map/ppermute | solution.py:840
  268.7 3.3 collective-permute-done.54
  272.0 2.7 collective-permute-done.52
  290.3 5.7 %collective-permute-done.60 = bf16[1536,128]{1,0:T(8,128)(2,1)S(1)} collective-permute-done((bf16[1536,128]{1,0:T(8,128)(2,1)S(1)}, bf16[1536,128]{1,0:T(8,128)(2,1)S(1)}, u32[]{:S(2)}, u32[]{:S(2)}) %collective-permute-start.60) | collective-permute-done | bytes 393248 | tf_op jit(solution)/shard_map/ppermute | solution.py:840
  296.1 34.4 %soap.1 = (f32[12,128,128]{2,1,0:T(8,128)}, bf16[12,128,128]{2,1,0:T(8,128)(2,1)}, f32[12,128,128]{2,1,0:T(8,128)}, f32[12,128,128]{2,1,0:T(8,128)}, f32[12,128,...) custom-call(bf16[12,128,128]{2,1,0:T(8,128)(2,1)S(1)} %bitcast.158, ...), custom_call_target="tpu_custom_call" | custom-call | flops 40000000 | tf_op jit(solution)/shard_map/soap/pallas_call | solution.py:208
  (316 shorter events, 100.3 us)
Async XLA Ops:
  1.9 12.2 %collective-permute-start.1 = (bf16[12,128,128]{2,1,0:T(8,128)(2,1)S(1)}, bf16[12,128,128]{2,1,0:T(8,128)(2,1)S(1)}, u32[]{:S(2)}, u32[]{:S(2)}) collective-permute-start(bf16[12,128,128]{2,1,0:T(8,128)(2,1)S(1)} %bitcast_convert_fusion.refs_0_), channel_id=1, source_target_pairs={{0,4},{8,0},{16,8},{24,16},{28,24},{20,28},{12,20},{4,12},{1,5},{9... | collective-permute-start | bytes 1179656 | tf_op jit(solution)/shard_map/ppermute | solution.py:840
  4.9 10.9 %collective-permute-start = (bf16[12,128,128]{2,1,0:T(8,128)(2,1)S(1)}, bf16[12,128,128]{2,1,0:T(8,128)(2,1)S(1)}, u32[]{:S(2)}, u32[]{:S(2)}) collective-permute-start(bf16[12,128,128]{2,1,0:T(8,128)(2,1)S(1)} %bitcast_convert_fusion.refs_0_), channel_id=1, source_target_pairs={{0,8},{8,16},{16,24},{24,28},{28,20},{20,12},{12,4},{4,0},{1,9},{9... | collective-permute-start | bytes 1179656 | tf_op jit(solution)/shard_map/ppermute | solution.py:840
  14.1 10.3 %collective-permute-start.3 = (bf16[12,128,128]{2,1,0:T(8,128)(2,1)S(1)}, bf16[12,128,128]{2,1,0:T(8,128)(2,1)S(1)}, u32[]{:S(2)}, u32[]{:S(2)}) collective-permute-start(bf16[12,128,128]{2,1,0:T(8,128)(2,1)S(1)} %collective-permute-done.1.refs_2_), channel_id=1, source_target_pairs={{0,4},{8,0},{16,8},{24,16},{28,24},{20,28},{12,20},{4,12},{1,5},{9... | collective-permute-start | bytes 1179656 | tf_op jit(solution)/shard_map/ppermute | solution.py:840
  15.8 10.0 %collective-permute-start.2 = (bf16[12,128,128]{2,1,0:T(8,128)(2,1)S(1)}, bf16[12,128,128]{2,1,0:T(8,128)(2,1)S(1)}, u32[]{:S(2)}, u32[]{:S(2)}) collective-permute-start(bf16[12,128,128]{2,1,0:T(8,128)(2,1)S(1)} %collective-permute-done.refs_1_), channel_id=1, source_target_pairs={{0,8},{8,16},{16,24},{24,28},{28,20},{20,12},{12,4},{4,0},{1,9},{9... | collective-permute-start | bytes 1179656 | tf_op jit(solution)/shard_map/ppermute | solution.py:840
  24.4 9.4 %collective-permute-start.5 = (bf16[12,128,128]{2,1,0:T(8,128)(2,1)S(1)}, bf16[12,128,128]{2,1,0:T(8,128)(2,1)S(1)}, u32[]{:S(2)}, u32[]{:S(2)}) collective-permute-start(bf16[12,128,128]{2,1,0:T(8,128)(2,1)S(1)} %collective-permute-done.3.refs_4_), channel_id=1, source_target_pairs={{0,4},{8,0},{16,8},{24,16},{28,24},{20,28},{12,20},{4,12},{1,5},{9... | collective-permute-start | bytes 1179656 | tf_op jit(solution)/shard_map/ppermute | solution.py:840
  25.8 9.3 %collective-permute-start.4 = (bf16[12,128,128]{2,1,0:T(8,128)(2,1)S(1)}, bf16[12,128,128]{2,1,0:T(8,128)(2,1)S(1)}, u32[]{:S(2)}, u32[]{:S(2)}) collective-permute-start(bf16[12,128,128]{2,1,0:T(8,128)(2,1)S(1)} %collective-permute-done.2.refs_3_), channel_id=1, source_target_pairs={{0,8},{8,16},{16,24},{24,28},{28,20},{20,12},{12,4},{4,0},{1,9},{9... | collective-permute-start | bytes 1179656 | tf_op jit(solution)/shard_map/ppermute | solution.py:840
  42.7 7.8 %collective-permute-start.9 = (bf16[12,128,128]{2,1,0:T(8,128)(2,1)S(1)}, bf16[12,128,128]{2,1,0:T(8,128)(2,1)S(1)}, u32[]{:S(2)}, u32[]{:S(2)}) collective-permute-start(bf16[12,128,128]{2,1,0:T(8,128)(2,1)S(1)} %get-tuple-element.186.w0), channel_id=1, source_target_pairs={{0,2},{1,3},{2,0},{3,1},{4,6},{5,7},{6,4},{7,5},{8,10},{9,11},{10,... | collective-permute-start | bytes 1179656 | tf_op jit(solution)/shard_map/ppermute | solution.py:895
  50.5 17.5 %collective-permute-start.14 = (bf16[20,128,128]{2,1,0:T(8,128)(2,1)S(1)}, bf16[20,128,128]{2,1,0:T(8,128)(2,1)S(1)}, u32[]{:S(2)}, u32[]{:S(2)}) collective-permute-start(bf16[20,128,128]{2,1,0:T(8,128)(2,1)S(1)} %get-tuple-element.199.a0), channel_id=1, source_target_pairs={{0,2},{1,3},{2,0},{3,1},{4,6},{5,7},{6,4},{7,5},{8,10},{9,11},{10,... | collective-permute-start | bytes 1966088 | tf_op jit(solution)/shard_map/ppermute | solution.py:895
  54.0 24.9 %collective-permute-start.17 = (bf16[16,128,128]{2,1,0:T(8,128)(2,1)S(1)}, bf16[16,128,128]{2,1,0:T(8,128)(2,1)S(1)}, u32[]{:S(2)}, u32[]{:S(2)}) collective-permute-start(bf16[16,128,128]{2,1,0:T(8,128)(2,1)S(1)} %get-tuple-element.202.f0), channel_id=1, source_target_pairs={{0,2},{1,3},{2,0},{3,1},{4,6},{5,7},{6,4},{7,5},{8,10},{9,11},{10,... | collective-permute-start | bytes 1572872 | tf_op jit(solution)/shard_map/ppermute | solution.py:895
  55.6 25.1 %collective-permute-start.13 = (bf16[20,128,128]{2,1,0:T(8,128)(2,1)S(1)}, bf16[20,128,128]{2,1,0:T(8,128)(2,1)S(1)}, u32[]{:S(2)}, u32[]{:S(2)}) collective-permute-start(bf16[20,128,128]{2,1,0:T(8,128)(2,1)S(1)} %get-tuple-element.199.a0), channel_id=1, source_target_pairs={{0,1},{1,0},{2,3},{3,2},{4,5},{5,4},{6,7},{7,6},{8,9},{9,8},{10,11... | collective-permute-start | bytes 1966088 | tf_op jit(solution)/shard_map/ppermute | solution.py:891
  68.1 12.8 %collective-permute-start.15 = (bf16[20,128,128]{2,1,0:T(8,128)(2,1)S(1)}, bf16[20,128,128]{2,1,0:T(8,128)(2,1)S(1)}, u32[]{:S(2)}, u32[]{:S(2)}) collective-permute-start(bf16[20,128,128]{2,1,0:T(8,128)(2,1)S(1)} %collective-permute-done.14.a2), channel_id=1, source_target_pairs={{0,1},{1,0},{2,3},{3,2},{4,5},{5,4},{6,7},{7,6},{8,9},{9,8},{10,11... | collective-permute-start | bytes 1966088 | tf_op jit(solution)/shard_map/ppermute | solution.py:891
  68.1 12.4 %collective-permute-start.16 = (bf16[16,128,128]{2,1,0:T(8,128)(2,1)S(1)}, bf16[16,128,128]{2,1,0:T(8,128)(2,1)S(1)}, u32[]{:S(2)}, u32[]{:S(2)}) collective-permute-start(bf16[16,128,128]{2,1,0:T(8,128)(2,1)S(1)} %get-tuple-element.202.f0), channel_id=1, source_target_pairs={{0,1},{1,0},{2,3},{3,2},{4,5},{5,4},{6,7},{7,6},{8,9},{9,8},{10,11... | collective-permute-start | bytes 1572872 | tf_op jit(solution)/shard_map/ppermute | solution.py:891
  78.9 11.6 %collective-permute-start.20 = (bf16[12,128,128]{2,1,0:T(8,128)(2,1)S(1)}, bf16[12,128,128]{2,1,0:T(8,128)(2,1)S(1)}, u32[]{:S(2)}, u32[]{:S(2)}) collective-permute-start(bf16[12,128,128]{2,1,0:T(8,128)(2,1)S(1)} %get-tuple-element.206.w0), channel_id=1, source_target_pairs={{0,2},{1,3},{2,0},{3,1},{4,6},{5,7},{6,4},{7,5},{8,10},{9,11},{10,... | collective-permute-start | bytes 1179656 | tf_op jit(solution)/shard_map/ppermute | solution.py:895
  80.5 11.7 %collective-permute-start.19 = (bf16[12,128,128]{2,1,0:T(8,128)(2,1)S(1)}, bf16[12,128,128]{2,1,0:T(8,128)(2,1)S(1)}, u32[]{:S(2)}, u32[]{:S(2)}) collective-permute-start(bf16[12,128,128]{2,1,0:T(8,128)(2,1)S(1)} %get-tuple-element.206.w0), channel_id=1, source_target_pairs={{0,1},{1,0},{2,3},{3,2},{4,5},{5,4},{6,7},{7,6},{8,9},{9,8},{10,11... | collective-permute-start | bytes 1179656 | tf_op jit(solution)/shard_map/ppermute | solution.py:891
  90.8 17.6 %collective-permute-start.25 = (bf16[20,128,128]{2,1,0:T(8,128)(2,1)S(1)}, bf16[20,128,128]{2,1,0:T(8,128)(2,1)S(1)}, u32[]{:S(2)}, u32[]{:S(2)}) collective-permute-start(bf16[20,128,128]{2,1,0:T(8,128)(2,1)S(1)} %copy-done.5), channel_id=1, source_target_pairs={{0,2},{1,3},{2,0},{3,1},{4,6},{5,7},{6,4},{7,5},{8,10},{9,11},{10,... | collective-permute-start | bytes 1966088 | tf_op jit(solution)/shard_map/ppermute | solution.py:895
  96.1 22.8 %collective-permute-start.28 = (bf16[16,128,128]{2,1,0:T(8,128)(2,1)}, bf16[16,128,128]{2,1,0:T(8,128)(2,1)S(1)}, u32[]{:S(2)}, u32[]{:S(2)}) collective-permute-start(bf16[16,128,128]{2,1,0:T(8,128)(2,1)} %get-tuple-element.221.f0), channel_id=1, source_target_pairs={{0,2},{1,3},{2,0},{3,1},{4,6},{5,7},{6,4},{7,5},{8,10},{9,11},{10,... | collective-permute-start | bytes 1572872 | tf_op jit(solution)/shard_map/ppermute | solution.py:895
  97.5 21.4 %collective-permute-start.24 = (bf16[20,128,128]{2,1,0:T(8,128)(2,1)S(1)}, bf16[20,128,128]{2,1,0:T(8,128)(2,1)S(1)}, u32[]{:S(2)}, u32[]{:S(2)}) collective-permute-start(bf16[20,128,128]{2,1,0:T(8,128)(2,1)S(1)} %copy-done.5), channel_id=1, source_target_pairs={{0,1},{1,0},{2,3},{3,2},{4,5},{5,4},{6,7},{7,6},{8,9},{9,8},{10,11... | collective-permute-start | bytes 1966088 | tf_op jit(solution)/shard_map/ppermute | solution.py:891
  108.4 12.4 %collective-permute-start.26 = (bf16[20,128,128]{2,1,0:T(8,128)(2,1)S(1)}, bf16[20,128,128]{2,1,0:T(8,128)(2,1)S(1)}, u32[]{:S(2)}, u32[]{:S(2)}) collective-permute-start(bf16[20,128,128]{2,1,0:T(8,128)(2,1)S(1)} %collective-permute-done.25.a2), channel_id=1, source_target_pairs={{0,1},{1,0},{2,3},{3,2},{4,5},{5,4},{6,7},{7,6},{8,9},{9,8},{10,11... | collective-permute-start | bytes 1966088 | tf_op jit(solution)/shard_map/ppermute | solution.py:891
  108.6 10.4 %collective-permute-start.27 = (bf16[16,128,128]{2,1,0:T(8,128)(2,1)}, bf16[16,128,128]{2,1,0:T(8,128)(2,1)S(1)}, u32[]{:S(2)}, u32[]{:S(2)}) collective-permute-start(bf16[16,128,128]{2,1,0:T(8,128)(2,1)} %get-tuple-element.221.f0), channel_id=1, source_target_pairs={{0,1},{1,0},{2,3},{3,2},{4,5},{5,4},{6,7},{7,6},{8,9},{9,8},{10,11... | collective-permute-start | bytes 1572872 | tf_op jit(solution)/shard_map/ppermute | solution.py:891
  146.9 20.0 %collective-permute-start.32 = (bf16[20,128,128]{2,1,0:T(8,128)(2,1)}, bf16[20,128,128]{2,1,0:T(8,128)(2,1)S(1)}, u32[]{:S(2)}, u32[]{:S(2)}) collective-permute-start(bf16[20,128,128]{2,1,0:T(8,128)(2,1)} %fusion.4), channel_id=1, source_target_pairs={{0,2},{1,3},{2,0},{3,1},{4,6},{5,7},{6,4},{7,5},{8,10},{9,11},{10,... | collective-permute-start | bytes 1966088 | tf_op jit(solution)/shard_map/ppermute | solution.py:895
  174.1 16.1 %collective-permute-start.37 = (bf16[16,128,128]{2,1,0:T(8,128)(2,1)}, bf16[16,128,128]{2,1,0:T(8,128)(2,1)S(1)}, u32[]{:S(2)}, u32[]{:S(2)}) collective-permute-start(bf16[16,128,128]{2,1,0:T(8,128)(2,1)} %fusion.6), channel_id=1, source_target_pairs={{0,2},{1,3},{2,0},{3,1},{4,6},{5,7},{6,4},{7,5},{8,10},{9,11},{10,... | collective-permute-start | bytes 1572872 | tf_op jit(solution)/shard_map/ppermute | solution.py:895
  176.5 20.4 %collective-permute-start.36 = (bf16[12,128,128]{2,1,0:T(8,128)(2,1)S(1)}, bf16[12,128,128]{2,1,0:T(8,128)(2,1)S(1)}, u32[]{:S(2)}, u32[]{:S(2)}) collective-permute-start(bf16[12,128,128]{2,1,0:T(8,128)(2,1)S(1)} %fusion.8), channel_id=1, source_target_pairs={{0,2},{1,3},{2,0},{3,1},{4,6},{5,7},{6,4},{7,5},{8,10},{9,11},{10,... | collective-permute-start | bytes 1179656 | tf_op jit(solution)/shard_map/ppermute | solution.py:895
  201.2 18.4 %collective-permute-start.40 = (bf16[20,128,128]{2,1,0:T(8,128)(2,1)}, bf16[20,128,128]{2,1,0:T(8,128)(2,1)S(1)}, u32[]{:S(2)}, u32[]{:S(2)}) collective-permute-start(bf16[20,128,128]{2,1,0:T(8,128)(2,1)} %fusion.5), channel_id=1, source_target_pairs={{0,2},{1,3},{2,0},{3,1},{4,6},{5,7},{6,4},{7,5},{8,10},{9,11},{10,... | collective-permute-start | bytes 1966088 | tf_op jit(solution)/shard_map/ppermute | solution.py:895
  220.4 31.1 %collective-permute-start.45 = (bf16[16,128,128]{2,1,0:T(8,128)(2,1)}, bf16[16,128,128]{2,1,0:T(8,128)(2,1)S(1)}, u32[]{:S(2)}, u32[]{:S(2)}) collective-permute-start(bf16[16,128,128]{2,1,0:T(8,128)(2,1)} %fusion.7), channel_id=1, source_target_pairs={{0,2},{1,3},{2,0},{3,1},{4,6},{5,7},{6,4},{7,5},{8,10},{9,11},{10,... | collective-permute-start | bytes 1572872 | tf_op jit(solution)/shard_map/ppermute | solution.py:895
  230.3 9.0 %collective-permute-start.43 = (bf16[2,12,128,128]{3,2,1,0:T(8,128)(2,1)S(1)}, bf16[2,12,128,128]{3,2,1,0:T(8,128)(2,1)S(1)}, u32[]{:S(2)}, u32[]{:S(2)}) collective-permute-start(bf16[2,12,128,128]{3,2,1,0:T(8,128)(2,1)S(1)} %copy-done.64), channel_id=1, source_target_pairs={{0,1},{1,0},{2,3},{3,2},{4,5},{5,4},{6,7},{7,6},{8,9},{9,8},{10,11... | collective-permute-start | bytes 2359304 | tf_op jit(solution)/shard_map/ppermute | solution.py:891
  239.4 9.3 %collective-permute-start.44 = (bf16[12,128,128]{2,1,0:T(8,128)(2,1)S(1)}, bf16[12,128,128]{2,1,0:T(8,128)(2,1)S(1)}, u32[]{:S(2)}, u32[]{:S(2)}) collective-permute-start(bf16[12,128,128]{2,1,0:T(8,128)(2,1)S(1)} %fusion.9), channel_id=1, source_target_pairs={{0,2},{1,3},{2,0},{3,1},{4,6},{5,7},{6,4},{7,5},{8,10},{9,11},{10,... | collective-permute-start | bytes 1179656 | tf_op jit(solution)/shard_map/ppermute | solution.py:895
  248.7 10.1 %collective-permute-start.51 = (bf16[2,128,128]{2,1,0:T(8,128)(2,1)S(1)}, bf16[2,128,128]{2,1,0:T(8,128)(2,1)S(1)}, u32[]{:S(2)}, u32[]{:S(2)}) collective-permute-start(bf16[2,128,128]{2,1,0:T(8,128)(2,1)S(1)} %convert_add_fusion.7), channel_id=1, source_target_pairs={{0,16},{4,20},{8,24},{12,28},{16,0},{20,4},{24,8},{28,12},{1,17},{... | collective-permute-start | bytes 196616 | tf_op jit(solution)/shard_map/ppermute | solution.py:880
  265.6 9.1 %collective-permute-start.52 = (bf16[1536,128]{1,0:T(8,128)(2,1)S(1)}, bf16[1536,128]{1,0:T(8,128)(2,1)S(1)}, u32[]{:S(2)}, u32[]{:S(2)}) collective-permute-start(bf16[1536,128]{1,0:T(8,128)(2,1)S(1)} %pad_maximum_fusion), channel_id=1, source_target_pairs={{0,8},{8,16},{16,24},{24,28},{28,20},{20,12},{12,4},{4,0},{1,9},{9... | collective-permute-start | bytes 1179656 | tf_op jit(solution)/shard_map/ppermute | solution.py:840
  265.9 9.1 %collective-permute-start.53 = (bf16[1536,128]{1,0:T(8,128)(2,1)S(1)}, bf16[1536,128]{1,0:T(8,128)(2,1)S(1)}, u32[]{:S(2)}, u32[]{:S(2)}) collective-permute-start(bf16[1536,128]{1,0:T(8,128)(2,1)S(1)} %pad_maximum_fusion.1), channel_id=1, source_target_pairs={{0,4},{8,0},{16,8},{24,16},{28,24},{20,28},{12,20},{4,12},{1,5},{9... | collective-permute-start | bytes 1179656 | tf_op jit(solution)/shard_map/ppermute | solution.py:840
  276.3 7.8 %collective-permute-start.55 = (bf16[1536,128]{1,0:T(8,128)(2,1)S(1)}, bf16[1536,128]{1,0:T(8,128)(2,1)S(1)}, u32[]{:S(2)}, u32[]{:S(2)}) collective-permute-start(bf16[1536,128]{1,0:T(8,128)(2,1)S(1)} %get-tuple-element.315), channel_id=1, source_target_pairs={{0,8},{8,16},{16,24},{24,28},{28,20},{20,12},{12,4},{4,0},{1,9},{9... | collective-permute-start | bytes 1179656 | tf_op jit(solution)/shard_map/ppermute | solution.py:840
  286.1 10.0 %collective-permute-start.60 = (bf16[1536,128]{1,0:T(8,128)(2,1)S(1)}, bf16[1536,128]{1,0:T(8,128)(2,1)S(1)}, u32[]{:S(2)}, u32[]{:S(2)}) collective-permute-start(bf16[1536,128]{1,0:T(8,128)(2,1)S(1)} %get-tuple-element.317), channel_id=1, source_target_pairs={{0,8},{8,16},{16,24},{24,28},{28,20},{20,12},{12,4},{4,0},{1,9},{9... | collective-permute-start | bytes 1179656 | tf_op jit(solution)/shard_map/ppermute | solution.py:840
  286.2 9.8 %collective-permute-start.61 = (bf16[1536,128]{1,0:T(8,128)(2,1)S(1)}, bf16[1536,128]{1,0:T(8,128)(2,1)S(1)}, u32[]{:S(2)}, u32[]{:S(2)}) collective-permute-start(bf16[1536,128]{1,0:T(8,128)(2,1)S(1)} %get-tuple-element.318), channel_id=1, source_target_pairs={{0,4},{8,0},{16,8},{24,16},{28,24},{20,28},{12,20},{4,12},{1,5},{9... | collective-permute-start | bytes 1179656 | tf_op jit(solution)/shard_map/ppermute | solution.py:840
  (96 other events, 755.9 us)

commit v6 on v5

--- a/solution.py
+++ b/solution.py
@@ -212,7 +212,7 @@
         out_specs=[one] * 6 + [whole] * 2,
         out_shape=[sh, shb, sh, sh, sh, sh, sh, sh],
         scratch_shapes=[pltpu.VMEM((2 * n, BLK, BLK), f32)] * 2,
-        compiler_params=pltpu.CompilerParams(vmem_limit_bytes=50 * 2**20),
+        compiler_params=pltpu.CompilerParams(vmem_limit_bytes=16 * 2**20),
         cost_estimate=pl.CostEstimate(flops=40 * 10**6, bytes_accessed=0, transcendentals=0),
         name="soap",
     )(*gs, master, m1, m2, ls, rs, lb, rb)
@@ -230,6 +230,11 @@
 
 def params(mib=48):
     return pltpu.CompilerParams(vmem_limit_bytes=mib * 2**20)
+
+
+MIB = dict(
+    embed=6, project=8, attend=16, post=20, ffn_grad=24, attend_grad=16, proj_grad=12, embed_grad=8, vector=4, natural=6, routed=8,
+)
 
 
 def cost(micros):
@@ -257,7 +262,7 @@
     for r, ref in enumerate(refs):
         for j in range(12):
             row, col = divmod(j, 3)
-            c0 = col * D + r * BLK
+            c0 = D + (2 * r + col - 1) * BLK if col else r * BLK
             dst[row * BLK : (row + 1) * BLK, c0 : c0 + BLK] = ref[j]
 
 
@@ -287,32 +292,34 @@
 def embed(series, table):
     rows = series.shape[0]
     return pl.pallas_call(
-        embed_kernel, out_shape=shape((rows, D)), compiler_params=params(), name="embed"
+        embed_kernel, out_shape=shape((rows, D)), compiler_params=params(MIB["embed"]), name="embed"
     )(series, table[:LOOK], table[LOOK : LOOK + 1])
 
 
-def proj_kernel(x_ref, bq_ref, bv_ref, w0, w1, w2, w3, xs_ref, q_ref, k_ref, v_ref, w_s):
+def proj_kernel(x_ref, bq_ref, bv_ref, w0, w1, w2, w3, xs_ref, q_ref, kv_ref, w_s):
     place_qkv(w_s, (w0, w1, w2, w3))
-
-    def tile(t, c):
-        at = pl.ds(t * ROW_TILE, ROW_TILE)
-        xs = x_ref[at].astype(bf16)
-        xs_ref[at] = xs
-        q_ref[at] = (dot(xs, w_s[:, :D]) + bq_ref[...]).astype(bf16)
-        k_ref[at] = dot(xs, w_s[:, D : 2 * D]).astype(bf16)
-        v_ref[at] = (dot(xs, w_s[:, 2 * D :]) + bv_ref[...]).astype(bf16)
-        return c
-
-    lax.fori_loop(0, x_ref.shape[0] // ROW_TILE, tile, 0)
+    xs = x_ref[...].astype(bf16)
+    xs_ref[...] = xs
+    q_ref[...] = (dot(xs, w_s[:, :D]) + bq_ref[...]).astype(bf16)
+    kv = dot(xs, w_s[:, D:])
+    for r in range(4):
+        at = 2 * r * BLK
+        kv_ref[:, at : at + BLK] = kv[:, at : at + BLK].astype(bf16)
+        value = kv[:, at + BLK : at + 2 * BLK] + bv_ref[:, r * BLK : (r + 1) * BLK]
+        kv_ref[:, at + BLK : at + 2 * BLK] = value.astype(bf16)
 
 
 def project(x, bq, bv, wqkv):
     rows = x.shape[0]
     return pl.pallas_call(
         proj_kernel,
-        out_shape=[shape((rows, D), bf16)] * 4,
+        out_shape=[
+            shape((rows, D), bf16),
+            shape((rows, D), bf16),
+            shape((rows, 2 * D), bf16),
+        ],
         scratch_shapes=[pltpu.VMEM((D, 3 * D), bf16)],
-        compiler_params=params(),
+        compiler_params=params(MIB["project"]),
         name="project",
         cost_estimate=cost(3),
     )(x, bq, bv, *wqkv)
@@ -336,16 +343,16 @@
     return base.astype(bf16)
 
 
-def attend_kernel(q_ref, k_ref, kp_ref, v_ref, vp_ref, ohq_ref, ohk_ref, o_ref, lse_ref, ka, va):
+def attend_kernel(q_ref, kv_ref, kvp_ref, ohq_ref, ohk_ref, o_ref, lse_ref, ka, va):
     rows = q_ref.shape[0]
-    ka[:rows, :LANES] = k_ref[...]
-    ka[rows:, :LANES] = kp_ref[...]
+    ka[:rows, :LANES] = kv_ref[:, :LANES]
+    ka[rows:, :LANES] = kvp_ref[:, :LANES]
     ka[:, LANES:] = ohk_ref[...]
     lane = lax.broadcasted_iota(jnp.int32, (ROW_TILE, LANES), 1)
     for i in range(2):
         m = half_mask(i)
-        va[i, :rows, :LANES] = v_ref[...] * m
-        va[i, rows:, :LANES] = vp_ref[...] * m
+        va[i, :rows, :LANES] = kv_ref[:, LANES:] * m
+        va[i, rows:, :LANES] = kvp_ref[:, LANES:] * m
         va[i, :, LANES:] = jnp.ones((2 * rows, LANES), bf16)
 
     def tile(t, c):
@@ -368,14 +375,15 @@
     lax.fori_loop(0, rows // ROW_TILE, tile, 0)
 
 
-def attend(q, k, kp, v, vp, ohq, ohk):
+def attend(q, kv, kvp, ohq, ohk):
     rows = q.shape[0]
     pair = pl.BlockSpec((rows, LANES), lambda h: (0, h))
-    other = pl.BlockSpec((rows, LANES), lambda h: (0, h + 1 - 2 * lax.rem(h, 2)))
+    both = pl.BlockSpec((rows, 2 * LANES), lambda h: (0, h))
+    other = pl.BlockSpec((rows, 2 * LANES), lambda h: (0, h + 1 - 2 * lax.rem(h, 2)))
     return pl.pallas_call(
         attend_kernel,
         grid=(D // LANES,),
-        in_specs=[pair, pair, other, pair, other]
+        in_specs=[pair, both, other]
         + [
             pl.BlockSpec((rows, LANES), lambda h: (0, 0)),
             pl.BlockSpec((2 * rows, LANES), lambda h: (0, 0)),
@@ -386,20 +394,20 @@
             pltpu.VMEM((2 * rows, 2 * LANES), bf16),
             pltpu.VMEM((2, 2 * rows, 2 * LANES), bf16),
         ],
-        compiler_params=params(),
+        compiler_params=params(MIB["attend"]),
         name="attend",
         cost_estimate=cost(11),
-    )(q, k, kp, v, vp, ohq, ohk)
+    )(q, kv, kvp, ohq, ohk)
 
 
 def post_kernel(
-    o_ref, x_ref, vec_ref, b1_ref, a0, a1, a2, a3, f0, f1, f2, f3,
+    o_ref, x_ref, vec_ref, b1_ref, a0, a1, a2, a3,
     n1_ref, i1_ref, y_ref, hid_ref, slope_ref, n2_ref, i2_ref, x2_ref,
     wo_s, w1_s, w2_s,
 ):
     place_blocks(wo_s, (a0, a1, a2, a3), 0, 1, 4, BLK, 0)
     place_blocks(w1_s, (a0, a1, a2, a3), 4, 4, 4, 0, D)
-    place_blocks(w2_s, (f0, f1, f2, f3), 0, 4, 4, D, 0)
+    place_blocks(w2_s, (a0, a1, a2, a3), 20, 4, 4, D, 0)
 
     def tile(t, c):
         at = pl.ds(t * ROW_TILE, ROW_TILE)
@@ -426,7 +434,7 @@
     lax.fori_loop(0, x_ref.shape[0] // ROW_TILE, tile, 0)
 
 
-def post(o, x, vec, b1, wmid, wdown):
+def post(o, x, vec, b1, wfeed):
     rows = x.shape[0]
     return pl.pallas_call(
         post_kernel,
@@ -445,10 +453,10 @@
             pltpu.VMEM((D, FF), bf16),
             pltpu.VMEM((FF, D), bf16),
         ],
-        compiler_params=params(),
+        compiler_params=params(MIB["post"]),
         name="post",
         cost_estimate=cost(11),
-    )(o, x, vec, b1, *wmid, *wdown)
+    )(o, x, vec, b1, *wfeed)
 
 
 def store_blocks(refs, r, first, rows, cols, value):
@@ -461,14 +469,14 @@
 
 def ffn_grad_kernel(
     e_ref, n2_ref, i2_ref, n1_ref, i1_ref, y_ref, hid_ref, slope_ref, o_ref, vec_ref,
-    a0, a1, a2, a3, f0, f1, f2, f3,
+    a0, a1, a2, a3,
     gk_ref, gs_ref, ok_ref, os_ref, dr1_ref, do_ref, db1_ref, sums_ref,
     wo_s, w1_s, w2_s, dr2_s, dfr_s, dpre_s, dar_s,
 ):
     rows = e_ref.shape[0]
     place_blocks(wo_s, (a0, a1, a2, a3), 0, 1, 4, BLK, 0)
     place_blocks(w1_s, (a0, a1, a2, a3), 4, 4, 4, 0, D)
-    place_blocks(w2_s, (f0, f1, f2, f3), 0, 4, 4, D, 0)
+    place_blocks(w2_s, (a0, a1, a2, a3), 20, 4, 4, D, 0)
     tiles = rows // ROW_TILE
     gain_two = vec_ref[4:5, :]
     gain_one = vec_ref[1:2, :]
@@ -519,7 +527,7 @@
         sums_ref[i : i + 1, :] = value
 
 
-def ffn_grad(e, n2, i2, n1, i1, y, hid, slope, o, vec, wmid, wdown):
+def ffn_grad(e, n2, i2, n1, i1, y, hid, slope, o, vec, wfeed):
     rows = e.shape[0]
     return pl.pallas_call(
         ffn_grad_kernel,
@@ -542,23 +550,23 @@
             pltpu.VMEM((rows, FF), bf16),
             pltpu.VMEM((rows, D), bf16),
         ],
-        compiler_params=params(),
+        compiler_params=params(MIB["ffn_grad"]),
         name="ffn_grad",
         cost_estimate=cost(16),
-    )(e, n2, i2, n1, i1, y, hid, slope, o, vec, *wmid, *wdown)
+    )(e, n2, i2, n1, i1, y, hid, slope, o, vec, *wfeed)
 
 
 def attend_grad_kernel(
-    q_ref, k_ref, kp_ref, v_ref, vp_ref, do_ref, o_ref, lse_ref, ohq_ref, ohk_ref,
-    dq_ref, dk_ref, dkp_ref, dv_ref, dvp_ref,
+    q_ref, kv_ref, kvp_ref, do_ref, o_ref, lse_ref, ohq_ref, ohk_ref,
+    dq_ref, dkv_ref, dkvp_ref,
     ka, va, qa, da, kt,
 ):
     rows = q_ref.shape[0]
-    ka[:rows, :LANES] = k_ref[...]
-    ka[rows:, :LANES] = kp_ref[...]
+    ka[:rows, :LANES] = kv_ref[:, :LANES]
+    ka[rows:, :LANES] = kvp_ref[:, :LANES]
     ka[:, LANES:] = ohk_ref[...]
-    va[:rows, :LANES] = v_ref[...]
-    va[rows:, :LANES] = vp_ref[...]
+    va[:rows, :LANES] = kv_ref[:, LANES:]
+    va[rows:, :LANES] = kvp_ref[:, LANES:]
     va[:, LANES:] = jnp.ones((2 * rows, LANES), bf16)
     kt[...] = ka[:, :LANES].T
     product = do_ref[...].astype(f32) * o_ref[...].astype(f32)
@@ -591,15 +599,15 @@
     def own(t, sums):
         sums, dk, dv = tile(t, sums)
         at = pl.ds(t * ROW_TILE, ROW_TILE)
-        dk_ref[at] = dk
-        dv_ref[at] = dv
+        dkv_ref[at, :LANES] = dk
+        dkv_ref[at, LANES:] = dv
         return sums
 
     def other(t, sums):
         sums, dk, dv = tile(t + half, sums)
         at = pl.ds(t * ROW_TILE, ROW_TILE)
-        dkp_ref[at] = dk
-        dvp_ref[at] = dv
+        dkvp_ref[at, :LANES] = dk
+        dkvp_ref[at, LANES:] = dv
         return sums
 
     sums = lax.fori_loop(0, half, own, sums)
@@ -608,20 +616,21 @@
     dq_ref[...] = (jnp.where(row < HD, sums[0], sums[1]) * 0.125).T.astype(bf16)
 
 
-def attend_grad(q, k, kp, v, vp, do, o, lse, ohq, ohk):
+def attend_grad(q, kv, kvp, do, o, lse, ohq, ohk):
     rows = q.shape[0]
     pair = pl.BlockSpec((rows, LANES), lambda h: (0, h))
-    other = pl.BlockSpec((rows, LANES), lambda h: (0, h + 1 - 2 * lax.rem(h, 2)))
+    both = pl.BlockSpec((rows, 2 * LANES), lambda h: (0, h))
+    other = pl.BlockSpec((rows, 2 * LANES), lambda h: (0, h + 1 - 2 * lax.rem(h, 2)))
     return pl.pallas_call(
         attend_grad_kernel,
         grid=(D // LANES,),
-        in_specs=[pair, pair, other, pair, other, pair, pair, pair]
+        in_specs=[pair, both, other, pair, pair, pair]
         + [
             pl.BlockSpec((rows, LANES), lambda h: (0, 0)),
             pl.BlockSpec((2 * rows, LANES), lambda h: (0, 0)),
         ],
-        out_specs=[pair, pair, other, pair, other],
-        out_shape=[shape((rows, D), bf16)] * 5,
+        out_specs=[pair, both, other],
+        out_shape=[shape((rows, D), bf16)] + [shape((rows, 2 * D), bf16)] * 2,
         scratch_shapes=[
             pltpu.VMEM((2 * rows, 2 * LANES), bf16),
             pltpu.VMEM((2 * rows, 2 * LANES), bf16),
@@ -629,47 +638,36 @@
             pltpu.VMEM((2, rows, 2 * LANES), bf16),
             pltpu.VMEM((LANES, 2 * rows), bf16),
         ],
-        compiler_params=params(),
+        compiler_params=params(MIB["attend_grad"]),
         name="attend_grad",
         cost_estimate=cost(23),
-    )(q, k, kp, v, vp, do, o, lse, ohq, ohk)
+    )(q, kv, kvp, do, o, lse, ohq, ohk)
 
 
 def proj_grad_kernel(
-    dq_ref, dk_ref, dv_ref, dkr_ref, dvr_ref, xs_ref, dr1_ref, w0, w1, w2, w3,
-    gk_ref, gs_ref, dx_ref, sums_ref, w_s, dk_s, dv_s,
+    dq_ref, dkv_ref, dkvr_ref, xs_ref, dr1_ref, w0, w1, w2, w3, gk_ref, gs_ref, dx_ref, sums_ref, w_s
 ):
     place_qkv(w_s, (w0, w1, w2, w3))
-    zero = jnp.zeros((1, D), f32)
-
-    def tile(t, c):
-        at = pl.ds(t * ROW_TILE, ROW_TILE)
-        dq = dq_ref[at]
-        dk = (dk_ref[at].astype(f32) + dkr_ref[at].astype(f32)).astype(bf16)
-        dv = (dv_ref[at].astype(f32) + dvr_ref[at].astype(f32)).astype(bf16)
-        dk_s[at] = dk
-        dv_s[at] = dv
-        dx_ref[at] = (
-            dr1_ref[at]
-            + dot(dq, w_s[:, :D], 1, 1)
-            + dot(dk, w_s[:, D : 2 * D], 1, 1)
-            + dot(dv, w_s[:, 2 * D :], 1, 1)
-        )
-        return (c[0] + col_sum(dq.astype(f32)), c[1] + col_sum(dv.astype(f32)))
-
-    dbq, dbv = lax.fori_loop(0, xs_ref.shape[0] // ROW_TILE, tile, (zero, zero))
-    sums_ref[0:1, :] = dbq
-    sums_ref[1:2, :] = dbv
+    dq = dq_ref[...]
+    dkv = (dkv_ref[...].astype(f32) + dkvr_ref[...].astype(f32)).astype(bf16)
+    xs = xs_ref[...]
+    sums_ref[0:1, :] = col_sum(dq.astype(f32))
     sums_ref[2:8, :] = jnp.zeros((6, D), f32)
-    for part, ref in enumerate((dq_ref, dk_s, dv_s)):
-        grad = dot(xs_ref[...], ref[...], 0, 0).astype(bf16)
-        for r in range(4):
-            out = gs_ref if r % 2 else gk_ref
-            for row in range(4):
-                out[r // 2, row * 3 + part] = grad[row * BLK : (row + 1) * BLK, r * BLK : (r + 1) * BLK]
-
-
-def proj_grad(dq, dk, dv, dkr, dvr, xs, dr1, wqkv):
+    grads = (dot(xs, dq, 0, 0).astype(bf16), dot(xs, dkv, 0, 0).astype(bf16))
+    for r in range(4):
+        out = gs_ref if r % 2 else gk_ref
+        c0 = (2 * r + 1) * BLK
+        sums_ref[1:2, r * BLK : (r + 1) * BLK] = col_sum(dkv[:, c0 : c0 + BLK].astype(f32))
+        for row in range(4):
+            rows = slice(row * BLK, (row + 1) * BLK)
+            out[r // 2, row * 3] = grads[0][rows, r * BLK : (r + 1) * BLK]
+            for part in range(2):
+                c0 = (2 * r + part) * BLK
+                out[r // 2, row * 3 + 1 + part] = grads[1][rows, c0 : c0 + BLK]
+    dx_ref[...] = dr1_ref[...] + dot(dq, w_s[:, :D], 1, 1) + dot(dkv, w_s[:, D:], 1, 1)
+
+
+def proj_grad(dq, dkv, dkvr, xs, dr1, wqkv):
     rows = xs.shape[0]
     return pl.pallas_call(
         proj_grad_kernel,
@@ -679,15 +677,11 @@
             shape((rows, D)),
             shape((8, D)),
         ],
-        scratch_shapes=[
-            pltpu.VMEM((D, 3 * D), bf16),
-            pltpu.VMEM((rows, D), bf16),
-            pltpu.VMEM((rows, D), bf16),
-        ],
-        compiler_params=params(),
+        scratch_shapes=[pltpu.VMEM((D, 3 * D), bf16)],
+        compiler_params=params(MIB["proj_grad"]),
         name="proj_grad",
         cost_estimate=cost(5),
-    )(dq, dk, dv, dkr, dvr, xs, dr1, *wqkv)
+    )(dq, dkv, dkvr, xs, dr1, *wqkv)
 
 
 def embed_grad_kernel(
@@ -729,7 +723,7 @@
             shape((2, BLK, BLK)),
         ],
         scratch_shapes=[pltpu.VMEM((BLK, D), f32)],
-        compiler_params=params(),
+        compiler_params=params(MIB["embed_grad"]),
         name="embed_grad",
         cost_estimate=cost(2),
     )(place, series, g, table[:LOOK], *sums)
@@ -765,13 +759,14 @@
         in_specs=[pl.BlockSpec(memory_space=pltpu.SMEM)] + [spec] * 7,
         out_shape=[shape(values.shape)] * 3 + [shape((2 * LAYERS, D))],
         scratch_shapes=[pltpu.VMEM((BLK, D), f32)],
-        compiler_params=params(),
+        compiler_params=params(MIB["vector"]),
         name="vector",
         cost_estimate=cost(2),
     )(place, values, first, second, *parts)
 
 
 PARTS = ((0, 12), (12, 20), (32, 16))
+HELD = ((0, 12), (12, 36))
 
 
 def natural_kernel(plan, at_ref, *refs):
@@ -780,9 +775,9 @@
     for ref, start in zip(slots, plan):
         held[start : start + ref.shape[0]] = ref[...]
     for i, out in enumerate(outs):
-        plane, rest = divmod(i, 3 * LAYERS)
-        layer, part = divmod(rest, 3)
-        first, n = PARTS[part]
+        plane, rest = divmod(i, len(HELD) * LAYERS)
+        layer, part = divmod(rest, len(HELD))
+        first, n = HELD[part]
         for j in range(n):
             out[j] = held[at_ref[plane * 96 + layer * 48 + first + j]]
 
@@ -796,10 +791,10 @@
         out_shape=[
             shape((n, BLK, BLK), bf16)
             for _ in range(at.shape[0] // 96 * LAYERS)
-            for _, n in PARTS
+            for _, n in HELD
         ],
         scratch_shapes=[pltpu.VMEM((total, BLK, BLK), bf16)],
-        compiler_params=params(),
+        compiler_params=params(MIB["natural"]),
         name="natural",
         cost_estimate=cost(4),
     )(at, *slots)
@@ -824,7 +819,7 @@
         routed_kernel,
         in_specs=[pl.BlockSpec(memory_space=pltpu.SMEM)] + [spec] * 12,
         out_shape=shape((count, slots_each * BLK, BLK), bf16),
-        compiler_params=params(),
+        compiler_params=params(MIB["routed"]),
         name="routed",
         cost_estimate=cost(4),
     )(at, *own, *got)
@@ -985,22 +980,21 @@
         vec, bq, bv, b1 = vectors[layer]
         if layer == 0:
             cross(0)
-        wqkv = four(3 * layer, x if layer else None)
+        wqkv = four(2 * layer, x if layer else None)
         x = tied(x, wqkv)
         if layer == 0:
             cross(1, moved[0])
-            cross(2, moved[0])
-        xs, q, k, v = project(x, bq, bv, wqkv)
-        kp, vp = core_swap(k), core_swap(v)
-        o, lse = attend(q, k, kp, v, vp, ohq, ohk)
-        wmid, wdown = four(3 * layer + 1, o), four(3 * layer + 2, o)
-        weights += [wqkv, wmid, wdown]
+        xs, q, kv = project(x, bq, bv, wqkv)
+        kvp = core_swap(kv)
+        o, lse = attend(q, kv, kvp, ohq, ohk)
+        wfeed = four(2 * layer + 1, o)
+        weights.append((wqkv, wfeed))
         if layer + 1 < LAYERS:
             done = moved[-1]
-            for i in range(3):
-                cross(3 * layer + 3 + i, done if i == 0 else (done, moved[3 * layer + 3]))
-        n1, i1, y, hid, slope, n2, i2, x = post(o, x, vec, b1, wmid, wdown)
-        saved.append((xs, q, k, v, kp, vp, o, lse, vec, n1, i1, y, hid, slope, n2, i2))
+            cross(2 * layer + 2, done)
+            cross(2 * layer + 3, (done, moved[-1]))
+        n1, i1, y, hid, slope, n2, i2, x = post(o, x, vec, b1, wfeed)
+        saved.append((xs, q, kv, kvp, o, lse, vec, n1, i1, y, hid, slope, n2, i2))
     activations = x * valid
 
     own_sums = [None] * (3 * LAYERS)
@@ -1021,10 +1015,10 @@
 
     moving = []
     for layer in reversed(range(LAYERS)):
-        xs, q, k, v, kp, vp, o, lse, vec, n1, i1, y, hid, slope, n2, i2 = saved[layer]
-        wqkv, wmid, wdown = weights[3 * layer : 3 * layer + 3]
+        xs, q, kv, kvp, o, lse, vec, n1, i1, y, hid, slope, n2, i2 = saved[layer]
+        wqkv, wfeed = weights[layer]
         gk, gs, ok, os, dr1, do, db1, sums = ffn_grad(
-            grad, n2, i2, n1, i1, y, hid, slope, o, vec, wmid, wdown
+            grad, n2, i2, n1, i1, y, hid, slope, o, vec, wfeed
         )
         os, gs, ok, gk, do = tied((os, gs, ok, gk, do), moving)
         own_chip_sums(sums)
@@ -1033,11 +1027,11 @@
         down = chip_sum(3 * layer + 2, gk, got[1])
         far_sums[3 * layer + 1] = far_swap(mid)
         do = tied(do, (mid, down))
-        dq, dk, dkp, dv, dvp = attend_grad(q, k, kp, v, vp, do, o, lse, ohq, ohk)
-        dkp, dvp = tied((dkp, dvp), far_sums[3 * layer + 1])
+        dq, dkv, dkvp = attend_grad(q, kv, kvp, do, o, lse, ohq, ohk)
+        dkvp = tied(dkvp, far_sums[3 * layer + 1])
         far_sums[3 * layer + 2] = far_swap(tied(down, far_sums[3 * layer + 1]))
-        dkr, dvr = core_swap(dkp), core_swap(dvp)
-        pk, ps, grad, qsums = proj_grad(dq, dk, dv, dkr, dvr, xs, dr1, wqkv)
+        dkvr = core_swap(dkvp)
+        pk, ps, grad, qsums = proj_grad(dq, dkv, dkvr, xs, dr1, wqkv)
         table_rows[layer] = (sums, qsums, db1)
         got = core_swap(ps)
         if layer:

time: 336 us -> 313 us (0.932)
  Pallas kernels: 145 us -> 115 us
  waiting for transfers between devices: 99.1 us -> 121 us
  other arithmetic: 17.2 us -> 10.4 us
  local copies, waits for them, and re-layouts: 22.7 us -> 19.3 us
    ppermute x14 -> x12, waiting for transfers between devices: 47.6 us -> 61.4 us  [far_swap(): return lax.ppermute(value, 'head', [(i, i ^ 2) for i in range(4)])]
    pallas_call x2, Pallas kernels: 23.1 us -> 12.7 us  [ffn_grad(): pl.pallas_call(ffn_grad_kernel, out_shape=[shape((2, 16, BLK, BLK), bf16)...]
    pallas_call x2, Pallas kernels: 16.2 us -> 8.7 us  [post(): pl.pallas_call(post_kernel, out_shape=[shape((rows, D)), shape((rows, LAN...]
    ppermute x29 -> x21, waiting for transfers between devices: 12.6 us -> 18.9 us  [core_swap(): return lax.ppermute(value, 'head', [(i, i ^ 1) for i in range(4)])]
    convert_element_type x15, other arithmetic: 10.2 us -> 4.38 us  [add_low(): return (a.astype(f32) + b.astype(f32)).astype(bf16)]
    pallas_call x2, Pallas kernels: 8.27 us -> 3.76 us  [proj_grad(): pl.pallas_call(proj_grad_kernel, out_shape=[shape((2, 12, BLK, BLK), bf16...]
    ppermute x14 -> x12, starting transfers between devices: 16.3 us -> 14.8 us  [far_swap(): return lax.ppermute(value, 'head', [(i, i ^ 2) for i in range(4)])]
    unnamed x136 -> x84, local copies, waits for them, and re-layouts: 12.3 us -> 12.3 us
  transfers between devices with their start and end apart: 62 -> 52, of which waited for: 35 -> 33; matrix products, arithmetic and copies ran while one was open for 7% -> 5% of each run, Pallas kernels for 26% -> 22%
where the time goes in v6:
time: 313 us; the launch traced here: 309 us
  waiting for transfers between devices  121 us (39%)
  Pallas kernels  115 us (37%)
  starting transfers between devices  42 us (13%)
  local copies, waits for them, and re-layouts  19.3 us (6%)
  other arithmetic  10.4 us (3%)
    ppermute x12, waiting for transfers between devices, far_swap(): return lax.ppermute(value, 'head', [(i, i ^ 2) for i in range(4)])  61.4 us
    ppermute x16, waiting for transfers between devices, ring_shift(): lax.ppermute(value, 'dp', [(order[i], order[(i + by) % n]) for i in range...  35.3 us
    pallas_call x1, Pallas kernels, soap(): pl.pallas_call(functools.partial(soap_kernel, len(gs)), grid=(n // group,...  33.2 us
    pallas_call x2, Pallas kernels, attend_grad(): pl.pallas_call(attend_grad_kernel, grid=(D // LANES,), in_specs=[pair, bo...  30.3 us
    ppermute x21, waiting for transfers between devices, core_swap(): return lax.ppermute(value, 'head', [(i, i ^ 1) for i in range(4)])  18.9 us
    ppermute x16, starting transfers between devices, ring_shift(): lax.ppermute(value, 'dp', [(order[i], order[(i + by) % n]) for i in range...  18.1 us
    pallas_call x2, Pallas kernels, attend(): pl.pallas_call(attend_kernel, grid=(D // LANES,), in_specs=[pair, both, o...  18 us
    ppermute x12, starting transfers between devices, far_swap(): return lax.ppermute(value, 'head', [(i, i ^ 2) for i in range(4)])  14.8 us
  transfers between devices with their start and end apart: 52, of which 33 were waited for; matrix products, arithmetic and copies ran while one was open for 5% of the time, Pallas kernels for 22%

profile of v6, /device:TPU:0, one launch (start us, length us, event | category | flops | bytes accessed | tf_op | source)
XLA Modules:
  0.0 309.4 jit_solution(7222616428752597669)
XLA Ops:
  1.9 3.0 collective-permute-start.1
  18.2 6.3 %collective-permute-done.3.refs_4_ = bf16[12,128,128]{2,1,0:T(8,128)(2,1)S(1)} collective-permute-done((bf16[12,128,128]{2,1,0:T(8,128)(2,1)S(1)}, bf16[12,128,128]{2,1,0:T(8,128)(2,1)S(1)}, u32[]{:S(2)}, u32[]{:S(2)}) %collective-permute-start.3) | collective-permute-done | bytes 393248 | tf_op jit(solution)/shard_map/ppermute | solution.py:835
  27.9 5.9 %collective-permute-done.5.refs_6_ = bf16[12,128,128]{2,1,0:T(8,128)(2,1)S(1)} collective-permute-done((bf16[12,128,128]{2,1,0:T(8,128)(2,1)S(1)}, bf16[12,128,128]{2,1,0:T(8,128)(2,1)S(1)}, u32[]{:S(2)}, u32[]{:S(2)}) %collective-permute-start.5) | collective-permute-done | bytes 393248 | tf_op jit(solution)/shard_map/ppermute | solution.py:835
  36.8 2.7 collective-permute-done.7.refs_8_
  43.5 6.3 %collective-permute-done.9.w2 = bf16[12,128,128]{2,1,0:T(8,128)(2,1)S(1)} collective-permute-done((bf16[12,128,128]{2,1,0:T(8,128)(2,1)S(1)}, bf16[12,128,128]{2,1,0:T(8,128)(2,1)S(1)}, u32[]{:S(2)}, u32[]{:S(2)}) %collective-permute-start.9) | collective-permute-done | bytes 393248 | tf_op jit(solution)/shard_map/ppermute | solution.py:890
  55.3 8.9 %attend.2 = (bf16[512,512]{1,0:T(8,128)(2,1)S(1)}, f32[512,512]{1,0:T(8,128)S(1)}) custom-call(bf16[512,512]{1,0:T(8,128)(2,1)S(1)} %get-tuple-element.176.q_ref, bf16[512,1024]{1,0:T(8,128)(2,1)S(1)} %get-tuple-element.177.kv_ref, bf16[512,1024]{1,0:T(8,128)(2,1)S(1)} %collective-permute-done.11.kvp_ref, bf16[512,128]{1,0:T(8,128)(2,1)S(1)} %get-tuple-element.178.ohq_ref, ...), custom_call_target="tpu_custom_call" | custom-call | flops 11000000 | tf_op jit(solution)/shard_map/attend/pallas_call | solution.py:383
  65.2 12.9 %collective-permute-done.13.a2 = bf16[36,128,128]{2,1,0:T(8,128)(2,1)S(1)} collective-permute-done((bf16[36,128,128]{2,1,0:T(8,128)(2,1)S(1)}, bf16[36,128,128]{2,1,0:T(8,128)(2,1)S(1)}, u32[]{:S(2)}, u32[]{:S(2)}) %collective-permute-start.13) | collective-permute-done | bytes 1179680 | tf_op jit(solution)/shard_map/ppermute | solution.py:890
  81.0 4.4 %post.2 = (f32[512,512]{1,0:T(8,128)S(1)}, f32[512,128]{1,0:T(8,128)S(1)}, bf16[512,512]{1,0:T(8,128)(2,1)S(1)}, bf16[512,2048]{1,0:T(8,128)(2,1)S(1)}, bf16[512...) custom-call(bf16[512,512]{1,0:T(8,128)(2,1)S(1)} %get-tuple-element.180.o_ref, ...), custom_call_target="tpu_custom_call" | custom-call | flops 11000000 | tf_op jit(solution)/shard_map/post/pallas_call | solution.py:439
  87.0 2.6 collective-permute-done.16.w2
  95.3 9.1 %attend.3 = (bf16[512,512]{1,0:T(8,128)(2,1)S(1)}, f32[512,512]{1,0:T(8,128)S(1)}) custom-call(bf16[512,512]{1,0:T(8,128)(2,1)S(1)} %get-tuple-element.193.q_ref, bf16[512,1024]{1,0:T(8,128)(2,1)S(1)} %get-tuple-element.194.kv_ref, bf16[512,1024]{1,0:T(8,128)(2,1)S(1)} %collective-permute-done.18.kvp_ref, bf16[512,128]{1,0:T(8,128)(2,1)S(1)} %get-tuple-element.178.ohq_ref, ...), custom_call_target="tpu_custom_call" | custom-call | flops 11000000 | tf_op jit(solution)/shard_map/attend/pallas_call | solution.py:383
  104.4 13.6 %collective-permute-done.20.a2 = bf16[36,128,128]{2,1,0:T(8,128)(2,1)S(1)} collective-permute-done((bf16[36,128,128]{2,1,0:T(8,128)(2,1)S(1)}, bf16[36,128,128]{2,1,0:T(8,128)(2,1)S(1)}, u32[]{:S(2)}, u32[]{:S(2)}) %collective-permute-start.20) | collective-permute-done | bytes 1179680 | tf_op jit(solution)/shard_map/ppermute | solution.py:890
  118.1 2.8 collective-permute-done.21.a3
  120.9 4.3 %post.3 = (f32[512,512]{1,0:T(8,128)S(1)}, f32[512,128]{1,0:T(8,128)S(1)}, bf16[512,512]{1,0:T(8,128)(2,1)S(1)}, bf16[512,2048]{1,0:T(8,128)(2,1)S(1)}, bf16[512...) custom-call(bf16[512,512]{1,0:T(8,128)(2,1)S(1)} %get-tuple-element.195.o_ref, ...), custom_call_target="tpu_custom_call" | custom-call | flops 11000000 | tf_op jit(solution)/shard_map/post/pallas_call | solution.py:439
  128.1 6.4 %ffn_grad.2 = (bf16[2,16,128,128]{3,2,1,0:T(8,128)(2,1)S(1)}, bf16[2,16,128,128]{3,2,1,0:T(8,128)(2,1)S(1)}, bf16[2,20,128,128]{3,2,1,0:T(8,128)(2,1)S(1)}, bf16...) custom-call(f32[512,512]{1,0:T(8,128)S(1)} %broadcast_multiply_fusio, ...), custom_call_target="tpu_custom_call" | custom-call | flops 16000000 | tf_op jit(solution)/shard_map/ffn_grad/pallas_call | solution.py:532
  135.1 2.5 collective-permute-done.22
  139.6 15.3 %attend_grad.2 = (bf16[512,512]{1,0:T(8,128)(2,1)S(1)}, bf16[512,1024]{1,0:T(8,128)(2,1)S(1)}, bf16[512,1024]{1,0:T(8,128)(2,1)S(1)}) custom-call(bf16[512,512]{1,0:T(8,128)(2,1)S(1)} %get-tuple-element.193.q_ref, bf16[512,1024]{1,0:T(8,128)(2,1)S(1)} %get-tuple-element.194.kv_ref, bf16[512,1024]{1,0:T(8,128)(2,1)S(1)} %collective-permute-done.18.kvp_ref, ...), custom_call_target="tpu_custom_call" | custom-call | flops 23000000 | tf_op jit(solution)/shard_map/attend_grad/pallas_call | solution.py:624
  155.0 2.6 collective-permute-done.25.dkvr_ref
  163.5 6.4 %ffn_grad.3 = (bf16[2,16,128,128]{3,2,1,0:T(8,128)(2,1)S(1)}, bf16[2,16,128,128]{3,2,1,0:T(8,128)(2,1)S(1)}, bf16[2,20,128,128]{3,2,1,0:T(8,128)(2,1)S(1)}, bf16...) custom-call(f32[512,512]{1,0:T(8,128)S(1)} %get-tuple-element.232.e_, ...), custom_call_target="tpu_custom_call" | custom-call | flops 16000000 | tf_op jit(solution)/shard_map/ffn_grad/pallas_call | solution.py:532
  169.9 4.7 %collective-permute-done.28.refs_11_ = bf16[16,128,128]{2,1,0:T(8,128)(2,1)S(1)} collective-permute-done((bf16[16,128,128]{2,1,0:T(8,128)(2,1)S(1)}, bf16[16,128,128]{2,1,0:T(8,128)(2,1)S(1)}, u32[]{:S(2)}, u32[]{:S(2)}) %collective-permute-start.28) | collective-permute-done | bytes 524320 | tf_op jit(solution)/shard_map/ppermute | solution.py:890
  174.5 7.9 %collective-permute-done.27.refs_9_ = bf16[12,128,128]{2,1,0:T(8,128)(2,1)S(1)} collective-permute-done((bf16[12,128,128]{2,1,0:T(8,128)(2,1)S(1)}, bf16[12,128,128]{2,1,0:T(8,128)(2,1)S(1)}, u32[]{:S(2)}, u32[]{:S(2)}) %collective-permute-start.27) | collective-permute-done | bytes 393248 | tf_op jit(solution)/shard_map/ppermute | solution.py:890
  188.2 15.0 %attend_grad.3 = (bf16[512,512]{1,0:T(8,128)(2,1)S(1)}, bf16[512,1024]{1,0:T(8,128)(2,1)S(1)}, bf16[512,1024]{1,0:T(8,128)(2,1)S(1)}) custom-call(bf16[512,512]{1,0:T(8,128)(2,1)S(1)} %get-tuple-element.176.q_ref, bf16[512,1024]{1,0:T(8,128)(2,1)S(1)} %get-tuple-element.177.kv_ref, bf16[512,1024]{1,0:T(8,128)(2,1)S(1)} %collective-permute-done.11.kvp_ref, ...), custom_call_target="tpu_custom_call" | custom-call | flops 23000000 | tf_op jit(solution)/shard_map/attend_grad/pallas_call | solution.py:624
  213.2 2.5 collective-permute-done.39
  217.1 2.9 collective-permute-done.40
  221.2 8.3 %collective-permute-done.34.refs_6_ = bf16[12,128,128]{2,1,0:T(8,128)(2,1)S(1)} collective-permute-done((bf16[12,128,128]{2,1,0:T(8,128)(2,1)S(1)}, bf16[12,128,128]{2,1,0:T(8,128)(2,1)S(1)}, u32[]{:S(2)}, u32[]{:S(2)}) %collective-permute-start.34) | collective-permute-done | bytes 393248 | tf_op jit(solution)/shard_map/ppermute | solution.py:890
  229.4 2.6 collective-permute-start.41
  235.9 3.6 %collective-permute-done.37 = bf16[768,128]{1,0:T(8,128)(2,1)S(1)} collective-permute-done((bf16[768,128]{1,0:T(8,128)(2,1)S(1)}, bf16[768,128]{1,0:T(8,128)(2,1)S(1)}, u32[]{:S(2)}, u32[]{:S(2)}) %collective-permute-start.37) | collective-permute-done | bytes 196640 | tf_op jit(solution)/shard_map/ppermute | solution.py:835
  239.5 3.3 %collective-permute-done.36 = bf16[768,128]{1,0:T(8,128)(2,1)S(1)} collective-permute-done((bf16[768,128]{1,0:T(8,128)(2,1)S(1)}, bf16[768,128]{1,0:T(8,128)(2,1)S(1)}, u32[]{:S(2)}, u32[]{:S(2)}) %collective-permute-start.36) | collective-permute-done | bytes 196640 | tf_op jit(solution)/shard_map/ppermute | solution.py:835
  245.8 3.5 %collective-permute-done.44 = f32[128,128]{1,0:T(8,128)S(1)} collective-permute-done((f32[128,128]{1,0:T(8,128)S(1)}, f32[128,128]{1,0:T(8,128)S(1)}, u32[]{:S(2)}, u32[]{:S(2)}) %collective-permute-start.44) | collective-permute-done | bytes 65568 | tf_op jit(solution)/shard_map/ppermute | solution.py:890
  249.3 3.2 %collective-permute-done.42 = bf16[1536,128]{1,0:T(8,128)(2,1)S(1)} collective-permute-done((bf16[1536,128]{1,0:T(8,128)(2,1)S(1)}, bf16[1536,128]{1,0:T(8,128)(2,1)S(1)}, u32[]{:S(2)}, u32[]{:S(2)}) %collective-permute-start.42) | collective-permute-done | bytes 393248 | tf_op jit(solution)/shard_map/ppermute | solution.py:835
  253.7 2.3 collective-permute-start.46
  268.7 4.9 %collective-permute-done.50 = bf16[1536,128]{1,0:T(8,128)(2,1)S(1)} collective-permute-done((bf16[1536,128]{1,0:T(8,128)(2,1)S(1)}, bf16[1536,128]{1,0:T(8,128)(2,1)S(1)}, u32[]{:S(2)}, u32[]{:S(2)}) %collective-permute-start.50) | collective-permute-done | bytes 393248 | tf_op jit(solution)/shard_map/ppermute | solution.py:835
  276.0 33.2 %soap.1 = (f32[12,128,128]{2,1,0:T(8,128)}, bf16[12,128,128]{2,1,0:T(8,128)(2,1)}, f32[12,128,128]{2,1,0:T(8,128)}, f32[12,128,128]{2,1,0:T(8,128)}, f32[12,128,...) custom-call(bf16[12,128,128]{2,1,0:T(8,128)(2,1)S(1)} %bitcast.158, ...), custom_call_target="tpu_custom_call" | custom-call | flops 40000000 | tf_op jit(solution)/shard_map/soap/pallas_call | solution.py:208
  (244 shorter events, 93.5 us)
Async XLA Ops:
  1.9 12.2 %collective-permute-start.1 = (bf16[12,128,128]{2,1,0:T(8,128)(2,1)S(1)}, bf16[12,128,128]{2,1,0:T(8,128)(2,1)S(1)}, u32[]{:S(2)}, u32[]{:S(2)}) collective-permute-start(bf16[12,128,128]{2,1,0:T(8,128)(2,1)S(1)} %bitcast_convert_fusion.refs_0_), channel_id=1, source_target_pairs={{0,4},{8,0},{16,8},{24,16},{28,24},{20,28},{12,20},{4,12},{1,5},{9... | collective-permute-start | bytes 1179656 | tf_op jit(solution)/shard_map/ppermute | solution.py:835
  4.9 10.9 %collective-permute-start = (bf16[12,128,128]{2,1,0:T(8,128)(2,1)S(1)}, bf16[12,128,128]{2,1,0:T(8,128)(2,1)S(1)}, u32[]{:S(2)}, u32[]{:S(2)}) collective-permute-start(bf16[12,128,128]{2,1,0:T(8,128)(2,1)S(1)} %bitcast_convert_fusion.refs_0_), channel_id=1, source_target_pairs={{0,8},{8,16},{16,24},{24,28},{28,20},{20,12},{12,4},{4,0},{1,9},{9... | collective-permute-start | bytes 1179656 | tf_op jit(solution)/shard_map/ppermute | solution.py:835
  14.1 10.3 %collective-permute-start.3 = (bf16[12,128,128]{2,1,0:T(8,128)(2,1)S(1)}, bf16[12,128,128]{2,1,0:T(8,128)(2,1)S(1)}, u32[]{:S(2)}, u32[]{:S(2)}) collective-permute-start(bf16[12,128,128]{2,1,0:T(8,128)(2,1)S(1)} %collective-permute-done.1.refs_2_), channel_id=1, source_target_pairs={{0,4},{8,0},{16,8},{24,16},{28,24},{20,28},{12,20},{4,12},{1,5},{9... | collective-permute-start | bytes 1179656 | tf_op jit(solution)/shard_map/ppermute | solution.py:835
  15.8 10.0 %collective-permute-start.2 = (bf16[12,128,128]{2,1,0:T(8,128)(2,1)S(1)}, bf16[12,128,128]{2,1,0:T(8,128)(2,1)S(1)}, u32[]{:S(2)}, u32[]{:S(2)}) collective-permute-start(bf16[12,128,128]{2,1,0:T(8,128)(2,1)S(1)} %collective-permute-done.refs_1_), channel_id=1, source_target_pairs={{0,8},{8,16},{16,24},{24,28},{28,20},{20,12},{12,4},{4,0},{1,9},{9... | collective-permute-start | bytes 1179656 | tf_op jit(solution)/shard_map/ppermute | solution.py:835
  24.4 9.4 %collective-permute-start.5 = (bf16[12,128,128]{2,1,0:T(8,128)(2,1)S(1)}, bf16[12,128,128]{2,1,0:T(8,128)(2,1)S(1)}, u32[]{:S(2)}, u32[]{:S(2)}) collective-permute-start(bf16[12,128,128]{2,1,0:T(8,128)(2,1)S(1)} %collective-permute-done.3.refs_4_), channel_id=1, source_target_pairs={{0,4},{8,0},{16,8},{24,16},{28,24},{20,28},{12,20},{4,12},{1,5},{9... | collective-permute-start | bytes 1179656 | tf_op jit(solution)/shard_map/ppermute | solution.py:835
  25.8 9.3 %collective-permute-start.4 = (bf16[12,128,128]{2,1,0:T(8,128)(2,1)S(1)}, bf16[12,128,128]{2,1,0:T(8,128)(2,1)S(1)}, u32[]{:S(2)}, u32[]{:S(2)}) collective-permute-start(bf16[12,128,128]{2,1,0:T(8,128)(2,1)S(1)} %collective-permute-done.2.refs_3_), channel_id=1, source_target_pairs={{0,8},{8,16},{16,24},{24,28},{28,20},{20,12},{12,4},{4,0},{1,9},{9... | collective-permute-start | bytes 1179656 | tf_op jit(solution)/shard_map/ppermute | solution.py:835
  33.8 5.7 %collective-permute-start.7 = (bf16[6,128,128]{2,1,0:T(8,128)(2,1)S(1)}, bf16[6,128,128]{2,1,0:T(8,128)(2,1)S(1)}, u32[]{:S(2)}, u32[]{:S(2)}) collective-permute-start(bf16[6,128,128]{2,1,0:T(8,128)(2,1)S(1)} %slice.274), channel_id=1, source_target_pairs={{0,4},{8,0},{16,8},{24,16},{28,24},{20,28},{12,20},{4,12},{1,5},{9... | collective-permute-start | bytes 589832 | tf_op jit(solution)/shard_map/ppermute | solution.py:835
  35.1 5.9 %collective-permute-start.6 = (bf16[6,128,128]{2,1,0:T(8,128)(2,1)S(1)}, bf16[6,128,128]{2,1,0:T(8,128)(2,1)S(1)}, u32[]{:S(2)}, u32[]{:S(2)}) collective-permute-start(bf16[6,128,128]{2,1,0:T(8,128)(2,1)S(1)} %slice.273), channel_id=1, source_target_pairs={{0,8},{8,16},{16,24},{24,28},{28,20},{20,12},{12,4},{4,0},{1,9},{9... | collective-permute-start | bytes 589832 | tf_op jit(solution)/shard_map/ppermute | solution.py:835
  41.9 7.8 %collective-permute-start.9 = (bf16[12,128,128]{2,1,0:T(8,128)(2,1)S(1)}, bf16[12,128,128]{2,1,0:T(8,128)(2,1)S(1)}, u32[]{:S(2)}, u32[]{:S(2)}) collective-permute-start(bf16[12,128,128]{2,1,0:T(8,128)(2,1)S(1)} %get-tuple-element.172.w0), channel_id=1, source_target_pairs={{0,2},{1,3},{2,0},{3,1},{4,6},{5,7},{6,4},{7,5},{8,10},{9,11},{10,... | collective-permute-start | bytes 1179656 | tf_op jit(solution)/shard_map/ppermute | solution.py:890
  43.5 7.8 %collective-permute-start.8 = (bf16[12,128,128]{2,1,0:T(8,128)(2,1)S(1)}, bf16[12,128,128]{2,1,0:T(8,128)(2,1)S(1)}, u32[]{:S(2)}, u32[]{:S(2)}) collective-permute-start(bf16[12,128,128]{2,1,0:T(8,128)(2,1)S(1)} %get-tuple-element.172.w0), channel_id=1, source_target_pairs={{0,1},{1,0},{2,3},{3,2},{4,5},{5,4},{6,7},{7,6},{8,9},{9,8},{10,11... | collective-permute-start | bytes 1179656 | tf_op jit(solution)/shard_map/ppermute | solution.py:886
  49.8 28.4 %collective-permute-start.13 = (bf16[36,128,128]{2,1,0:T(8,128)(2,1)S(1)}, bf16[36,128,128]{2,1,0:T(8,128)(2,1)S(1)}, u32[]{:S(2)}, u32[]{:S(2)}) collective-permute-start(bf16[36,128,128]{2,1,0:T(8,128)(2,1)S(1)} %get-tuple-element.184.a0), channel_id=1, source_target_pairs={{0,2},{1,3},{2,0},{3,1},{4,6},{5,7},{6,4},{7,5},{8,10},{9,11},{10,... | collective-permute-start | bytes 3538952 | tf_op jit(solution)/shard_map/ppermute | solution.py:890
  52.8 27.1 %collective-permute-start.12 = (bf16[36,128,128]{2,1,0:T(8,128)(2,1)S(1)}, bf16[36,128,128]{2,1,0:T(8,128)(2,1)S(1)}, u32[]{:S(2)}, u32[]{:S(2)}) collective-permute-start(bf16[36,128,128]{2,1,0:T(8,128)(2,1)S(1)} %get-tuple-element.184.a0), channel_id=1, source_target_pairs={{0,1},{1,0},{2,3},{3,2},{4,5},{5,4},{6,7},{7,6},{8,9},{9,8},{10,11... | collective-permute-start | bytes 3538952 | tf_op jit(solution)/shard_map/ppermute | solution.py:886
  78.1 11.5 %collective-permute-start.16 = (bf16[12,128,128]{2,1,0:T(8,128)(2,1)S(1)}, bf16[12,128,128]{2,1,0:T(8,128)(2,1)S(1)}, u32[]{:S(2)}, u32[]{:S(2)}) collective-permute-start(bf16[12,128,128]{2,1,0:T(8,128)(2,1)S(1)} %get-tuple-element.188.w0), channel_id=1, source_target_pairs={{0,2},{1,3},{2,0},{3,1},{4,6},{5,7},{6,4},{7,5},{8,10},{9,11},{10,... | collective-permute-start | bytes 1179656 | tf_op jit(solution)/shard_map/ppermute | solution.py:890
  79.7 11.5 %collective-permute-start.15 = (bf16[12,128,128]{2,1,0:T(8,128)(2,1)S(1)}, bf16[12,128,128]{2,1,0:T(8,128)(2,1)S(1)}, u32[]{:S(2)}, u32[]{:S(2)}) collective-permute-start(bf16[12,128,128]{2,1,0:T(8,128)(2,1)S(1)} %get-tuple-element.188.w0), channel_id=1, source_target_pairs={{0,1},{1,0},{2,3},{3,2},{4,5},{5,4},{6,7},{7,6},{8,9},{9,8},{10,11... | collective-permute-start | bytes 1179656 | tf_op jit(solution)/shard_map/ppermute | solution.py:886
  89.7 28.4 %collective-permute-start.20 = (bf16[36,128,128]{2,1,0:T(8,128)(2,1)S(1)}, bf16[36,128,128]{2,1,0:T(8,128)(2,1)S(1)}, u32[]{:S(2)}, u32[]{:S(2)}) collective-permute-start(bf16[36,128,128]{2,1,0:T(8,128)(2,1)S(1)} %get-tuple-element.199.a0), channel_id=1, source_target_pairs={{0,2},{1,3},{2,0},{3,1},{4,6},{5,7},{6,4},{7,5},{8,10},{9,11},{10,... | collective-permute-start | bytes 3538952 | tf_op jit(solution)/shard_map/ppermute | solution.py:890
  92.8 25.3 %collective-permute-start.19 = (bf16[36,128,128]{2,1,0:T(8,128)(2,1)S(1)}, bf16[36,128,128]{2,1,0:T(8,128)(2,1)S(1)}, u32[]{:S(2)}, u32[]{:S(2)}) collective-permute-start(bf16[36,128,128]{2,1,0:T(8,128)(2,1)S(1)} %get-tuple-element.199.a0), channel_id=1, source_target_pairs={{0,1},{1,0},{2,3},{3,2},{4,5},{5,4},{6,7},{7,6},{8,9},{9,8},{10,11... | collective-permute-start | bytes 3538952 | tf_op jit(solution)/shard_map/ppermute | solution.py:886
  137.8 17.1 %collective-permute-start.24 = (bf16[20,128,128]{2,1,0:T(8,128)(2,1)S(1)}, bf16[20,128,128]{2,1,0:T(8,128)(2,1)S(1)}, u32[]{:S(2)}, u32[]{:S(2)}) collective-permute-start(bf16[20,128,128]{2,1,0:T(8,128)(2,1)S(1)} %fusion.4), channel_id=1, source_target_pairs={{0,2},{1,3},{2,0},{3,1},{4,6},{5,7},{6,4},{7,5},{8,10},{9,11},{10,... | collective-permute-start | bytes 1966088 | tf_op jit(solution)/shard_map/ppermute | solution.py:890
  159.8 14.8 %collective-permute-start.28 = (bf16[16,128,128]{2,1,0:T(8,128)(2,1)S(1)}, bf16[16,128,128]{2,1,0:T(8,128)(2,1)S(1)}, u32[]{:S(2)}, u32[]{:S(2)}) collective-permute-start(bf16[16,128,128]{2,1,0:T(8,128)(2,1)S(1)} %fusion.6), channel_id=1, source_target_pairs={{0,2},{1,3},{2,0},{3,1},{4,6},{5,7},{6,4},{7,5},{8,10},{9,11},{10,... | collective-permute-start | bytes 1572872 | tf_op jit(solution)/shard_map/ppermute | solution.py:890
  162.0 20.4 %collective-permute-start.27 = (bf16[12,128,128]{2,1,0:T(8,128)(2,1)S(1)}, bf16[12,128,128]{2,1,0:T(8,128)(2,1)S(1)}, u32[]{:S(2)}, u32[]{:S(2)}) collective-permute-start(bf16[12,128,128]{2,1,0:T(8,128)(2,1)S(1)} %fusion.8), channel_id=1, source_target_pairs={{0,2},{1,3},{2,0},{3,1},{4,6},{5,7},{6,4},{7,5},{8,10},{9,11},{10,... | collective-permute-start | bytes 1179656 | tf_op jit(solution)/shard_map/ppermute | solution.py:890
  185.6 17.6 %collective-permute-start.31 = (bf16[20,128,128]{2,1,0:T(8,128)(2,1)S(1)}, bf16[20,128,128]{2,1,0:T(8,128)(2,1)S(1)}, u32[]{:S(2)}, u32[]{:S(2)}) collective-permute-start(bf16[20,128,128]{2,1,0:T(8,128)(2,1)S(1)} %fusion.5), channel_id=1, source_target_pairs={{0,2},{1,3},{2,0},{3,1},{4,6},{5,7},{6,4},{7,5},{8,10},{9,11},{10,... | collective-permute-start | bytes 1966088 | tf_op jit(solution)/shard_map/ppermute | solution.py:890
  203.6 28.5 %collective-permute-start.35 = (bf16[16,128,128]{2,1,0:T(8,128)(2,1)S(1)}, bf16[16,128,128]{2,1,0:T(8,128)(2,1)S(1)}, u32[]{:S(2)}, u32[]{:S(2)}) collective-permute-start(bf16[16,128,128]{2,1,0:T(8,128)(2,1)S(1)} %fusion.7), channel_id=1, source_target_pairs={{0,2},{1,3},{2,0},{3,1},{4,6},{5,7},{6,4},{7,5},{8,10},{9,11},{10,... | collective-permute-start | bytes 1572872 | tf_op jit(solution)/shard_map/ppermute | solution.py:890
  210.1 9.9 %collective-permute-start.33 = (bf16[2,12,128,128]{3,2,1,0:T(8,128)(2,1)S(1)}, bf16[2,12,128,128]{3,2,1,0:T(8,128)(2,1)S(1)}, u32[]{:S(2)}, u32[]{:S(2)}) collective-permute-start(bf16[2,12,128,128]{3,2,1,0:T(8,128)(2,1)S(1)} %get-tuple-element.268), channel_id=1, source_target_pairs={{0,1},{1,0},{2,3},{3,2},{4,5},{5,4},{6,7},{7,6},{8,9},{9,8},{10,11... | collective-permute-start | bytes 2359304 | tf_op jit(solution)/shard_map/ppermute | solution.py:886
  220.2 9.2 %collective-permute-start.34 = (bf16[12,128,128]{2,1,0:T(8,128)(2,1)S(1)}, bf16[12,128,128]{2,1,0:T(8,128)(2,1)S(1)}, u32[]{:S(2)}, u32[]{:S(2)}) collective-permute-start(bf16[12,128,128]{2,1,0:T(8,128)(2,1)S(1)} %fusion.9), channel_id=1, source_target_pairs={{0,2},{1,3},{2,0},{3,1},{4,6},{5,7},{6,4},{7,5},{8,10},{9,11},{10,... | collective-permute-start | bytes 1179656 | tf_op jit(solution)/shard_map/ppermute | solution.py:890
  229.4 6.5 %collective-permute-start.41 = (bf16[2,128,128]{2,1,0:T(8,128)(2,1)S(1)}, bf16[2,128,128]{2,1,0:T(8,128)(2,1)S(1)}, u32[]{:S(2)}, u32[]{:S(2)}) collective-permute-start(bf16[2,128,128]{2,1,0:T(8,128)(2,1)S(1)} %convert_add_fusion.7), channel_id=1, source_target_pairs={{0,16},{4,20},{8,24},{12,28},{16,0},{20,4},{24,8},{28,12},{1,17},{... | collective-permute-start | bytes 196616 | tf_op jit(solution)/shard_map/ppermute | solution.py:875
  233.8 5.7 %collective-permute-start.37 = (bf16[768,128]{1,0:T(8,128)(2,1)S(1)}, bf16[768,128]{1,0:T(8,128)(2,1)S(1)}, u32[]{:S(2)}, u32[]{:S(2)}) collective-permute-start(bf16[768,128]{1,0:T(8,128)(2,1)S(1)} %get-tuple-element.358), channel_id=1, source_target_pairs={{0,4},{8,0},{16,8},{24,16},{28,24},{20,28},{12,20},{4,12},{1,5},{9... | collective-permute-start | bytes 589832 | tf_op jit(solution)/shard_map/ppermute | solution.py:835
  235.4 7.4 %collective-permute-start.36 = (bf16[768,128]{1,0:T(8,128)(2,1)S(1)}, bf16[768,128]{1,0:T(8,128)(2,1)S(1)}, u32[]{:S(2)}, u32[]{:S(2)}) collective-permute-start(bf16[768,128]{1,0:T(8,128)(2,1)S(1)} %get-tuple-element.360), channel_id=1, source_target_pairs={{0,8},{8,16},{16,24},{24,28},{28,20},{20,12},{12,4},{4,0},{1,9},{9... | collective-permute-start | bytes 589832 | tf_op jit(solution)/shard_map/ppermute | solution.py:835
  243.0 9.6 %collective-permute-start.42 = (bf16[1536,128]{1,0:T(8,128)(2,1)S(1)}, bf16[1536,128]{1,0:T(8,128)(2,1)S(1)}, u32[]{:S(2)}, u32[]{:S(2)}) collective-permute-start(bf16[1536,128]{1,0:T(8,128)(2,1)S(1)} %pad_maximum_fusion), channel_id=1, source_target_pairs={{0,8},{8,16},{16,24},{24,28},{28,20},{20,12},{12,4},{4,0},{1,9},{9... | collective-permute-start | bytes 1179656 | tf_op jit(solution)/shard_map/ppermute | solution.py:835
  243.0 9.5 %collective-permute-start.43 = (bf16[1536,128]{1,0:T(8,128)(2,1)S(1)}, bf16[1536,128]{1,0:T(8,128)(2,1)S(1)}, u32[]{:S(2)}, u32[]{:S(2)}) collective-permute-start(bf16[1536,128]{1,0:T(8,128)(2,1)S(1)} %pad_maximum_fusion.1), channel_id=1, source_target_pairs={{0,4},{8,0},{16,8},{24,16},{28,24},{20,28},{12,20},{4,12},{1,5},{9... | collective-permute-start | bytes 1179656 | tf_op jit(solution)/shard_map/ppermute | solution.py:835
  253.7 8.4 %collective-permute-start.45 = (bf16[1536,128]{1,0:T(8,128)(2,1)}, bf16[1536,128]{1,0:T(8,128)(2,1)}, u32[]{:S(2)}, u32[]{:S(2)}) collective-permute-start(bf16[1536,128]{1,0:T(8,128)(2,1)} %get-tuple-element.287), channel_id=1, source_target_pairs={{0,8},{8,16},{16,24},{24,28},{28,20},{20,12},{12,4},{4,0},{1,9},{9... | collective-permute-start | bytes 1179656 | tf_op jit(solution)/shard_map/ppermute | solution.py:835
  253.7 8.4 %collective-permute-start.46 = (bf16[1536,128]{1,0:T(8,128)(2,1)}, bf16[1536,128]{1,0:T(8,128)(2,1)}, u32[]{:S(2)}, u32[]{:S(2)}) collective-permute-start(bf16[1536,128]{1,0:T(8,128)(2,1)} %get-tuple-element.288), channel_id=1, source_target_pairs={{0,4},{8,0},{16,8},{24,16},{28,24},{20,28},{12,20},{4,12},{1,5},{9... | collective-permute-start | bytes 1179656 | tf_op jit(solution)/shard_map/ppermute | solution.py:835
  263.6 10.1 %collective-permute-start.50 = (bf16[1536,128]{1,0:T(8,128)(2,1)S(1)}, bf16[1536,128]{1,0:T(8,128)(2,1)S(1)}, u32[]{:S(2)}, u32[]{:S(2)}) collective-permute-start(bf16[1536,128]{1,0:T(8,128)(2,1)S(1)} %get-tuple-element.289), channel_id=1, source_target_pairs={{0,8},{8,16},{16,24},{24,28},{28,20},{20,12},{12,4},{4,0},{1,9},{9... | collective-permute-start | bytes 1179656 | tf_op jit(solution)/shard_map/ppermute | solution.py:835
  263.6 10.0 %collective-permute-start.51 = (bf16[1536,128]{1,0:T(8,128)(2,1)S(1)}, bf16[1536,128]{1,0:T(8,128)(2,1)S(1)}, u32[]{:S(2)}, u32[]{:S(2)}) collective-permute-start(bf16[1536,128]{1,0:T(8,128)(2,1)S(1)} %get-tuple-element.290), channel_id=1, source_target_pairs={{0,4},{8,0},{16,8},{24,16},{28,24},{20,28},{12,20},{4,12},{1,5},{9... | collective-permute-start | bytes 1179656 | tf_op jit(solution)/shard_map/ppermute | solution.py:835
  (60 other events, 346.9 us)

commit v7 on v6

--- a/solution.py
+++ b/solution.py
@@ -223,6 +223,7 @@
 
 bf16 = jnp.bfloat16
 LANES = 128
+TOP = 64
 ROW_TILE = 512
 BIG = 1e30
 CORR = 1.0 - 0.5**STEP
@@ -249,21 +250,29 @@
     return lax.dot_general(a, b, (((ca,), (cb,)), ((), ())), preferred_element_type=f32)
 
 
-def place_blocks(dst, refs, first, rows, cols, row_step, col_step, col_base=0):
-    for r, ref in enumerate(refs):
+def planes(refs):
+    return (refs[0],), (refs[1],), (refs[2], refs[3]), (refs[4], refs[5])
+
+
+def place_block(dst, refs, j, r0, c0):
+    for ref in refs:
+        dst[r0 : r0 + ref.shape[1], c0 : c0 + BLK] = ref[j]
+        r0 += ref.shape[1]
+
+
+def place_blocks(dst, refs, first, rows, cols, row_step, col_step):
+    for r, plane in enumerate(planes(refs)):
         for j in range(rows * cols):
             row, col = divmod(j, cols)
-            r0 = r * row_step + row * BLK
-            c0 = col_base + r * col_step + col * BLK
-            dst[r0 : r0 + BLK, c0 : c0 + BLK] = ref[first + j]
+            place_block(dst, plane, first + j, r * row_step + row * BLK, r * col_step + col * BLK)
 
 
 def place_qkv(dst, refs):
-    for r, ref in enumerate(refs):
+    for r, plane in enumerate(planes(refs)):
         for j in range(12):
             row, col = divmod(j, 3)
             c0 = D + (2 * r + col - 1) * BLK if col else r * BLK
-            dst[row * BLK : (row + 1) * BLK, c0 : c0 + BLK] = ref[j]
+            place_block(dst, plane, j, row * BLK, c0)
 
 
 def layer_norm(resid):
@@ -296,8 +305,8 @@
     )(series, table[:LOOK], table[LOOK : LOOK + 1])
 
 
-def proj_kernel(x_ref, bq_ref, bv_ref, w0, w1, w2, w3, xs_ref, q_ref, kv_ref, w_s):
-    place_qkv(w_s, (w0, w1, w2, w3))
+def proj_kernel(x_ref, bq_ref, bv_ref, w0, w1, w2, w3, w4, w5, xs_ref, q_ref, kv_ref, w_s):
+    place_qkv(w_s, (w0, w1, w2, w3, w4, w5))
     xs = x_ref[...].astype(bf16)
     xs_ref[...] = xs
     q_ref[...] = (dot(xs, w_s[:, :D]) + bq_ref[...]).astype(bf16)
@@ -401,13 +410,13 @@
 
 
 def post_kernel(
-    o_ref, x_ref, vec_ref, b1_ref, a0, a1, a2, a3,
+    o_ref, x_ref, vec_ref, b1_ref, a0, a1, a2, a3, a4, a5,
     n1_ref, i1_ref, y_ref, hid_ref, slope_ref, n2_ref, i2_ref, x2_ref,
     wo_s, w1_s, w2_s,
 ):
-    place_blocks(wo_s, (a0, a1, a2, a3), 0, 1, 4, BLK, 0)
-    place_blocks(w1_s, (a0, a1, a2, a3), 4, 4, 4, 0, D)
-    place_blocks(w2_s, (a0, a1, a2, a3), 20, 4, 4, D, 0)
+    place_blocks(wo_s, (a0, a1, a2, a3, a4, a5), 0, 1, 4, BLK, 0)
+    place_blocks(w1_s, (a0, a1, a2, a3, a4, a5), 4, 4, 4, 0, D)
+    place_blocks(w2_s, (a0, a1, a2, a3, a4, a5), 20, 4, 4, D, 0)
 
     def tile(t, c):
         at = pl.ds(t * ROW_TILE, ROW_TILE)
@@ -469,14 +478,14 @@
 
 def ffn_grad_kernel(
     e_ref, n2_ref, i2_ref, n1_ref, i1_ref, y_ref, hid_ref, slope_ref, o_ref, vec_ref,
-    a0, a1, a2, a3,
+    a0, a1, a2, a3, a4, a5,
     gk_ref, gs_ref, ok_ref, os_ref, dr1_ref, do_ref, db1_ref, sums_ref,
     wo_s, w1_s, w2_s, dr2_s, dfr_s, dpre_s, dar_s,
 ):
     rows = e_ref.shape[0]
-    place_blocks(wo_s, (a0, a1, a2, a3), 0, 1, 4, BLK, 0)
-    place_blocks(w1_s, (a0, a1, a2, a3), 4, 4, 4, 0, D)
-    place_blocks(w2_s, (a0, a1, a2, a3), 20, 4, 4, D, 0)
+    place_blocks(wo_s, (a0, a1, a2, a3, a4, a5), 0, 1, 4, BLK, 0)
+    place_blocks(w1_s, (a0, a1, a2, a3, a4, a5), 4, 4, 4, 0, D)
+    place_blocks(w2_s, (a0, a1, a2, a3, a4, a5), 20, 4, 4, D, 0)
     tiles = rows // ROW_TILE
     gain_two = vec_ref[4:5, :]
     gain_one = vec_ref[1:2, :]
@@ -645,9 +654,10 @@
 
 
 def proj_grad_kernel(
-    dq_ref, dkv_ref, dkvr_ref, xs_ref, dr1_ref, w0, w1, w2, w3, gk_ref, gs_ref, dx_ref, sums_ref, w_s
+    dq_ref, dkv_ref, dkvr_ref, xs_ref, dr1_ref, w0, w1, w2, w3, w4, w5,
+    gk_ref, gs_ref, dx_ref, sums_ref, w_s,
 ):
-    place_qkv(w_s, (w0, w1, w2, w3))
+    place_qkv(w_s, (w0, w1, w2, w3, w4, w5))
     dq = dq_ref[...]
     dkv = (dkv_ref[...].astype(f32) + dkvr_ref[...].astype(f32)).astype(bf16)
     xs = xs_ref[...]
@@ -774,29 +784,34 @@
     slots, outs, held = refs[:count], refs[count:-1], refs[-1]
     for ref, start in zip(slots, plan):
         held[start : start + ref.shape[0]] = ref[...]
-    for i, out in enumerate(outs):
-        plane, rest = divmod(i, len(HELD) * LAYERS)
-        layer, part = divmod(rest, len(HELD))
+    for i in range(len(HELD) * LAYERS):
+        layer, part = divmod(i, len(HELD))
         first, n = HELD[part]
         for j in range(n):
-            out[j] = held[at_ref[plane * 96 + layer * 48 + first + j]]
-
-
-def natural_order(at, slots, plan):
+            block = held[at_ref[layer * 48 + first + j]]
+            outs[i][j] = block
+            if len(outs) > len(HELD) * LAYERS:
+                outs[len(HELD) * LAYERS + i][j] = block[TOP:]
+
+
+def natural_order(at, slots, plan, lower):
     total = sum(s.shape[0] for s in slots)
+    rows = slots[0].shape[1]
     spec = pl.BlockSpec(memory_space=pltpu.VMEM)
+    heights = (rows, BLK - TOP) if lower else (rows,)
     return pl.pallas_call(
         functools.partial(natural_kernel, plan),
         in_specs=[pl.BlockSpec(memory_space=pltpu.SMEM)] + [spec] * len(slots),
         out_shape=[
-            shape((n, BLK, BLK), bf16)
-            for _ in range(at.shape[0] // 96 * LAYERS)
+            shape((n, height, BLK), bf16)
+            for height in heights
+            for _ in range(LAYERS)
             for _, n in HELD
         ],
-        scratch_shapes=[pltpu.VMEM((total, BLK, BLK), bf16)],
+        scratch_shapes=[pltpu.VMEM((total, rows, BLK), bf16)],
         compiler_params=params(MIB["natural"]),
         name="natural",
-        cost_estimate=cost(4),
+        cost_estimate=cost(3),
     )(at, *slots)
 
 
@@ -838,15 +853,28 @@
 def ring_gather(value, order):
     n = len(order)
     half = value.shape[0] // 2
+
+    def top(items):
+        return [(far_swap(array[:, :TOP]), k, start) for array, k, start in items]
+
     held = [(value, 0, 0)]
+    far = top(held)
+    crossing = far
     ahead = behind = value
     for step in range(1, n // 2):
+        if step > 1:
+            behind, ahead = tied((behind, ahead), [x[0] for x in crossing])
+            crossing = top(held[-2:])
+            far = far + crossing
         behind = ring_shift(behind, order, 1)
         ahead = ring_shift(ahead, order, -1)
         held += [(behind, n - step, 0), (ahead, step, 0)]
+    behind, ahead = tied((behind, ahead), [x[0] for x in crossing])
+    far = far + top(held[-2:])
     held.append((ring_shift(behind[:half], order, 1), n // 2, 0))
     held.append((ring_shift(ahead[half:], order, -1), n // 2, half))
-    return held
+    far = far + top(held[-2:])
+    return held, far
 
 
 def ring_reduce(pieces, order, meanwhile):
@@ -940,10 +968,13 @@
 
     copies = master[0].astype(bf16)
     if ringed:
-        held = ring_gather(copies, order)
+        held, far = ring_gather(copies, order)
         slots, plan = [x[0] for x in held], tuple(x[1] * own_slots + x[2] for x in held)
+        tops, far_plan = [x[0] for x in far], tuple(x[1] * own_slots + x[2] for x in far)
     else:
         slots, plan = [lax.all_gather(copies, "dp", axis=0, tiled=True)], (0,)
+        tops, far_plan = [far_swap(slots[0][:, :TOP])], (0,)
+    far_at = far_swap(gather_at)
     windows = window_ids(window_lengths, bucket_rows)
     ids = windows.reshape(4, rows)
     own_ids = lax.dynamic_index_in_dim(ids, place, 0, False)
@@ -959,20 +990,24 @@
         vec = jnp.stack([bo, g1, c1, b2, g2, c2, g2, c2])
         vectors.append([vec] + [relative(row, place) for row in (bq, bv, b1)])
     grad = cotangent * valid
-    slots, (x, vectors, ohq, ohk, valid, gather_at, grad) = lax.optimization_barrier(
-        (slots, (x, vectors, ohq, ohk, valid, gather_at, grad))
-    )
-    mine = natural_order(gather_at, slots, plan)
+    slots, (x, vectors, ohq, ohk, valid, gather_at, far_at, grad) = lax.optimization_barrier(
+        (slots, (x, vectors, ohq, ohk, valid, gather_at, far_at, grad))
+    )
+    mine = natural_order(gather_at, slots, plan, True)
+    mine, lower = mine[: len(HELD) * LAYERS], mine[len(HELD) * LAYERS :]
+    upper = natural_order(far_at, tops, far_plan, False)
     moved = []
 
     def cross(i, after=None):
-        own = mine[i] if after is None else tied(mine[i], after)
+        own = lower[i] if after is None else tied(lower[i], after)
         moved.append(far_swap(own))
         return moved[-1]
 
     def four(i, after=None):
         there = moved[i] if after is None else tied(moved[i], after)
-        return [mine[i], core_swap(mine[i]), there, core_swap(there)]
+        return [
+            mine[i], core_swap(mine[i]), upper[i], there, core_swap(upper[i]), core_swap(there)
+        ]
 
     weights = []
     saved = []

time: 313 us -> 304 us (0.971)
  waiting for transfers between devices: 121 us -> 88.8 us
  starting transfers between devices: 42 us -> 53.3 us
  local copies, waits for them, and re-layouts: 19.3 us -> 24 us
    ppermute x16, waiting for transfers between devices: 35.3 us -> 15.8 us  [ring_shift(): lax.ppermute(value, 'dp', [(order[i], order[(i + by) % n]) for i in range...]
    ppermute x12 -> x22, starting transfers between devices: 14.8 us -> 24.9 us  [far_swap(): return lax.ppermute(value, 'head', [(i, i ^ 2) for i in range(4)])]
    ppermute x12 -> x22, waiting for transfers between devices: 61.4 us -> 51.9 us  [far_swap(): return lax.ppermute(value, 'head', [(i, i ^ 2) for i in range(4)])]
    ppermute x21 -> x25, waiting for transfers between devices: 18.9 us -> 15.8 us  [core_swap(): return lax.ppermute(value, 'head', [(i, i ^ 1) for i in range(4)])]
    unnamed x84 -> x132, local copies, waits for them, and re-layouts: 12.3 us -> 15.1 us
  transfers between devices with their start and end apart: 52 -> 66, of which waited for: 33 -> 33; matrix products, arithmetic and copies ran while one was open for 5% -> 8% of each run, Pallas kernels for 22% -> 23%
where the time goes in v7:
time: 304 us; the launch traced here: 298 us
  Pallas kernels  117 us (38%)
  waiting for transfers between devices  88.8 us (29%)
  starting transfers between devices  53.3 us (18%)
  local copies, waits for them, and re-layouts  24 us (8%)
  other arithmetic  13.3 us (4%)
    ppermute x22, waiting for transfers between devices, far_swap(): return lax.ppermute(value, 'head', [(i, i ^ 2) for i in range(4)])  51.9 us
    pallas_call x1, Pallas kernels, soap(): pl.pallas_call(functools.partial(soap_kernel, len(gs)), grid=(n // group,...  33.2 us
    pallas_call x2, Pallas kernels, attend_grad(): pl.pallas_call(attend_grad_kernel, grid=(D // LANES,), in_specs=[pair, bo...  30.4 us
    ppermute x22, starting transfers between devices, far_swap(): return lax.ppermute(value, 'head', [(i, i ^ 2) for i in range(4)])  24.9 us
    pallas_call x2, Pallas kernels, attend(): pl.pallas_call(attend_kernel, grid=(D // LANES,), in_specs=[pair, both, o...  18.2 us
    ppermute x16, starting transfers between devices, ring_shift(): lax.ppermute(value, 'dp', [(order[i], order[(i + by) % n]) for i in range...  17.8 us
    ppermute x25, waiting for transfers between devices, core_swap(): return lax.ppermute(value, 'head', [(i, i ^ 1) for i in range(4)])  15.8 us
    ppermute x16, waiting for transfers between devices, ring_shift(): lax.ppermute(value, 'dp', [(order[i], order[(i + by) % n]) for i in range...  15.8 us
  transfers between devices with their start and end apart: 66, of which 33 were waited for; matrix products, arithmetic and copies ran while one was open for 8% of the time, Pallas kernels for 23%

profile of v7, /device:TPU:0, one launch (start us, length us, event | category | flops | bytes accessed | tf_op | source)
XLA Modules:
  0.0 298.3 jit_solution(7409226441782495280)
XLA Ops:
  1.9 3.0 %collective-permute-start.1 = (bf16[12,128,128]{2,1,0:T(8,128)(2,1)S(1)}, bf16[12,128,128]{2,1,0:T(8,128)(2,1)S(1)}, u32[]{:S(2)}, u32[]{:S(2)}) collective-permute-start(bf16[12,128,128]{2,1,0:T(8,128)(2,1)S(1)} %bitcast_convert_fusion.refs_0_), channel_id=1, source_target_pairs={{0,4},{8,0},{16,8},{24,16},{28,24},{20,28},{12,20},{4,12},{1,5},{9... | collective-permute-start | bytes 1179656 | tf_op jit(solution)/shard_map/ppermute | solution.py:850
  22.4 5.2 %collective-permute-done.6.refs_2_ = bf16[12,64,128]{2,1,0:T(8,128)(2,1)S(1)} collective-permute-done((bf16[12,64,128]{2,1,0:T(8,128)(2,1)S(1)}, bf16[12,64,128]{2,1,0:T(8,128)(2,1)S(1)}, u32[]{:S(2)}, u32[]{:S(2)}) %collective-permute-start.6) | collective-permute-done | bytes 196640 | tf_op jit(solution)/shard_map/ppermute | solution.py:918
  34.7 3.1 %collective-permute-done.9.refs_3_ = bf16[12,64,128]{2,1,0:T(8,128)(2,1)S(1)} collective-permute-done((bf16[12,64,128]{2,1,0:T(8,128)(2,1)S(1)}, bf16[12,64,128]{2,1,0:T(8,128)(2,1)S(1)}, u32[]{:S(2)}, u32[]{:S(2)}) %collective-permute-start.9) | collective-permute-done | bytes 196640 | tf_op jit(solution)/shard_map/ppermute | solution.py:918
  37.8 2.1 collective-permute-done.10.refs_4_
  56.7 3.6 %collective-permute-done.18.refs_8_ = bf16[6,64,128]{2,1,0:T(8,128)(2,1)S(1)} collective-permute-done((bf16[6,64,128]{2,1,0:T(8,128)(2,1)S(1)}, bf16[6,64,128]{2,1,0:T(8,128)(2,1)S(1)}, u32[]{:S(2)}, u32[]{:S(2)}) %collective-permute-start.18) | collective-permute-done | bytes 98336 | tf_op jit(solution)/shard_map/ppermute | solution.py:918
  69.0 9.2 %attend.2 = (bf16[512,512]{1,0:T(8,128)(2,1)S(1)}, f32[512,512]{1,0:T(8,128)S(1)}) custom-call(bf16[512,512]{1,0:T(8,128)(2,1)S(1)} %get-tuple-element.200.q_ref, bf16[512,1024]{1,0:T(8,128)(2,1)S(1)} %get-tuple-element.201.kv_ref, bf16[512,1024]{1,0:T(8,128)(2,1)S(1)} %collective-permute-done.22.kvp_ref, bf16[512,128]{1,0:T(8,128)(2,1)S(1)} %get-tuple-element.202.ohq_ref, ...), custom_call_target="tpu_custom_call" | custom-call | flops 11000000 | tf_op jit(solution)/shard_map/attend/pallas_call | solution.py:392
  78.2 3.8 %collective-permute-done.24.a3 = bf16[36,64,128]{2,1,0:T(8,128)(2,1)S(1)} collective-permute-done((bf16[36,64,128]{2,1,0:T(8,128)(2,1)S(1)}, bf16[36,64,128]{2,1,0:T(8,128)(2,1)S(1)}, u32[]{:S(2)}, u32[]{:S(2)}) %collective-permute-start.24) | collective-permute-done | bytes 589856 | tf_op jit(solution)/shard_map/ppermute | solution.py:918
  84.1 4.4 %post.2 = (f32[512,512]{1,0:T(8,128)S(1)}, f32[512,128]{1,0:T(8,128)S(1)}, bf16[512,512]{1,0:T(8,128)(2,1)S(1)}, bf16[512,2048]{1,0:T(8,128)(2,1)S(1)}, bf16[512...) custom-call(bf16[512,512]{1,0:T(8,128)(2,1)S(1)} %get-tuple-element.204.o_ref, ...), custom_call_target="tpu_custom_call" | custom-call | flops 11000000 | tf_op jit(solution)/shard_map/post/pallas_call | solution.py:448
  96.3 8.9 %attend.3 = (bf16[512,512]{1,0:T(8,128)(2,1)S(1)}, f32[512,512]{1,0:T(8,128)S(1)}) custom-call(bf16[512,512]{1,0:T(8,128)(2,1)S(1)} %get-tuple-element.221.q_ref, bf16[512,1024]{1,0:T(8,128)(2,1)S(1)} %get-tuple-element.222.kv_ref, bf16[512,1024]{1,0:T(8,128)(2,1)S(1)} %collective-permute-done.31.kvp_ref, bf16[512,128]{1,0:T(8,128)(2,1)S(1)} %get-tuple-element.202.ohq_ref, ...), custom_call_target="tpu_custom_call" | custom-call | flops 11000000 | tf_op jit(solution)/shard_map/attend/pallas_call | solution.py:392
  105.2 4.1 %collective-permute-done.33.a3 = bf16[36,64,128]{2,1,0:T(8,128)(2,1)S(1)} collective-permute-done((bf16[36,64,128]{2,1,0:T(8,128)(2,1)S(1)}, bf16[36,64,128]{2,1,0:T(8,128)(2,1)S(1)}, u32[]{:S(2)}, u32[]{:S(2)}) %collective-permute-start.33) | collective-permute-done | bytes 589856 | tf_op jit(solution)/shard_map/ppermute | solution.py:918
  111.3 4.3 %post.3 = (f32[512,512]{1,0:T(8,128)S(1)}, f32[512,128]{1,0:T(8,128)S(1)}, bf16[512,512]{1,0:T(8,128)(2,1)S(1)}, bf16[512,2048]{1,0:T(8,128)(2,1)S(1)}, bf16[512...) custom-call(bf16[512,512]{1,0:T(8,128)(2,1)S(1)} %get-tuple-element.223.o_ref, ...), custom_call_target="tpu_custom_call" | custom-call | flops 11000000 | tf_op jit(solution)/shard_map/post/pallas_call | solution.py:448
  118.6 6.2 %ffn_grad.2 = (bf16[2,16,128,128]{3,2,1,0:T(8,128)(2,1)S(1)}, bf16[2,16,128,128]{3,2,1,0:T(8,128)(2,1)S(1)}, bf16[2,20,128,128]{3,2,1,0:T(8,128)(2,1)S(1)}, bf16...) custom-call(f32[512,512]{1,0:T(8,128)S(1)} %broadcast_multiply_fusio, ...), custom_call_target="tpu_custom_call" | custom-call | flops 16000000 | tf_op jit(solution)/shard_map/ffn_grad/pallas_call | solution.py:541
  125.4 2.5 collective-permute-done.36
  129.8 15.1 %attend_grad.2 = (bf16[512,512]{1,0:T(8,128)(2,1)S(1)}, bf16[512,1024]{1,0:T(8,128)(2,1)S(1)}, bf16[512,1024]{1,0:T(8,128)(2,1)S(1)}) custom-call(bf16[512,512]{1,0:T(8,128)(2,1)S(1)} %get-tuple-element.221.q_ref, bf16[512,1024]{1,0:T(8,128)(2,1)S(1)} %get-tuple-element.222.kv_ref, bf16[512,1024]{1,0:T(8,128)(2,1)S(1)} %collective-permute-done.31.kvp_ref, ...), custom_call_target="tpu_custom_call" | custom-call | flops 23000000 | tf_op jit(solution)/shard_map/attend_grad/pallas_call | solution.py:633
  145.0 2.6 collective-permute-done.39.dkvr_ref
  153.7 6.3 %ffn_grad.3 = (bf16[2,16,128,128]{3,2,1,0:T(8,128)(2,1)S(1)}, bf16[2,16,128,128]{3,2,1,0:T(8,128)(2,1)S(1)}, bf16[2,20,128,128]{3,2,1,0:T(8,128)(2,1)S(1)}, bf16...) custom-call(f32[512,512]{1,0:T(8,128)S(1)} %get-tuple-element.262.e_, ...), custom_call_target="tpu_custom_call" | custom-call | flops 16000000 | tf_op jit(solution)/shard_map/ffn_grad/pallas_call | solution.py:541
  159.9 4.6 %collective-permute-done.42.refs_11_ = bf16[16,128,128]{2,1,0:T(8,128)(2,1)S(1)} collective-permute-done((bf16[16,128,128]{2,1,0:T(8,128)(2,1)S(1)}, bf16[16,128,128]{2,1,0:T(8,128)(2,1)S(1)}, u32[]{:S(2)}, u32[]{:S(2)}) %collective-permute-start.42) | collective-permute-done | bytes 524320 | tf_op jit(solution)/shard_map/ppermute | solution.py:918
  164.6 7.9 %collective-permute-done.41.refs_9_ = bf16[12,128,128]{2,1,0:T(8,128)(2,1)S(1)} collective-permute-done((bf16[12,128,128]{2,1,0:T(8,128)(2,1)S(1)}, bf16[12,128,128]{2,1,0:T(8,128)(2,1)S(1)}, u32[]{:S(2)}, u32[]{:S(2)}) %collective-permute-start.41) | collective-permute-done | bytes 393248 | tf_op jit(solution)/shard_map/ppermute | solution.py:918
  173.4 2.1 collective-permute-done.43
  178.4 15.3 %attend_grad.3 = (bf16[512,512]{1,0:T(8,128)(2,1)S(1)}, bf16[512,1024]{1,0:T(8,128)(2,1)S(1)}, bf16[512,1024]{1,0:T(8,128)(2,1)S(1)}) custom-call(bf16[512,512]{1,0:T(8,128)(2,1)S(1)} %get-tuple-element.200.q_ref, bf16[512,1024]{1,0:T(8,128)(2,1)S(1)} %get-tuple-element.201.kv_ref, bf16[512,1024]{1,0:T(8,128)(2,1)S(1)} %collective-permute-done.22.kvp_ref, ...), custom_call_target="tpu_custom_call" | custom-call | flops 23000000 | tf_op jit(solution)/shard_map/attend_grad/pallas_call | solution.py:633
  202.9 2.6 collective-permute-done.53
  207.3 2.7 collective-permute-done.54
  210.9 8.7 %collective-permute-done.48.refs_6_ = bf16[12,128,128]{2,1,0:T(8,128)(2,1)S(1)} collective-permute-done((bf16[12,128,128]{2,1,0:T(8,128)(2,1)S(1)}, bf16[12,128,128]{2,1,0:T(8,128)(2,1)S(1)}, u32[]{:S(2)}, u32[]{:S(2)}) %collective-permute-start.48) | collective-permute-done | bytes 393248 | tf_op jit(solution)/shard_map/ppermute | solution.py:918
  219.6 2.6 collective-permute-start.55
  226.0 3.6 %collective-permute-done.51 = bf16[768,128]{1,0:T(8,128)(2,1)S(1)} collective-permute-done((bf16[768,128]{1,0:T(8,128)(2,1)S(1)}, bf16[768,128]{1,0:T(8,128)(2,1)S(1)}, u32[]{:S(2)}, u32[]{:S(2)}) %collective-permute-start.51) | collective-permute-done | bytes 196640 | tf_op jit(solution)/shard_map/ppermute | solution.py:850
  229.6 2.9 collective-permute-done.50
  232.8 2.0 collective-permute-start.57
  235.5 3.7 %collective-permute-done.58 = f32[128,128]{1,0:T(8,128)S(1)} collective-permute-done((f32[128,128]{1,0:T(8,128)S(1)}, f32[128,128]{1,0:T(8,128)S(1)}, u32[]{:S(2)}, u32[]{:S(2)}) %collective-permute-start.58) | collective-permute-done | bytes 65568 | tf_op jit(solution)/shard_map/ppermute | solution.py:918
  239.1 2.5 collective-permute-done.56
  242.7 2.0 collective-permute-start.60
  257.7 4.9 %collective-permute-done.64 = bf16[1536,128]{1,0:T(8,128)(2,1)S(1)} collective-permute-done((bf16[1536,128]{1,0:T(8,128)(2,1)S(1)}, bf16[1536,128]{1,0:T(8,128)(2,1)S(1)}, u32[]{:S(2)}, u32[]{:S(2)}) %collective-permute-start.64) | collective-permute-done | bytes 393248 | tf_op jit(solution)/shard_map/ppermute | solution.py:850
  264.9 33.2 %soap.1 = (f32[12,128,128]{2,1,0:T(8,128)}, bf16[12,128,128]{2,1,0:T(8,128)(2,1)}, f32[12,128,128]{2,1,0:T(8,128)}, f32[12,128,128]{2,1,0:T(8,128)}, f32[12,128,...) custom-call(bf16[12,128,128]{2,1,0:T(8,128)(2,1)S(1)} %bitcast.158, ...), custom_call_target="tpu_custom_call" | custom-call | flops 40000000 | tf_op jit(solution)/shard_map/soap/pallas_call | solution.py:208
  (330 shorter events, 110.5 us)
Async XLA Ops:
  1.9 16.0 %collective-permute-start.1 = (bf16[12,128,128]{2,1,0:T(8,128)(2,1)S(1)}, bf16[12,128,128]{2,1,0:T(8,128)(2,1)S(1)}, u32[]{:S(2)}, u32[]{:S(2)}) collective-permute-start(bf16[12,128,128]{2,1,0:T(8,128)(2,1)S(1)} %bitcast_convert_fusion.refs_0_), channel_id=1, source_target_pairs={{0,4},{8,0},{16,8},{24,16},{28,24},{20,28},{12,20},{4,12},{1,5},{9... | collective-permute-start | bytes 1179656 | tf_op jit(solution)/shard_map/ppermute | solution.py:850
  4.9 13.0 %collective-permute-start = (bf16[12,128,128]{2,1,0:T(8,128)(2,1)S(1)}, bf16[12,128,128]{2,1,0:T(8,128)(2,1)S(1)}, u32[]{:S(2)}, u32[]{:S(2)}) collective-permute-start(bf16[12,128,128]{2,1,0:T(8,128)(2,1)S(1)} %bitcast_convert_fusion.refs_0_), channel_id=1, source_target_pairs={{0,8},{8,16},{16,24},{24,28},{28,20},{20,12},{12,4},{4,0},{1,9},{9... | collective-permute-start | bytes 1179656 | tf_op jit(solution)/shard_map/ppermute | solution.py:850
  8.2 42.1 %collective-permute-start.13 = (s32[96]{0:T(128)}, s32[96]{0:T(128)}, u32[]{:S(2)}, u32[]{:S(2)}) collective-permute-start(s32[96]{0:T(128)} %get-tuple-element.183.at_ref), channel_id=1, source_target_pairs={{0,2},{1,3},{2,0},{3,1},{4,6},{5,7},{6,4},{7,5},{8,10},{9,11},{10,... | collective-permute-start | bytes 1160 | tf_op jit(solution)/shard_map/ppermute | solution.py:918
  10.1 7.7 %collective-permute-start.2 = (bf16[12,64,128]{2,1,0:T(8,128)(2,1)S(1)}, bf16[12,64,128]{2,1,0:T(8,128)(2,1)S(1)}, u32[]{:S(2)}, u32[]{:S(2)}) collective-permute-start(bf16[12,64,128]{2,1,0:T(8,128)(2,1)S(1)} %slice.309), channel_id=1, source_target_pairs={{0,2},{1,3},{2,0},{3,1},{4,6},{5,7},{6,4},{7,5},{8,10},{9,11},{10,... | collective-permute-start | bytes 589832 | tf_op jit(solution)/shard_map/ppermute | solution.py:918
  17.9 11.8 %collective-permute-start.3 = (bf16[12,128,128]{2,1,0:T(8,128)(2,1)S(1)}, bf16[12,128,128]{2,1,0:T(8,128)(2,1)S(1)}, u32[]{:S(2)}, u32[]{:S(2)}) collective-permute-start(bf16[12,128,128]{2,1,0:T(8,128)(2,1)S(1)} %collective-permute-done.refs_1_), channel_id=1, source_target_pairs={{0,8},{8,16},{16,24},{24,28},{28,20},{20,12},{12,4},{4,0},{1,9},{9... | collective-permute-start | bytes 1179656 | tf_op jit(solution)/shard_map/ppermute | solution.py:850
  19.9 9.8 %collective-permute-start.4 = (bf16[12,128,128]{2,1,0:T(8,128)(2,1)S(1)}, bf16[12,128,128]{2,1,0:T(8,128)(2,1)S(1)}, u32[]{:S(2)}, u32[]{:S(2)}) collective-permute-start(bf16[12,128,128]{2,1,0:T(8,128)(2,1)S(1)} %collective-permute-done.1.refs_2_), channel_id=1, source_target_pairs={{0,4},{8,0},{16,8},{24,16},{28,24},{20,28},{12,20},{4,12},{1,5},{9... | collective-permute-start | bytes 1179656 | tf_op jit(solution)/shard_map/ppermute | solution.py:850
  29.8 10.1 %collective-permute-start.7 = (bf16[12,128,128]{2,1,0:T(8,128)(2,1)S(1)}, bf16[12,128,128]{2,1,0:T(8,128)(2,1)S(1)}, u32[]{:S(2)}, u32[]{:S(2)}) collective-permute-start(bf16[12,128,128]{2,1,0:T(8,128)(2,1)S(1)} %collective-permute-done.3.refs_3_), channel_id=1, source_target_pairs={{0,8},{8,16},{16,24},{24,28},{28,20},{20,12},{12,4},{4,0},{1,9},{9... | collective-permute-start | bytes 1179656 | tf_op jit(solution)/shard_map/ppermute | solution.py:850
  31.5 8.4 %collective-permute-start.8 = (bf16[12,128,128]{2,1,0:T(8,128)(2,1)S(1)}, bf16[12,128,128]{2,1,0:T(8,128)(2,1)S(1)}, u32[]{:S(2)}, u32[]{:S(2)}) collective-permute-start(bf16[12,128,128]{2,1,0:T(8,128)(2,1)S(1)} %collective-permute-done.4.refs_4_), channel_id=1, source_target_pairs={{0,4},{8,0},{16,8},{24,16},{28,24},{20,28},{12,20},{4,12},{1,5},{9... | collective-permute-start | bytes 1179656 | tf_op jit(solution)/shard_map/ppermute | solution.py:850
  41.4 8.9 %collective-permute-start.12 = (bf16[6,128,128]{2,1,0:T(8,128)(2,1)}, bf16[6,128,128]{2,1,0:T(8,128)(2,1)}, u32[]{:S(2)}, u32[]{:S(2)}) collective-permute-start(bf16[6,128,128]{2,1,0:T(8,128)(2,1)} %slice.228), channel_id=1, source_target_pairs={{0,4},{8,0},{16,8},{24,16},{28,24},{20,28},{12,20},{4,12},{1,5},{9... | collective-permute-start | bytes 589832 | tf_op jit(solution)/shard_map/ppermute | solution.py:850
  44.1 11.0 %collective-permute-start.15 = (bf16[12,64,128]{2,1,0:T(8,128)(2,1)}, bf16[12,64,128]{2,1,0:T(8,128)(2,1)}, u32[]{:S(2)}, u32[]{:S(2)}) collective-permute-start(bf16[12,64,128]{2,1,0:T(8,128)(2,1)} %slice.314), channel_id=1, source_target_pairs={{0,2},{1,3},{2,0},{3,1},{4,6},{5,7},{6,4},{7,5},{8,10},{9,11},{10,... | collective-permute-start | bytes 589832 | tf_op jit(solution)/shard_map/ppermute | solution.py:918
  52.2 11.2 %collective-permute-start.19 = (bf16[12,64,128]{2,1,0:T(8,128)(2,1)S(1)}, bf16[12,64,128]{2,1,0:T(8,128)(2,1)S(1)}, u32[]{:S(2)}, u32[]{:S(2)}) collective-permute-start(bf16[12,64,128]{2,1,0:T(8,128)(2,1)S(1)} %get-tuple-element.196), channel_id=1, source_target_pairs={{0,2},{1,3},{2,0},{3,1},{4,6},{5,7},{6,4},{7,5},{8,10},{9,11},{10,... | collective-permute-start | bytes 589832 | tf_op jit(solution)/shard_map/ppermute | solution.py:918
  53.7 11.4 %collective-permute-start.14 = (bf16[12,128,128]{2,1,0:T(8,128)(2,1)S(1)}, bf16[12,128,128]{2,1,0:T(8,128)(2,1)S(1)}, u32[]{:S(2)}, u32[]{:S(2)}) collective-permute-start(bf16[12,128,128]{2,1,0:T(8,128)(2,1)S(1)} %get-tuple-element.193.w0), channel_id=1, source_target_pairs={{0,1},{1,0},{2,3},{3,2},{4,5},{5,4},{6,7},{7,6},{8,9},{9,8},{10,11... | collective-permute-start | bytes 1179656 | tf_op jit(solution)/shard_map/ppermute | solution.py:914
  66.5 15.5 %collective-permute-start.24 = (bf16[36,64,128]{2,1,0:T(8,128)(2,1)S(1)}, bf16[36,64,128]{2,1,0:T(8,128)(2,1)S(1)}, u32[]{:S(2)}, u32[]{:S(2)}) collective-permute-start(bf16[36,64,128]{2,1,0:T(8,128)(2,1)S(1)} %get-tuple-element.210), channel_id=1, source_target_pairs={{0,2},{1,3},{2,0},{3,1},{4,6},{5,7},{6,4},{7,5},{8,10},{9,11},{10,... | collective-permute-start | bytes 1769480 | tf_op jit(solution)/shard_map/ppermute | solution.py:918
  68.0 16.0 %collective-permute-start.23 = (bf16[36,128,128]{2,1,0:T(8,128)(2,1)S(1)}, bf16[36,128,128]{2,1,0:T(8,128)(2,1)S(1)}, u32[]{:S(2)}, u32[]{:S(2)}) collective-permute-start(bf16[36,128,128]{2,1,0:T(8,128)(2,1)S(1)} %get-tuple-element.207.a0), channel_id=1, source_target_pairs={{0,1},{1,0},{2,3},{3,2},{4,5},{5,4},{6,7},{7,6},{8,9},{9,8},{10,11... | collective-permute-start | bytes 3538952 | tf_op jit(solution)/shard_map/ppermute | solution.py:914
  68.0 15.7 %collective-permute-start.25 = (bf16[36,64,128]{2,1,0:T(8,128)(2,1)S(1)}, bf16[36,64,128]{2,1,0:T(8,128)(2,1)S(1)}, u32[]{:S(2)}, u32[]{:S(2)}) collective-permute-start(bf16[36,64,128]{2,1,0:T(8,128)(2,1)S(1)} %get-tuple-element.208.a2), channel_id=1, source_target_pairs={{0,1},{1,0},{2,3},{3,2},{4,5},{5,4},{6,7},{7,6},{8,9},{9,8},{10,11... | collective-permute-start | bytes 1769480 | tf_op jit(solution)/shard_map/ppermute | solution.py:914
  82.1 8.1 %collective-permute-start.28 = (bf16[12,64,128]{2,1,0:T(8,128)(2,1)S(1)}, bf16[12,64,128]{2,1,0:T(8,128)(2,1)S(1)}, u32[]{:S(2)}, u32[]{:S(2)}) collective-permute-start(bf16[12,64,128]{2,1,0:T(8,128)(2,1)S(1)} %get-tuple-element.216), channel_id=1, source_target_pairs={{0,2},{1,3},{2,0},{3,1},{4,6},{5,7},{6,4},{7,5},{8,10},{9,11},{10,... | collective-permute-start | bytes 589832 | tf_op jit(solution)/shard_map/ppermute | solution.py:918
  93.8 15.6 %collective-permute-start.33 = (bf16[36,64,128]{2,1,0:T(8,128)(2,1)S(1)}, bf16[36,64,128]{2,1,0:T(8,128)(2,1)S(1)}, u32[]{:S(2)}, u32[]{:S(2)}) collective-permute-start(bf16[36,64,128]{2,1,0:T(8,128)(2,1)S(1)} %get-tuple-element.229), channel_id=1, source_target_pairs={{0,2},{1,3},{2,0},{3,1},{4,6},{5,7},{6,4},{7,5},{8,10},{9,11},{10,... | collective-permute-start | bytes 1769480 | tf_op jit(solution)/shard_map/ppermute | solution.py:918
  95.2 14.2 %collective-permute-start.32 = (bf16[36,128,128]{2,1,0:T(8,128)(2,1)S(1)}, bf16[36,128,128]{2,1,0:T(8,128)(2,1)S(1)}, u32[]{:S(2)}, u32[]{:S(2)}) collective-permute-start(bf16[36,128,128]{2,1,0:T(8,128)(2,1)S(1)} %get-tuple-element.226.a0), channel_id=1, source_target_pairs={{0,1},{1,0},{2,3},{3,2},{4,5},{5,4},{6,7},{7,6},{8,9},{9,8},{10,11... | collective-permute-start | bytes 3538952 | tf_op jit(solution)/shard_map/ppermute | solution.py:914
  95.3 14.1 %collective-permute-start.34 = (bf16[36,64,128]{2,1,0:T(8,128)(2,1)S(1)}, bf16[36,64,128]{2,1,0:T(8,128)(2,1)S(1)}, u32[]{:S(2)}, u32[]{:S(2)}) collective-permute-start(bf16[36,64,128]{2,1,0:T(8,128)(2,1)S(1)} %get-tuple-element.227.a2), channel_id=1, source_target_pairs={{0,1},{1,0},{2,3},{3,2},{4,5},{5,4},{6,7},{7,6},{8,9},{9,8},{10,11... | collective-permute-start | bytes 1769480 | tf_op jit(solution)/shard_map/ppermute | solution.py:914
  128.1 16.8 %collective-permute-start.38 = (bf16[20,128,128]{2,1,0:T(8,128)(2,1)S(1)}, bf16[20,128,128]{2,1,0:T(8,128)(2,1)S(1)}, u32[]{:S(2)}, u32[]{:S(2)}) collective-permute-start(bf16[20,128,128]{2,1,0:T(8,128)(2,1)S(1)} %fusion.4), channel_id=1, source_target_pairs={{0,2},{1,3},{2,0},{3,1},{4,6},{5,7},{6,4},{7,5},{8,10},{9,11},{10,... | collective-permute-start | bytes 1966088 | tf_op jit(solution)/shard_map/ppermute | solution.py:918
  149.8 14.8 %collective-permute-start.42 = (bf16[16,128,128]{2,1,0:T(8,128)(2,1)S(1)}, bf16[16,128,128]{2,1,0:T(8,128)(2,1)S(1)}, u32[]{:S(2)}, u32[]{:S(2)}) collective-permute-start(bf16[16,128,128]{2,1,0:T(8,128)(2,1)S(1)} %fusion.6), channel_id=1, source_target_pairs={{0,2},{1,3},{2,0},{3,1},{4,6},{5,7},{6,4},{7,5},{8,10},{9,11},{10,... | collective-permute-start | bytes 1572872 | tf_op jit(solution)/shard_map/ppermute | solution.py:918
  152.1 20.4 %collective-permute-start.41 = (bf16[12,128,128]{2,1,0:T(8,128)(2,1)S(1)}, bf16[12,128,128]{2,1,0:T(8,128)(2,1)S(1)}, u32[]{:S(2)}, u32[]{:S(2)}) collective-permute-start(bf16[12,128,128]{2,1,0:T(8,128)(2,1)S(1)} %fusion.8), channel_id=1, source_target_pairs={{0,2},{1,3},{2,0},{3,1},{4,6},{5,7},{6,4},{7,5},{8,10},{9,11},{10,... | collective-permute-start | bytes 1179656 | tf_op jit(solution)/shard_map/ppermute | solution.py:918
  175.7 18.0 %collective-permute-start.45 = (bf16[20,128,128]{2,1,0:T(8,128)(2,1)S(1)}, bf16[20,128,128]{2,1,0:T(8,128)(2,1)S(1)}, u32[]{:S(2)}, u32[]{:S(2)}) collective-permute-start(bf16[20,128,128]{2,1,0:T(8,128)(2,1)S(1)} %fusion.5), channel_id=1, source_target_pairs={{0,2},{1,3},{2,0},{3,1},{4,6},{5,7},{6,4},{7,5},{8,10},{9,11},{10,... | collective-permute-start | bytes 1966088 | tf_op jit(solution)/shard_map/ppermute | solution.py:918
  194.1 28.1 %collective-permute-start.49 = (bf16[16,128,128]{2,1,0:T(8,128)(2,1)S(1)}, bf16[16,128,128]{2,1,0:T(8,128)(2,1)S(1)}, u32[]{:S(2)}, u32[]{:S(2)}) collective-permute-start(bf16[16,128,128]{2,1,0:T(8,128)(2,1)S(1)} %fusion.7), channel_id=1, source_target_pairs={{0,2},{1,3},{2,0},{3,1},{4,6},{5,7},{6,4},{7,5},{8,10},{9,11},{10,... | collective-permute-start | bytes 1572872 | tf_op jit(solution)/shard_map/ppermute | solution.py:918
  200.0 9.9 %collective-permute-start.47 = (bf16[2,12,128,128]{3,2,1,0:T(8,128)(2,1)S(1)}, bf16[2,12,128,128]{3,2,1,0:T(8,128)(2,1)S(1)}, u32[]{:S(2)}, u32[]{:S(2)}) collective-permute-start(bf16[2,12,128,128]{3,2,1,0:T(8,128)(2,1)S(1)} %get-tuple-element.298), channel_id=1, source_target_pairs={{0,1},{1,0},{2,3},{3,2},{4,5},{5,4},{6,7},{7,6},{8,9},{9,8},{10,11... | collective-permute-start | bytes 2359304 | tf_op jit(solution)/shard_map/ppermute | solution.py:914
  210.1 9.5 %collective-permute-start.48 = (bf16[12,128,128]{2,1,0:T(8,128)(2,1)S(1)}, bf16[12,128,128]{2,1,0:T(8,128)(2,1)S(1)}, u32[]{:S(2)}, u32[]{:S(2)}) collective-permute-start(bf16[12,128,128]{2,1,0:T(8,128)(2,1)S(1)} %fusion.9), channel_id=1, source_target_pairs={{0,2},{1,3},{2,0},{3,1},{4,6},{5,7},{6,4},{7,5},{8,10},{9,11},{10,... | collective-permute-start | bytes 1179656 | tf_op jit(solution)/shard_map/ppermute | solution.py:918
  232.7 8.9 %collective-permute-start.56 = (bf16[1536,128]{1,0:T(8,128)(2,1)S(1)}, bf16[1536,128]{1,0:T(8,128)(2,1)S(1)}, u32[]{:S(2)}, u32[]{:S(2)}) collective-permute-start(bf16[1536,128]{1,0:T(8,128)(2,1)S(1)} %pad_maximum_fusion), channel_id=1, source_target_pairs={{0,8},{8,16},{16,24},{24,28},{28,20},{20,12},{12,4},{4,0},{1,9},{9... | collective-permute-start | bytes 1179656 | tf_op jit(solution)/shard_map/ppermute | solution.py:850
  232.8 8.9 %collective-permute-start.57 = (bf16[1536,128]{1,0:T(8,128)(2,1)S(1)}, bf16[1536,128]{1,0:T(8,128)(2,1)S(1)}, u32[]{:S(2)}, u32[]{:S(2)}) collective-permute-start(bf16[1536,128]{1,0:T(8,128)(2,1)S(1)} %pad_maximum_fusion.1), channel_id=1, source_target_pairs={{0,4},{8,0},{16,8},{24,16},{28,24},{20,28},{12,20},{4,12},{1,5},{9... | collective-permute-start | bytes 1179656 | tf_op jit(solution)/shard_map/ppermute | solution.py:850
  242.7 8.1 %collective-permute-start.59 = (bf16[1536,128]{1,0:T(8,128)(2,1)}, bf16[1536,128]{1,0:T(8,128)(2,1)}, u32[]{:S(2)}, u32[]{:S(2)}) collective-permute-start(bf16[1536,128]{1,0:T(8,128)(2,1)} %get-tuple-element.317), channel_id=1, source_target_pairs={{0,8},{8,16},{16,24},{24,28},{28,20},{20,12},{12,4},{4,0},{1,9},{9... | collective-permute-start | bytes 1179656 | tf_op jit(solution)/shard_map/ppermute | solution.py:850
  242.7 8.1 %collective-permute-start.60 = (bf16[1536,128]{1,0:T(8,128)(2,1)}, bf16[1536,128]{1,0:T(8,128)(2,1)}, u32[]{:S(2)}, u32[]{:S(2)}) collective-permute-start(bf16[1536,128]{1,0:T(8,128)(2,1)} %get-tuple-element.318), channel_id=1, source_target_pairs={{0,4},{8,0},{16,8},{24,16},{28,24},{20,28},{12,20},{4,12},{1,5},{9... | collective-permute-start | bytes 1179656 | tf_op jit(solution)/shard_map/ppermute | solution.py:850
  252.3 10.3 %collective-permute-start.64 = (bf16[1536,128]{1,0:T(8,128)(2,1)S(1)}, bf16[1536,128]{1,0:T(8,128)(2,1)S(1)}, u32[]{:S(2)}, u32[]{:S(2)}) collective-permute-start(bf16[1536,128]{1,0:T(8,128)(2,1)S(1)} %get-tuple-element.319), channel_id=1, source_target_pairs={{0,8},{8,16},{16,24},{24,28},{28,20},{20,12},{12,4},{4,0},{1,9},{9... | collective-permute-start | bytes 1179656 | tf_op jit(solution)/shard_map/ppermute | solution.py:850
  252.7 9.9 %collective-permute-start.65 = (bf16[1536,128]{1,0:T(8,128)(2,1)S(1)}, bf16[1536,128]{1,0:T(8,128)(2,1)S(1)}, u32[]{:S(2)}, u32[]{:S(2)}) collective-permute-start(bf16[1536,128]{1,0:T(8,128)(2,1)S(1)} %get-tuple-element.320), channel_id=1, source_target_pairs={{0,4},{8,0},{16,8},{24,16},{28,24},{20,28},{12,20},{4,12},{1,5},{9... | collective-permute-start | bytes 1179656 | tf_op jit(solution)/shard_map/ppermute | solution.py:850
  (98 other events, 661.4 us)

commit v8 on v7

--- a/solution.py
+++ b/solution.py
@@ -862,10 +862,11 @@
     crossing = far
     ahead = behind = value
     for step in range(1, n // 2):
+        if step > 2:
+            behind, ahead = tied((behind, ahead), [x[0] for x in crossing])
         if step > 1:
-            behind, ahead = tied((behind, ahead), [x[0] for x in crossing])
-            crossing = top(held[-2:])
-            far = far + crossing
+            crossing = top(held[-2:]) if step > 2 else crossing + top(held[-2:])
+            far = far + crossing[-2:]
         behind = ring_shift(behind, order, 1)
         ahead = ring_shift(ahead, order, -1)
         held += [(behind, n - step, 0), (ahead, step, 0)]

time: 304 us -> 300 us (0.987)
  starting transfers between devices: 53.3 us -> 50.1 us
    ppermute x25, waiting for transfers between devices: 15.8 us -> 19 us  [core_swap(): return lax.ppermute(value, 'head', [(i, i ^ 1) for i in range(4)])]
    ppermute x22, starting transfers between devices: 24.9 us -> 21.8 us  [far_swap(): return lax.ppermute(value, 'head', [(i, i ^ 2) for i in range(4)])]
    unnamed x132 -> x140, local copies, waits for them, and re-layouts: 15.1 us -> 15.5 us
  transfers between devices with their start and end apart: 66 -> 66, of which waited for: 33 -> 36; matrix products, arithmetic and copies ran while one was open for 8% -> 7% of each run, Pallas kernels for 23% -> 23%
where the time goes in v8:
time: 300 us; the launch traced here: 295 us
  Pallas kernels  117 us (39%)
  waiting for transfers between devices  89.5 us (30%)
  starting transfers between devices  50.1 us (17%)
  local copies, waits for them, and re-layouts  23.7 us (8%)
  other arithmetic  12.7 us (4%)
    ppermute x22, waiting for transfers between devices, far_swap(): return lax.ppermute(value, 'head', [(i, i ^ 2) for i in range(4)])  49.4 us
    pallas_call x1, Pallas kernels, soap(): pl.pallas_call(functools.partial(soap_kernel, len(gs)), grid=(n // group,...  33.2 us
    pallas_call x2, Pallas kernels, attend_grad(): pl.pallas_call(attend_grad_kernel, grid=(D // LANES,), in_specs=[pair, bo...  30.5 us
    ppermute x22, starting transfers between devices, far_swap(): return lax.ppermute(value, 'head', [(i, i ^ 2) for i in range(4)])  21.8 us
    ppermute x25, waiting for transfers between devices, core_swap(): return lax.ppermute(value, 'head', [(i, i ^ 1) for i in range(4)])  19 us
    pallas_call x2, Pallas kernels, attend(): pl.pallas_call(attend_kernel, grid=(D // LANES,), in_specs=[pair, both, o...  18.2 us
    ppermute x16, starting transfers between devices, ring_shift(): lax.ppermute(value, 'dp', [(order[i], order[(i + by) % n]) for i in range...  17.8 us
    ppermute x16, waiting for transfers between devices, ring_shift(): lax.ppermute(value, 'dp', [(order[i], order[(i + by) % n]) for i in range...  15.8 us
  transfers between devices with their start and end apart: 66, of which 36 were waited for; matrix products, arithmetic and copies ran while one was open for 7% of the time, Pallas kernels for 23%

profile of v8, /device:TPU:0, one launch (start us, length us, event | category | flops | bytes accessed | tf_op | source)
XLA Modules:
  0.0 295.0 jit_solution(3173388182385698227)
XLA Ops:
  1.9 3.0 %collective-permute-start.1 = (bf16[12,128,128]{2,1,0:T(8,128)(2,1)S(1)}, bf16[12,128,128]{2,1,0:T(8,128)(2,1)S(1)}, u32[]{:S(2)}, u32[]{:S(2)}) collective-permute-start(bf16[12,128,128]{2,1,0:T(8,128)(2,1)S(1)} %bitcast_convert_fusion.refs_0_), channel_id=1, source_target_pairs={{0,4},{8,0},{16,8},{24,16},{28,24},{20,28},{12,20},{4,12},{1,5},{9... | collective-permute-start | bytes 1179656 | tf_op jit(solution)/shard_map/ppermute | solution.py:850
  22.0 3.1 %collective-permute-done.6.refs_2_ = bf16[12,64,128]{2,1,0:T(8,128)(2,1)S(1)} collective-permute-done((bf16[12,64,128]{2,1,0:T(8,128)(2,1)S(1)}, bf16[12,64,128]{2,1,0:T(8,128)(2,1)S(1)}, u32[]{:S(2)}, u32[]{:S(2)}) %collective-permute-start.6) | collective-permute-done | bytes 196640 | tf_op jit(solution)/shard_map/ppermute | solution.py:919
  32.2 3.1 %collective-permute-done.10.refs_4_ = bf16[12,64,128]{2,1,0:T(8,128)(2,1)S(1)} collective-permute-done((bf16[12,64,128]{2,1,0:T(8,128)(2,1)S(1)}, bf16[12,64,128]{2,1,0:T(8,128)(2,1)S(1)}, u32[]{:S(2)}, u32[]{:S(2)}) %collective-permute-start.10) | collective-permute-done | bytes 196640 | tf_op jit(solution)/shard_map/ppermute | solution.py:919
  35.2 2.1 collective-permute-done.9.refs_3_
  53.3 5.2 %collective-permute-done.18.refs_8_ = bf16[6,64,128]{2,1,0:T(8,128)(2,1)S(1)} collective-permute-done((bf16[6,64,128]{2,1,0:T(8,128)(2,1)S(1)}, bf16[6,64,128]{2,1,0:T(8,128)(2,1)S(1)}, u32[]{:S(2)}, u32[]{:S(2)}) %collective-permute-start.18) | collective-permute-done | bytes 98336 | tf_op jit(solution)/shard_map/ppermute | solution.py:919
  66.4 9.2 %attend.2 = (bf16[512,512]{1,0:T(8,128)(2,1)S(1)}, f32[512,512]{1,0:T(8,128)S(1)}) custom-call(bf16[512,512]{1,0:T(8,128)(2,1)S(1)} %get-tuple-element.196.q_ref, bf16[512,1024]{1,0:T(8,128)(2,1)S(1)} %get-tuple-element.197.kv_ref, bf16[512,1024]{1,0:T(8,128)(2,1)S(1)} %collective-permute-done.22.kvp_ref, bf16[512,128]{1,0:T(8,128)(2,1)S(1)} %get-tuple-element.198.ohq_ref, ...), custom_call_target="tpu_custom_call" | custom-call | flops 11000000 | tf_op jit(solution)/shard_map/attend/pallas_call | solution.py:392
  75.6 3.8 %collective-permute-done.24.a3 = bf16[36,64,128]{2,1,0:T(8,128)(2,1)S(1)} collective-permute-done((bf16[36,64,128]{2,1,0:T(8,128)(2,1)S(1)}, bf16[36,64,128]{2,1,0:T(8,128)(2,1)S(1)}, u32[]{:S(2)}, u32[]{:S(2)}) %collective-permute-start.24) | collective-permute-done | bytes 589856 | tf_op jit(solution)/shard_map/ppermute | solution.py:919
  81.5 4.4 %post.2 = (f32[512,512]{1,0:T(8,128)S(1)}, f32[512,128]{1,0:T(8,128)S(1)}, bf16[512,512]{1,0:T(8,128)(2,1)S(1)}, bf16[512,2048]{1,0:T(8,128)(2,1)S(1)}, bf16[512...) custom-call(bf16[512,512]{1,0:T(8,128)(2,1)S(1)} %get-tuple-element.200.o_ref, ...), custom_call_target="tpu_custom_call" | custom-call | flops 11000000 | tf_op jit(solution)/shard_map/post/pallas_call | solution.py:448
  93.7 8.9 %attend.3 = (bf16[512,512]{1,0:T(8,128)(2,1)S(1)}, f32[512,512]{1,0:T(8,128)S(1)}) custom-call(bf16[512,512]{1,0:T(8,128)(2,1)S(1)} %get-tuple-element.217.q_ref, bf16[512,1024]{1,0:T(8,128)(2,1)S(1)} %get-tuple-element.218.kv_ref, bf16[512,1024]{1,0:T(8,128)(2,1)S(1)} %collective-permute-done.31.kvp_ref, bf16[512,128]{1,0:T(8,128)(2,1)S(1)} %get-tuple-element.198.ohq_ref, ...), custom_call_target="tpu_custom_call" | custom-call | flops 11000000 | tf_op jit(solution)/shard_map/attend/pallas_call | solution.py:392
  102.6 4.1 %collective-permute-done.33.a3 = bf16[36,64,128]{2,1,0:T(8,128)(2,1)S(1)} collective-permute-done((bf16[36,64,128]{2,1,0:T(8,128)(2,1)S(1)}, bf16[36,64,128]{2,1,0:T(8,128)(2,1)S(1)}, u32[]{:S(2)}, u32[]{:S(2)}) %collective-permute-start.33) | collective-permute-done | bytes 589856 | tf_op jit(solution)/shard_map/ppermute | solution.py:919
  108.8 4.3 %post.3 = (f32[512,512]{1,0:T(8,128)S(1)}, f32[512,128]{1,0:T(8,128)S(1)}, bf16[512,512]{1,0:T(8,128)(2,1)S(1)}, bf16[512,2048]{1,0:T(8,128)(2,1)S(1)}, bf16[512...) custom-call(bf16[512,512]{1,0:T(8,128)(2,1)S(1)} %get-tuple-element.219.o_ref, ...), custom_call_target="tpu_custom_call" | custom-call | flops 11000000 | tf_op jit(solution)/shard_map/post/pallas_call | solution.py:448
  116.0 6.2 %ffn_grad.2 = (bf16[2,16,128,128]{3,2,1,0:T(8,128)(2,1)S(1)}, bf16[2,16,128,128]{3,2,1,0:T(8,128)(2,1)S(1)}, bf16[2,20,128,128]{3,2,1,0:T(8,128)(2,1)S(1)}, bf16...) custom-call(f32[512,512]{1,0:T(8,128)S(1)} %broadcast_multiply_fusio, ...), custom_call_target="tpu_custom_call" | custom-call | flops 16000000 | tf_op jit(solution)/shard_map/ffn_grad/pallas_call | solution.py:541
  122.8 2.5 collective-permute-done.36
  127.0 15.1 %attend_grad.2 = (bf16[512,512]{1,0:T(8,128)(2,1)S(1)}, bf16[512,1024]{1,0:T(8,128)(2,1)S(1)}, bf16[512,1024]{1,0:T(8,128)(2,1)S(1)}) custom-call(bf16[512,512]{1,0:T(8,128)(2,1)S(1)} %get-tuple-element.217.q_ref, bf16[512,1024]{1,0:T(8,128)(2,1)S(1)} %get-tuple-element.218.kv_ref, bf16[512,1024]{1,0:T(8,128)(2,1)S(1)} %collective-permute-done.31.kvp_ref, ...), custom_call_target="tpu_custom_call" | custom-call | flops 23000000 | tf_op jit(solution)/shard_map/attend_grad/pallas_call | solution.py:633
  142.4 2.7 collective-permute-done.39.dkvr_ref
  150.3 6.3 %ffn_grad.3 = (bf16[2,16,128,128]{3,2,1,0:T(8,128)(2,1)S(1)}, bf16[2,16,128,128]{3,2,1,0:T(8,128)(2,1)S(1)}, bf16[2,20,128,128]{3,2,1,0:T(8,128)(2,1)S(1)}, bf16...) custom-call(f32[512,512]{1,0:T(8,128)S(1)} %get-tuple-element.258.e_, ...), custom_call_target="tpu_custom_call" | custom-call | flops 16000000 | tf_op jit(solution)/shard_map/ffn_grad/pallas_call | solution.py:541
  156.6 5.3 %collective-permute-done.42.refs_11_ = bf16[16,128,128]{2,1,0:T(8,128)(2,1)S(1)} collective-permute-done((bf16[16,128,128]{2,1,0:T(8,128)(2,1)S(1)}, bf16[16,128,128]{2,1,0:T(8,128)(2,1)S(1)}, u32[]{:S(2)}, u32[]{:S(2)}) %collective-permute-start.42) | collective-permute-done | bytes 524320 | tf_op jit(solution)/shard_map/ppermute | solution.py:919
  162.0 7.9 %collective-permute-done.41.refs_9_ = bf16[12,128,128]{2,1,0:T(8,128)(2,1)S(1)} collective-permute-done((bf16[12,128,128]{2,1,0:T(8,128)(2,1)S(1)}, bf16[12,128,128]{2,1,0:T(8,128)(2,1)S(1)}, u32[]{:S(2)}, u32[]{:S(2)}) %collective-permute-start.41) | collective-permute-done | bytes 393248 | tf_op jit(solution)/shard_map/ppermute | solution.py:919
  170.8 2.1 collective-permute-done.43
  175.1 15.3 %attend_grad.3 = (bf16[512,512]{1,0:T(8,128)(2,1)S(1)}, bf16[512,1024]{1,0:T(8,128)(2,1)S(1)}, bf16[512,1024]{1,0:T(8,128)(2,1)S(1)}) custom-call(bf16[512,512]{1,0:T(8,128)(2,1)S(1)} %get-tuple-element.196.q_ref, bf16[512,1024]{1,0:T(8,128)(2,1)S(1)} %get-tuple-element.197.kv_ref, bf16[512,1024]{1,0:T(8,128)(2,1)S(1)} %collective-permute-done.22.kvp_ref, ...), custom_call_target="tpu_custom_call" | custom-call | flops 23000000 | tf_op jit(solution)/shard_map/attend_grad/pallas_call | solution.py:633
  199.7 2.6 collective-permute-done.53
  204.0 2.7 collective-permute-done.54
  208.3 8.0 %collective-permute-done.48.refs_6_ = bf16[12,128,128]{2,1,0:T(8,128)(2,1)S(1)} collective-permute-done((bf16[12,128,128]{2,1,0:T(8,128)(2,1)S(1)}, bf16[12,128,128]{2,1,0:T(8,128)(2,1)S(1)}, u32[]{:S(2)}, u32[]{:S(2)}) %collective-permute-start.48) | collective-permute-done | bytes 393248 | tf_op jit(solution)/shard_map/ppermute | solution.py:919
  216.3 2.6 collective-permute-start.55
  222.8 3.6 %collective-permute-done.51 = bf16[768,128]{1,0:T(8,128)(2,1)S(1)} collective-permute-done((bf16[768,128]{1,0:T(8,128)(2,1)S(1)}, bf16[768,128]{1,0:T(8,128)(2,1)S(1)}, u32[]{:S(2)}, u32[]{:S(2)}) %collective-permute-start.51) | collective-permute-done | bytes 196640 | tf_op jit(solution)/shard_map/ppermute | solution.py:850
  226.4 2.9 collective-permute-done.50
  229.5 2.0 collective-permute-start.57
  232.9 3.0 %collective-permute-done.58 = f32[128,128]{1,0:T(8,128)S(1)} collective-permute-done((f32[128,128]{1,0:T(8,128)S(1)}, f32[128,128]{1,0:T(8,128)S(1)}, u32[]{:S(2)}, u32[]{:S(2)}) %collective-permute-start.58) | collective-permute-done | bytes 65568 | tf_op jit(solution)/shard_map/ppermute | solution.py:919
  235.9 2.5 collective-permute-done.56
  239.5 2.0 collective-permute-start.60
  254.4 4.9 %collective-permute-done.64 = bf16[1536,128]{1,0:T(8,128)(2,1)S(1)} collective-permute-done((bf16[1536,128]{1,0:T(8,128)(2,1)S(1)}, bf16[1536,128]{1,0:T(8,128)(2,1)S(1)}, u32[]{:S(2)}, u32[]{:S(2)}) %collective-permute-start.64) | collective-permute-done | bytes 393248 | tf_op jit(solution)/shard_map/ppermute | solution.py:850
  261.7 33.2 %soap.1 = (f32[12,128,128]{2,1,0:T(8,128)}, bf16[12,128,128]{2,1,0:T(8,128)(2,1)}, f32[12,128,128]{2,1,0:T(8,128)}, f32[12,128,128]{2,1,0:T(8,128)}, f32[12,128,...) custom-call(bf16[12,128,128]{2,1,0:T(8,128)(2,1)S(1)} %bitcast.158, ...), custom_call_target="tpu_custom_call" | custom-call | flops 40000000 | tf_op jit(solution)/shard_map/soap/pallas_call | solution.py:208
  (338 shorter events, 108.3 us)
Async XLA Ops:
  1.9 13.6 %collective-permute-start.1 = (bf16[12,128,128]{2,1,0:T(8,128)(2,1)S(1)}, bf16[12,128,128]{2,1,0:T(8,128)(2,1)S(1)}, u32[]{:S(2)}, u32[]{:S(2)}) collective-permute-start(bf16[12,128,128]{2,1,0:T(8,128)(2,1)S(1)} %bitcast_convert_fusion.refs_0_), channel_id=1, source_target_pairs={{0,4},{8,0},{16,8},{24,16},{28,24},{20,28},{12,20},{4,12},{1,5},{9... | collective-permute-start | bytes 1179656 | tf_op jit(solution)/shard_map/ppermute | solution.py:850
  4.9 12.2 %collective-permute-start = (bf16[12,128,128]{2,1,0:T(8,128)(2,1)S(1)}, bf16[12,128,128]{2,1,0:T(8,128)(2,1)S(1)}, u32[]{:S(2)}, u32[]{:S(2)}) collective-permute-start(bf16[12,128,128]{2,1,0:T(8,128)(2,1)S(1)} %bitcast_convert_fusion.refs_0_), channel_id=1, source_target_pairs={{0,8},{8,16},{16,24},{24,28},{28,20},{20,12},{12,4},{4,0},{1,9},{9... | collective-permute-start | bytes 1179656 | tf_op jit(solution)/shard_map/ppermute | solution.py:850
  5.1 16.0 %collective-permute-start.4 = (bf16[12,64,128]{2,1,0:T(8,128)(2,1)S(1)}, bf16[12,64,128]{2,1,0:T(8,128)(2,1)S(1)}, u32[]{:S(2)}, u32[]{:S(2)}) collective-permute-start(bf16[12,64,128]{2,1,0:T(8,128)(2,1)S(1)} %slice.309), channel_id=1, source_target_pairs={{0,2},{1,3},{2,0},{3,1},{4,6},{5,7},{6,4},{7,5},{8,10},{9,11},{10,... | collective-permute-start | bytes 589832 | tf_op jit(solution)/shard_map/ppermute | solution.py:919
  15.5 11.6 %collective-permute-start.3 = (bf16[12,128,128]{2,1,0:T(8,128)(2,1)S(1)}, bf16[12,128,128]{2,1,0:T(8,128)(2,1)S(1)}, u32[]{:S(2)}, u32[]{:S(2)}) collective-permute-start(bf16[12,128,128]{2,1,0:T(8,128)(2,1)S(1)} %collective-permute-done.1.refs_2_), channel_id=1, source_target_pairs={{0,4},{8,0},{16,8},{24,16},{28,24},{20,28},{12,20},{4,12},{1,5},{9... | collective-permute-start | bytes 1179656 | tf_op jit(solution)/shard_map/ppermute | solution.py:850
  17.1 10.1 %collective-permute-start.2 = (bf16[12,128,128]{2,1,0:T(8,128)(2,1)S(1)}, bf16[12,128,128]{2,1,0:T(8,128)(2,1)S(1)}, u32[]{:S(2)}, u32[]{:S(2)}) collective-permute-start(bf16[12,128,128]{2,1,0:T(8,128)(2,1)S(1)} %collective-permute-done.refs_1_), channel_id=1, source_target_pairs={{0,8},{8,16},{16,24},{24,28},{28,20},{20,12},{12,4},{4,0},{1,9},{9... | collective-permute-start | bytes 1179656 | tf_op jit(solution)/shard_map/ppermute | solution.py:850
  18.0 9.2 %collective-permute-start.5 = (bf16[12,64,128]{2,1,0:T(8,128)(2,1)S(1)}, bf16[12,64,128]{2,1,0:T(8,128)(2,1)S(1)}, u32[]{:S(2)}, u32[]{:S(2)}) collective-permute-start(bf16[12,64,128]{2,1,0:T(8,128)(2,1)S(1)} %slice.310), channel_id=1, source_target_pairs={{0,2},{1,3},{2,0},{3,1},{4,6},{5,7},{6,4},{7,5},{8,10},{9,11},{10,... | collective-permute-start | bytes 589832 | tf_op jit(solution)/shard_map/ppermute | solution.py:919
  21.8 25.9 %collective-permute-start.13 = (s32[96]{0:T(128)}, s32[96]{0:T(128)}, u32[]{:S(2)}, u32[]{:S(2)}) collective-permute-start(s32[96]{0:T(128)} %get-tuple-element.179.at_ref), channel_id=1, source_target_pairs={{0,2},{1,3},{2,0},{3,1},{4,6},{5,7},{6,4},{7,5},{8,10},{9,11},{10,... | collective-permute-start | bytes 1160 | tf_op jit(solution)/shard_map/ppermute | solution.py:919
  27.2 10.1 %collective-permute-start.7 = (bf16[12,128,128]{2,1,0:T(8,128)(2,1)S(1)}, bf16[12,128,128]{2,1,0:T(8,128)(2,1)S(1)}, u32[]{:S(2)}, u32[]{:S(2)}) collective-permute-start(bf16[12,128,128]{2,1,0:T(8,128)(2,1)S(1)} %collective-permute-done.2.refs_3_), channel_id=1, source_target_pairs={{0,8},{8,16},{16,24},{24,28},{28,20},{20,12},{12,4},{4,0},{1,9},{9... | collective-permute-start | bytes 1179656 | tf_op jit(solution)/shard_map/ppermute | solution.py:850
  28.8 8.5 %collective-permute-start.8 = (bf16[12,128,128]{2,1,0:T(8,128)(2,1)S(1)}, bf16[12,128,128]{2,1,0:T(8,128)(2,1)S(1)}, u32[]{:S(2)}, u32[]{:S(2)}) collective-permute-start(bf16[12,128,128]{2,1,0:T(8,128)(2,1)S(1)} %collective-permute-done.3.refs_4_), channel_id=1, source_target_pairs={{0,4},{8,0},{16,8},{24,16},{28,24},{20,28},{12,20},{4,12},{1,5},{9... | collective-permute-start | bytes 1179656 | tf_op jit(solution)/shard_map/ppermute | solution.py:850
  38.8 8.9 %collective-permute-start.12 = (bf16[6,128,128]{2,1,0:T(8,128)(2,1)}, bf16[6,128,128]{2,1,0:T(8,128)(2,1)}, u32[]{:S(2)}, u32[]{:S(2)}) collective-permute-start(bf16[6,128,128]{2,1,0:T(8,128)(2,1)} %slice.228), channel_id=1, source_target_pairs={{0,4},{8,0},{16,8},{24,16},{28,24},{20,28},{12,20},{4,12},{1,5},{9... | collective-permute-start | bytes 589832 | tf_op jit(solution)/shard_map/ppermute | solution.py:850
  41.5 11.0 %collective-permute-start.15 = (bf16[12,64,128]{2,1,0:T(8,128)(2,1)}, bf16[12,64,128]{2,1,0:T(8,128)(2,1)}, u32[]{:S(2)}, u32[]{:S(2)}) collective-permute-start(bf16[12,64,128]{2,1,0:T(8,128)(2,1)} %slice.314), channel_id=1, source_target_pairs={{0,2},{1,3},{2,0},{3,1},{4,6},{5,7},{6,4},{7,5},{8,10},{9,11},{10,... | collective-permute-start | bytes 589832 | tf_op jit(solution)/shard_map/ppermute | solution.py:919
  49.6 11.2 %collective-permute-start.19 = (bf16[12,64,128]{2,1,0:T(8,128)(2,1)S(1)}, bf16[12,64,128]{2,1,0:T(8,128)(2,1)S(1)}, u32[]{:S(2)}, u32[]{:S(2)}) collective-permute-start(bf16[12,64,128]{2,1,0:T(8,128)(2,1)S(1)} %get-tuple-element.192), channel_id=1, source_target_pairs={{0,2},{1,3},{2,0},{3,1},{4,6},{5,7},{6,4},{7,5},{8,10},{9,11},{10,... | collective-permute-start | bytes 589832 | tf_op jit(solution)/shard_map/ppermute | solution.py:919
  50.3 12.2 %collective-permute-start.14 = (bf16[12,128,128]{2,1,0:T(8,128)(2,1)S(1)}, bf16[12,128,128]{2,1,0:T(8,128)(2,1)S(1)}, u32[]{:S(2)}, u32[]{:S(2)}) collective-permute-start(bf16[12,128,128]{2,1,0:T(8,128)(2,1)S(1)} %get-tuple-element.189.w0), channel_id=1, source_target_pairs={{0,1},{1,0},{2,3},{3,2},{4,5},{5,4},{6,7},{7,6},{8,9},{9,8},{10,11... | collective-permute-start | bytes 1179656 | tf_op jit(solution)/shard_map/ppermute | solution.py:915
  64.0 15.5 %collective-permute-start.24 = (bf16[36,64,128]{2,1,0:T(8,128)(2,1)S(1)}, bf16[36,64,128]{2,1,0:T(8,128)(2,1)S(1)}, u32[]{:S(2)}, u32[]{:S(2)}) collective-permute-start(bf16[36,64,128]{2,1,0:T(8,128)(2,1)S(1)} %get-tuple-element.206), channel_id=1, source_target_pairs={{0,2},{1,3},{2,0},{3,1},{4,6},{5,7},{6,4},{7,5},{8,10},{9,11},{10,... | collective-permute-start | bytes 1769480 | tf_op jit(solution)/shard_map/ppermute | solution.py:919
  64.6 16.0 %collective-permute-start.23 = (bf16[36,128,128]{2,1,0:T(8,128)(2,1)S(1)}, bf16[36,128,128]{2,1,0:T(8,128)(2,1)S(1)}, u32[]{:S(2)}, u32[]{:S(2)}) collective-permute-start(bf16[36,128,128]{2,1,0:T(8,128)(2,1)S(1)} %get-tuple-element.203.a0), channel_id=1, source_target_pairs={{0,1},{1,0},{2,3},{3,2},{4,5},{5,4},{6,7},{7,6},{8,9},{9,8},{10,11... | collective-permute-start | bytes 3538952 | tf_op jit(solution)/shard_map/ppermute | solution.py:915
  64.7 15.7 %collective-permute-start.25 = (bf16[36,64,128]{2,1,0:T(8,128)(2,1)S(1)}, bf16[36,64,128]{2,1,0:T(8,128)(2,1)S(1)}, u32[]{:S(2)}, u32[]{:S(2)}) collective-permute-start(bf16[36,64,128]{2,1,0:T(8,128)(2,1)S(1)} %get-tuple-element.204.a2), channel_id=1, source_target_pairs={{0,1},{1,0},{2,3},{3,2},{4,5},{5,4},{6,7},{7,6},{8,9},{9,8},{10,11... | collective-permute-start | bytes 1769480 | tf_op jit(solution)/shard_map/ppermute | solution.py:915
  91.1 15.6 %collective-permute-start.33 = (bf16[36,64,128]{2,1,0:T(8,128)(2,1)S(1)}, bf16[36,64,128]{2,1,0:T(8,128)(2,1)S(1)}, u32[]{:S(2)}, u32[]{:S(2)}) collective-permute-start(bf16[36,64,128]{2,1,0:T(8,128)(2,1)S(1)} %get-tuple-element.225), channel_id=1, source_target_pairs={{0,2},{1,3},{2,0},{3,1},{4,6},{5,7},{6,4},{7,5},{8,10},{9,11},{10,... | collective-permute-start | bytes 1769480 | tf_op jit(solution)/shard_map/ppermute | solution.py:919
  91.9 14.9 %collective-permute-start.32 = (bf16[36,128,128]{2,1,0:T(8,128)(2,1)S(1)}, bf16[36,128,128]{2,1,0:T(8,128)(2,1)S(1)}, u32[]{:S(2)}, u32[]{:S(2)}) collective-permute-start(bf16[36,128,128]{2,1,0:T(8,128)(2,1)S(1)} %get-tuple-element.222.a0), channel_id=1, source_target_pairs={{0,1},{1,0},{2,3},{3,2},{4,5},{5,4},{6,7},{7,6},{8,9},{9,8},{10,11... | collective-permute-start | bytes 3538952 | tf_op jit(solution)/shard_map/ppermute | solution.py:915
  91.9 14.8 %collective-permute-start.34 = (bf16[36,64,128]{2,1,0:T(8,128)(2,1)S(1)}, bf16[36,64,128]{2,1,0:T(8,128)(2,1)S(1)}, u32[]{:S(2)}, u32[]{:S(2)}) collective-permute-start(bf16[36,64,128]{2,1,0:T(8,128)(2,1)S(1)} %get-tuple-element.223.a2), channel_id=1, source_target_pairs={{0,1},{1,0},{2,3},{3,2},{4,5},{5,4},{6,7},{7,6},{8,9},{9,8},{10,11... | collective-permute-start | bytes 1769480 | tf_op jit(solution)/shard_map/ppermute | solution.py:915
  125.6 16.8 %collective-permute-start.38 = (bf16[20,128,128]{2,1,0:T(8,128)(2,1)S(1)}, bf16[20,128,128]{2,1,0:T(8,128)(2,1)S(1)}, u32[]{:S(2)}, u32[]{:S(2)}) collective-permute-start(bf16[20,128,128]{2,1,0:T(8,128)(2,1)S(1)} %fusion.4), channel_id=1, source_target_pairs={{0,2},{1,3},{2,0},{3,1},{4,6},{5,7},{6,4},{7,5},{8,10},{9,11},{10,... | collective-permute-start | bytes 1966088 | tf_op jit(solution)/shard_map/ppermute | solution.py:919
  147.2 14.8 %collective-permute-start.42 = (bf16[16,128,128]{2,1,0:T(8,128)(2,1)S(1)}, bf16[16,128,128]{2,1,0:T(8,128)(2,1)S(1)}, u32[]{:S(2)}, u32[]{:S(2)}) collective-permute-start(bf16[16,128,128]{2,1,0:T(8,128)(2,1)S(1)} %fusion.6), channel_id=1, source_target_pairs={{0,2},{1,3},{2,0},{3,1},{4,6},{5,7},{6,4},{7,5},{8,10},{9,11},{10,... | collective-permute-start | bytes 1572872 | tf_op jit(solution)/shard_map/ppermute | solution.py:919
  149.5 20.4 %collective-permute-start.41 = (bf16[12,128,128]{2,1,0:T(8,128)(2,1)S(1)}, bf16[12,128,128]{2,1,0:T(8,128)(2,1)S(1)}, u32[]{:S(2)}, u32[]{:S(2)}) collective-permute-start(bf16[12,128,128]{2,1,0:T(8,128)(2,1)S(1)} %fusion.8), channel_id=1, source_target_pairs={{0,2},{1,3},{2,0},{3,1},{4,6},{5,7},{6,4},{7,5},{8,10},{9,11},{10,... | collective-permute-start | bytes 1179656 | tf_op jit(solution)/shard_map/ppermute | solution.py:919
  173.1 17.4 %collective-permute-start.45 = (bf16[20,128,128]{2,1,0:T(8,128)(2,1)S(1)}, bf16[20,128,128]{2,1,0:T(8,128)(2,1)S(1)}, u32[]{:S(2)}, u32[]{:S(2)}) collective-permute-start(bf16[20,128,128]{2,1,0:T(8,128)(2,1)S(1)} %fusion.5), channel_id=1, source_target_pairs={{0,2},{1,3},{2,0},{3,1},{4,6},{5,7},{6,4},{7,5},{8,10},{9,11},{10,... | collective-permute-start | bytes 1966088 | tf_op jit(solution)/shard_map/ppermute | solution.py:919
  190.9 28.1 %collective-permute-start.49 = (bf16[16,128,128]{2,1,0:T(8,128)(2,1)S(1)}, bf16[16,128,128]{2,1,0:T(8,128)(2,1)S(1)}, u32[]{:S(2)}, u32[]{:S(2)}) collective-permute-start(bf16[16,128,128]{2,1,0:T(8,128)(2,1)S(1)} %fusion.7), channel_id=1, source_target_pairs={{0,2},{1,3},{2,0},{3,1},{4,6},{5,7},{6,4},{7,5},{8,10},{9,11},{10,... | collective-permute-start | bytes 1572872 | tf_op jit(solution)/shard_map/ppermute | solution.py:919
  196.8 9.9 %collective-permute-start.47 = (bf16[2,12,128,128]{3,2,1,0:T(8,128)(2,1)S(1)}, bf16[2,12,128,128]{3,2,1,0:T(8,128)(2,1)S(1)}, u32[]{:S(2)}, u32[]{:S(2)}) collective-permute-start(bf16[2,12,128,128]{3,2,1,0:T(8,128)(2,1)S(1)} %get-tuple-element.294), channel_id=1, source_target_pairs={{0,1},{1,0},{2,3},{3,2},{4,5},{5,4},{6,7},{7,6},{8,9},{9,8},{10,11... | collective-permute-start | bytes 2359304 | tf_op jit(solution)/shard_map/ppermute | solution.py:915
  206.8 9.5 %collective-permute-start.48 = (bf16[12,128,128]{2,1,0:T(8,128)(2,1)S(1)}, bf16[12,128,128]{2,1,0:T(8,128)(2,1)S(1)}, u32[]{:S(2)}, u32[]{:S(2)}) collective-permute-start(bf16[12,128,128]{2,1,0:T(8,128)(2,1)S(1)} %fusion.9), channel_id=1, source_target_pairs={{0,2},{1,3},{2,0},{3,1},{4,6},{5,7},{6,4},{7,5},{8,10},{9,11},{10,... | collective-permute-start | bytes 1179656 | tf_op jit(solution)/shard_map/ppermute | solution.py:919
  229.4 8.9 %collective-permute-start.56 = (bf16[1536,128]{1,0:T(8,128)(2,1)S(1)}, bf16[1536,128]{1,0:T(8,128)(2,1)S(1)}, u32[]{:S(2)}, u32[]{:S(2)}) collective-permute-start(bf16[1536,128]{1,0:T(8,128)(2,1)S(1)} %pad_maximum_fusion), channel_id=1, source_target_pairs={{0,8},{8,16},{16,24},{24,28},{28,20},{20,12},{12,4},{4,0},{1,9},{9... | collective-permute-start | bytes 1179656 | tf_op jit(solution)/shard_map/ppermute | solution.py:850
  229.5 8.9 %collective-permute-start.57 = (bf16[1536,128]{1,0:T(8,128)(2,1)S(1)}, bf16[1536,128]{1,0:T(8,128)(2,1)S(1)}, u32[]{:S(2)}, u32[]{:S(2)}) collective-permute-start(bf16[1536,128]{1,0:T(8,128)(2,1)S(1)} %pad_maximum_fusion.1), channel_id=1, source_target_pairs={{0,4},{8,0},{16,8},{24,16},{28,24},{20,28},{12,20},{4,12},{1,5},{9... | collective-permute-start | bytes 1179656 | tf_op jit(solution)/shard_map/ppermute | solution.py:850
  239.5 8.1 %collective-permute-start.59 = (bf16[1536,128]{1,0:T(8,128)(2,1)}, bf16[1536,128]{1,0:T(8,128)(2,1)}, u32[]{:S(2)}, u32[]{:S(2)}) collective-permute-start(bf16[1536,128]{1,0:T(8,128)(2,1)} %get-tuple-element.313), channel_id=1, source_target_pairs={{0,8},{8,16},{16,24},{24,28},{28,20},{20,12},{12,4},{4,0},{1,9},{9... | collective-permute-start | bytes 1179656 | tf_op jit(solution)/shard_map/ppermute | solution.py:850
  239.5 8.1 %collective-permute-start.60 = (bf16[1536,128]{1,0:T(8,128)(2,1)}, bf16[1536,128]{1,0:T(8,128)(2,1)}, u32[]{:S(2)}, u32[]{:S(2)}) collective-permute-start(bf16[1536,128]{1,0:T(8,128)(2,1)} %get-tuple-element.314), channel_id=1, source_target_pairs={{0,4},{8,0},{16,8},{24,16},{28,24},{20,28},{12,20},{4,12},{1,5},{9... | collective-permute-start | bytes 1179656 | tf_op jit(solution)/shard_map/ppermute | solution.py:850
  249.1 10.3 %collective-permute-start.64 = (bf16[1536,128]{1,0:T(8,128)(2,1)S(1)}, bf16[1536,128]{1,0:T(8,128)(2,1)S(1)}, u32[]{:S(2)}, u32[]{:S(2)}) collective-permute-start(bf16[1536,128]{1,0:T(8,128)(2,1)S(1)} %get-tuple-element.315), channel_id=1, source_target_pairs={{0,8},{8,16},{16,24},{24,28},{28,20},{20,12},{12,4},{4,0},{1,9},{9... | collective-permute-start | bytes 1179656 | tf_op jit(solution)/shard_map/ppermute | solution.py:850
  249.5 9.9 %collective-permute-start.65 = (bf16[1536,128]{1,0:T(8,128)(2,1)S(1)}, bf16[1536,128]{1,0:T(8,128)(2,1)S(1)}, u32[]{:S(2)}, u32[]{:S(2)}) collective-permute-start(bf16[1536,128]{1,0:T(8,128)(2,1)S(1)} %get-tuple-element.316), channel_id=1, source_target_pairs={{0,4},{8,0},{16,8},{24,16},{28,24},{20,28},{12,20},{4,12},{1,5},{9... | collective-permute-start | bytes 1179656 | tf_op jit(solution)/shard_map/ppermute | solution.py:850
  (102 other events, 691.7 us)

commit v9 on v8

--- a/solution.py
+++ b/solution.py
@@ -1066,6 +1066,8 @@
         dq, dkv, dkvp = attend_grad(q, kv, kvp, do, o, lse, ohq, ohk)
         dkvp = tied(dkvp, far_sums[3 * layer + 1])
         far_sums[3 * layer + 2] = far_swap(tied(down, far_sums[3 * layer + 1]))
+        if layer == 0:
+            far_sums[late[0]] = far_swap(tied(late[1], far_sums[1]))
         dkvr = core_swap(dkvp)
         pk, ps, grad, qsums = proj_grad(dq, dkv, dkvr, xs, dr1, wqkv)
         table_rows[layer] = (sums, qsums, db1)
@@ -1073,8 +1075,8 @@
         if layer:
             far = chip_sum(3 * layer, pk, got)
             grad = tied(grad, far)
-            far_sums[3 * layer] = far_swap(far)
-            moving = far_sums[3 * layer : 3 * layer + 3]
+            late = (3 * layer, far)
+            moving = [far_sums[3 * layer + 2]]
     input_grad, tab_keep, tab_send = embed_grad(
         place.astype(jnp.int32)[None], series, grad, vec_values, table_rows[0] + table_rows[1]
     )

time: 300 us -> 299 us (level)
  transfers between devices with their start and end apart: 66 -> 66, of which waited for: 36 -> 38; matrix products, arithmetic and copies ran while one was open for 7% -> 7% of each run, Pallas kernels for 23% -> 24%
where the time goes in v9:
time: 299 us; the launch traced here: 294 us
  Pallas kernels  117 us (39%)
  waiting for transfers between devices  88.5 us (30%)
  starting transfers between devices  49.9 us (17%)
  local copies, waits for them, and re-layouts  23.8 us (8%)
  other arithmetic  12.7 us (4%)
    ppermute x22, waiting for transfers between devices, far_swap(): return lax.ppermute(value, 'head', [(i, i ^ 2) for i in range(4)])  47.7 us
    pallas_call x1, Pallas kernels, soap(): pl.pallas_call(functools.partial(soap_kernel, len(gs)), grid=(n // group,...  33.2 us
    pallas_call x2, Pallas kernels, attend_grad(): pl.pallas_call(attend_grad_kernel, grid=(D // LANES,), in_specs=[pair, bo...  30.5 us
    ppermute x22, starting transfers between devices, far_swap(): return lax.ppermute(value, 'head', [(i, i ^ 2) for i in range(4)])  21.8 us
    ppermute x25, waiting for transfers between devices, core_swap(): return lax.ppermute(value, 'head', [(i, i ^ 1) for i in range(4)])  18.2 us
    pallas_call x2, Pallas kernels, attend(): pl.pallas_call(attend_kernel, grid=(D // LANES,), in_specs=[pair, both, o...  18.2 us
    ppermute x16, starting transfers between devices, ring_shift(): lax.ppermute(value, 'dp', [(order[i], order[(i + by) % n]) for i in range...  17.6 us
    ppermute x16, waiting for transfers between devices, ring_shift(): lax.ppermute(value, 'dp', [(order[i], order[(i + by) % n]) for i in range...  17.4 us
  transfers between devices with their start and end apart: 66, of which 38 were waited for; matrix products, arithmetic and copies ran while one was open for 7% of the time, Pallas kernels for 24%

profile of v9, /device:TPU:0, one launch (start us, length us, event | category | flops | bytes accessed | tf_op | source)
XLA Modules:
  0.0 294.0 jit_solution(4794634204333465282)
XLA Ops:
  1.9 3.0 %collective-permute-start.1 = (bf16[12,128,128]{2,1,0:T(8,128)(2,1)S(1)}, bf16[12,128,128]{2,1,0:T(8,128)(2,1)S(1)}, u32[]{:S(2)}, u32[]{:S(2)}) collective-permute-start(bf16[12,128,128]{2,1,0:T(8,128)(2,1)S(1)} %bitcast_convert_fusion.refs_0_), channel_id=1, source_target_pairs={{0,4},{8,0},{16,8},{24,16},{28,24},{20,28},{12,20},{4,12},{1,5},{9... | collective-permute-start | bytes 1179656 | tf_op jit(solution)/shard_map/ppermute | solution.py:850
  5.1 2.0 collective-permute-start.4
  22.0 3.1 %collective-permute-done.6.refs_2_ = bf16[12,64,128]{2,1,0:T(8,128)(2,1)S(1)} collective-permute-done((bf16[12,64,128]{2,1,0:T(8,128)(2,1)S(1)}, bf16[12,64,128]{2,1,0:T(8,128)(2,1)S(1)}, u32[]{:S(2)}, u32[]{:S(2)}) %collective-permute-start.6) | collective-permute-done | bytes 196640 | tf_op jit(solution)/shard_map/ppermute | solution.py:919
  32.2 3.1 %collective-permute-done.10.refs_4_ = bf16[12,64,128]{2,1,0:T(8,128)(2,1)S(1)} collective-permute-done((bf16[12,64,128]{2,1,0:T(8,128)(2,1)S(1)}, bf16[12,64,128]{2,1,0:T(8,128)(2,1)S(1)}, u32[]{:S(2)}, u32[]{:S(2)}) %collective-permute-start.10) | collective-permute-done | bytes 196640 | tf_op jit(solution)/shard_map/ppermute | solution.py:919
  35.2 2.1 collective-permute-done.9.refs_3_
  53.3 5.2 %collective-permute-done.18.refs_8_ = bf16[6,64,128]{2,1,0:T(8,128)(2,1)S(1)} collective-permute-done((bf16[6,64,128]{2,1,0:T(8,128)(2,1)S(1)}, bf16[6,64,128]{2,1,0:T(8,128)(2,1)S(1)}, u32[]{:S(2)}, u32[]{:S(2)}) %collective-permute-start.18) | collective-permute-done | bytes 98336 | tf_op jit(solution)/shard_map/ppermute | solution.py:919
  66.4 9.2 %attend.2 = (bf16[512,512]{1,0:T(8,128)(2,1)S(1)}, f32[512,512]{1,0:T(8,128)S(1)}) custom-call(bf16[512,512]{1,0:T(8,128)(2,1)S(1)} %get-tuple-element.197.q_ref, bf16[512,1024]{1,0:T(8,128)(2,1)S(1)} %get-tuple-element.198.kv_ref, bf16[512,1024]{1,0:T(8,128)(2,1)S(1)} %collective-permute-done.22.kvp_ref, bf16[512,128]{1,0:T(8,128)(2,1)S(1)} %get-tuple-element.199.ohq_ref, ...), custom_call_target="tpu_custom_call" | custom-call | flops 11000000 | tf_op jit(solution)/shard_map/attend/pallas_call | solution.py:392
  75.6 3.8 %collective-permute-done.24.a3 = bf16[36,64,128]{2,1,0:T(8,128)(2,1)S(1)} collective-permute-done((bf16[36,64,128]{2,1,0:T(8,128)(2,1)S(1)}, bf16[36,64,128]{2,1,0:T(8,128)(2,1)S(1)}, u32[]{:S(2)}, u32[]{:S(2)}) %collective-permute-start.24) | collective-permute-done | bytes 589856 | tf_op jit(solution)/shard_map/ppermute | solution.py:919
  81.5 4.4 %post.2 = (f32[512,512]{1,0:T(8,128)S(1)}, f32[512,128]{1,0:T(8,128)S(1)}, bf16[512,512]{1,0:T(8,128)(2,1)S(1)}, bf16[512,2048]{1,0:T(8,128)(2,1)S(1)}, bf16[512...) custom-call(bf16[512,512]{1,0:T(8,128)(2,1)S(1)} %get-tuple-element.201.o_ref, ...), custom_call_target="tpu_custom_call" | custom-call | flops 11000000 | tf_op jit(solution)/shard_map/post/pallas_call | solution.py:448
  93.7 8.9 %attend.3 = (bf16[512,512]{1,0:T(8,128)(2,1)S(1)}, f32[512,512]{1,0:T(8,128)S(1)}) custom-call(bf16[512,512]{1,0:T(8,128)(2,1)S(1)} %get-tuple-element.218.q_ref, bf16[512,1024]{1,0:T(8,128)(2,1)S(1)} %get-tuple-element.219.kv_ref, bf16[512,1024]{1,0:T(8,128)(2,1)S(1)} %collective-permute-done.31.kvp_ref, bf16[512,128]{1,0:T(8,128)(2,1)S(1)} %get-tuple-element.199.ohq_ref, ...), custom_call_target="tpu_custom_call" | custom-call | flops 11000000 | tf_op jit(solution)/shard_map/attend/pallas_call | solution.py:392
  102.6 4.1 %collective-permute-done.33.a3 = bf16[36,64,128]{2,1,0:T(8,128)(2,1)S(1)} collective-permute-done((bf16[36,64,128]{2,1,0:T(8,128)(2,1)S(1)}, bf16[36,64,128]{2,1,0:T(8,128)(2,1)S(1)}, u32[]{:S(2)}, u32[]{:S(2)}) %collective-permute-start.33) | collective-permute-done | bytes 589856 | tf_op jit(solution)/shard_map/ppermute | solution.py:919
  106.8 2.0 collective-permute-done.35.a5
  108.8 4.3 %post.3 = (f32[512,512]{1,0:T(8,128)S(1)}, f32[512,128]{1,0:T(8,128)S(1)}, bf16[512,512]{1,0:T(8,128)(2,1)S(1)}, bf16[512,2048]{1,0:T(8,128)(2,1)S(1)}, bf16[512...) custom-call(bf16[512,512]{1,0:T(8,128)(2,1)S(1)} %get-tuple-element.220.o_ref, ...), custom_call_target="tpu_custom_call" | custom-call | flops 11000000 | tf_op jit(solution)/shard_map/post/pallas_call | solution.py:448
  116.0 6.2 %ffn_grad.2 = (bf16[2,16,128,128]{3,2,1,0:T(8,128)(2,1)S(1)}, bf16[2,16,128,128]{3,2,1,0:T(8,128)(2,1)S(1)}, bf16[2,20,128,128]{3,2,1,0:T(8,128)(2,1)S(1)}, bf16...) custom-call(f32[512,512]{1,0:T(8,128)S(1)} %broadcast_multiply_fusio, ...), custom_call_target="tpu_custom_call" | custom-call | flops 16000000 | tf_op jit(solution)/shard_map/ffn_grad/pallas_call | solution.py:541
  122.8 2.5 collective-permute-done.36
  127.0 15.1 %attend_grad.2 = (bf16[512,512]{1,0:T(8,128)(2,1)S(1)}, bf16[512,1024]{1,0:T(8,128)(2,1)S(1)}, bf16[512,1024]{1,0:T(8,128)(2,1)S(1)}) custom-call(bf16[512,512]{1,0:T(8,128)(2,1)S(1)} %get-tuple-element.218.q_ref, bf16[512,1024]{1,0:T(8,128)(2,1)S(1)} %get-tuple-element.219.kv_ref, bf16[512,1024]{1,0:T(8,128)(2,1)S(1)} %collective-permute-done.31.kvp_ref, ...), custom_call_target="tpu_custom_call" | custom-call | flops 23000000 | tf_op jit(solution)/shard_map/attend_grad/pallas_call | solution.py:633
  142.4 2.7 collective-permute-done.39.dkvr_ref
  149.5 6.3 %ffn_grad.3 = (bf16[2,16,128,128]{3,2,1,0:T(8,128)(2,1)S(1)}, bf16[2,16,128,128]{3,2,1,0:T(8,128)(2,1)S(1)}, bf16[2,20,128,128]{3,2,1,0:T(8,128)(2,1)S(1)}, bf16...) custom-call(f32[512,512]{1,0:T(8,128)S(1)} %get-tuple-element.259.e_, ...), custom_call_target="tpu_custom_call" | custom-call | flops 16000000 | tf_op jit(solution)/shard_map/ffn_grad/pallas_call | solution.py:541
  155.8 5.6 %collective-permute-done.41.refs_11_ = bf16[16,128,128]{2,1,0:T(8,128)(2,1)S(1)} collective-permute-done((bf16[16,128,128]{2,1,0:T(8,128)(2,1)S(1)}, bf16[16,128,128]{2,1,0:T(8,128)(2,1)S(1)}, u32[]{:S(2)}, u32[]{:S(2)}) %collective-permute-start.41) | collective-permute-done | bytes 524320 | tf_op jit(solution)/shard_map/ppermute | solution.py:919
  162.3 2.2 collective-permute-done.42
  166.7 15.3 %attend_grad.3 = (bf16[512,512]{1,0:T(8,128)(2,1)S(1)}, bf16[512,1024]{1,0:T(8,128)(2,1)S(1)}, bf16[512,1024]{1,0:T(8,128)(2,1)S(1)}) custom-call(bf16[512,512]{1,0:T(8,128)(2,1)S(1)} %get-tuple-element.197.q_ref, bf16[512,1024]{1,0:T(8,128)(2,1)S(1)} %get-tuple-element.198.kv_ref, bf16[512,1024]{1,0:T(8,128)(2,1)S(1)} %collective-permute-done.22.kvp_ref, ...), custom_call_target="tpu_custom_call" | custom-call | flops 23000000 | tf_op jit(solution)/shard_map/attend_grad/pallas_call | solution.py:633
  191.3 2.6 collective-permute-done.53
  195.7 2.7 collective-permute-done.54
  200.0 13.9 %collective-permute-done.47.refs_6_ = bf16[12,128,128]{2,1,0:T(8,128)(2,1)S(1)} collective-permute-done((bf16[12,128,128]{2,1,0:T(8,128)(2,1)S(1)}, bf16[12,128,128]{2,1,0:T(8,128)(2,1)S(1)}, u32[]{:S(2)}, u32[]{:S(2)}) %collective-permute-start.47) | collective-permute-done | bytes 393248 | tf_op jit(solution)/shard_map/ppermute | solution.py:919
  213.9 2.6 collective-permute-start.55
  220.3 4.2 %collective-permute-done.51 = bf16[768,128]{1,0:T(8,128)(2,1)S(1)} collective-permute-done((bf16[768,128]{1,0:T(8,128)(2,1)S(1)}, bf16[768,128]{1,0:T(8,128)(2,1)S(1)}, u32[]{:S(2)}, u32[]{:S(2)}) %collective-permute-start.51) | collective-permute-done | bytes 196640 | tf_op jit(solution)/shard_map/ppermute | solution.py:850
  229.4 2.9 %collective-permute-done.58 = f32[128,128]{1,0:T(8,128)S(1)} collective-permute-done((f32[128,128]{1,0:T(8,128)S(1)}, f32[128,128]{1,0:T(8,128)S(1)}, u32[]{:S(2)}, u32[]{:S(2)}) %collective-permute-start.58) | collective-permute-done | bytes 65568 | tf_op jit(solution)/shard_map/ppermute | solution.py:919
  232.3 2.9 collective-permute-done.56
  243.0 2.2 collective-permute-done.59
  245.2 2.0 collective-permute-done.60
  253.8 2.7 collective-permute-done.64
  260.6 33.2 %soap.1 = (f32[12,128,128]{2,1,0:T(8,128)}, bf16[12,128,128]{2,1,0:T(8,128)(2,1)}, f32[12,128,128]{2,1,0:T(8,128)}, f32[12,128,128]{2,1,0:T(8,128)}, f32[12,128,...) custom-call(bf16[12,128,128]{2,1,0:T(8,128)(2,1)S(1)} %bitcast.158, ...), custom_call_target="tpu_custom_call" | custom-call | flops 40000000 | tf_op jit(solution)/shard_map/soap/pallas_call | solution.py:208
  (338 shorter events, 108.8 us)
Async XLA Ops:
  1.9 13.6 %collective-permute-start.1 = (bf16[12,128,128]{2,1,0:T(8,128)(2,1)S(1)}, bf16[12,128,128]{2,1,0:T(8,128)(2,1)S(1)}, u32[]{:S(2)}, u32[]{:S(2)}) collective-permute-start(bf16[12,128,128]{2,1,0:T(8,128)(2,1)S(1)} %bitcast_convert_fusion.refs_0_), channel_id=1, source_target_pairs={{0,4},{8,0},{16,8},{24,16},{28,24},{20,28},{12,20},{4,12},{1,5},{9... | collective-permute-start | bytes 1179656 | tf_op jit(solution)/shard_map/ppermute | solution.py:850
  4.9 12.2 %collective-permute-start = (bf16[12,128,128]{2,1,0:T(8,128)(2,1)S(1)}, bf16[12,128,128]{2,1,0:T(8,128)(2,1)S(1)}, u32[]{:S(2)}, u32[]{:S(2)}) collective-permute-start(bf16[12,128,128]{2,1,0:T(8,128)(2,1)S(1)} %bitcast_convert_fusion.refs_0_), channel_id=1, source_target_pairs={{0,8},{8,16},{16,24},{24,28},{28,20},{20,12},{12,4},{4,0},{1,9},{9... | collective-permute-start | bytes 1179656 | tf_op jit(solution)/shard_map/ppermute | solution.py:850
  5.1 16.0 %collective-permute-start.4 = (bf16[12,64,128]{2,1,0:T(8,128)(2,1)S(1)}, bf16[12,64,128]{2,1,0:T(8,128)(2,1)S(1)}, u32[]{:S(2)}, u32[]{:S(2)}) collective-permute-start(bf16[12,64,128]{2,1,0:T(8,128)(2,1)S(1)} %slice.309), channel_id=1, source_target_pairs={{0,2},{1,3},{2,0},{3,1},{4,6},{5,7},{6,4},{7,5},{8,10},{9,11},{10,... | collective-permute-start | bytes 589832 | tf_op jit(solution)/shard_map/ppermute | solution.py:919
  15.5 11.6 %collective-permute-start.3 = (bf16[12,128,128]{2,1,0:T(8,128)(2,1)S(1)}, bf16[12,128,128]{2,1,0:T(8,128)(2,1)S(1)}, u32[]{:S(2)}, u32[]{:S(2)}) collective-permute-start(bf16[12,128,128]{2,1,0:T(8,128)(2,1)S(1)} %collective-permute-done.1.refs_2_), channel_id=1, source_target_pairs={{0,4},{8,0},{16,8},{24,16},{28,24},{20,28},{12,20},{4,12},{1,5},{9... | collective-permute-start | bytes 1179656 | tf_op jit(solution)/shard_map/ppermute | solution.py:850
  17.1 10.1 %collective-permute-start.2 = (bf16[12,128,128]{2,1,0:T(8,128)(2,1)S(1)}, bf16[12,128,128]{2,1,0:T(8,128)(2,1)S(1)}, u32[]{:S(2)}, u32[]{:S(2)}) collective-permute-start(bf16[12,128,128]{2,1,0:T(8,128)(2,1)S(1)} %collective-permute-done.refs_1_), channel_id=1, source_target_pairs={{0,8},{8,16},{16,24},{24,28},{28,20},{20,12},{12,4},{4,0},{1,9},{9... | collective-permute-start | bytes 1179656 | tf_op jit(solution)/shard_map/ppermute | solution.py:850
  18.0 9.2 %collective-permute-start.5 = (bf16[12,64,128]{2,1,0:T(8,128)(2,1)S(1)}, bf16[12,64,128]{2,1,0:T(8,128)(2,1)S(1)}, u32[]{:S(2)}, u32[]{:S(2)}) collective-permute-start(bf16[12,64,128]{2,1,0:T(8,128)(2,1)S(1)} %slice.310), channel_id=1, source_target_pairs={{0,2},{1,3},{2,0},{3,1},{4,6},{5,7},{6,4},{7,5},{8,10},{9,11},{10,... | collective-permute-start | bytes 589832 | tf_op jit(solution)/shard_map/ppermute | solution.py:919
  21.8 25.9 %collective-permute-start.13 = (s32[96]{0:T(128)}, s32[96]{0:T(128)}, u32[]{:S(2)}, u32[]{:S(2)}) collective-permute-start(s32[96]{0:T(128)} %get-tuple-element.180.at_ref), channel_id=1, source_target_pairs={{0,2},{1,3},{2,0},{3,1},{4,6},{5,7},{6,4},{7,5},{8,10},{9,11},{10,... | collective-permute-start | bytes 1160 | tf_op jit(solution)/shard_map/ppermute | solution.py:919
  27.2 10.1 %collective-permute-start.7 = (bf16[12,128,128]{2,1,0:T(8,128)(2,1)S(1)}, bf16[12,128,128]{2,1,0:T(8,128)(2,1)S(1)}, u32[]{:S(2)}, u32[]{:S(2)}) collective-permute-start(bf16[12,128,128]{2,1,0:T(8,128)(2,1)S(1)} %collective-permute-done.2.refs_3_), channel_id=1, source_target_pairs={{0,8},{8,16},{16,24},{24,28},{28,20},{20,12},{12,4},{4,0},{1,9},{9... | collective-permute-start | bytes 1179656 | tf_op jit(solution)/shard_map/ppermute | solution.py:850
  28.8 8.5 %collective-permute-start.8 = (bf16[12,128,128]{2,1,0:T(8,128)(2,1)S(1)}, bf16[12,128,128]{2,1,0:T(8,128)(2,1)S(1)}, u32[]{:S(2)}, u32[]{:S(2)}) collective-permute-start(bf16[12,128,128]{2,1,0:T(8,128)(2,1)S(1)} %collective-permute-done.3.refs_4_), channel_id=1, source_target_pairs={{0,4},{8,0},{16,8},{24,16},{28,24},{20,28},{12,20},{4,12},{1,5},{9... | collective-permute-start | bytes 1179656 | tf_op jit(solution)/shard_map/ppermute | solution.py:850
  38.8 8.9 %collective-permute-start.12 = (bf16[6,128,128]{2,1,0:T(8,128)(2,1)}, bf16[6,128,128]{2,1,0:T(8,128)(2,1)}, u32[]{:S(2)}, u32[]{:S(2)}) collective-permute-start(bf16[6,128,128]{2,1,0:T(8,128)(2,1)} %slice.228), channel_id=1, source_target_pairs={{0,4},{8,0},{16,8},{24,16},{28,24},{20,28},{12,20},{4,12},{1,5},{9... | collective-permute-start | bytes 589832 | tf_op jit(solution)/shard_map/ppermute | solution.py:850
  41.5 11.0 %collective-permute-start.15 = (bf16[12,64,128]{2,1,0:T(8,128)(2,1)}, bf16[12,64,128]{2,1,0:T(8,128)(2,1)}, u32[]{:S(2)}, u32[]{:S(2)}) collective-permute-start(bf16[12,64,128]{2,1,0:T(8,128)(2,1)} %slice.314), channel_id=1, source_target_pairs={{0,2},{1,3},{2,0},{3,1},{4,6},{5,7},{6,4},{7,5},{8,10},{9,11},{10,... | collective-permute-start | bytes 589832 | tf_op jit(solution)/shard_map/ppermute | solution.py:919
  49.6 11.2 %collective-permute-start.19 = (bf16[12,64,128]{2,1,0:T(8,128)(2,1)S(1)}, bf16[12,64,128]{2,1,0:T(8,128)(2,1)S(1)}, u32[]{:S(2)}, u32[]{:S(2)}) collective-permute-start(bf16[12,64,128]{2,1,0:T(8,128)(2,1)S(1)} %get-tuple-element.193), channel_id=1, source_target_pairs={{0,2},{1,3},{2,0},{3,1},{4,6},{5,7},{6,4},{7,5},{8,10},{9,11},{10,... | collective-permute-start | bytes 589832 | tf_op jit(solution)/shard_map/ppermute | solution.py:919
  50.3 12.2 %collective-permute-start.14 = (bf16[12,128,128]{2,1,0:T(8,128)(2,1)S(1)}, bf16[12,128,128]{2,1,0:T(8,128)(2,1)S(1)}, u32[]{:S(2)}, u32[]{:S(2)}) collective-permute-start(bf16[12,128,128]{2,1,0:T(8,128)(2,1)S(1)} %get-tuple-element.190.w0), channel_id=1, source_target_pairs={{0,1},{1,0},{2,3},{3,2},{4,5},{5,4},{6,7},{7,6},{8,9},{9,8},{10,11... | collective-permute-start | bytes 1179656 | tf_op jit(solution)/shard_map/ppermute | solution.py:915
  64.0 15.5 %collective-permute-start.24 = (bf16[36,64,128]{2,1,0:T(8,128)(2,1)S(1)}, bf16[36,64,128]{2,1,0:T(8,128)(2,1)S(1)}, u32[]{:S(2)}, u32[]{:S(2)}) collective-permute-start(bf16[36,64,128]{2,1,0:T(8,128)(2,1)S(1)} %get-tuple-element.207), channel_id=1, source_target_pairs={{0,2},{1,3},{2,0},{3,1},{4,6},{5,7},{6,4},{7,5},{8,10},{9,11},{10,... | collective-permute-start | bytes 1769480 | tf_op jit(solution)/shard_map/ppermute | solution.py:919
  64.6 16.0 %collective-permute-start.23 = (bf16[36,128,128]{2,1,0:T(8,128)(2,1)S(1)}, bf16[36,128,128]{2,1,0:T(8,128)(2,1)S(1)}, u32[]{:S(2)}, u32[]{:S(2)}) collective-permute-start(bf16[36,128,128]{2,1,0:T(8,128)(2,1)S(1)} %get-tuple-element.204.a0), channel_id=1, source_target_pairs={{0,1},{1,0},{2,3},{3,2},{4,5},{5,4},{6,7},{7,6},{8,9},{9,8},{10,11... | collective-permute-start | bytes 3538952 | tf_op jit(solution)/shard_map/ppermute | solution.py:915
  64.7 15.7 %collective-permute-start.25 = (bf16[36,64,128]{2,1,0:T(8,128)(2,1)S(1)}, bf16[36,64,128]{2,1,0:T(8,128)(2,1)S(1)}, u32[]{:S(2)}, u32[]{:S(2)}) collective-permute-start(bf16[36,64,128]{2,1,0:T(8,128)(2,1)S(1)} %get-tuple-element.205.a2), channel_id=1, source_target_pairs={{0,1},{1,0},{2,3},{3,2},{4,5},{5,4},{6,7},{7,6},{8,9},{9,8},{10,11... | collective-permute-start | bytes 1769480 | tf_op jit(solution)/shard_map/ppermute | solution.py:915
  79.5 8.1 %collective-permute-start.28 = (bf16[12,64,128]{2,1,0:T(8,128)(2,1)S(1)}, bf16[12,64,128]{2,1,0:T(8,128)(2,1)S(1)}, u32[]{:S(2)}, u32[]{:S(2)}) collective-permute-start(bf16[12,64,128]{2,1,0:T(8,128)(2,1)S(1)} %get-tuple-element.213), channel_id=1, source_target_pairs={{0,2},{1,3},{2,0},{3,1},{4,6},{5,7},{6,4},{7,5},{8,10},{9,11},{10,... | collective-permute-start | bytes 589832 | tf_op jit(solution)/shard_map/ppermute | solution.py:919
  91.1 15.6 %collective-permute-start.33 = (bf16[36,64,128]{2,1,0:T(8,128)(2,1)S(1)}, bf16[36,64,128]{2,1,0:T(8,128)(2,1)S(1)}, u32[]{:S(2)}, u32[]{:S(2)}) collective-permute-start(bf16[36,64,128]{2,1,0:T(8,128)(2,1)S(1)} %get-tuple-element.226), channel_id=1, source_target_pairs={{0,2},{1,3},{2,0},{3,1},{4,6},{5,7},{6,4},{7,5},{8,10},{9,11},{10,... | collective-permute-start | bytes 1769480 | tf_op jit(solution)/shard_map/ppermute | solution.py:919
  91.9 14.9 %collective-permute-start.32 = (bf16[36,128,128]{2,1,0:T(8,128)(2,1)S(1)}, bf16[36,128,128]{2,1,0:T(8,128)(2,1)S(1)}, u32[]{:S(2)}, u32[]{:S(2)}) collective-permute-start(bf16[36,128,128]{2,1,0:T(8,128)(2,1)S(1)} %get-tuple-element.223.a0), channel_id=1, source_target_pairs={{0,1},{1,0},{2,3},{3,2},{4,5},{5,4},{6,7},{7,6},{8,9},{9,8},{10,11... | collective-permute-start | bytes 3538952 | tf_op jit(solution)/shard_map/ppermute | solution.py:915
  91.9 14.8 %collective-permute-start.34 = (bf16[36,64,128]{2,1,0:T(8,128)(2,1)S(1)}, bf16[36,64,128]{2,1,0:T(8,128)(2,1)S(1)}, u32[]{:S(2)}, u32[]{:S(2)}) collective-permute-start(bf16[36,64,128]{2,1,0:T(8,128)(2,1)S(1)} %get-tuple-element.224.a2), channel_id=1, source_target_pairs={{0,1},{1,0},{2,3},{3,2},{4,5},{5,4},{6,7},{7,6},{8,9},{9,8},{10,11... | collective-permute-start | bytes 1769480 | tf_op jit(solution)/shard_map/ppermute | solution.py:915
  125.6 16.8 %collective-permute-start.38 = (bf16[20,128,128]{2,1,0:T(8,128)(2,1)S(1)}, bf16[20,128,128]{2,1,0:T(8,128)(2,1)S(1)}, u32[]{:S(2)}, u32[]{:S(2)}) collective-permute-start(bf16[20,128,128]{2,1,0:T(8,128)(2,1)S(1)} %fusion.4), channel_id=1, source_target_pairs={{0,2},{1,3},{2,0},{3,1},{4,6},{5,7},{6,4},{7,5},{8,10},{9,11},{10,... | collective-permute-start | bytes 1966088 | tf_op jit(solution)/shard_map/ppermute | solution.py:919
  147.2 14.2 %collective-permute-start.41 = (bf16[16,128,128]{2,1,0:T(8,128)(2,1)S(1)}, bf16[16,128,128]{2,1,0:T(8,128)(2,1)S(1)}, u32[]{:S(2)}, u32[]{:S(2)}) collective-permute-start(bf16[16,128,128]{2,1,0:T(8,128)(2,1)S(1)} %fusion.6), channel_id=1, source_target_pairs={{0,2},{1,3},{2,0},{3,1},{4,6},{5,7},{6,4},{7,5},{8,10},{9,11},{10,... | collective-permute-start | bytes 1572872 | tf_op jit(solution)/shard_map/ppermute | solution.py:919
  164.6 17.4 %collective-permute-start.44 = (bf16[20,128,128]{2,1,0:T(8,128)(2,1)S(1)}, bf16[20,128,128]{2,1,0:T(8,128)(2,1)S(1)}, u32[]{:S(2)}, u32[]{:S(2)}) collective-permute-start(bf16[20,128,128]{2,1,0:T(8,128)(2,1)S(1)} %fusion.5), channel_id=1, source_target_pairs={{0,2},{1,3},{2,0},{3,1},{4,6},{5,7},{6,4},{7,5},{8,10},{9,11},{10,... | collective-permute-start | bytes 1966088 | tf_op jit(solution)/shard_map/ppermute | solution.py:919
  182.7 33.8 %collective-permute-start.49 = (bf16[12,128,128]{2,1,0:T(8,128)(2,1)S(1)}, bf16[12,128,128]{2,1,0:T(8,128)(2,1)S(1)}, u32[]{:S(2)}, u32[]{:S(2)}) collective-permute-start(bf16[12,128,128]{2,1,0:T(8,128)(2,1)S(1)} %fusion.8), channel_id=1, source_target_pairs={{0,2},{1,3},{2,0},{3,1},{4,6},{5,7},{6,4},{7,5},{8,10},{9,11},{10,... | collective-permute-start | bytes 1179656 | tf_op jit(solution)/shard_map/ppermute | solution.py:919
  184.1 32.4 %collective-permute-start.48 = (bf16[16,128,128]{2,1,0:T(8,128)(2,1)S(1)}, bf16[16,128,128]{2,1,0:T(8,128)(2,1)S(1)}, u32[]{:S(2)}, u32[]{:S(2)}) collective-permute-start(bf16[16,128,128]{2,1,0:T(8,128)(2,1)S(1)} %fusion.7), channel_id=1, source_target_pairs={{0,2},{1,3},{2,0},{3,1},{4,6},{5,7},{6,4},{7,5},{8,10},{9,11},{10,... | collective-permute-start | bytes 1572872 | tf_op jit(solution)/shard_map/ppermute | solution.py:919
  188.4 9.9 %collective-permute-start.46 = (bf16[2,12,128,128]{3,2,1,0:T(8,128)(2,1)S(1)}, bf16[2,12,128,128]{3,2,1,0:T(8,128)(2,1)S(1)}, u32[]{:S(2)}, u32[]{:S(2)}) collective-permute-start(bf16[2,12,128,128]{3,2,1,0:T(8,128)(2,1)S(1)} %get-tuple-element.295), channel_id=1, source_target_pairs={{0,1},{1,0},{2,3},{3,2},{4,5},{5,4},{6,7},{7,6},{8,9},{9,8},{10,11... | collective-permute-start | bytes 2359304 | tf_op jit(solution)/shard_map/ppermute | solution.py:915
  198.5 15.5 %collective-permute-start.47 = (bf16[12,128,128]{2,1,0:T(8,128)(2,1)S(1)}, bf16[12,128,128]{2,1,0:T(8,128)(2,1)S(1)}, u32[]{:S(2)}, u32[]{:S(2)}) collective-permute-start(bf16[12,128,128]{2,1,0:T(8,128)(2,1)S(1)} %fusion.9), channel_id=1, source_target_pairs={{0,2},{1,3},{2,0},{3,1},{4,6},{5,7},{6,4},{7,5},{8,10},{9,11},{10,... | collective-permute-start | bytes 1179656 | tf_op jit(solution)/shard_map/ppermute | solution.py:919
  225.9 9.3 %collective-permute-start.56 = (bf16[1536,128]{1,0:T(8,128)(2,1)S(1)}, bf16[1536,128]{1,0:T(8,128)(2,1)S(1)}, u32[]{:S(2)}, u32[]{:S(2)}) collective-permute-start(bf16[1536,128]{1,0:T(8,128)(2,1)S(1)} %pad_maximum_fusion), channel_id=1, source_target_pairs={{0,8},{8,16},{16,24},{24,28},{28,20},{20,12},{12,4},{4,0},{1,9},{9... | collective-permute-start | bytes 1179656 | tf_op jit(solution)/shard_map/ppermute | solution.py:850
  226.5 9.1 %collective-permute-start.57 = (bf16[1536,128]{1,0:T(8,128)(2,1)S(1)}, bf16[1536,128]{1,0:T(8,128)(2,1)S(1)}, u32[]{:S(2)}, u32[]{:S(2)}) collective-permute-start(bf16[1536,128]{1,0:T(8,128)(2,1)S(1)} %pad_maximum_fusion.1), channel_id=1, source_target_pairs={{0,4},{8,0},{16,8},{24,16},{28,24},{20,28},{12,20},{4,12},{1,5},{9... | collective-permute-start | bytes 1179656 | tf_op jit(solution)/shard_map/ppermute | solution.py:850
  236.7 8.5 %collective-permute-start.59 = (bf16[1536,128]{1,0:T(8,128)(2,1)}, bf16[1536,128]{1,0:T(8,128)(2,1)}, u32[]{:S(2)}, u32[]{:S(2)}) collective-permute-start(bf16[1536,128]{1,0:T(8,128)(2,1)} %get-tuple-element.315), channel_id=1, source_target_pairs={{0,8},{8,16},{16,24},{24,28},{28,20},{20,12},{12,4},{4,0},{1,9},{9... | collective-permute-start | bytes 1179656 | tf_op jit(solution)/shard_map/ppermute | solution.py:850
  238.2 9.0 %collective-permute-start.60 = (bf16[1536,128]{1,0:T(8,128)(2,1)}, bf16[1536,128]{1,0:T(8,128)(2,1)}, u32[]{:S(2)}, u32[]{:S(2)}) collective-permute-start(bf16[1536,128]{1,0:T(8,128)(2,1)} %get-tuple-element.316), channel_id=1, source_target_pairs={{0,4},{8,0},{16,8},{24,16},{28,24},{20,28},{12,20},{4,12},{1,5},{9... | collective-permute-start | bytes 1179656 | tf_op jit(solution)/shard_map/ppermute | solution.py:850
  248.7 7.8 %collective-permute-start.64 = (bf16[1536,128]{1,0:T(8,128)(2,1)S(1)}, bf16[1536,128]{1,0:T(8,128)(2,1)S(1)}, u32[]{:S(2)}, u32[]{:S(2)}) collective-permute-start(bf16[1536,128]{1,0:T(8,128)(2,1)S(1)} %get-tuple-element.317), channel_id=1, source_target_pairs={{0,8},{8,16},{16,24},{24,28},{28,20},{20,12},{12,4},{4,0},{1,9},{9... | collective-permute-start | bytes 1179656 | tf_op jit(solution)/shard_map/ppermute | solution.py:850
  (102 other events, 686.3 us)

commit v10 on v9

--- a/solution.py
+++ b/solution.py
@@ -218,7 +218,7 @@
     )(*gs, master, m1, m2, ls, rs, lb, rb)
 
 
-SOAP_GROUP = 2
+SOAP_GROUP = 4
 
 
 bf16 = jnp.bfloat16

time: 299 us -> 299 us (level)
  no operation moved by 1% of the time
where the time goes in v10:
time: 299 us; the launch traced here: 294 us
  Pallas kernels  117 us (39%)
  waiting for transfers between devices  88.5 us (30%)
  starting transfers between devices  49.9 us (17%)
  local copies, waits for them, and re-layouts  23.8 us (8%)
  other arithmetic  12.7 us (4%)
    ppermute x22, waiting for transfers between devices, far_swap(): return lax.ppermute(value, 'head', [(i, i ^ 2) for i in range(4)])  47.7 us
    pallas_call x1, Pallas kernels, soap(): pl.pallas_call(functools.partial(soap_kernel, len(gs)), grid=(n // group,...  32.7 us
    pallas_call x2, Pallas kernels, attend_grad(): pl.pallas_call(attend_grad_kernel, grid=(D // LANES,), in_specs=[pair, bo...  30.5 us
    ppermute x22, starting transfers between devices, far_swap(): return lax.ppermute(value, 'head', [(i, i ^ 2) for i in range(4)])  21.8 us
    ppermute x25, waiting for transfers between devices, core_swap(): return lax.ppermute(value, 'head', [(i, i ^ 1) for i in range(4)])  18.2 us
    pallas_call x2, Pallas kernels, attend(): pl.pallas_call(attend_kernel, grid=(D // LANES,), in_specs=[pair, both, o...  18.2 us
    ppermute x16, starting transfers between devices, ring_shift(): lax.ppermute(value, 'dp', [(order[i], order[(i + by) % n]) for i in range...  17.6 us
    ppermute x16, waiting for transfers between devices, ring_shift(): lax.ppermute(value, 'dp', [(order[i], order[(i + by) % n]) for i in range...  17.4 us
  transfers between devices with their start and end apart: 66, of which 38 were waited for; matrix products, arithmetic and copies ran while one was open for 7% of the time, Pallas kernels for 24%

profile of v10, /device:TPU:0, one launch (start us, length us, event | category | flops | bytes accessed | tf_op | source)
XLA Modules:
  0.0 293.6 jit_solution(9800088085979431482)
XLA Ops:
  1.9 3.0 %collective-permute-start.1 = (bf16[12,128,128]{2,1,0:T(8,128)(2,1)S(1)}, bf16[12,128,128]{2,1,0:T(8,128)(2,1)S(1)}, u32[]{:S(2)}, u32[]{:S(2)}) collective-permute-start(bf16[12,128,128]{2,1,0:T(8,128)(2,1)S(1)} %bitcast_convert_fusion.refs_0_), channel_id=1, source_target_pairs={{0,4},{8,0},{16,8},{24,16},{28,24},{20,28},{12,20},{4,12},{1,5},{9... | collective-permute-start | bytes 1179656 | tf_op jit(solution)/shard_map/ppermute | solution.py:850
  5.1 2.0 collective-permute-start.4
  22.0 3.1 %collective-permute-done.6.refs_2_ = bf16[12,64,128]{2,1,0:T(8,128)(2,1)S(1)} collective-permute-done((bf16[12,64,128]{2,1,0:T(8,128)(2,1)S(1)}, bf16[12,64,128]{2,1,0:T(8,128)(2,1)S(1)}, u32[]{:S(2)}, u32[]{:S(2)}) %collective-permute-start.6) | collective-permute-done | bytes 196640 | tf_op jit(solution)/shard_map/ppermute | solution.py:919
  32.2 3.1 %collective-permute-done.10.refs_4_ = bf16[12,64,128]{2,1,0:T(8,128)(2,1)S(1)} collective-permute-done((bf16[12,64,128]{2,1,0:T(8,128)(2,1)S(1)}, bf16[12,64,128]{2,1,0:T(8,128)(2,1)S(1)}, u32[]{:S(2)}, u32[]{:S(2)}) %collective-permute-start.10) | collective-permute-done | bytes 196640 | tf_op jit(solution)/shard_map/ppermute | solution.py:919
  35.2 2.1 collective-permute-done.9.refs_3_
  53.3 5.2 %collective-permute-done.18.refs_8_ = bf16[6,64,128]{2,1,0:T(8,128)(2,1)S(1)} collective-permute-done((bf16[6,64,128]{2,1,0:T(8,128)(2,1)S(1)}, bf16[6,64,128]{2,1,0:T(8,128)(2,1)S(1)}, u32[]{:S(2)}, u32[]{:S(2)}) %collective-permute-start.18) | collective-permute-done | bytes 98336 | tf_op jit(solution)/shard_map/ppermute | solution.py:919
  66.4 9.2 %attend.2 = (bf16[512,512]{1,0:T(8,128)(2,1)S(1)}, f32[512,512]{1,0:T(8,128)S(1)}) custom-call(bf16[512,512]{1,0:T(8,128)(2,1)S(1)} %get-tuple-element.197.q_ref, bf16[512,1024]{1,0:T(8,128)(2,1)S(1)} %get-tuple-element.198.kv_ref, bf16[512,1024]{1,0:T(8,128)(2,1)S(1)} %collective-permute-done.22.kvp_ref, bf16[512,128]{1,0:T(8,128)(2,1)S(1)} %get-tuple-element.199.ohq_ref, ...), custom_call_target="tpu_custom_call" | custom-call | flops 11000000 | tf_op jit(solution)/shard_map/attend/pallas_call | solution.py:392
  75.6 3.8 %collective-permute-done.24.a3 = bf16[36,64,128]{2,1,0:T(8,128)(2,1)S(1)} collective-permute-done((bf16[36,64,128]{2,1,0:T(8,128)(2,1)S(1)}, bf16[36,64,128]{2,1,0:T(8,128)(2,1)S(1)}, u32[]{:S(2)}, u32[]{:S(2)}) %collective-permute-start.24) | collective-permute-done | bytes 589856 | tf_op jit(solution)/shard_map/ppermute | solution.py:919
  81.5 4.4 %post.2 = (f32[512,512]{1,0:T(8,128)S(1)}, f32[512,128]{1,0:T(8,128)S(1)}, bf16[512,512]{1,0:T(8,128)(2,1)S(1)}, bf16[512,2048]{1,0:T(8,128)(2,1)S(1)}, bf16[512...) custom-call(bf16[512,512]{1,0:T(8,128)(2,1)S(1)} %get-tuple-element.201.o_ref, ...), custom_call_target="tpu_custom_call" | custom-call | flops 11000000 | tf_op jit(solution)/shard_map/post/pallas_call | solution.py:448
  93.7 8.9 %attend.3 = (bf16[512,512]{1,0:T(8,128)(2,1)S(1)}, f32[512,512]{1,0:T(8,128)S(1)}) custom-call(bf16[512,512]{1,0:T(8,128)(2,1)S(1)} %get-tuple-element.218.q_ref, bf16[512,1024]{1,0:T(8,128)(2,1)S(1)} %get-tuple-element.219.kv_ref, bf16[512,1024]{1,0:T(8,128)(2,1)S(1)} %collective-permute-done.31.kvp_ref, bf16[512,128]{1,0:T(8,128)(2,1)S(1)} %get-tuple-element.199.ohq_ref, ...), custom_call_target="tpu_custom_call" | custom-call | flops 11000000 | tf_op jit(solution)/shard_map/attend/pallas_call | solution.py:392
  102.6 4.1 %collective-permute-done.33.a3 = bf16[36,64,128]{2,1,0:T(8,128)(2,1)S(1)} collective-permute-done((bf16[36,64,128]{2,1,0:T(8,128)(2,1)S(1)}, bf16[36,64,128]{2,1,0:T(8,128)(2,1)S(1)}, u32[]{:S(2)}, u32[]{:S(2)}) %collective-permute-start.33) | collective-permute-done | bytes 589856 | tf_op jit(solution)/shard_map/ppermute | solution.py:919
  106.8 2.0 collective-permute-done.35.a5
  108.8 4.3 %post.3 = (f32[512,512]{1,0:T(8,128)S(1)}, f32[512,128]{1,0:T(8,128)S(1)}, bf16[512,512]{1,0:T(8,128)(2,1)S(1)}, bf16[512,2048]{1,0:T(8,128)(2,1)S(1)}, bf16[512...) custom-call(bf16[512,512]{1,0:T(8,128)(2,1)S(1)} %get-tuple-element.220.o_ref, ...), custom_call_target="tpu_custom_call" | custom-call | flops 11000000 | tf_op jit(solution)/shard_map/post/pallas_call | solution.py:448
  116.0 6.2 %ffn_grad.2 = (bf16[2,16,128,128]{3,2,1,0:T(8,128)(2,1)S(1)}, bf16[2,16,128,128]{3,2,1,0:T(8,128)(2,1)S(1)}, bf16[2,20,128,128]{3,2,1,0:T(8,128)(2,1)S(1)}, bf16...) custom-call(f32[512,512]{1,0:T(8,128)S(1)} %broadcast_multiply_fusio, ...), custom_call_target="tpu_custom_call" | custom-call | flops 16000000 | tf_op jit(solution)/shard_map/ffn_grad/pallas_call | solution.py:541
  122.8 2.5 collective-permute-done.36
  127.0 15.1 %attend_grad.2 = (bf16[512,512]{1,0:T(8,128)(2,1)S(1)}, bf16[512,1024]{1,0:T(8,128)(2,1)S(1)}, bf16[512,1024]{1,0:T(8,128)(2,1)S(1)}) custom-call(bf16[512,512]{1,0:T(8,128)(2,1)S(1)} %get-tuple-element.218.q_ref, bf16[512,1024]{1,0:T(8,128)(2,1)S(1)} %get-tuple-element.219.kv_ref, bf16[512,1024]{1,0:T(8,128)(2,1)S(1)} %collective-permute-done.31.kvp_ref, ...), custom_call_target="tpu_custom_call" | custom-call | flops 23000000 | tf_op jit(solution)/shard_map/attend_grad/pallas_call | solution.py:633
  142.4 2.7 collective-permute-done.39.dkvr_ref
  149.5 6.3 %ffn_grad.3 = (bf16[2,16,128,128]{3,2,1,0:T(8,128)(2,1)S(1)}, bf16[2,16,128,128]{3,2,1,0:T(8,128)(2,1)S(1)}, bf16[2,20,128,128]{3,2,1,0:T(8,128)(2,1)S(1)}, bf16...) custom-call(f32[512,512]{1,0:T(8,128)S(1)} %get-tuple-element.259.e_, ...), custom_call_target="tpu_custom_call" | custom-call | flops 16000000 | tf_op jit(solution)/shard_map/ffn_grad/pallas_call | solution.py:541
  155.8 5.6 %collective-permute-done.41.refs_11_ = bf16[16,128,128]{2,1,0:T(8,128)(2,1)S(1)} collective-permute-done((bf16[16,128,128]{2,1,0:T(8,128)(2,1)S(1)}, bf16[16,128,128]{2,1,0:T(8,128)(2,1)S(1)}, u32[]{:S(2)}, u32[]{:S(2)}) %collective-permute-start.41) | collective-permute-done | bytes 524320 | tf_op jit(solution)/shard_map/ppermute | solution.py:919
  162.3 2.2 collective-permute-done.42
  166.7 15.3 %attend_grad.3 = (bf16[512,512]{1,0:T(8,128)(2,1)S(1)}, bf16[512,1024]{1,0:T(8,128)(2,1)S(1)}, bf16[512,1024]{1,0:T(8,128)(2,1)S(1)}) custom-call(bf16[512,512]{1,0:T(8,128)(2,1)S(1)} %get-tuple-element.197.q_ref, bf16[512,1024]{1,0:T(8,128)(2,1)S(1)} %get-tuple-element.198.kv_ref, bf16[512,1024]{1,0:T(8,128)(2,1)S(1)} %collective-permute-done.22.kvp_ref, ...), custom_call_target="tpu_custom_call" | custom-call | flops 23000000 | tf_op jit(solution)/shard_map/attend_grad/pallas_call | solution.py:633
  191.3 2.6 collective-permute-done.53
  195.7 2.7 collective-permute-done.54
  200.0 13.9 %collective-permute-done.47.refs_6_ = bf16[12,128,128]{2,1,0:T(8,128)(2,1)S(1)} collective-permute-done((bf16[12,128,128]{2,1,0:T(8,128)(2,1)S(1)}, bf16[12,128,128]{2,1,0:T(8,128)(2,1)S(1)}, u32[]{:S(2)}, u32[]{:S(2)}) %collective-permute-start.47) | collective-permute-done | bytes 393248 | tf_op jit(solution)/shard_map/ppermute | solution.py:919
  213.9 2.6 collective-permute-start.55
  220.3 4.2 %collective-permute-done.51 = bf16[768,128]{1,0:T(8,128)(2,1)S(1)} collective-permute-done((bf16[768,128]{1,0:T(8,128)(2,1)S(1)}, bf16[768,128]{1,0:T(8,128)(2,1)S(1)}, u32[]{:S(2)}, u32[]{:S(2)}) %collective-permute-start.51) | collective-permute-done | bytes 196640 | tf_op jit(solution)/shard_map/ppermute | solution.py:850
  229.4 2.9 %collective-permute-done.58 = f32[128,128]{1,0:T(8,128)S(1)} collective-permute-done((f32[128,128]{1,0:T(8,128)S(1)}, f32[128,128]{1,0:T(8,128)S(1)}, u32[]{:S(2)}, u32[]{:S(2)}) %collective-permute-start.58) | collective-permute-done | bytes 65568 | tf_op jit(solution)/shard_map/ppermute | solution.py:919
  232.3 2.9 collective-permute-done.56
  243.0 2.2 collective-permute-done.59
  245.2 2.0 collective-permute-done.60
  253.8 2.7 collective-permute-done.64
  260.6 32.7 %soap.1 = (f32[12,128,128]{2,1,0:T(8,128)}, bf16[12,128,128]{2,1,0:T(8,128)(2,1)}, f32[12,128,128]{2,1,0:T(8,128)}, f32[12,128,128]{2,1,0:T(8,128)}, f32[12,128,...) custom-call(bf16[12,128,128]{2,1,0:T(8,128)(2,1)S(1)} %bitcast.158, ...), custom_call_target="tpu_custom_call" | custom-call | flops 40000000 | tf_op jit(solution)/shard_map/soap/pallas_call | solution.py:208
  (338 shorter events, 108.8 us)
Async XLA Ops:
  1.9 13.6 %collective-permute-start.1 = (bf16[12,128,128]{2,1,0:T(8,128)(2,1)S(1)}, bf16[12,128,128]{2,1,0:T(8,128)(2,1)S(1)}, u32[]{:S(2)}, u32[]{:S(2)}) collective-permute-start(bf16[12,128,128]{2,1,0:T(8,128)(2,1)S(1)} %bitcast_convert_fusion.refs_0_), channel_id=1, source_target_pairs={{0,4},{8,0},{16,8},{24,16},{28,24},{20,28},{12,20},{4,12},{1,5},{9... | collective-permute-start | bytes 1179656 | tf_op jit(solution)/shard_map/ppermute | solution.py:850
  4.9 12.2 %collective-permute-start = (bf16[12,128,128]{2,1,0:T(8,128)(2,1)S(1)}, bf16[12,128,128]{2,1,0:T(8,128)(2,1)S(1)}, u32[]{:S(2)}, u32[]{:S(2)}) collective-permute-start(bf16[12,128,128]{2,1,0:T(8,128)(2,1)S(1)} %bitcast_convert_fusion.refs_0_), channel_id=1, source_target_pairs={{0,8},{8,16},{16,24},{24,28},{28,20},{20,12},{12,4},{4,0},{1,9},{9... | collective-permute-start | bytes 1179656 | tf_op jit(solution)/shard_map/ppermute | solution.py:850
  5.1 16.0 %collective-permute-start.4 = (bf16[12,64,128]{2,1,0:T(8,128)(2,1)S(1)}, bf16[12,64,128]{2,1,0:T(8,128)(2,1)S(1)}, u32[]{:S(2)}, u32[]{:S(2)}) collective-permute-start(bf16[12,64,128]{2,1,0:T(8,128)(2,1)S(1)} %slice.309), channel_id=1, source_target_pairs={{0,2},{1,3},{2,0},{3,1},{4,6},{5,7},{6,4},{7,5},{8,10},{9,11},{10,... | collective-permute-start | bytes 589832 | tf_op jit(solution)/shard_map/ppermute | solution.py:919
  15.5 11.6 %collective-permute-start.3 = (bf16[12,128,128]{2,1,0:T(8,128)(2,1)S(1)}, bf16[12,128,128]{2,1,0:T(8,128)(2,1)S(1)}, u32[]{:S(2)}, u32[]{:S(2)}) collective-permute-start(bf16[12,128,128]{2,1,0:T(8,128)(2,1)S(1)} %collective-permute-done.1.refs_2_), channel_id=1, source_target_pairs={{0,4},{8,0},{16,8},{24,16},{28,24},{20,28},{12,20},{4,12},{1,5},{9... | collective-permute-start | bytes 1179656 | tf_op jit(solution)/shard_map/ppermute | solution.py:850
  17.1 10.1 %collective-permute-start.2 = (bf16[12,128,128]{2,1,0:T(8,128)(2,1)S(1)}, bf16[12,128,128]{2,1,0:T(8,128)(2,1)S(1)}, u32[]{:S(2)}, u32[]{:S(2)}) collective-permute-start(bf16[12,128,128]{2,1,0:T(8,128)(2,1)S(1)} %collective-permute-done.refs_1_), channel_id=1, source_target_pairs={{0,8},{8,16},{16,24},{24,28},{28,20},{20,12},{12,4},{4,0},{1,9},{9... | collective-permute-start | bytes 1179656 | tf_op jit(solution)/shard_map/ppermute | solution.py:850
  18.0 9.2 %collective-permute-start.5 = (bf16[12,64,128]{2,1,0:T(8,128)(2,1)S(1)}, bf16[12,64,128]{2,1,0:T(8,128)(2,1)S(1)}, u32[]{:S(2)}, u32[]{:S(2)}) collective-permute-start(bf16[12,64,128]{2,1,0:T(8,128)(2,1)S(1)} %slice.310), channel_id=1, source_target_pairs={{0,2},{1,3},{2,0},{3,1},{4,6},{5,7},{6,4},{7,5},{8,10},{9,11},{10,... | collective-permute-start | bytes 589832 | tf_op jit(solution)/shard_map/ppermute | solution.py:919
  21.8 25.9 %collective-permute-start.13 = (s32[96]{0:T(128)}, s32[96]{0:T(128)}, u32[]{:S(2)}, u32[]{:S(2)}) collective-permute-start(s32[96]{0:T(128)} %get-tuple-element.180.at_ref), channel_id=1, source_target_pairs={{0,2},{1,3},{2,0},{3,1},{4,6},{5,7},{6,4},{7,5},{8,10},{9,11},{10,... | collective-permute-start | bytes 1160 | tf_op jit(solution)/shard_map/ppermute | solution.py:919
  27.2 10.1 %collective-permute-start.7 = (bf16[12,128,128]{2,1,0:T(8,128)(2,1)S(1)}, bf16[12,128,128]{2,1,0:T(8,128)(2,1)S(1)}, u32[]{:S(2)}, u32[]{:S(2)}) collective-permute-start(bf16[12,128,128]{2,1,0:T(8,128)(2,1)S(1)} %collective-permute-done.2.refs_3_), channel_id=1, source_target_pairs={{0,8},{8,16},{16,24},{24,28},{28,20},{20,12},{12,4},{4,0},{1,9},{9... | collective-permute-start | bytes 1179656 | tf_op jit(solution)/shard_map/ppermute | solution.py:850
  28.8 8.5 %collective-permute-start.8 = (bf16[12,128,128]{2,1,0:T(8,128)(2,1)S(1)}, bf16[12,128,128]{2,1,0:T(8,128)(2,1)S(1)}, u32[]{:S(2)}, u32[]{:S(2)}) collective-permute-start(bf16[12,128,128]{2,1,0:T(8,128)(2,1)S(1)} %collective-permute-done.3.refs_4_), channel_id=1, source_target_pairs={{0,4},{8,0},{16,8},{24,16},{28,24},{20,28},{12,20},{4,12},{1,5},{9... | collective-permute-start | bytes 1179656 | tf_op jit(solution)/shard_map/ppermute | solution.py:850
  38.8 8.9 %collective-permute-start.12 = (bf16[6,128,128]{2,1,0:T(8,128)(2,1)}, bf16[6,128,128]{2,1,0:T(8,128)(2,1)}, u32[]{:S(2)}, u32[]{:S(2)}) collective-permute-start(bf16[6,128,128]{2,1,0:T(8,128)(2,1)} %slice.228), channel_id=1, source_target_pairs={{0,4},{8,0},{16,8},{24,16},{28,24},{20,28},{12,20},{4,12},{1,5},{9... | collective-permute-start | bytes 589832 | tf_op jit(solution)/shard_map/ppermute | solution.py:850
  41.5 11.0 %collective-permute-start.15 = (bf16[12,64,128]{2,1,0:T(8,128)(2,1)}, bf16[12,64,128]{2,1,0:T(8,128)(2,1)}, u32[]{:S(2)}, u32[]{:S(2)}) collective-permute-start(bf16[12,64,128]{2,1,0:T(8,128)(2,1)} %slice.314), channel_id=1, source_target_pairs={{0,2},{1,3},{2,0},{3,1},{4,6},{5,7},{6,4},{7,5},{8,10},{9,11},{10,... | collective-permute-start | bytes 589832 | tf_op jit(solution)/shard_map/ppermute | solution.py:919
  49.6 11.2 %collective-permute-start.19 = (bf16[12,64,128]{2,1,0:T(8,128)(2,1)S(1)}, bf16[12,64,128]{2,1,0:T(8,128)(2,1)S(1)}, u32[]{:S(2)}, u32[]{:S(2)}) collective-permute-start(bf16[12,64,128]{2,1,0:T(8,128)(2,1)S(1)} %get-tuple-element.193), channel_id=1, source_target_pairs={{0,2},{1,3},{2,0},{3,1},{4,6},{5,7},{6,4},{7,5},{8,10},{9,11},{10,... | collective-permute-start | bytes 589832 | tf_op jit(solution)/shard_map/ppermute | solution.py:919
  50.3 12.2 %collective-permute-start.14 = (bf16[12,128,128]{2,1,0:T(8,128)(2,1)S(1)}, bf16[12,128,128]{2,1,0:T(8,128)(2,1)S(1)}, u32[]{:S(2)}, u32[]{:S(2)}) collective-permute-start(bf16[12,128,128]{2,1,0:T(8,128)(2,1)S(1)} %get-tuple-element.190.w0), channel_id=1, source_target_pairs={{0,1},{1,0},{2,3},{3,2},{4,5},{5,4},{6,7},{7,6},{8,9},{9,8},{10,11... | collective-permute-start | bytes 1179656 | tf_op jit(solution)/shard_map/ppermute | solution.py:915
  64.0 15.5 %collective-permute-start.24 = (bf16[36,64,128]{2,1,0:T(8,128)(2,1)S(1)}, bf16[36,64,128]{2,1,0:T(8,128)(2,1)S(1)}, u32[]{:S(2)}, u32[]{:S(2)}) collective-permute-start(bf16[36,64,128]{2,1,0:T(8,128)(2,1)S(1)} %get-tuple-element.207), channel_id=1, source_target_pairs={{0,2},{1,3},{2,0},{3,1},{4,6},{5,7},{6,4},{7,5},{8,10},{9,11},{10,... | collective-permute-start | bytes 1769480 | tf_op jit(solution)/shard_map/ppermute | solution.py:919
  64.6 16.0 %collective-permute-start.23 = (bf16[36,128,128]{2,1,0:T(8,128)(2,1)S(1)}, bf16[36,128,128]{2,1,0:T(8,128)(2,1)S(1)}, u32[]{:S(2)}, u32[]{:S(2)}) collective-permute-start(bf16[36,128,128]{2,1,0:T(8,128)(2,1)S(1)} %get-tuple-element.204.a0), channel_id=1, source_target_pairs={{0,1},{1,0},{2,3},{3,2},{4,5},{5,4},{6,7},{7,6},{8,9},{9,8},{10,11... | collective-permute-start | bytes 3538952 | tf_op jit(solution)/shard_map/ppermute | solution.py:915
  64.7 15.7 %collective-permute-start.25 = (bf16[36,64,128]{2,1,0:T(8,128)(2,1)S(1)}, bf16[36,64,128]{2,1,0:T(8,128)(2,1)S(1)}, u32[]{:S(2)}, u32[]{:S(2)}) collective-permute-start(bf16[36,64,128]{2,1,0:T(8,128)(2,1)S(1)} %get-tuple-element.205.a2), channel_id=1, source_target_pairs={{0,1},{1,0},{2,3},{3,2},{4,5},{5,4},{6,7},{7,6},{8,9},{9,8},{10,11... | collective-permute-start | bytes 1769480 | tf_op jit(solution)/shard_map/ppermute | solution.py:915
  79.5 8.1 %collective-permute-start.28 = (bf16[12,64,128]{2,1,0:T(8,128)(2,1)S(1)}, bf16[12,64,128]{2,1,0:T(8,128)(2,1)S(1)}, u32[]{:S(2)}, u32[]{:S(2)}) collective-permute-start(bf16[12,64,128]{2,1,0:T(8,128)(2,1)S(1)} %get-tuple-element.213), channel_id=1, source_target_pairs={{0,2},{1,3},{2,0},{3,1},{4,6},{5,7},{6,4},{7,5},{8,10},{9,11},{10,... | collective-permute-start | bytes 589832 | tf_op jit(solution)/shard_map/ppermute | solution.py:919
  91.1 15.6 %collective-permute-start.33 = (bf16[36,64,128]{2,1,0:T(8,128)(2,1)S(1)}, bf16[36,64,128]{2,1,0:T(8,128)(2,1)S(1)}, u32[]{:S(2)}, u32[]{:S(2)}) collective-permute-start(bf16[36,64,128]{2,1,0:T(8,128)(2,1)S(1)} %get-tuple-element.226), channel_id=1, source_target_pairs={{0,2},{1,3},{2,0},{3,1},{4,6},{5,7},{6,4},{7,5},{8,10},{9,11},{10,... | collective-permute-start | bytes 1769480 | tf_op jit(solution)/shard_map/ppermute | solution.py:919
  91.9 14.9 %collective-permute-start.32 = (bf16[36,128,128]{2,1,0:T(8,128)(2,1)S(1)}, bf16[36,128,128]{2,1,0:T(8,128)(2,1)S(1)}, u32[]{:S(2)}, u32[]{:S(2)}) collective-permute-start(bf16[36,128,128]{2,1,0:T(8,128)(2,1)S(1)} %get-tuple-element.223.a0), channel_id=1, source_target_pairs={{0,1},{1,0},{2,3},{3,2},{4,5},{5,4},{6,7},{7,6},{8,9},{9,8},{10,11... | collective-permute-start | bytes 3538952 | tf_op jit(solution)/shard_map/ppermute | solution.py:915
  91.9 14.8 %collective-permute-start.34 = (bf16[36,64,128]{2,1,0:T(8,128)(2,1)S(1)}, bf16[36,64,128]{2,1,0:T(8,128)(2,1)S(1)}, u32[]{:S(2)}, u32[]{:S(2)}) collective-permute-start(bf16[36,64,128]{2,1,0:T(8,128)(2,1)S(1)} %get-tuple-element.224.a2), channel_id=1, source_target_pairs={{0,1},{1,0},{2,3},{3,2},{4,5},{5,4},{6,7},{7,6},{8,9},{9,8},{10,11... | collective-permute-start | bytes 1769480 | tf_op jit(solution)/shard_map/ppermute | solution.py:915
  125.6 16.8 %collective-permute-start.38 = (bf16[20,128,128]{2,1,0:T(8,128)(2,1)S(1)}, bf16[20,128,128]{2,1,0:T(8,128)(2,1)S(1)}, u32[]{:S(2)}, u32[]{:S(2)}) collective-permute-start(bf16[20,128,128]{2,1,0:T(8,128)(2,1)S(1)} %fusion.4), channel_id=1, source_target_pairs={{0,2},{1,3},{2,0},{3,1},{4,6},{5,7},{6,4},{7,5},{8,10},{9,11},{10,... | collective-permute-start | bytes 1966088 | tf_op jit(solution)/shard_map/ppermute | solution.py:919
  147.2 14.2 %collective-permute-start.41 = (bf16[16,128,128]{2,1,0:T(8,128)(2,1)S(1)}, bf16[16,128,128]{2,1,0:T(8,128)(2,1)S(1)}, u32[]{:S(2)}, u32[]{:S(2)}) collective-permute-start(bf16[16,128,128]{2,1,0:T(8,128)(2,1)S(1)} %fusion.6), channel_id=1, source_target_pairs={{0,2},{1,3},{2,0},{3,1},{4,6},{5,7},{6,4},{7,5},{8,10},{9,11},{10,... | collective-permute-start | bytes 1572872 | tf_op jit(solution)/shard_map/ppermute | solution.py:919
  164.6 17.4 %collective-permute-start.44 = (bf16[20,128,128]{2,1,0:T(8,128)(2,1)S(1)}, bf16[20,128,128]{2,1,0:T(8,128)(2,1)S(1)}, u32[]{:S(2)}, u32[]{:S(2)}) collective-permute-start(bf16[20,128,128]{2,1,0:T(8,128)(2,1)S(1)} %fusion.5), channel_id=1, source_target_pairs={{0,2},{1,3},{2,0},{3,1},{4,6},{5,7},{6,4},{7,5},{8,10},{9,11},{10,... | collective-permute-start | bytes 1966088 | tf_op jit(solution)/shard_map/ppermute | solution.py:919
  182.7 33.8 %collective-permute-start.49 = (bf16[12,128,128]{2,1,0:T(8,128)(2,1)S(1)}, bf16[12,128,128]{2,1,0:T(8,128)(2,1)S(1)}, u32[]{:S(2)}, u32[]{:S(2)}) collective-permute-start(bf16[12,128,128]{2,1,0:T(8,128)(2,1)S(1)} %fusion.8), channel_id=1, source_target_pairs={{0,2},{1,3},{2,0},{3,1},{4,6},{5,7},{6,4},{7,5},{8,10},{9,11},{10,... | collective-permute-start | bytes 1179656 | tf_op jit(solution)/shard_map/ppermute | solution.py:919
  184.1 32.4 %collective-permute-start.48 = (bf16[16,128,128]{2,1,0:T(8,128)(2,1)S(1)}, bf16[16,128,128]{2,1,0:T(8,128)(2,1)S(1)}, u32[]{:S(2)}, u32[]{:S(2)}) collective-permute-start(bf16[16,128,128]{2,1,0:T(8,128)(2,1)S(1)} %fusion.7), channel_id=1, source_target_pairs={{0,2},{1,3},{2,0},{3,1},{4,6},{5,7},{6,4},{7,5},{8,10},{9,11},{10,... | collective-permute-start | bytes 1572872 | tf_op jit(solution)/shard_map/ppermute | solution.py:919
  188.4 9.9 %collective-permute-start.46 = (bf16[2,12,128,128]{3,2,1,0:T(8,128)(2,1)S(1)}, bf16[2,12,128,128]{3,2,1,0:T(8,128)(2,1)S(1)}, u32[]{:S(2)}, u32[]{:S(2)}) collective-permute-start(bf16[2,12,128,128]{3,2,1,0:T(8,128)(2,1)S(1)} %get-tuple-element.295), channel_id=1, source_target_pairs={{0,1},{1,0},{2,3},{3,2},{4,5},{5,4},{6,7},{7,6},{8,9},{9,8},{10,11... | collective-permute-start | bytes 2359304 | tf_op jit(solution)/shard_map/ppermute | solution.py:915
  198.5 15.5 %collective-permute-start.47 = (bf16[12,128,128]{2,1,0:T(8,128)(2,1)S(1)}, bf16[12,128,128]{2,1,0:T(8,128)(2,1)S(1)}, u32[]{:S(2)}, u32[]{:S(2)}) collective-permute-start(bf16[12,128,128]{2,1,0:T(8,128)(2,1)S(1)} %fusion.9), channel_id=1, source_target_pairs={{0,2},{1,3},{2,0},{3,1},{4,6},{5,7},{6,4},{7,5},{8,10},{9,11},{10,... | collective-permute-start | bytes 1179656 | tf_op jit(solution)/shard_map/ppermute | solution.py:919
  225.9 9.3 %collective-permute-start.56 = (bf16[1536,128]{1,0:T(8,128)(2,1)S(1)}, bf16[1536,128]{1,0:T(8,128)(2,1)S(1)}, u32[]{:S(2)}, u32[]{:S(2)}) collective-permute-start(bf16[1536,128]{1,0:T(8,128)(2,1)S(1)} %pad_maximum_fusion), channel_id=1, source_target_pairs={{0,8},{8,16},{16,24},{24,28},{28,20},{20,12},{12,4},{4,0},{1,9},{9... | collective-permute-start | bytes 1179656 | tf_op jit(solution)/shard_map/ppermute | solution.py:850
  226.5 9.1 %collective-permute-start.57 = (bf16[1536,128]{1,0:T(8,128)(2,1)S(1)}, bf16[1536,128]{1,0:T(8,128)(2,1)S(1)}, u32[]{:S(2)}, u32[]{:S(2)}) collective-permute-start(bf16[1536,128]{1,0:T(8,128)(2,1)S(1)} %pad_maximum_fusion.1), channel_id=1, source_target_pairs={{0,4},{8,0},{16,8},{24,16},{28,24},{20,28},{12,20},{4,12},{1,5},{9... | collective-permute-start | bytes 1179656 | tf_op jit(solution)/shard_map/ppermute | solution.py:850
  236.7 8.5 %collective-permute-start.59 = (bf16[1536,128]{1,0:T(8,128)(2,1)}, bf16[1536,128]{1,0:T(8,128)(2,1)}, u32[]{:S(2)}, u32[]{:S(2)}) collective-permute-start(bf16[1536,128]{1,0:T(8,128)(2,1)} %get-tuple-element.315), channel_id=1, source_target_pairs={{0,8},{8,16},{16,24},{24,28},{28,20},{20,12},{12,4},{4,0},{1,9},{9... | collective-permute-start | bytes 1179656 | tf_op jit(solution)/shard_map/ppermute | solution.py:850
  238.2 9.0 %collective-permute-start.60 = (bf16[1536,128]{1,0:T(8,128)(2,1)}, bf16[1536,128]{1,0:T(8,128)(2,1)}, u32[]{:S(2)}, u32[]{:S(2)}) collective-permute-start(bf16[1536,128]{1,0:T(8,128)(2,1)} %get-tuple-element.316), channel_id=1, source_target_pairs={{0,4},{8,0},{16,8},{24,16},{28,24},{20,28},{12,20},{4,12},{1,5},{9... | collective-permute-start | bytes 1179656 | tf_op jit(solution)/shard_map/ppermute | solution.py:850
  248.7 7.8 %collective-permute-start.64 = (bf16[1536,128]{1,0:T(8,128)(2,1)S(1)}, bf16[1536,128]{1,0:T(8,128)(2,1)S(1)}, u32[]{:S(2)}, u32[]{:S(2)}) collective-permute-start(bf16[1536,128]{1,0:T(8,128)(2,1)S(1)} %get-tuple-element.317), channel_id=1, source_target_pairs={{0,8},{8,16},{16,24},{24,28},{28,20},{20,12},{12,4},{4,0},{1,9},{9... | collective-permute-start | bytes 1179656 | tf_op jit(solution)/shard_map/ppermute | solution.py:850
  (102 other events, 686.3 us)
